TPU v7x, 32 devices: a whole 2x2x4 slice. The times are simulated.
32 devices in a mesh: fsdp: 32 (over z, y, x, core).
Axes of the slice: x: 2, y: 2, z: 4, core: 2. Of those that a mesh axis runs over, the one named last changes fastest.
Arguments:
- tokens: bfloat16 [16384, 1024], P('fsdp'), may hold values from -6 to 6
- lengths: int32 [32], P('fsdp'), may hold values from 1 to 512, 10240 in all
- routes: int32 [16384, 8], P('fsdp'), may hold values from 0 to 15, all different within a row; in each aligned block of 512 rows (0 to 511, 512 to 1023, ...) at most 384 rows name the same one
- attention_gain: bfloat16 [1024], P('fsdp'), may hold values from 0.25 to 1.75
- query_weight: bfloat16 [1024, 1024], P('fsdp'), may hold values from -1.75 to 1.75
- key_weight: bfloat16 [1024, 512], P('fsdp'), may hold values from -1.75 to 1.75
- value_weight: bfloat16 [1024, 512], P('fsdp'), may hold values from -0.1875 to 0.1875
- output_weight: bfloat16 [1024, 1024], P(None, 'fsdp'), may hold values from -6 to 6
- expert_gain: bfloat16 [1024], P('fsdp'), may hold values from 0.25 to 1.75
- router_weight: bfloat16 [1024, 16], P('fsdp'), may hold values from -0.25 to 0.25
- gate_weight: bfloat16 [16, 1024, 512], P(None, 'fsdp'), may hold values from -0.1875 to 0.1875
- up_weight: bfloat16 [16, 1024, 512], P(None, 'fsdp'), may hold values from -0.1875 to 0.1875
- down_weight: bfloat16 [16, 512, 1024], P(None, None, 'fsdp'), may hold values from -6 to 6
- cotangent: bfloat16 [16384, 1024], P('fsdp'), may hold values from -6 to 6
Outputs:
- layer_out: bfloat16 [16384, 1024], P('fsdp')
- grad_tokens: float32 [16384, 1024], P('fsdp')
- grad_attention_gain: float32 [1024], P('fsdp')
- grad_query_weight: float32 [1024, 1024], P('fsdp')
- grad_key_weight: float32 [1024, 512], P('fsdp')
- grad_value_weight: float32 [1024, 512], P('fsdp')
- grad_output_weight: float32 [1024, 1024], P(None, 'fsdp')
- grad_expert_gain: float32 [1024], P('fsdp')
- grad_router_weight: float32 [1024, 16], P('fsdp')
- grad_gate_weight: float32 [16, 1024, 512], P(None, 'fsdp')
- grad_up_weight: float32 [16, 1024, 512], P(None, 'fsdp')
- grad_down_weight: float32 [16, 512, 1024], P(None, None, 'fsdp')
Inputs may be any that keep to these rules, and one draw needn't show every extreme that they name: `lengths`: each device's 512 rows hold one sequence of this length, followed by padding rows. The longest is exactly 512, and they sum to 10240. `routes`: each row names 8 different experts. Among the 512 rows of one device no expert is named by more than 384 rows, a bound that some block reaches.
All inputs are finite; a program needn't handle non-finite values.
Results may differ from a plain program's by a relative error of at most 0.015.
The roundings to bfloat16 on the way count: a program that leaves them out, or rounds other values in their place, can miss the bound.
Values may be sent and summed in bfloat16 or wider, within the bound.
No kernel may reach another device: no remote copies, remote signals or barrier semaphores. Data moves between devices by JAX's collectives and lax.ppermute only.
A program may use at most 384 MiB of HBM per device.

v0:
```python
import jax
import jax.numpy as jnp
from jax import lax
from jax.sharding import PartitionSpec as P

HEADS = 16
KV_HEADS = 8
HEAD_DIM = 64
EXPERTS = 16
CAP = 384


norm_eps = 1e-06
attention_scale = 0.015625
residual_scale = 0.22
rope_base = 10000.0
masked_value = -1e30


def rope_tables(row_count):
    half_dim = HEAD_DIM // 2
    frequency = rope_base ** (-2.0 * jnp.arange(half_dim, dtype=jnp.float32) / HEAD_DIM)
    angles = jnp.arange(row_count, dtype=jnp.float32)[:, None] * frequency[None, :]
    angles = jnp.concatenate([angles, angles], axis=1)
    return (jnp.cos(angles), jnp.sin(angles))


def rotate_apply(values, cosine_table, sine_table):
    half_dim = values.shape[-1] // 2
    turned = jnp.concatenate([-values[..., half_dim:], values[..., :half_dim]], axis=-1)
    return values * cosine_table + turned * sine_table


def rotate_back(grads, cosine_table, sine_table):
    half_dim = grads.shape[-1] // 2
    scaled = grads * sine_table
    turned = jnp.concatenate([scaled[..., half_dim:], -scaled[..., :half_dim]], axis=-1)
    return grads * cosine_table + turned


def norm_rows(values, gain_row):
    row_scale = lax.rsqrt(jnp.mean(values * values, axis=-1, keepdims=True) + norm_eps)
    return (row_scale, values * row_scale * gain_row)


def norm_back(values, row_scale, gain_row, normed_grad):
    weighted = normed_grad * gain_row
    grad_gain = jnp.sum(normed_grad * values * row_scale, axis=0)
    correction = jnp.mean(weighted * values, axis=-1, keepdims=True)
    return (row_scale * weighted - values * row_scale**3 * correction, grad_gain)


def attention_scores(query_rot, key_rot, allowed):
    raw_scores = jnp.einsum(
        "qkgd,pkd->kgqp", query_rot, key_rot, preferred_element_type=jnp.float32
    )
    return jnp.where(allowed, attention_scale * raw_scores, masked_value)


def local(
    tokens,
    lengths,
    routes,
    attention_gain,
    query_weight,
    key_weight,
    value_weight,
    output_weight,
    expert_gain,
    router_weight,
    gate_weight,
    up_weight,
    down_weight,
    cotangent,
):
    attention_full = (
        lax.all_gather(attention_gain, "fsdp", axis=0, tiled=True),
        lax.all_gather(query_weight, "fsdp", axis=0, tiled=True),
        lax.all_gather(key_weight, "fsdp", axis=0, tiled=True),
        lax.all_gather(value_weight, "fsdp", axis=0, tiled=True),
        lax.all_gather(output_weight, "fsdp", axis=1, tiled=True),
    )
    expert_full = (
        lax.all_gather(expert_gain, "fsdp", axis=0, tiled=True),
        lax.all_gather(router_weight, "fsdp", axis=0, tiled=True),
        lax.all_gather(gate_weight, "fsdp", axis=1, tiled=True),
        lax.all_gather(up_weight, "fsdp", axis=1, tiled=True),
        lax.all_gather(down_weight, "fsdp", axis=2, tiled=True),
    )
    gain_one, query_full, key_full, value_full, output_full = attention_full
    gain_two, router_full, gate_full, up_full, down_full = expert_full
    inputs = tokens.astype(jnp.float32)
    row_count = inputs.shape[0]
    width = inputs.shape[1]
    top_count = routes.shape[1]
    group_size = HEADS // KV_HEADS
    cosine_table, sine_table = rope_tables(row_count)
    scale_one, normed_raw = norm_rows(inputs, gain_one.astype(jnp.float32))
    normed_one = normed_raw.astype(jnp.bfloat16)
    queries = jnp.dot(normed_one, query_full, preferred_element_type=jnp.float32).reshape(
        row_count, KV_HEADS, group_size, HEAD_DIM
    )
    key_rows = jnp.dot(normed_one, key_full, preferred_element_type=jnp.float32).reshape(
        row_count, KV_HEADS, HEAD_DIM
    )
    value_rows = (
        jnp.dot(normed_one, value_full, preferred_element_type=jnp.float32)
        .astype(jnp.bfloat16)
        .reshape(row_count, KV_HEADS, HEAD_DIM)
    )
    query_rot = rotate_apply(
        queries, cosine_table[:, None, None, :], sine_table[:, None, None, :]
    ).astype(jnp.bfloat16)
    key_rot = rotate_apply(key_rows, cosine_table[:, None, :], sine_table[:, None, :]).astype(
        jnp.bfloat16
    )
    position = jnp.arange(row_count, dtype=jnp.int32)
    allowed = (position[None, :] <= position[:, None]) & (position[None, :] < lengths[0])
    scores = attention_scores(query_rot, key_rot, allowed)
    maxima = jnp.max(scores, axis=-1, keepdims=True)
    exponent = jnp.exp(scores - maxima)
    totals = jnp.sum(exponent, axis=-1, keepdims=True)
    log_total = maxima + jnp.log(totals)
    softmax_rows = exponent / totals
    mixed = (
        jnp.einsum(
            "kgqp,pkd->qkgd",
            softmax_rows.astype(jnp.bfloat16),
            value_rows,
            preferred_element_type=jnp.float32,
        )
        .astype(jnp.bfloat16)
        .reshape(row_count, HEADS * HEAD_DIM)
    )
    branch = jnp.dot(mixed, output_full, preferred_element_type=jnp.float32)
    middle = inputs + residual_scale * branch
    scale_two, normed_raw_two = norm_rows(middle, gain_two.astype(jnp.float32))
    normed_two = normed_raw_two.astype(jnp.bfloat16)
    logits = jnp.dot(normed_two, router_full, preferred_element_type=jnp.float32)
    expert_ids = jnp.arange(EXPERTS, dtype=jnp.int32)
    route_match = routes[:, :, None] == expert_ids[None, None, :]
    chosen = jnp.sum(jnp.where(route_match, logits[:, None, :], 0.0), axis=2)
    gate_values = jax.nn.softmax(chosen, axis=-1)
    route_hits = jnp.sum(route_match.astype(jnp.int32), axis=1)
    before = jnp.cumsum(route_hits, axis=0) - route_hits
    slot_index = jnp.sum(jnp.where(route_match, before[:, None, :], 0), axis=2)
    where_to = (routes * CAP + slot_index).reshape(-1)
    token_of = (
        jnp.full((EXPERTS * CAP,), row_count, jnp.int32)
        .at[where_to]
        .set(jnp.repeat(position, top_count))
    )
    padded_rows = jnp.concatenate([normed_two, jnp.zeros((1, width), jnp.bfloat16)], axis=0)
    expert_in = padded_rows[token_of].reshape(EXPERTS, CAP, width)
    gate_pre = jnp.einsum("ecd,edf->ecf", expert_in, gate_full, preferred_element_type=jnp.float32)
    up_pre = jnp.einsum("ecd,edf->ecf", expert_in, up_full, preferred_element_type=jnp.float32)
    sigmoid_gate = jax.nn.sigmoid(gate_pre)
    activated = gate_pre * sigmoid_gate
    inner = (activated * up_pre).astype(jnp.bfloat16)
    expert_out = jnp.einsum(
        "ecf,efd->ecd", inner, down_full, preferred_element_type=jnp.float32
    ).reshape(EXPERTS * CAP, width)
    picked = expert_out[where_to].reshape(row_count, top_count, width)
    mixture = jnp.sum(gate_values[:, :, None] * picked, axis=1)
    layer_out = (middle + residual_scale * mixture).astype(jnp.bfloat16)
    attention_full = (
        lax.all_gather(attention_gain, "fsdp", axis=0, tiled=True),
        lax.all_gather(query_weight, "fsdp", axis=0, tiled=True),
        lax.all_gather(key_weight, "fsdp", axis=0, tiled=True),
        lax.all_gather(value_weight, "fsdp", axis=0, tiled=True),
        lax.all_gather(output_weight, "fsdp", axis=1, tiled=True),
    )
    expert_full = (
        lax.all_gather(expert_gain, "fsdp", axis=0, tiled=True),
        lax.all_gather(router_weight, "fsdp", axis=0, tiled=True),
        lax.all_gather(gate_weight, "fsdp", axis=1, tiled=True),
        lax.all_gather(up_weight, "fsdp", axis=1, tiled=True),
        lax.all_gather(down_weight, "fsdp", axis=2, tiled=True),
    )
    gain_one, query_full, key_full, value_full, output_full = attention_full
    gain_two, router_full, gate_full, up_full, down_full = expert_full
    upstream = cotangent.astype(jnp.float32)
    mix_grad = residual_scale * upstream
    gate_grad = jnp.sum(picked * mix_grad[:, None, :], axis=2)
    chosen_grad = gate_values * (
        gate_grad - jnp.sum(gate_values * gate_grad, axis=1, keepdims=True)
    )
    logit_grad = jnp.sum(jnp.where(route_match, chosen_grad[:, :, None], 0.0), axis=1).astype(
        jnp.bfloat16
    )
    slot_gate = jnp.zeros((EXPERTS * CAP,), jnp.float32).at[where_to].set(gate_values.reshape(-1))
    padded_grad = jnp.concatenate([mix_grad, jnp.zeros((1, width), jnp.float32)], axis=0)
    out_grad = (
        (slot_gate[:, None] * padded_grad[token_of])
        .astype(jnp.bfloat16)
        .reshape(EXPERTS, CAP, width)
    )
    inner_grad = jnp.einsum("ecd,efd->ecf", out_grad, down_full, preferred_element_type=jnp.float32)
    gate_pre_grad = (
        inner_grad * up_pre * sigmoid_gate * (1.0 + gate_pre * (1.0 - sigmoid_gate))
    ).astype(jnp.bfloat16)
    up_pre_grad = (inner_grad * activated).astype(jnp.bfloat16)
    grad_down = jnp.einsum("ecf,ecd->efd", inner, out_grad, preferred_element_type=jnp.float32)
    grad_gate = jnp.einsum(
        "ecd,ecf->edf", expert_in, gate_pre_grad, preferred_element_type=jnp.float32
    )
    grad_up = jnp.einsum("ecd,ecf->edf", expert_in, up_pre_grad, preferred_element_type=jnp.float32)
    slot_grad = jnp.einsum(
        "ecf,edf->ecd", gate_pre_grad, gate_full, preferred_element_type=jnp.float32
    )
    slot_grad = (
        slot_grad
        + jnp.einsum("ecf,edf->ecd", up_pre_grad, up_full, preferred_element_type=jnp.float32)
    ).reshape(EXPERTS * CAP, width)
    normed_two_grad = jnp.sum(slot_grad[where_to].reshape(row_count, top_count, width), axis=1)
    normed_two_grad = normed_two_grad + jnp.dot(
        logit_grad, router_full.T, preferred_element_type=jnp.float32
    )
    grad_router = jnp.dot(normed_two.T, logit_grad, preferred_element_type=jnp.float32)
    middle_norm_grad, grad_gain_two = norm_back(
        middle, scale_two, gain_two.astype(jnp.float32), normed_two_grad
    )
    middle_grad = upstream + middle_norm_grad
    branch_grad = (residual_scale * middle_grad).astype(jnp.bfloat16)
    grad_output = jnp.dot(mixed.T, branch_grad, preferred_element_type=jnp.float32)
    mixed_grad = (
        jnp.dot(branch_grad, output_full.T, preferred_element_type=jnp.float32)
        .astype(jnp.bfloat16)
        .reshape(row_count, KV_HEADS, group_size, HEAD_DIM)
    )
    scores_again = attention_scores(query_rot, key_rot, allowed)
    softmax_again = jnp.exp(scores_again - log_total)
    prob_grad = jnp.einsum(
        "qkgd,pkd->kgqp", mixed_grad, value_rows, preferred_element_type=jnp.float32
    )
    row_delta = jnp.sum(prob_grad * softmax_again, axis=-1, keepdims=True)
    score_grad = (attention_scale * softmax_again * (prob_grad - row_delta)).astype(jnp.bfloat16)
    value_grad = (
        jnp.einsum(
            "kgqp,qkgd->pkd",
            softmax_again.astype(jnp.bfloat16),
            mixed_grad,
            preferred_element_type=jnp.float32,
        )
        .astype(jnp.bfloat16)
        .reshape(row_count, KV_HEADS * HEAD_DIM)
    )
    query_rot_grad = jnp.einsum(
        "kgqp,pkd->qkgd", score_grad, key_rot, preferred_element_type=jnp.float32
    )
    key_rot_grad = jnp.einsum(
        "kgqp,qkgd->pkd", score_grad, query_rot, preferred_element_type=jnp.float32
    )
    query_grad = (
        rotate_back(query_rot_grad, cosine_table[:, None, None, :], sine_table[:, None, None, :])
        .astype(jnp.bfloat16)
        .reshape(row_count, HEADS * HEAD_DIM)
    )
    key_grad = (
        rotate_back(key_rot_grad, cosine_table[:, None, :], sine_table[:, None, :])
        .astype(jnp.bfloat16)
        .reshape(row_count, KV_HEADS * HEAD_DIM)
    )
    grad_query = jnp.dot(normed_one.T, query_grad, preferred_element_type=jnp.float32)
    grad_key = jnp.dot(normed_one.T, key_grad, preferred_element_type=jnp.float32)
    grad_value = jnp.dot(normed_one.T, value_grad, preferred_element_type=jnp.float32)
    normed_one_grad = jnp.dot(query_grad, query_full.T, preferred_element_type=jnp.float32)
    normed_one_grad = normed_one_grad + jnp.dot(
        key_grad, key_full.T, preferred_element_type=jnp.float32
    )
    normed_one_grad = normed_one_grad + jnp.dot(
        value_grad, value_full.T, preferred_element_type=jnp.float32
    )
    input_norm_grad, grad_gain_one = norm_back(
        inputs, scale_one, gain_one.astype(jnp.float32), normed_one_grad
    )
    grad_tokens = middle_grad + input_norm_grad
    every_shard = (
        lax.psum_scatter(grad_gain_one, "fsdp", scatter_dimension=0, tiled=True),
        lax.psum_scatter(grad_query, "fsdp", scatter_dimension=0, tiled=True),
        lax.psum_scatter(grad_key, "fsdp", scatter_dimension=0, tiled=True),
        lax.psum_scatter(grad_value, "fsdp", scatter_dimension=0, tiled=True),
        lax.psum_scatter(grad_output, "fsdp", scatter_dimension=1, tiled=True),
        lax.psum_scatter(grad_gain_two, "fsdp", scatter_dimension=0, tiled=True),
        lax.psum_scatter(grad_router, "fsdp", scatter_dimension=0, tiled=True),
        lax.psum_scatter(grad_gate, "fsdp", scatter_dimension=1, tiled=True),
        lax.psum_scatter(grad_up, "fsdp", scatter_dimension=1, tiled=True),
        lax.psum_scatter(grad_down, "fsdp", scatter_dimension=2, tiled=True),
    )
    attention_shards = every_shard[:5]
    expert_shards = every_shard[5:]
    return (
        layer_out,
        grad_tokens,
        attention_shards[0],
        attention_shards[1],
        attention_shards[2],
        attention_shards[3],
        attention_shards[4],
        expert_shards[0],
        expert_shards[1],
        expert_shards[2],
        expert_shards[3],
        expert_shards[4],
    )


def solution(mesh):
    placed = (
        P("fsdp", None),
        P("fsdp"),
        P("fsdp", None),
        P("fsdp"),
        P("fsdp", None),
        P("fsdp", None),
        P("fsdp", None),
        P(None, "fsdp"),
        P("fsdp"),
        P("fsdp", None),
        P(None, "fsdp", None),
        P(None, "fsdp", None),
        P(None, None, "fsdp"),
        P("fsdp", None),
    )
    return jax.shard_map(
        local,
        mesh=mesh,
        in_specs=placed,
        out_specs=(
            P("fsdp", None),
            P("fsdp", None),
            P("fsdp"),
            P("fsdp", None),
            P("fsdp", None),
            P("fsdp", None),
            P(None, "fsdp"),
            P("fsdp"),
            P("fsdp", None),
            P(None, "fsdp", None),
            P(None, "fsdp", None),
            P(None, None, "fsdp"),
        ),
        check_vma=False,
    )
```

profile of v0, /device:TPU:0, one launch (start us, length us, event | category | flops | bytes accessed | tf_op | source)
XLA Modules:
  0.0 2579.2 jit_solution(11686524081487273695)
XLA Ops:
  13.6 42.0 %all-reduce.7 = (bf16[1024]{0:T(1024)(128)(2,1)S(1)}, bf16[1024]{0:T(1024)(128)(2,1)S(1)}) all-reduce(bf16[1024]{0:T(1024)(128)(2,1)S(1)} %dynamic-update-slice, bf16[1024]{0:T(1024)(128)(2,1)S(1)} %dynamic-update-slice.1), channel_id=1, replica_groups=mesh['fsdp'=32] {'fsdp'}, use_global_device_ids=true, to_apply=%add.2 | all-reduce | flops 2048 | bytes 8192
  79.3 27.2 %gather_fusion.2 = f32[6144,1024]{1,0:T(8,128)} fusion(f32[513,1024]{1,0:T(8,128)S(1)} %concatenate.41, s32[6144]{0:T(1024)S(1)} %fusion.42), kind=kCustom, calls=%fused_computation.2 | custom fusion | bytes 50356224 | tf_op jit(solution)/shard_map/gather | solution.py:194
  106.5 24.9 copy.99
  131.4 41.0 %all-gather = bf16[32,32,16]{1,2,0:T(8,128)(2,1)S(1)} all-gather(bf16[1,32,16]{1,2,0:T(8,128)(2,1)S(1)} %bitcast.167), channel_id=1, replica_groups=mesh['fsdp'=32] {'fsdp'}, dimensions={0}, use_global_device_ids=true | all-gather | bytes 33792 | tf_op jit(solution)/shard_map/all_gather | solution.py:85
  208.5 30.6 %all-gather.15.cloned.1.call-done = bf16[1024,1024]{0,1:T(8,128)(2,1)} async-done(((bf16[1024,32]{0,1:T(8,128)(2,1)}), bf16[1024,1024]{0,1:T(8,128)(2,1)}) %all-gather.15.cloned.1.call-update) | async-done | bytes 2097168 | tf_op jit(solution)/shard_map/all_gather | solution.py:81
  243.9 26.8 %gather_fusion = bf16[6144,1024]{1,0:T(8,128)(2,1)} fusion(bf16[513,1024]{1,0:T(8,128)(2,1)S(1)} %concatenate.40, s32[6144]{0:T(1024)S(1)} %fusion.42), kind=kCustom, calls=%fused_computation | custom fusion | bytes 25190400 | tf_op jit(solution)/shard_map/gather | solution.py:154
  288.7 67.0 %all-gather.17.cloned.1.call-done = bf16[16,1024,512]{2,1,0:T(8,128)(2,1)} async-done(((bf16[16,32,512]{2,1,0:T(8,128)(2,1)}), bf16[16,1024,512]{2,1,0:T(8,128)(2,1)}) %all-gather.17.cloned.1.call-update) | async-done | bytes 16777232 | tf_op jit(solution)/shard_map/all_gather | solution.py:86
  373.4 98.5 %all-gather.19.cloned.1.call-done = bf16[16,1024,512]{2,1,0:T(8,128)(2,1)} async-done(((bf16[16,32,512]{2,1,0:T(8,128)(2,1)}), bf16[16,1024,512]{2,1,0:T(8,128)(2,1)}) %all-gather.19.cloned.1.call-update) | async-done | bytes 16777232 | tf_op jit(solution)/shard_map/all_gather | solution.py:87
  489.1 99.0 %all-gather.21.cloned.1.call-done = bf16[16,512,1024]{1,2,0:T(8,128)(2,1)} async-done(((bf16[16,512,32]{1,2,0:T(8,128)(2,1)}), bf16[16,512,1024]{1,2,0:T(8,128)(2,1)}) %all-gather.21.cloned.1.call-update) | async-done | bytes 16777232 | tf_op jit(solution)/shard_map/all_gather | solution.py:88
  588.1 30.4 %multiply_convert_fusion.1 = (bf16[16,384,512]{2,1,0:T(8,128)(2,1)}, bf16[16,384,512]{2,1,0:T(8,128)(2,1)}, bf16[16,384,512]{2,1,0:T(8,128)(2,1)}) fusion(f32[16,384,512]{2,1,0:T(8,128)} %fusion.69, f32[16,384,512]{2,1,0:T(8,128)} %fusion.70, bf16[16,512,1024]{1,2,0:T(8,128)(2,1)} %all-gather.21.cloned.1.call-done, f32[16,384,1024]{1,2,0:T(8,128)} %copy.99, ...), kind=kOutput, calls=%fused_computation.23 | convolution fusion | flops 6502219776 | bytes 86007808 | tf_op jit(solution)/shard_map/ecd,efd->ecf/dot_general | solution.py:198
  636.7 24.0 convolution_add_fusion
  660.7 30.6 %gather_fusion.3 = f32[4096,1024]{1,0:T(8,128)} fusion(f32[6144,1024]{1,0:T(8,128)} %bitcast.135, s32[4096]{0:T(1024)S(1)} %copy-done.35), kind=kCustom, calls=%fused_computation.3 | custom fusion | bytes 33570816 | tf_op jit(solution)/shard_map/gather | solution.py:215
  718.9 30.5 %gather_fusion.1 = f32[4096,1024]{1,0:T(8,128)} fusion(f32[6144,1024]{1,0:T(8,128)} %bitcast.134, s32[4096]{0:T(1024)S(1)} %copy-done.35), kind=kCustom, calls=%fused_computation.1 | custom fusion | bytes 33570816 | tf_op jit(solution)/shard_map/gather | solution.py:163
  838.2 19.9 fusion.75
  858.1 19.8 fusion.76
  878.7 24.7 fusion.12
  911.4 38.9 %all-reduce.6 = (f32[1024]{0:T(1024)S(1)}, f32[1024]{0:T(1024)S(1)}) all-reduce(f32[1024]{0:T(1024)S(1)} %get-tuple-element.16, f32[1024]{0:T(1024)S(1)} %get-tuple-element.14), channel_id=2, replica_groups=mesh['fsdp'=32] {'fsdp'}, use_global_device_ids=true, to_apply=%region_22.23.clone | all-reduce | flops 2048 | bytes 16384
  956.4 117.7 %reduce-scatter.13.cloned.1.call-done = f32[32,512]{1,0:T(8,128)} async-done(((f32[1024,512]{1,0:T(8,128)}), f32[32,512]{1,0:T(8,128)}) %reduce-scatter.13.cloned.1.call-update) | async-done | bytes 65552 | tf_op jit(solution)/shard_map/reduce_scatter | solution.py:281
  1074.1 135.3 %reduce-scatter.15.cloned.1.call-done = f32[32,512]{1,0:T(8,128)} async-done(((f32[1024,512]{1,0:T(8,128)}), f32[32,512]{1,0:T(8,128)}) %reduce-scatter.15.cloned.1.call-update) | async-done | bytes 65552 | tf_op jit(solution)/shard_map/reduce_scatter | solution.py:282
  1209.5 140.0 %reduce-scatter.11.cloned.1.call-done = f32[32,1024]{1,0:T(8,128)} async-done(((f32[1024,1024]{1,0:T(8,128)}), f32[32,1024]{1,0:T(8,128)}) %reduce-scatter.11.cloned.1.call-update) | async-done | bytes 131088 | tf_op jit(solution)/shard_map/reduce_scatter | solution.py:280
  1349.5 140.0 %reduce-scatter.17.cloned.1.call-done = f32[1024,32]{0,1:T(8,128)} async-done(((f32[1024,1024]{0,1:T(8,128)}), f32[1024,32]{0,1:T(8,128)}) %reduce-scatter.17.cloned.1.call-update) | async-done | bytes 131088 | tf_op jit(solution)/shard_map/reduce_scatter | solution.py:283
  1489.4 353.2 %reduce-scatter.19.cloned.1.call-done = f32[16,32,512]{2,1,0:T(8,128)} async-done(((f32[16,1024,512]{2,1,0:T(8,128)}), f32[16,32,512]{2,1,0:T(8,128)}) %reduce-scatter.19.cloned.1.call-update) | async-done | bytes 1048592 | tf_op jit(solution)/shard_map/reduce_scatter | solution.py:286
  1842.6 364.8 %reduce-scatter.21.cloned.1.call-done = f32[16,32,512]{2,1,0:T(8,128)} async-done(((f32[16,1024,512]{2,1,0:T(8,128)}), f32[16,32,512]{2,1,0:T(8,128)}) %reduce-scatter.21.cloned.1.call-update) | async-done | bytes 1048592 | tf_op jit(solution)/shard_map/reduce_scatter | solution.py:287
  2207.4 364.8 %reduce-scatter.23.cloned.1.call-done = f32[16,512,32]{1,2,0:T(8,128)} async-done(((f32[16,512,1024]{1,2,0:T(8,128)}), f32[16,512,32]{1,2,0:T(8,128)}) %reduce-scatter.23.cloned.1.call-update) | async-done | bytes 1048592 | tf_op jit(solution)/shard_map/reduce_scatter | solution.py:288
  (242 shorter events, 271.6 us)
Async XLA Ops:
  7.2 167.5 %all-gather.11.cloned.1.call-start = ((), (), s32[]{:S(2)}) async-start(), calls=%async_computation.9 | async-start | bytes 1081344 | tf_op jit(solution)/shard_map/all_gather | solution.py:79
  7.9 169.3 %all-gather.9.cloned.1.call-start = ((), (), s32[]{:S(2)}) async-start(), calls=%async_computation.8 | async-start | bytes 1081344 | tf_op jit(solution)/shard_map/all_gather | solution.py:80
  8.7 172.5 %all-gather.13.cloned.1.call-start = ((), (), s32[]{:S(2)}) async-start(), calls=%async_computation.10 | async-start | bytes 2162688 | tf_op jit(solution)/shard_map/all_gather | solution.py:78
  9.4 229.8 %all-gather.15.cloned.1.call-start = ((), (), s32[]{:S(2)}) async-start(), calls=%async_computation.11 | async-start | bytes 2162688 | tf_op jit(solution)/shard_map/all_gather | solution.py:81
  10.0 345.8 %all-gather.17.cloned.1.call-start = ((), (), s32[]{:S(2)}) async-start(), calls=%async_computation.12 | async-start | bytes 17301504 | tf_op jit(solution)/shard_map/all_gather | solution.py:86
  10.6 461.3 %all-gather.19.cloned.1.call-start = ((), (), s32[]{:S(2)}) async-start(), calls=%async_computation.13 | async-start | bytes 17301504 | tf_op jit(solution)/shard_map/all_gather | solution.py:87
  11.1 576.9 %all-gather.21.cloned.1.call-start = ((), (), s32[]{:S(2)}) async-start(), calls=%async_computation.14 | async-start | bytes 17301504 | tf_op jit(solution)/shard_map/all_gather | solution.py:88
  11.9 943.1 %reduce-scatter.25.cloned.1.call-start = ((), (), s32[]{:S(2)}) async-start(), calls=%async_computation.22 | async-start | bytes 540672
  55.6 125.5 %copy-start.36 = (f32[1024]{0:T(1024)}, f32[1024]{0:T(1024)S(1)}, u32[]{:S(2)}) copy-start(f32[1024]{0:T(1024)S(1)} %convert_element_type.85) | copy-start | bytes 12292
  56.3 186.5 %copy-start.38 = (f32[1024]{0:T(1024)}, f32[1024]{0:T(1024)S(1)}, u32[]{:S(2)}) copy-start(f32[1024]{0:T(1024)S(1)} %convert_element_type.93) | copy-start | bytes 12292
  106.5 66.5 %copy-start = (bf16[512,1024]{1,0:T(8,128)(2,1)S(1)}, bf16[512,1024]{1,0:T(8,128)(2,1)}, u32[]{:S(2)}) copy-start(bf16[512,1024]{1,0:T(8,128)(2,1)} %param.14) | copy-start | bytes 3145732
  172.6 98.1 %copy-start.31 = (bf16[1024,16]{0,1:T(8,128)(2,1)}, bf16[1024,16]{0,1:T(8,128)(2,1)S(1)}, u32[]{:S(2)}) copy-start(bf16[1024,16]{0,1:T(8,128)(2,1)S(1)} %reshape.427) | copy-start | bytes 98308
  208.5 34.3 %copy-start.20 = (bf16[8,64,2,512]{3,1,2,0:T(8,128)(2,1)}, bf16[8,64,2,512]{3,1,2,0:T(8,128)(2,1)S(1)}, u32[]{:S(2)}) copy-start(bf16[8,64,2,512]{3,1,2,0:T(8,128)(2,1)S(1)} %fusion.26) | copy-start | bytes 3145732
  271.2 102.2 %copy-start.42 = (f32[512]{0:T(512)}, f32[512]{0:T(512)S(1)}, u32[]{:S(2)}) copy-start(f32[512]{0:T(512)S(1)} %reduce_max.19) | copy-start | bytes 6148
  272.4 101.0 %copy-start.21 = (f32[512,8]{1,0:T(8,128)}, f32[512,8]{1,0:T(8,128)S(1)}, u32[]{:S(2)}) copy-start(f32[512,8]{1,0:T(8,128)S(1)} %copy.94) | copy-start | bytes 49156
  288.1 300.0 %copy-start.33 = (f32[16,384]{1,0:T(8,128)}, f32[16,384]{1,0:T(8,128)S(1)}, u32[]{:S(2)}) copy-start(f32[16,384]{1,0:T(8,128)S(1)} %mul.333) | copy-start | bytes 73732
  806.0 268.2 %reduce-scatter.13.cloned.1.call-start = ((), (), s32[]{:S(2)}) async-start(), calls=%async_computation.16 | async-start | bytes 2162688 | tf_op jit(solution)/shard_map/reduce_scatter | solution.py:281
  810.9 398.5 %reduce-scatter.15.cloned.1.call-start = ((), (), s32[]{:S(2)}) async-start(), calls=%async_computation.17 | async-start | bytes 2162688 | tf_op jit(solution)/shard_map/reduce_scatter | solution.py:282
  822.9 526.6 %reduce-scatter.11.cloned.1.call-start = ((), (), s32[]{:S(2)}) async-start(), calls=%async_computation.15 | async-start | bytes 4325376 | tf_op jit(solution)/shard_map/reduce_scatter | solution.py:280
  833.5 655.9 %reduce-scatter.17.cloned.1.call-start = ((), (), s32[]{:S(2)}) async-start(), calls=%async_computation.18 | async-start | bytes 4325376 | tf_op jit(solution)/shard_map/reduce_scatter | solution.py:283
  838.1 1004.5 %reduce-scatter.19.cloned.1.call-start = ((), (), s32[]{:S(2)}) async-start(), calls=%async_computation.19 | async-start | bytes 34603008 | tf_op jit(solution)/shard_map/reduce_scatter | solution.py:286
  858.1 1349.4 %reduce-scatter.21.cloned.1.call-start = ((), (), s32[]{:S(2)}) async-start(), calls=%async_computation.20 | async-start | bytes 34603008 | tf_op jit(solution)/shard_map/reduce_scatter | solution.py:287
  877.9 1694.2 %reduce-scatter.23.cloned.1.call-start = ((), (), s32[]{:S(2)}) async-start(), calls=%async_computation.21 | async-start | bytes 34603008 | tf_op jit(solution)/shard_map/reduce_scatter | solution.py:288
  908.9 42.6 %copy-start.48 = (f32[512]{0:T(512)S(1)}, f32[512]{0:T(512)}, u32[]{:S(2)}) copy-start(f32[512]{0:T(512)} %get-tuple-element.37) | copy-start | bytes 6148
  (47 other events, 482.1 us)
Sparse Core Ops, SparseCore 0:
  10.9 56.3 all-gather.10
  70.1 52.6 all-gather.8
  125.7 55.4 all-gather.12
  183.9 55.2 all-gather.14
  242.0 113.7 all-gather.16
  358.6 113.2 all-gather.18
  474.8 113.2 all-gather.20
  806.1 132.2 reduce-scatter.24
  941.4 132.7 reduce-scatter.12
  1076.8 132.6 reduce-scatter.14
  1212.4 137.0 reduce-scatter.10
  1352.3 137.1 reduce-scatter.16
  1492.4 350.1 reduce-scatter.18
  1845.4 361.9 reduce-scatter.20
  2210.2 361.8 reduce-scatter.22
where the time goes:
time: 2590 us; the launch traced here: 2580 us
  waiting for transfers between devices  1920 us (74%)
  matrix products  278 us (11%)
  local copies, waits for them, and re-layouts  186 us (7%)
  blocking collectives  122 us (5%)
  other arithmetic  58.7 us (2%)
    reduce_scatter x1, waiting for transfers between devices, local(): lax.psum_scatter(grad_up, 'fsdp', scatter_dimension=1, tiled=True)  365 us
    reduce_scatter x1, waiting for transfers between devices, local(): lax.psum_scatter(grad_down, 'fsdp', scatter_dimension=2, tiled=True)  365 us
    reduce_scatter x1, waiting for transfers between devices, local(): lax.psum_scatter(grad_gate, 'fsdp', scatter_dimension=1, tiled=True)  353 us
    reduce_scatter x1, waiting for transfers between devices, local(): lax.psum_scatter(grad_query, 'fsdp', scatter_dimension=0, tiled=True)  140 us
    reduce_scatter x1, waiting for transfers between devices, local(): lax.psum_scatter(grad_output, 'fsdp', scatter_dimension=1, tiled=True)  140 us
    reduce_scatter x1, waiting for transfers between devices, local(): lax.psum_scatter(grad_value, 'fsdp', scatter_dimension=0, tiled=True)  135 us
    reduce_scatter x1, waiting for transfers between devices, local(): lax.psum_scatter(grad_key, 'fsdp', scatter_dimension=0, tiled=True)  118 us
    all_gather x1, waiting for transfers between devices, local(): lax.all_gather(down_weight, 'fsdp', axis=2, tiled=True)  99 us
  transfers between devices with their start and end apart: 15, of which 12 were waited for; matrix products, arithmetic and copies ran while one was open for 12% of the time, Pallas kernels for 0%

commit v1 on v0

v1 whole, which is shorter than its diff:
```python
import jax
import jax.numpy as jnp
from jax import lax
from jax.experimental import pallas as pl
from jax.experimental.pallas import tpu as pltpu
from jax.sharding import PartitionSpec as P

HEADS = 16
KV_HEADS = 8
HEAD_DIM = 64
EXPERTS = 16
MEMBERS = 8
LOCAL_EXPERTS = EXPERTS // MEMBERS
EXTRA = 128

norm_eps = 1e-06
attention_scale = 0.015625
residual_scale = 0.22
rope_base = 10000.0
masked_value = -1e30
f32 = jnp.float32
bf16 = jnp.bfloat16


def rope_tables(row_count):
    half_dim = HEAD_DIM // 2
    frequency = rope_base ** (-2.0 * jnp.arange(half_dim, dtype=jnp.float32) / HEAD_DIM)
    angles = jnp.arange(row_count, dtype=jnp.float32)[:, None] * frequency[None, :]
    angles = jnp.concatenate([angles, angles], axis=1)
    return (jnp.cos(angles), jnp.sin(angles))


def rotate_apply(values, cosine_table, sine_table):
    half_dim = values.shape[-1] // 2
    turned = jnp.concatenate([-values[..., half_dim:], values[..., :half_dim]], axis=-1)
    return values * cosine_table + turned * sine_table


def rotate_back(grads, cosine_table, sine_table):
    half_dim = grads.shape[-1] // 2
    scaled = grads * sine_table
    turned = jnp.concatenate([scaled[..., half_dim:], -scaled[..., :half_dim]], axis=-1)
    return grads * cosine_table + turned


def norm_rows(values, gain_row):
    row_scale = lax.rsqrt(jnp.mean(values * values, axis=-1, keepdims=True) + norm_eps)
    return (row_scale, values * row_scale * gain_row)


def norm_back(values, row_scale, gain_row, normed_grad):
    weighted = normed_grad * gain_row
    grad_gain = jnp.sum(normed_grad * values * row_scale, axis=0)
    correction = jnp.mean(weighted * values, axis=-1, keepdims=True)
    return (row_scale * weighted - values * row_scale**3 * correction, grad_gain)


def attention_scores(query_rot, key_rot, allowed):
    raw_scores = jnp.einsum("qkgd,pkd->kgqp", query_rot, key_rot, preferred_element_type=f32)
    return jnp.where(allowed, attention_scale * raw_scores, masked_value)


class Exchange:
    def __init__(self, count):
        self.count = count
        self.groups = count // MEMBERS
        index = lax.axis_index("fsdp")
        self.member = index % MEMBERS
        self.group = index // MEMBERS

    def swap(self, value, bits):
        return lax.ppermute(value, "fsdp", [(i, i ^ bits) for i in range(self.count)])

    def shift(self, value, senders, step):
        pairs = [
            (g * MEMBERS + m, (g + step) * MEMBERS + m) for g in senders for m in range(MEMBERS)
        ]
        return lax.ppermute(value, "fsdp", pairs)

    def line_gather(self, piece):
        groups = self.groups
        rising, falling = [piece], [piece]
        for step in range(1, groups):
            rising.append(self.shift(rising[-1], range(step - 1, groups - 1), 1))
            falling.append(self.shift(falling[-1], range(1, groups - step + 1), -1))
        found = [piece]
        for step in range(1, groups):
            found.append(jnp.where(self.group >= step, rising[step], falling[groups - step]))
        return found

    def line_reduce(self, pick):
        groups = self.groups
        rising = falling = None
        for step in range(1, groups):
            up = pick((self.group + groups - step) % groups)
            down = pick((self.group + step) % groups)
            up_owner = self.group + groups - step
            down_owner = self.group - groups + step
            if rising is not None:
                up = up + rising.astype(f32)
                down = down + falling.astype(f32)
            del up_owner, down_owner
            rising = self.shift(up.astype(bf16), range(0, step), 1)
            falling = self.shift(down.astype(bf16), range(groups - step, groups), -1)
        own = pick(self.group)
        if rising is None:
            return own
        return own + rising.astype(f32) + falling.astype(f32)

    def group_gather(self, block):
        half = block.shape[0] // 2
        top, low = block[:half], block[half:]
        near_top = self.swap(top, 2)
        far_low = self.swap(low, 4)
        near_low = self.swap(low, 2)
        far_top = self.swap(top, 4)
        cross_top = self.swap(near_top, 4)
        cross_low = self.swap(far_low, 2)
        found = {0: (top, low), 2: (near_top, near_low), 4: (far_top, far_low), 6: (cross_top, cross_low)}
        found[1] = (self.swap(top, 1), self.swap(low, 1))
        for k in (2, 4, 6):
            found[k + 1] = tuple(self.swap(part, 1) for part in found[k])
        return found

    def group_reduce(self, blocks):
        half = blocks[0].shape[0] // 2
        joined = {}
        for k in (6, 2, 4, 0):
            joined[k] = blocks[k].astype(f32) + self.swap(blocks[k ^ 1], 1).astype(f32)
        cross_top = self.swap(joined[6][:half].astype(bf16), 2).astype(f32)
        cross_low = self.swap(joined[6][half:].astype(bf16), 4).astype(f32)
        near_top = self.swap(joined[2][:half].astype(bf16), 2).astype(f32)
        far_low = self.swap(joined[4][half:].astype(bf16), 4).astype(f32)
        near_low = self.swap((joined[2][half:] + cross_low).astype(bf16), 2).astype(f32)
        far_top = self.swap((joined[4][:half] + cross_top).astype(bf16), 4).astype(f32)
        return jnp.concatenate(
            [joined[0][:half] + near_top + far_top, joined[0][half:] + near_low + far_low], axis=0
        )


def dot(left, right):
    return jnp.dot(left, right, preferred_element_type=f32)


def dot_turned(left, right):
    return lax.dot_general(left, right, (((1,), (1,)), ((), ())), preferred_element_type=f32)


def expert_kernel(first_ref, packet_ref, cotangent_ref, weight_ref, out_ref, back_ref, grad_ref,
                  packet_turned, cotangent_turned, out_sum, back_sum, extra_sum):
    width = cotangent_ref.shape[-1]
    rows = cotangent_ref.shape[1]
    first = first_ref[0]

    @pl.when(pl.program_id(0) == 0)
    def _():
        grad_ref[...] = jnp.zeros_like(grad_ref)

    packet_turned[...] = packet_ref[0, :, :width].T
    cotangent_turned[...] = cotangent_ref[0].T
    out_sum[...] = jnp.zeros_like(out_sum)
    back_sum[...] = jnp.zeros_like(back_sum)
    extra_sum[...] = jnp.zeros_like(extra_sum)
    lane = lax.broadcasted_iota(jnp.int32, (rows, EXTRA), 1)

    def one_expert(local, carry):
        expert = first + local
        shares = packet_ref[0, :, width:].astype(f32)
        is_high, is_low = lane == expert, lane == expert + EXPERTS
        share = jnp.sum(jnp.where(is_high | is_low, shares, 0.0), axis=1, keepdims=True)
        normed = packet_ref[0, :, :width]
        upstream = cotangent_ref[0]
        gate_pre = dot(normed, weight_ref[local, 0])
        up_pre = dot(normed, weight_ref[local, 1])
        inner_raw = dot(upstream, weight_ref[local, 2]) * residual_scale
        sigmoid_gate = jax.nn.sigmoid(gate_pre)
        activated = gate_pre * sigmoid_gate
        inner = (activated * up_pre).astype(bf16).astype(f32)
        share_grad = jnp.sum(inner * inner_raw, axis=1, keepdims=True)
        inner_grad = inner_raw * share
        gate_grad = (
            inner_grad * up_pre * sigmoid_gate * (1.0 + gate_pre * (1.0 - sigmoid_gate))
        ).astype(bf16)
        up_grad = (inner_grad * activated).astype(bf16)
        inner_shared = (inner * (share * residual_scale)).astype(bf16)
        out_sum[...] += dot_turned(inner_shared, weight_ref[local, 2])
        back_sum[...] += dot_turned(gate_grad, weight_ref[local, 0]) + dot_turned(
            up_grad, weight_ref[local, 1]
        )
        grad_ref[local, 0] += dot(packet_turned[...], gate_grad)
        grad_ref[local, 1] += dot(packet_turned[...], up_grad)
        grad_ref[local, 2] += dot(cotangent_turned[...], inner_shared)
        high = share_grad.astype(bf16).astype(f32)
        extra_sum[...] += jnp.where(is_high, high, 0.0) + jnp.where(is_low, share_grad - high, 0.0)
        return carry

    lax.fori_loop(0, LOCAL_EXPERTS, one_expert, 0)
    out_ref[0] = out_sum[...].astype(bf16)
    back_ref[0, :, :width] = back_sum[...].astype(bf16)
    back_ref[0, :, width:] = extra_sum[...].astype(bf16)


def run_experts(first, packets, cotangents, weights):
    block_count, rows, wide = packets.shape
    width = cotangents.shape[-1]
    hidden = weights.shape[-1]
    grad_shape = (LOCAL_EXPERTS, 3, width, hidden)
    return pl.pallas_call(
        expert_kernel,
        grid_spec=pltpu.PrefetchScalarGridSpec(
            num_scalar_prefetch=1,
            grid=(block_count,),
            in_specs=[
                pl.BlockSpec((1, rows, wide), lambda i, s: (i, 0, 0)),
                pl.BlockSpec((1, rows, width), lambda i, s: (i, 0, 0)),
                pl.BlockSpec(grad_shape, lambda i, s: (0, 0, 0, 0), pipeline_mode=pl.Buffered(1)),
            ],
            out_specs=[
                pl.BlockSpec((1, rows, width), lambda i, s: (i, 0, 0)),
                pl.BlockSpec((1, rows, wide), lambda i, s: (i, 0, 0)),
                pl.BlockSpec(grad_shape, lambda i, s: (0, 0, 0, 0), pipeline_mode=pl.Buffered(1)),
            ],
            scratch_shapes=[
                pltpu.VMEM((width, rows), bf16),
                pltpu.VMEM((width, rows), bf16),
                pltpu.VMEM((rows, width), f32),
                pltpu.VMEM((rows, width), f32),
                pltpu.VMEM((rows, EXTRA), f32),
            ],
        ),
        out_shape=[
            jax.ShapeDtypeStruct((block_count, rows, width), bf16),
            jax.ShapeDtypeStruct((block_count, rows, wide), bf16),
            jax.ShapeDtypeStruct(grad_shape, f32),
        ],
        compiler_params=pltpu.CompilerParams(vmem_limit_bytes=60 * 1024 * 1024),
        cost_estimate=pl.CostEstimate(
            flops=block_count * LOCAL_EXPERTS * 9 * 2 * rows * width * hidden,
            bytes_accessed=block_count * rows * width * 8 + 36 * width * hidden,
            transcendentals=block_count * LOCAL_EXPERTS * rows * hidden,
        ),
        name="experts",
    )(first, packets, cotangents, weights)


def local(
    tokens,
    lengths,
    routes,
    attention_gain,
    query_weight,
    key_weight,
    value_weight,
    output_weight,
    expert_gain,
    router_weight,
    gate_weight,
    up_weight,
    down_weight,
    cotangent,
    *,
    count,
):
    links = Exchange(count)
    member, group, groups = links.member, links.group, links.groups
    row_count, width = tokens.shape
    shard = query_weight.shape[0]
    hidden = gate_weight.shape[2]
    head_columns, kv_columns = HEADS * HEAD_DIM, KV_HEADS * HEAD_DIM
    group_size = HEADS // KV_HEADS

    packed = jnp.concatenate(
        [
            query_weight,
            key_weight,
            value_weight,
            output_weight.T,
            router_weight,
            attention_gain[:, None],
            expert_gain[:, None],
            jnp.zeros((shard, EXTRA - EXPERTS - 2), bf16),
        ],
        axis=1,
    )
    pack_width = packed.shape[1]
    line = links.line_gather(packed)
    column = jnp.zeros((groups, shard, pack_width), bf16)
    for back, piece in enumerate(line):
        column = lax.dynamic_update_index_in_dim(column, piece, (group + groups - back) % groups, 0)
    spread = links.group_gather(column.reshape(groups * shard, pack_width))
    whole = jnp.zeros((groups, MEMBERS, shard, pack_width), bf16)
    for k in range(MEMBERS):
        part = jnp.concatenate(spread[k], axis=0).reshape(groups, shard, pack_width)
        whole = lax.dynamic_update_index_in_dim(whole, part, member ^ k, 1)
    whole = whole.reshape(width, pack_width)
    at_output = head_columns + 2 * kv_columns
    at_extra = at_output + head_columns
    qkv_full = whole[:, :at_output]
    output_turned = whole[:, at_output:at_extra]
    router_full = whole[:, at_extra : at_extra + EXPERTS]
    gain_one = whole[:, at_extra + EXPERTS].astype(f32)
    gain_two = whole[:, at_extra + EXPERTS + 1].astype(f32)

    mine = jnp.stack([gate_weight, up_weight, down_weight.transpose(0, 2, 1)], axis=1)
    mine = mine.reshape(MEMBERS, LOCAL_EXPERTS, 3, shard, hidden)
    shelf = jnp.zeros((LOCAL_EXPERTS, 3, MEMBERS, shard, hidden), bf16)
    for k in range(MEMBERS):
        part = lax.dynamic_index_in_dim(mine, member ^ k, 0, keepdims=False)
        if k:
            part = links.swap(part, k)
        shelf = lax.dynamic_update_index_in_dim(shelf, part, member ^ k, 2)
    shelf = shelf.reshape(LOCAL_EXPERTS, 3, MEMBERS * shard, hidden)
    expert_full = jnp.zeros((LOCAL_EXPERTS, 3, groups, MEMBERS * shard, hidden), bf16)
    for back, piece in enumerate(links.line_gather(shelf)):
        expert_full = lax.dynamic_update_index_in_dim(
            expert_full, piece, (group + groups - back) % groups, 2
        )
    expert_full = expert_full.reshape(LOCAL_EXPERTS, 3, width, hidden)
    cotangents = links.group_gather(cotangent)

    inputs = tokens.astype(f32)
    cosine_table, sine_table = rope_tables(row_count)
    scale_one, normed_raw = norm_rows(inputs, gain_one)
    normed_one = normed_raw.astype(bf16)
    projected = dot(normed_one, qkv_full)
    queries = projected[:, :head_columns].reshape(row_count, KV_HEADS, group_size, HEAD_DIM)
    key_rows = projected[:, head_columns : head_columns + kv_columns].reshape(
        row_count, KV_HEADS, HEAD_DIM
    )
    value_rows = (
        projected[:, head_columns + kv_columns :].astype(bf16).reshape(row_count, KV_HEADS, HEAD_DIM)
    )
    query_rot = rotate_apply(
        queries, cosine_table[:, None, None, :], sine_table[:, None, None, :]
    ).astype(bf16)
    key_rot = rotate_apply(key_rows, cosine_table[:, None, :], sine_table[:, None, :]).astype(bf16)
    position = jnp.arange(row_count, dtype=jnp.int32)
    allowed = (position[None, :] <= position[:, None]) & (position[None, :] < lengths[0])
    scores = attention_scores(query_rot, key_rot, allowed)
    maxima = jnp.max(scores, axis=-1, keepdims=True)
    exponent = jnp.exp(scores - maxima)
    totals = jnp.sum(exponent, axis=-1, keepdims=True)
    log_total = maxima + jnp.log(totals)
    softmax_rows = exponent / totals
    mixed = (
        jnp.einsum("kgqp,pkd->qkgd", softmax_rows.astype(bf16), value_rows, preferred_element_type=f32)
        .astype(bf16)
        .reshape(row_count, head_columns)
    )
    middle = inputs + residual_scale * dot_turned(mixed, output_turned)
    scale_two, normed_raw_two = norm_rows(middle, gain_two)
    normed_two = normed_raw_two.astype(bf16)
    logits = dot(normed_two, router_full)
    expert_ids = jnp.arange(EXPERTS, dtype=jnp.int32)
    routed = jnp.any(routes[:, :, None] == expert_ids[None, None, :], axis=1)
    best = jnp.max(jnp.where(routed, logits, masked_value), axis=1, keepdims=True)
    weights = jnp.where(routed, jnp.exp(jnp.where(routed, logits, best) - best), 0.0)
    shares = weights / jnp.sum(weights, axis=1, keepdims=True)
    share_high = lax.reduce_precision(shares, 8, 7)
    packet = jnp.concatenate(
        [
            normed_two,
            share_high.astype(bf16),
            (shares - share_high).astype(bf16),
            jnp.zeros((row_count, EXTRA - 2 * EXPERTS), bf16),
        ],
        axis=1,
    )
    packets = links.group_gather(packet)

    order = (0, 1, 2, 3, 6, 7, 4, 5)
    first = (member * LOCAL_EXPERTS).astype(jnp.int32).reshape(1)
    out_terms, back_terms, expert_grads = {}, {}, []
    for turn in (order[:4], order[4:]):
        packet_stack = jnp.concatenate([part for k in turn for part in packets[k]], axis=0)
        cotangent_stack = jnp.concatenate([part for k in turn for part in cotangents[k]], axis=0)
        outs, backs, grads = run_experts(
            first,
            packet_stack.reshape(len(turn), row_count, width + EXTRA),
            cotangent_stack.reshape(len(turn), row_count, width),
            expert_full,
        )
        expert_grads.append(grads)
        for at, k in enumerate(turn):
            out_terms[k], back_terms[k] = outs[at], backs[at]

    back_total = links.group_reduce(back_terms)

    def pick(owner):
        parts = [
            lax.dynamic_index_in_dim(
                grads.reshape(LOCAL_EXPERTS, 3, groups, MEMBERS, shard, hidden), owner, 2, keepdims=False
            )
            for grads in expert_grads
        ]
        return parts[0] + parts[1]

    shelf_grad = links.line_reduce(pick).astype(bf16)
    expert_shards = jnp.zeros((MEMBERS, LOCAL_EXPERTS, 3, shard, hidden), f32)
    for k in range(MEMBERS):
        part = lax.dynamic_index_in_dim(shelf_grad, member ^ k, 2, keepdims=False)
        if k:
            part = links.swap(part, k)
        expert_shards = lax.dynamic_update_index_in_dim(
            expert_shards, part.astype(f32), member ^ k, 0
        )
    expert_shards = expert_shards.reshape(EXPERTS, 3, shard, hidden)

    mixture = links.group_reduce(out_terms)
    layer_out = (middle + mixture).astype(bf16)

    upstream = cotangent.astype(f32)
    share_grad = (
        back_total[:, width : width + EXPERTS] + back_total[:, width + EXPERTS : width + 2 * EXPERTS]
    )
    share_grad = jnp.where(routed, share_grad, 0.0)
    logit_grad = (
        shares * (share_grad - jnp.sum(shares * share_grad, axis=1, keepdims=True))
    ).astype(bf16)
    normed_two_grad = back_total[:, :width] + dot_turned(logit_grad, router_full)
    grad_router = dot(normed_two.T, logit_grad)
    middle_norm_grad, grad_gain_two = norm_back(middle, scale_two, gain_two, normed_two_grad)
    middle_grad = upstream + middle_norm_grad
    branch_grad = (residual_scale * middle_grad).astype(bf16)
    grad_output_turned = dot(branch_grad.T, mixed)
    mixed_grad = (
        dot(branch_grad, output_turned)
        .astype(bf16)
        .reshape(row_count, KV_HEADS, group_size, HEAD_DIM)
    )
    scores_again = attention_scores(query_rot, key_rot, allowed)
    softmax_again = jnp.exp(scores_again - log_total)
    prob_grad = jnp.einsum("qkgd,pkd->kgqp", mixed_grad, value_rows, preferred_element_type=f32)
    row_delta = jnp.sum(prob_grad * softmax_again, axis=-1, keepdims=True)
    score_grad = (attention_scale * softmax_again * (prob_grad - row_delta)).astype(bf16)
    value_grad = (
        jnp.einsum("kgqp,qkgd->pkd", softmax_again.astype(bf16), mixed_grad, preferred_element_type=f32)
        .astype(bf16)
        .reshape(row_count, kv_columns)
    )
    query_rot_grad = jnp.einsum("kgqp,pkd->qkgd", score_grad, key_rot, preferred_element_type=f32)
    key_rot_grad = jnp.einsum("kgqp,qkgd->pkd", score_grad, query_rot, preferred_element_type=f32)
    query_grad = (
        rotate_back(query_rot_grad, cosine_table[:, None, None, :], sine_table[:, None, None, :])
        .astype(bf16)
        .reshape(row_count, head_columns)
    )
    key_grad = (
        rotate_back(key_rot_grad, cosine_table[:, None, :], sine_table[:, None, :])
        .astype(bf16)
        .reshape(row_count, kv_columns)
    )
    qkv_grad = jnp.concatenate([query_grad, key_grad, value_grad], axis=1)
    grad_qkv = dot(normed_one.T, qkv_grad)
    normed_one_grad = dot_turned(qkv_grad, qkv_full)
    input_norm_grad, grad_gain_one = norm_back(inputs, scale_one, gain_one, normed_one_grad)
    grad_tokens = middle_grad + input_norm_grad

    grad_pack = jnp.concatenate(
        [
            grad_qkv,
            grad_output_turned,
            grad_router,
            grad_gain_one[:, None],
            grad_gain_two[:, None],
            jnp.zeros((width, EXTRA - EXPERTS - 2), f32),
        ],
        axis=1,
    ).astype(bf16)
    grad_pack = grad_pack.reshape(groups, MEMBERS, shard, pack_width)
    terms = {
        k: lax.dynamic_index_in_dim(grad_pack, member ^ k, 1, keepdims=False).reshape(
            groups * shard, pack_width
        )
        for k in range(MEMBERS)
    }
    group_total = links.group_reduce(terms).reshape(groups, shard, pack_width)
    total = links.line_reduce(
        lambda owner: lax.dynamic_index_in_dim(group_total, owner, 0, keepdims=False)
    )
    return (
        layer_out,
        grad_tokens,
        total[:, at_extra + EXPERTS],
        total[:, :head_columns],
        total[:, head_columns : head_columns + kv_columns],
        total[:, head_columns + kv_columns : at_output],
        total[:, at_output:at_extra].T,
        total[:, at_extra + EXPERTS + 1],
        total[:, at_extra : at_extra + EXPERTS],
        expert_shards[:, 0],
        expert_shards[:, 1],
        expert_shards[:, 2].transpose(0, 2, 1),
    )


def solution(mesh):
    count = mesh.shape["fsdp"]
    placed = (
        P("fsdp", None),
        P("fsdp"),
        P("fsdp", None),
        P("fsdp"),
        P("fsdp", None),
        P("fsdp", None),
        P("fsdp", None),
        P(None, "fsdp"),
        P("fsdp"),
        P("fsdp", None),
        P(None, "fsdp", None),
        P(None, "fsdp", None),
        P(None, None, "fsdp"),
        P("fsdp", None),
    )

    def body(*args):
        return local(*args, count=count)

    return jax.shard_map(
        body,
        mesh=mesh,
        in_specs=placed,
        out_specs=(
            P("fsdp", None),
            P("fsdp", None),
            P("fsdp"),
            P("fsdp", None),
            P("fsdp", None),
            P("fsdp", None),
            P(None, "fsdp"),
            P("fsdp"),
            P("fsdp", None),
            P(None, "fsdp", None),
            P(None, "fsdp", None),
            P(None, None, "fsdp"),
        ),
        check_vma=False,
    )
```

time: 2590 us -> 777 us (0.30)
  waiting for transfers between devices: 1920 us -> 286 us
  matrix products: 278 us -> 70.8 us
  blocking collectives: 122 us -> 0 us
  Pallas kernels: 0 us -> 114 us
  starting transfers between devices: 1.14 us -> 112 us
  local copies, waits for them, and re-layouts: 186 us -> 112 us
    reduce_scatter x7 -> x0, waiting for transfers between devices: 1620 us -> none  [the longest x1 365 us: local(): lax.psum_scatter(grad_up, 'fsdp', scatter_dimension=1, tiled=True)]
    all_gather x7 -> x0, waiting for transfers between devices: 297 us -> none  [the longest x1 99 us: local(): lax.all_gather(down_weight, 'fsdp', axis=2, tiled=True)]
    ppermute x0 -> x110, waiting for transfers between devices: none -> 286 us  [the longest x86 200 us: swap(): lax.ppermute(value, 'fsdp', [(i, i ^ bits) for i in range(self.count)])]
    dot_general x26 -> x12, matrix products: 249 us -> 50.1 us  [the longest x6 15.8 us: dot(): return jnp.dot(left, right, preferred_element_type=f32)]
    gather x5 -> x0, local copies, waits for them, and re-layouts: 140 us -> none  [the longest x2 52.1 us: local(): padded_grad[token_of]]
    pallas_call x0 -> x2, Pallas kernels: none -> 114 us  [run_experts(): pl.pallas_call(expert_kernel, grid_spec=pltpu.PrefetchScalarGridSpec(num_...]
    ppermute x0 -> x110, starting transfers between devices: none -> 112 us  [the longest x24 57.2 us: shift(): return lax.ppermute(value, 'fsdp', pairs)]
    unnamed x2 -> x0, blocking collectives: 80.9 us -> none
  transfers between devices with their start and end apart: 15 -> 110, of which waited for: 12 -> 40; matrix products, arithmetic and copies ran while one was open for 12% -> 30% of each run, Pallas kernels for 0% -> 7%
where the time goes in v1:
time: 777 us; the launch traced here: 767 us
  waiting for transfers between devices  286 us (37%)
  Pallas kernels  114 us (15%)
  local copies, waits for them, and re-layouts  112 us (14%)
  starting transfers between devices  112 us (14%)
  matrix products  70.8 us (9%)
  other arithmetic  69 us (9%)
    ppermute x86, waiting for transfers between devices, swap(): lax.ppermute(value, 'fsdp', [(i, i ^ bits) for i in range(self.count)])  200 us
    pallas_call x2, Pallas kernels, run_experts(): pl.pallas_call(expert_kernel, grid_spec=pltpu.PrefetchScalarGridSpec(num_...  114 us
    ppermute x24, waiting for transfers between devices, shift(): return lax.ppermute(value, 'fsdp', pairs)  86.3 us
    ppermute x24, starting transfers between devices, shift(): return lax.ppermute(value, 'fsdp', pairs)  57.2 us
    ppermute x86, starting transfers between devices, swap(): lax.ppermute(value, 'fsdp', [(i, i ^ bits) for i in range(self.count)])  54.5 us
    unnamed x170, local copies, waits for them, and re-layouts  24.2 us
    dynamic_slice x1, local copies, waits for them, and re-layouts, pick(): lax.dynamic_index_in_dim(grads.reshape(LOCAL_EXPERTS, 3, groups, MEMBERS,...  16.9 us
    dot_general x6, matrix products, dot(): return jnp.dot(left, right, preferred_element_type=f32)  15.8 us
  transfers between devices with their start and end apart: 110, of which 40 were waited for; matrix products, arithmetic and copies ran while one was open for 30% of the time, Pallas kernels for 7%

profile of v1, /device:TPU:0, one launch (start us, length us, event | category | flops | bytes accessed | tf_op | source)
XLA Modules:
  0.0 767.1 jit_solution(13615744128313563893)
XLA Ops:
  100.8 10.1 %collective-permute-done.9 = bf16[64,3200]{1,0:T(8,128)(2,1)S(1)} collective-permute-done((bf16[64,3200]{1,0:T(8,128)(2,1)S(1)}, bf16[64,3200]{1,0:T(8,128)(2,1)S(1)}, u32[]{:S(2)}, u32[]{:S(2)}) %collective-permute-start.9) | collective-permute-done | bytes 409632 | tf_op jit(solution)/shard_map/ppermute | solution.py:72
  121.1 10.1 %collective-permute-done.12 = bf16[64,3200]{1,0:T(8,128)(2,1)S(1)} collective-permute-done((bf16[64,3200]{1,0:T(8,128)(2,1)S(1)}, bf16[64,3200]{1,0:T(8,128)(2,1)S(1)}, u32[]{:S(2)}, u32[]{:S(2)}) %collective-permute-start.12) | collective-permute-done | bytes 409632 | tf_op jit(solution)/shard_map/ppermute | solution.py:72
  133.3 7.8 %collective-permute-start.39 = (bf16[2,3,256,512]{3,2,1,0:T(8,128)(2,1)}, bf16[2,3,256,512]{3,2,1,0:T(8,128)(2,1)}, u32[]{:S(2)}, u32[]{:S(2)}) collective-permute-start(bf16[2,3,256,512]{3,2,1,0:T(8,128)(2,1)} %bitcast.60), channel_id=1, source_target_pairs={{0,8},{1,9},{2,10},{3,11},{4,12},{5,13},{6,14},{7,15},{8,16},{9,17... | collective-permute-start | bytes 4718600 | tf_op jit(solution)/shard_map/ppermute | solution.py:78
  147.6 9.8 %collective-permute-done.17 = bf16[64,3200]{1,0:T(8,128)(2,1)S(1)} collective-permute-done((bf16[64,3200]{1,0:T(8,128)(2,1)S(1)}, bf16[64,3200]{1,0:T(8,128)(2,1)S(1)}, u32[]{:S(2)}, u32[]{:S(2)}) %collective-permute-start.17) | collective-permute-done | bytes 409632 | tf_op jit(solution)/shard_map/ppermute | solution.py:72
  175.5 7.4 fusion.110
  182.9 8.2 %fusion.3 = f32[8,2,512]{2,1,0:T(2,128)S(1)} fusion(f32[8,2,512,512]{2,3,1,0:T(8,128)} %get-tuple-element.191, f32[8,2,512]{2,1,0:T(2,128)S(1)} %get-tuple-element.190), kind=kLoop, calls=%fused_computation.9 | loop fusion | flops 8380416 | bytes 16842752 | tf_op jit(solution)/shard_map/reduce_sum | solution.py:342
  191.2 7.6 fusion.44
  213.8 10.1 %collective-permute-done.22 = bf16[256,1152]{1,0:T(8,128)(2,1)S(1)} collective-permute-done((bf16[256,1152]{1,0:T(8,128)(2,1)S(1)}, bf16[256,1152]{1,0:T(8,128)(2,1)S(1)}, u32[]{:S(2)}, u32[]{:S(2)}) %collective-permute-start.22) | collective-permute-done | bytes 589856 | tf_op jit(solution)/shard_map/ppermute | solution.py:72
  225.4 10.6 %collective-permute-done.23 = bf16[256,1152]{1,0:T(8,128)(2,1)S(1)} collective-permute-done((bf16[256,1152]{1,0:T(8,128)(2,1)S(1)}, bf16[256,1152]{1,0:T(8,128)(2,1)S(1)}, u32[]{:S(2)}, u32[]{:S(2)}) %collective-permute-start.23) | collective-permute-done | bytes 589856 | tf_op jit(solution)/shard_map/ppermute | solution.py:72
  240.7 11.1 %collective-permute-done.50 = bf16[256,1152]{1,0:T(8,128)(2,1)S(1)} collective-permute-done((bf16[256,1152]{1,0:T(8,128)(2,1)S(1)}, bf16[256,1152]{1,0:T(8,128)(2,1)S(1)}, u32[]{:S(2)}, u32[]{:S(2)}) %collective-permute-start.50) | collective-permute-done | bytes 589856 | tf_op jit(solution)/shard_map/ppermute | solution.py:72
  258.9 33.1 %collective-permute-done.42 = bf16[2,3,256,512]{3,2,1,0:T(8,128)(2,1)S(1)} collective-permute-done((bf16[2,3,256,512]{3,2,1,0:T(8,128)(2,1)S(1)}, bf16[2,3,256,512]{3,2,1,0:T(8,128)(2,1)S(1)}, u32[]{:S(2)}, u32[]{:S(2)}) %collective-permute-start.42) | collective-permute-done | bytes 1572896 | tf_op jit(solution)/shard_map/ppermute | solution.py:78
  298.3 56.7 %experts.3 = (bf16[4,512,1024]{2,1,0:T(8,128)(2,1)}, bf16[4,512,1152]{2,1,0:T(8,128)(2,1)}, f32[2,3,1024,512]{3,2,1,0:T(8,128)}) custom-call(s32[1]{0:T(128)} %bitcast.29.first_ref, bf16[4,512,1152]{2,1,0:T(8,128)(2,1)} %bitcast.400, bf16[4,512,1024]{2,1,0:T(8,128)(2,1)} %bitcast.401, bf16[2,3,1024,512]{3,2,1,0:T(8,128)(2,1)} %bitcast.66.weight_ref), custom_call_target="tpu_custom_call" | custom-call | flops 38654705664 | bytes 35651584 | tf_op jit(solution)/shard_map/experts/pallas_call | solution.py:208
  358.7 56.9 %experts.2 = (bf16[4,512,1024]{2,1,0:T(8,128)(2,1)}, bf16[4,512,1152]{2,1,0:T(8,128)(2,1)}, f32[2,3,1024,512]{3,2,1,0:T(8,128)}) custom-call(s32[1]{0:T(128)} %bitcast.29.first_ref, bf16[4,512,1152]{2,1,0:T(8,128)(2,1)} %bitcast.397, bf16[4,512,1024]{2,1,0:T(8,128)(2,1)} %bitcast.398, bf16[2,3,1024,512]{3,2,1,0:T(8,128)(2,1)} %bitcast.66.weight_ref), custom_call_target="tpu_custom_call" | custom-call | flops 38654705664 | bytes 35651584 | tf_op jit(solution)/shard_map/experts/pallas_call | solution.py:208
  420.9 16.9 %constant_dynamic-slice_fusion = (f32[2,3,1,8,32,512]{5,4,3,2,1,0:T(8,128)}, f32[2,3,1,8,32,512]{5,4,3,2,1,0:T(8,128)}, f32[2,3,1,8,32,512]{5,4,3,2,1,0:T(8,128)...) fusion(f32[2,3,4,8,32,512]{5,4,3,2,1,0:T(8,128)} %bitcast.335, ...), kind=kLoop, calls=%fused_computation.279 | loop fusion | bytes 50331664 | tf_op jit(solution)/shard_map/jit(dynamic_index_in_dim)/dynamic_slice | solution.py:391
  467.6 14.0 %collective-permute-done.68 = bf16[256,1024]{1,0:T(8,128)(2,1)S(1)} collective-permute-done((bf16[256,1024]{1,0:T(8,128)(2,1)S(1)}, bf16[256,1024]{1,0:T(8,128)(2,1)S(1)}, u32[]{:S(2)}, u32[]{:S(2)}) %collective-permute-start.68) | collective-permute-done | bytes 524320 | tf_op jit(solution)/shard_map/ppermute | solution.py:72
  482.8 11.5 %collective-permute-done.78 = bf16[256,1152]{1,0:T(8,128)(2,1)S(1)} collective-permute-done((bf16[256,1152]{1,0:T(8,128)(2,1)S(1)}, bf16[256,1152]{1,0:T(8,128)(2,1)S(1)}, u32[]{:S(2)}, u32[]{:S(2)}) %collective-permute-start.78) | collective-permute-done | bytes 589856 | tf_op jit(solution)/shard_map/ppermute | solution.py:72
  498.2 18.8 %collective-permute-done.67 = bf16[256,1024]{1,0:T(8,128)(2,1)S(1)} collective-permute-done((bf16[256,1024]{1,0:T(8,128)(2,1)S(1)}, bf16[256,1024]{1,0:T(8,128)(2,1)S(1)}, u32[]{:S(2)}, u32[]{:S(2)}) %collective-permute-start.67) | collective-permute-done | bytes 524320 | tf_op jit(solution)/shard_map/ppermute | solution.py:72
  544.8 9.4 %fusion.51 = bf16[8,64,512]{2,1,0:T(8,128)(2,1)} fusion(bf16[512,8,2,64]{0,3,2,1:T(8,128)(2,1)S(1)} %bitcast.342, f32[8,2,512,512]{2,3,1,0:T(8,128)} %get-tuple-element.191, f32[8,2,512]{2,1,0:T(2,128)S(1)} %bitcast.393), kind=kOutput, calls=%fused_computation.101 | convolution fusion | flops 545521664 | bytes 18382848 | tf_op jit(solution)/shard_map/kgqp,qkgd->pkd/dot_general | solution.py:437
  554.2 13.1 %fusion = (f32[8,2,512]{2,1,0:T(2,128)S(1)}, f32[8,512,512,2]{2,1,3,0:T(8,128)}) fusion(f32[8,2,512,512]{2,3,1,0:T(8,128)} %get-tuple-element.191, f32[8,2,512]{2,1,0:T(2,128)S(1)} %bitcast.394, bf16[512,8,64,1]{0,2,3,1:T(8,128)(2,1)} %bitcast.368, bf16[512,8,2,64]{0,3,2,1:T(8,128)(2,1)S(1)} %bitcast.343), kind=kOutput, calls=%fused_computation.2 | convolution fusion | flops 549445632 | bytes 35192832 | tf_op jit(solution)/shard_map/qkgd,pkd->kgqp/dot_general | solution.py:433
  567.4 10.9 %fusion.2 = bf16[8,2,512,512]{2,3,1,0:T(8,128)(2,1)} fusion(f32[8,512,512,2]{2,1,3,0:T(8,128)} %get-tuple-element.198, f32[8,2,512,512]{2,3,1,0:T(8,128)S(1)} %bitcast.331, f32[8,2,512]{2,1,0:T(2,128)S(1)} %get-tuple-element.197, f32[8,2,512]{2,1,0:T(2,128)S(1)} %bitcast.395), kind=kLoop, calls=%fused_computation.4 | loop fusion | flops 20971520 | bytes 42008576 | tf_op jit(solution)/shard_map/convert_element_type | solution.py:435
  607.0 10.4 %concatenate.127 = bf16[4,8,32,3200]{3,2,1,0:T(8,128)(2,1)} concatenate(bf16[4,8,32,2048]{3,2,1,0:T(8,128)(2,1)} %bitcast.359, bf16[4,8,32,1024]{3,2,1,0:T(8,128)(2,1)S(1)} %convolution_convert_fusion.1, bf16[4,8,32,16]{3,2,1,0:T(8,128)(2,1)S(1)} %bitcast.378, bf16[4,8,32,1]{3,2,1,0:T(8,128)(2,1)} %concatenate.129, bf16[4,8,32,1]{3,2,1,0:T(8,128)(2,1)} %concatenate.130, ...), dimensions={3} | concatenate | bytes 13107200 | tf_op jit(solution)/shard_map/concatenate | solution.py:459
  641.1 11.6 %collective-permute-done.88 = bf16[64,3200]{1,0:T(8,128)(2,1)S(1)} collective-permute-done((bf16[64,3200]{1,0:T(8,128)(2,1)S(1)}, bf16[64,3200]{1,0:T(8,128)(2,1)S(1)}, u32[]{:S(2)}, u32[]{:S(2)}) %collective-permute-start.88) | collective-permute-done | bytes 409632 | tf_op jit(solution)/shard_map/ppermute | solution.py:72
  674.3 21.5 %collective-permute-done.91 = bf16[32,3200]{1,0:T(8,128)(2,1)S(1)} collective-permute-done((bf16[32,3200]{1,0:T(8,128)(2,1)S(1)}, bf16[32,3200]{1,0:T(8,128)(2,1)S(1)}, u32[]{:S(2)}, u32[]{:S(2)}) %collective-permute-start.91) | collective-permute-done | bytes 204832 | tf_op jit(solution)/shard_map/ppermute | solution.py:78
  715.0 24.3 %collective-permute-done.99 = bf16[2,3,8,32,512]{4,3,1,0,2:T(8,128)(2,1)S(1)} collective-permute-done((bf16[2,3,8,32,512]{4,3,1,0,2:T(8,128)(2,1)S(1)}, bf16[2,3,8,32,512]{4,3,1,0,2:T(8,128)(2,1)S(1)}, u32[]{:S(2)}, u32[]{:S(2)}) %collective-permute-start.99) | collective-permute-done | bytes 1572896 | tf_op jit(solution)/shard_map/ppermute | solution.py:78
  (544 shorter events, 361.2 us)
Async XLA Ops:
  2.9 73.8 %collective-permute-start.26 = (bf16[256,1024]{1,0:T(8,128)(2,1)}, bf16[256,1024]{1,0:T(8,128)(2,1)}, u32[]{:S(2)}, u32[]{:S(2)}) collective-permute-start(bf16[256,1024]{1,0:T(8,128)(2,1)} %get-tuple-element.173), channel_id=1, source_target_pairs={{0,1},{1,0},{2,3},{3,2},{4,5},{5,4},{6,7},{7,6},{8,9},{9,8},{10,11... | collective-permute-start | bytes 1572872 | tf_op jit(solution)/shard_map/ppermute | solution.py:72
  3.4 85.3 %collective-permute-start.28 = (bf16[256,1024]{1,0:T(8,128)(2,1)}, bf16[256,1024]{1,0:T(8,128)(2,1)}, u32[]{:S(2)}, u32[]{:S(2)}) collective-permute-start(bf16[256,1024]{1,0:T(8,128)(2,1)} %get-tuple-element.173), channel_id=1, source_target_pairs={{0,2},{1,3},{2,0},{3,1},{4,6},{5,7},{6,4},{7,5},{8,10},{9,11},{10,... | collective-permute-start | bytes 1572872 | tf_op jit(solution)/shard_map/ppermute | solution.py:72
  9.2 59.7 %collective-permute-start = (bf16[32,3200]{1,0:T(8,128)(2,1)S(1)}, bf16[32,3200]{1,0:T(8,128)(2,1)}, u32[]{:S(2)}, u32[]{:S(2)}) collective-permute-start(bf16[32,3200]{1,0:T(8,128)(2,1)S(1)} %concatenate.101), channel_id=1, source_target_pairs={{0,8},{1,9},{2,10},{3,11},{4,12},{5,13},{6,14},{7,15},{8,16},{9,17... | collective-permute-start | bytes 614408 | tf_op jit(solution)/shard_map/ppermute | solution.py:78
  13.3 74.6 %collective-permute-start.27 = (bf16[256,1024]{1,0:T(8,128)(2,1)}, bf16[256,1024]{1,0:T(8,128)(2,1)}, u32[]{:S(2)}, u32[]{:S(2)}) collective-permute-start(bf16[256,1024]{1,0:T(8,128)(2,1)} %get-tuple-element.172), channel_id=1, source_target_pairs={{0,1},{1,0},{2,3},{3,2},{4,5},{5,4},{6,7},{7,6},{8,9},{9,8},{10,11... | collective-permute-start | bytes 1572872 | tf_op jit(solution)/shard_map/ppermute | solution.py:72
  88.7 43.1 %collective-permute-start.30 = (bf16[256,1024]{1,0:T(8,128)(2,1)}, bf16[256,1024]{1,0:T(8,128)(2,1)S(1)}, u32[]{:S(2)}, u32[]{:S(2)}) collective-permute-start(bf16[256,1024]{1,0:T(8,128)(2,1)} %collective-permute-done.28), channel_id=1, source_target_pairs={{0,1},{1,0},{2,3},{3,2},{4,5},{5,4},{6,7},{7,6},{8,9},{9,8},{10,11... | collective-permute-start | bytes 1572872 | tf_op jit(solution)/shard_map/ppermute | solution.py:72
  92.5 39.4 %collective-permute-start.56 = (bf16[256,1024]{1,0:T(8,128)(2,1)}, bf16[256,1024]{1,0:T(8,128)(2,1)S(1)}, u32[]{:S(2)}, u32[]{:S(2)}) collective-permute-start(bf16[256,1024]{1,0:T(8,128)(2,1)} %collective-permute-done.28), channel_id=1, source_target_pairs={{0,4},{1,5},{2,6},{3,7},{4,0},{5,1},{6,2},{7,3},{8,12},{9,13},{10,... | collective-permute-start | bytes 1572872 | tf_op jit(solution)/shard_map/ppermute | solution.py:72
  133.3 77.5 %collective-permute-start.39 = (bf16[2,3,256,512]{3,2,1,0:T(8,128)(2,1)}, bf16[2,3,256,512]{3,2,1,0:T(8,128)(2,1)}, u32[]{:S(2)}, u32[]{:S(2)}) collective-permute-start(bf16[2,3,256,512]{3,2,1,0:T(8,128)(2,1)} %bitcast.60), channel_id=1, source_target_pairs={{0,8},{1,9},{2,10},{3,11},{4,12},{5,13},{6,14},{7,15},{8,16},{9,17... | collective-permute-start | bytes 4718600 | tf_op jit(solution)/shard_map/ppermute | solution.py:78
  142.0 69.9 %collective-permute-start.40 = (bf16[2,3,256,512]{3,2,1,0:T(8,128)(2,1)}, bf16[2,3,256,512]{3,2,1,0:T(8,128)(2,1)}, u32[]{:S(2)}, u32[]{:S(2)}) collective-permute-start(bf16[2,3,256,512]{3,2,1,0:T(8,128)(2,1)} %bitcast.60), channel_id=1, source_target_pairs={{8,0},{9,1},{10,2},{11,3},{12,4},{13,5},{14,6},{15,7},{16,8},{17,9... | collective-permute-start | bytes 4718600 | tf_op jit(solution)/shard_map/ppermute | solution.py:78
  161.3 47.4 %collective-permute-start.63 = (bf16[256,1024]{1,0:T(8,128)(2,1)}, bf16[256,1024]{1,0:T(8,128)(2,1)}, u32[]{:S(2)}, u32[]{:S(2)}) collective-permute-start(bf16[256,1024]{1,0:T(8,128)(2,1)} %collective-permute-done.57), channel_id=1, source_target_pairs={{0,1},{1,0},{2,3},{3,2},{4,5},{5,4},{6,7},{7,6},{8,9},{9,8},{10,11... | collective-permute-start | bytes 1572872 | tf_op jit(solution)/shard_map/ppermute | solution.py:72
  212.5 40.3 %collective-permute-start.41 = (bf16[2,3,256,512]{3,2,1,0:T(8,128)(2,1)}, bf16[2,3,256,512]{3,2,1,0:T(8,128)(2,1)S(1)}, u32[]{:S(2)}, u32[]{:S(2)}) collective-permute-start(bf16[2,3,256,512]{3,2,1,0:T(8,128)(2,1)} %collective-permute-done.40), channel_id=1, source_target_pairs={{8,0},{9,1},{10,2},{11,3},{12,4},{13,5},{14,6},{15,7},{16,8},{17,9... | collective-permute-start | bytes 4718600 | tf_op jit(solution)/shard_map/ppermute | solution.py:78
  252.7 39.3 %collective-permute-start.42 = (bf16[2,3,256,512]{3,2,1,0:T(8,128)(2,1)S(1)}, bf16[2,3,256,512]{3,2,1,0:T(8,128)(2,1)S(1)}, u32[]{:S(2)}, u32[]{:S(2)}) collective-permute-start(bf16[2,3,256,512]{3,2,1,0:T(8,128)(2,1)S(1)} %collective-permute-done.41), channel_id=1, source_target_pairs={{8,0},{9,1},{10,2},{11,3},{12,4},{13,5},{14,6},{15,7}} | collective-permute-start | bytes 4718600 | tf_op jit(solution)/shard_map/ppermute | solution.py:78
  256.4 38.8 %collective-permute-start.44 = (bf16[2,3,256,512]{3,2,1,0:T(8,128)(2,1)S(1)}, bf16[2,3,256,512]{3,2,1,0:T(8,128)(2,1)S(1)}, u32[]{:S(2)}, u32[]{:S(2)}) collective-permute-start(bf16[2,3,256,512]{3,2,1,0:T(8,128)(2,1)S(1)} %collective-permute-done.43), channel_id=1, source_target_pairs={{16,24},{17,25},{18,26},{19,27},{20,28},{21,29},{22,30},{23,31}} | collective-permute-start | bytes 4718600 | tf_op jit(solution)/shard_map/ppermute | solution.py:78
  358.2 96.3 %collective-permute-start.75 = (bf16[512,1152]{1,0:T(8,128)(2,1)}, bf16[512,1152]{1,0:T(8,128)(2,1)}, u32[]{:S(2)}, u32[]{:S(2)}) collective-permute-start(bf16[512,1152]{1,0:T(8,128)(2,1)} %get-tuple-element.122), channel_id=1, source_target_pairs={{0,1},{1,0},{2,3},{3,2},{4,5},{5,4},{6,7},{7,6},{8,9},{9,8},{10,11... | collective-permute-start | bytes 3538952 | tf_op jit(solution)/shard_map/ppermute | solution.py:72
  358.2 97.4 %collective-permute-start.74 = (bf16[512,1152]{1,0:T(8,128)(2,1)}, bf16[512,1152]{1,0:T(8,128)(2,1)}, u32[]{:S(2)}, u32[]{:S(2)}) collective-permute-start(bf16[512,1152]{1,0:T(8,128)(2,1)} %get-tuple-element.123), channel_id=1, source_target_pairs={{0,1},{1,0},{2,3},{3,2},{4,5},{5,4},{6,7},{7,6},{8,9},{9,8},{10,11... | collective-permute-start | bytes 3538952 | tf_op jit(solution)/shard_map/ppermute | solution.py:72
  454.5 41.6 %collective-permute-start.47 = (bf16[256,1024]{1,0:T(8,128)(2,1)S(1)}, bf16[256,1024]{1,0:T(8,128)(2,1)S(1)}, u32[]{:S(2)}, u32[]{:S(2)}) collective-permute-start(bf16[256,1024]{1,0:T(8,128)(2,1)S(1)} %slice.491), channel_id=1, source_target_pairs={{0,2},{1,3},{2,0},{3,1},{4,6},{5,7},{6,4},{7,5},{8,10},{9,11},{10,... | collective-permute-start | bytes 1572872 | tf_op jit(solution)/shard_map/ppermute | solution.py:72
  455.6 41.6 %collective-permute-start.70 = (bf16[256,1024]{1,0:T(8,128)(2,1)S(1)}, bf16[256,1024]{1,0:T(8,128)(2,1)S(1)}, u32[]{:S(2)}, u32[]{:S(2)}) collective-permute-start(bf16[256,1024]{1,0:T(8,128)(2,1)S(1)} %slice.490), channel_id=1, source_target_pairs={{0,4},{1,5},{2,6},{3,7},{4,0},{5,1},{6,2},{7,3},{8,12},{9,13},{10,... | collective-permute-start | bytes 1572872 | tf_op jit(solution)/shard_map/ppermute | solution.py:72
  465.9 58.1 %collective-permute-start.80 = (bf16[256,1152]{1,0:T(8,128)(2,1)S(1)}, bf16[256,1152]{1,0:T(8,128)(2,1)S(1)}, u32[]{:S(2)}, u32[]{:S(2)}) collective-permute-start(bf16[256,1152]{1,0:T(8,128)(2,1)S(1)} %slice.488), channel_id=1, source_target_pairs={{0,4},{1,5},{2,6},{3,7},{4,0},{5,1},{6,2},{7,3},{8,12},{9,13},{10,... | collective-permute-start | bytes 1769480 | tf_op jit(solution)/shard_map/ppermute | solution.py:72
  519.3 101.6 %collective-permute-start.97 = (bf16[2,3,8,32,512]{4,3,1,0,2:T(8,128)(2,1)}, bf16[2,3,8,32,512]{4,3,1,0,2:T(8,128)(2,1)}, u32[]{:S(2)}, u32[]{:S(2)}) collective-permute-start(bf16[2,3,8,32,512]{4,3,1,0,2:T(8,128)(2,1)} %fusion.67), channel_id=1, source_target_pairs={{0,8},{1,9},{2,10},{3,11},{4,12},{5,13},{6,14},{7,15}} | collective-permute-start | bytes 4718600 | tf_op jit(solution)/shard_map/ppermute | solution.py:78
  524.0 97.0 %collective-permute-start.100 = (bf16[2,3,8,32,512]{4,3,1,0,2:T(8,128)(2,1)}, bf16[2,3,8,32,512]{4,3,1,0,2:T(8,128)(2,1)}, u32[]{:S(2)}, u32[]{:S(2)}) collective-permute-start(bf16[2,3,8,32,512]{4,3,1,0,2:T(8,128)(2,1)} %fusion.66), channel_id=1, source_target_pairs={{24,16},{25,17},{26,18},{27,19},{28,20},{29,21},{30,22},{31,23}} | collective-permute-start | bytes 4718600 | tf_op jit(solution)/shard_map/ppermute | solution.py:78
  625.5 45.5 %collective-permute-start.101 = (bf16[2,3,8,32,512]{4,3,1,0,2:T(8,128)(2,1)S(1)}, bf16[2,3,8,32,512]{4,3,1,0,2:T(8,128)(2,1)S(1)}, u32[]{:S(2)}, u32[]{:S(2)}) collective-permute-start(bf16[2,3,8,32,512]{4,3,1,0,2:T(8,128)(2,1)S(1)} %get-tuple-element.115), channel_id=1, source_target_pairs={{16,8},{17,9},{18,10},{19,11},{20,12},{21,13},{22,14},{23,15},{24,... | collective-permute-start | bytes 4718600 | tf_op jit(solution)/shard_map/ppermute | solution.py:78
  655.7 44.8 %collective-permute-start.98 = (bf16[2,3,8,32,512]{4,3,1,0,2:T(8,128)(2,1)S(1)}, bf16[2,3,8,32,512]{4,3,1,0,2:T(8,128)(2,1)S(1)}, u32[]{:S(2)}, u32[]{:S(2)}) collective-permute-start(bf16[2,3,8,32,512]{4,3,1,0,2:T(8,128)(2,1)S(1)} %get-tuple-element.114), channel_id=1, source_target_pairs={{0,8},{1,9},{2,10},{3,11},{4,12},{5,13},{6,14},{7,15},{8,16},{9,17... | collective-permute-start | bytes 4718600 | tf_op jit(solution)/shard_map/ppermute | solution.py:78
  672.0 43.0 %collective-permute-start.102 = (bf16[2,3,8,32,512]{4,3,1,0,2:T(8,128)(2,1)S(1)}, bf16[2,3,8,32,512]{4,3,1,0,2:T(8,128)(2,1)S(1)}, u32[]{:S(2)}, u32[]{:S(2)}) collective-permute-start(bf16[2,3,8,32,512]{4,3,1,0,2:T(8,128)(2,1)S(1)} %add_convert_fusion), channel_id=1, source_target_pairs={{8,0},{9,1},{10,2},{11,3},{12,4},{13,5},{14,6},{15,7},{16,8},{17,9... | collective-permute-start | bytes 4718600 | tf_op jit(solution)/shard_map/ppermute | solution.py:78
  701.6 37.7 %collective-permute-start.99 = (bf16[2,3,8,32,512]{4,3,1,0,2:T(8,128)(2,1)S(1)}, bf16[2,3,8,32,512]{4,3,1,0,2:T(8,128)(2,1)S(1)}, u32[]{:S(2)}, u32[]{:S(2)}) collective-permute-start(bf16[2,3,8,32,512]{4,3,1,0,2:T(8,128)(2,1)S(1)} %add_convert_fusion.2), channel_id=1, source_target_pairs={{0,8},{1,9},{2,10},{3,11},{4,12},{5,13},{6,14},{7,15},{8,16},{9,17... | collective-permute-start | bytes 4718600 | tf_op jit(solution)/shard_map/ppermute | solution.py:78
  708.6 35.8 %collective-permute-start.93 = (bf16[32,3200]{1,0:T(8,128)(2,1)S(1)}, bf16[32,3200]{1,0:T(8,128)(2,1)S(1)}, u32[]{:S(2)}, u32[]{:S(2)}) collective-permute-start(bf16[32,3200]{1,0:T(8,128)(2,1)S(1)} %get-tuple-element.144), channel_id=1, source_target_pairs={{0,8},{1,9},{2,10},{3,11},{4,12},{5,13},{6,14},{7,15},{8,16},{9,17... | collective-permute-start | bytes 614408 | tf_op jit(solution)/shard_map/ppermute | solution.py:78
  (157 other events, 2308.4 us)

commit v2 on v1

--- a/solution.py
+++ b/solution.py
@@ -1,3 +1,5 @@
+import functools
+
 import jax
 import jax.numpy as jnp
 from jax import lax
@@ -107,7 +109,21 @@
             return own
         return own + rising.astype(f32) + falling.astype(f32)
 
-    def group_gather(self, block):
+    def direct_gather(self, piece):
+        stack = jnp.zeros((self.groups,) + piece.shape, piece.dtype)
+        for bits in range(self.groups):
+            part = self.swap(piece, bits * MEMBERS) if bits else piece
+            stack = lax.dynamic_update_index_in_dim(stack, part, self.group ^ bits, 0)
+        return stack
+
+    def direct_reduce(self, terms):
+        total = lax.dynamic_index_in_dim(terms, self.group, 0, keepdims=False)
+        for bits in range(1, self.groups):
+            part = lax.dynamic_index_in_dim(terms, self.group ^ bits, 0, keepdims=False)
+            total = total + self.swap(part.astype(bf16), bits * MEMBERS).astype(f32)
+        return total
+
+    def chips_gather(self, block):
         half = block.shape[0] // 2
         top, low = block[:half], block[half:]
         near_top = self.swap(top, 2)
@@ -116,17 +132,10 @@
         far_top = self.swap(top, 4)
         cross_top = self.swap(near_top, 4)
         cross_low = self.swap(far_low, 2)
-        found = {0: (top, low), 2: (near_top, near_low), 4: (far_top, far_low), 6: (cross_top, cross_low)}
-        found[1] = (self.swap(top, 1), self.swap(low, 1))
-        for k in (2, 4, 6):
-            found[k + 1] = tuple(self.swap(part, 1) for part in found[k])
-        return found
-
-    def group_reduce(self, blocks):
-        half = blocks[0].shape[0] // 2
-        joined = {}
-        for k in (6, 2, 4, 0):
-            joined[k] = blocks[k].astype(f32) + self.swap(blocks[k ^ 1], 1).astype(f32)
+        return {0: (top, low), 2: (near_top, near_low), 4: (far_top, far_low), 6: (cross_top, cross_low)}
+
+    def chips_reduce(self, joined):
+        half = joined[0].shape[0] // 2
         cross_top = self.swap(joined[6][:half].astype(bf16), 2).astype(f32)
         cross_low = self.swap(joined[6][half:].astype(bf16), 4).astype(f32)
         near_top = self.swap(joined[2][:half].astype(bf16), 2).astype(f32)
@@ -137,6 +146,24 @@
             [joined[0][:half] + near_top + far_top, joined[0][half:] + near_low + far_low], axis=0
         )
 
+    def join_cores(self, own, other):
+        return own.astype(f32) + self.swap(other, 1).astype(f32)
+
+    def send_parts(self, parts):
+        chips = parts.reshape((MEMBERS // 2, 2) + parts.shape[1:])
+        chip, core = self.member // 2, self.member % 2
+        arrived = jnp.zeros_like(chips)
+        for bits in range(MEMBERS // 2):
+            part = lax.dynamic_index_in_dim(chips, chip ^ bits, 0, keepdims=False)
+            if bits:
+                part = self.swap(part, 2 * bits)
+            arrived = lax.dynamic_update_index_in_dim(arrived, part, chip ^ bits, 0)
+        kept = lax.dynamic_index_in_dim(arrived, core, 1, keepdims=False)
+        other = self.swap(lax.dynamic_index_in_dim(arrived, 1 - core, 1, keepdims=False), 1)
+        even = jnp.where(core == 0, kept, other)
+        odd = jnp.where(core == 0, other, kept)
+        return jnp.stack([even, odd], axis=1).reshape(parts.shape)
+
 
 def dot(left, right):
     return jnp.dot(left, right, preferred_element_type=f32)
@@ -146,92 +173,116 @@
     return lax.dot_general(left, right, (((1,), (1,)), ((), ())), preferred_element_type=f32)
 
 
-def expert_kernel(first_ref, packet_ref, cotangent_ref, weight_ref, out_ref, back_ref, grad_ref,
-                  packet_turned, cotangent_turned, out_sum, back_sum, extra_sum):
+def expert_kernel(first_ref, packet_ref, cotangent_ref, weight_ref, *refs, fresh, last):
+    if fresh:
+        (out_ref, back_ref, grad_ref, packet_turned, cotangent_turned, sums) = refs
+    elif last:
+        (prior_ref, out_ref, back_ref, rounded_ref, packet_turned, cotangent_turned, grad_ref, sums,
+         arrival) = refs
+    else:
+        (prior_ref, out_ref, back_ref, grad_ref, packet_turned, cotangent_turned, sums, arrival) = refs
     width = cotangent_ref.shape[-1]
     rows = cotangent_ref.shape[1]
     first = first_ref[0]
-
-    @pl.when(pl.program_id(0) == 0)
+    start = pl.program_id(0) == 0
+
+    @pl.when(start)
     def _():
-        grad_ref[...] = jnp.zeros_like(grad_ref)
-
-    packet_turned[...] = packet_ref[0, :, :width].T
-    cotangent_turned[...] = cotangent_ref[0].T
-    out_sum[...] = jnp.zeros_like(out_sum)
-    back_sum[...] = jnp.zeros_like(back_sum)
-    extra_sum[...] = jnp.zeros_like(extra_sum)
+        if fresh:
+            grad_ref[...] = jnp.zeros_like(grad_ref)
+        else:
+            copy = pltpu.make_async_copy(prior_ref, grad_ref, arrival)
+            copy.start()
+            copy.wait()
+
     lane = lax.broadcasted_iota(jnp.int32, (rows, EXTRA), 1)
-
-    def one_expert(local, carry):
+    normed = packet_ref[0, :, :width]
+    upstream = cotangent_ref[0]
+    shares = packet_ref[0, :, width:].astype(f32)
+    extra = jnp.zeros((rows, EXTRA), f32)
+    packet_turned[...] = normed.T
+    cotangent_turned[...] = upstream.T
+    begun = []
+    for local in range(LOCAL_EXPERTS):
+        begun.append(
+            (
+                dot(normed, weight_ref[local, 0]),
+                dot(normed, weight_ref[local, 1]),
+                dot(upstream, weight_ref[local, 2]),
+            )
+        )
+    for local in range(LOCAL_EXPERTS):
+        gate_pre, up_pre, inner_raw = begun[local]
         expert = first + local
-        shares = packet_ref[0, :, width:].astype(f32)
         is_high, is_low = lane == expert, lane == expert + EXPERTS
         share = jnp.sum(jnp.where(is_high | is_low, shares, 0.0), axis=1, keepdims=True)
-        normed = packet_ref[0, :, :width]
-        upstream = cotangent_ref[0]
-        gate_pre = dot(normed, weight_ref[local, 0])
-        up_pre = dot(normed, weight_ref[local, 1])
-        inner_raw = dot(upstream, weight_ref[local, 2]) * residual_scale
         sigmoid_gate = jax.nn.sigmoid(gate_pre)
         activated = gate_pre * sigmoid_gate
         inner = (activated * up_pre).astype(bf16).astype(f32)
-        share_grad = jnp.sum(inner * inner_raw, axis=1, keepdims=True)
-        inner_grad = inner_raw * share
+        share_grad = residual_scale * jnp.sum(inner * inner_raw, axis=1, keepdims=True)
+        scaled = share * residual_scale
+        inner_grad = inner_raw * scaled
         gate_grad = (
-            inner_grad * up_pre * sigmoid_gate * (1.0 + gate_pre * (1.0 - sigmoid_gate))
+            inner_grad * up_pre * (sigmoid_gate + activated * (1.0 - sigmoid_gate))
         ).astype(bf16)
         up_grad = (inner_grad * activated).astype(bf16)
-        inner_shared = (inner * (share * residual_scale)).astype(bf16)
-        out_sum[...] += dot_turned(inner_shared, weight_ref[local, 2])
-        back_sum[...] += dot_turned(gate_grad, weight_ref[local, 0]) + dot_turned(
+        inner_shared = (inner * scaled).astype(bf16)
+        out_term = dot_turned(inner_shared, weight_ref[local, 2])
+        back_term = dot_turned(gate_grad, weight_ref[local, 0]) + dot_turned(
             up_grad, weight_ref[local, 1]
         )
+        if local == 0:
+            sums[0], sums[1] = out_term, back_term
+        else:
+            out_ref[0] = (sums[0] + out_term).astype(bf16)
+            back_ref[0, :, :width] = (sums[1] + back_term).astype(bf16)
         grad_ref[local, 0] += dot(packet_turned[...], gate_grad)
         grad_ref[local, 1] += dot(packet_turned[...], up_grad)
         grad_ref[local, 2] += dot(cotangent_turned[...], inner_shared)
         high = share_grad.astype(bf16).astype(f32)
-        extra_sum[...] += jnp.where(is_high, high, 0.0) + jnp.where(is_low, share_grad - high, 0.0)
-        return carry
-
-    lax.fori_loop(0, LOCAL_EXPERTS, one_expert, 0)
-    out_ref[0] = out_sum[...].astype(bf16)
-    back_ref[0, :, :width] = back_sum[...].astype(bf16)
-    back_ref[0, :, width:] = extra_sum[...].astype(bf16)
-
-
-def run_experts(first, packets, cotangents, weights):
+        extra = extra + jnp.where(is_high, high, 0.0) + jnp.where(is_low, share_grad - high, 0.0)
+    back_ref[0, :, width:] = extra.astype(bf16)
+    if last:
+        @pl.when(pl.program_id(0) == pl.num_programs(0) - 1)
+        def _():
+            rounded_ref[...] = grad_ref[...].astype(bf16)
+
+
+def run_experts(first, packets, cotangents, weights, prior, last):
     block_count, rows, wide = packets.shape
     width = cotangents.shape[-1]
     hidden = weights.shape[-1]
     grad_shape = (LOCAL_EXPERTS, 3, width, hidden)
+    fresh = prior is None
+    in_specs = [
+        pl.BlockSpec((1, rows, wide), lambda i, s: (i, 0, 0)),
+        pl.BlockSpec((1, rows, width), lambda i, s: (i, 0, 0)),
+        pl.BlockSpec(grad_shape, lambda i, s: (0, 0, 0, 0), pipeline_mode=pl.Buffered(1)),
+    ]
+    scratch = [pltpu.VMEM((width, rows), bf16), pltpu.VMEM((width, rows), bf16)]
+    if last:
+        scratch.append(pltpu.VMEM(grad_shape, f32))
+    scratch.append(pltpu.VMEM((2, rows, width), f32))
+    if not fresh:
+        in_specs.append(pl.BlockSpec(memory_space=pl.ANY))
+        scratch.append(pltpu.SemaphoreType.DMA)
     return pl.pallas_call(
-        expert_kernel,
+        functools.partial(expert_kernel, fresh=fresh, last=last),
         grid_spec=pltpu.PrefetchScalarGridSpec(
             num_scalar_prefetch=1,
             grid=(block_count,),
-            in_specs=[
-                pl.BlockSpec((1, rows, wide), lambda i, s: (i, 0, 0)),
-                pl.BlockSpec((1, rows, width), lambda i, s: (i, 0, 0)),
-                pl.BlockSpec(grad_shape, lambda i, s: (0, 0, 0, 0), pipeline_mode=pl.Buffered(1)),
-            ],
+            in_specs=in_specs,
             out_specs=[
                 pl.BlockSpec((1, rows, width), lambda i, s: (i, 0, 0)),
                 pl.BlockSpec((1, rows, wide), lambda i, s: (i, 0, 0)),
                 pl.BlockSpec(grad_shape, lambda i, s: (0, 0, 0, 0), pipeline_mode=pl.Buffered(1)),
             ],
-            scratch_shapes=[
-                pltpu.VMEM((width, rows), bf16),
-                pltpu.VMEM((width, rows), bf16),
-                pltpu.VMEM((rows, width), f32),
-                pltpu.VMEM((rows, width), f32),
-                pltpu.VMEM((rows, EXTRA), f32),
-            ],
+            scratch_shapes=scratch,
         ),
         out_shape=[
             jax.ShapeDtypeStruct((block_count, rows, width), bf16),
             jax.ShapeDtypeStruct((block_count, rows, wide), bf16),
-            jax.ShapeDtypeStruct(grad_shape, f32),
+            jax.ShapeDtypeStruct(grad_shape, bf16 if last else f32),
         ],
         compiler_params=pltpu.CompilerParams(vmem_limit_bytes=60 * 1024 * 1024),
         cost_estimate=pl.CostEstimate(
@@ -240,7 +291,7 @@
             transcendentals=block_count * LOCAL_EXPERTS * rows * hidden,
         ),
         name="experts",
-    )(first, packets, cotangents, weights)
+    )(first, packets, cotangents, weights, *(() if fresh else (prior,)))
 
 
 def local(
@@ -283,14 +334,13 @@
         axis=1,
     )
     pack_width = packed.shape[1]
-    line = links.line_gather(packed)
-    column = jnp.zeros((groups, shard, pack_width), bf16)
-    for back, piece in enumerate(line):
-        column = lax.dynamic_update_index_in_dim(column, piece, (group + groups - back) % groups, 0)
-    spread = links.group_gather(column.reshape(groups * shard, pack_width))
+    column = links.direct_gather(packed).reshape(groups * shard, pack_width)
+    spread = links.chips_gather(column)
+    even = jnp.stack([jnp.concatenate(spread[k], axis=0) for k in (0, 2, 4, 6)])
+    odd = links.swap(even, 1)
     whole = jnp.zeros((groups, MEMBERS, shard, pack_width), bf16)
     for k in range(MEMBERS):
-        part = jnp.concatenate(spread[k], axis=0).reshape(groups, shard, pack_width)
+        part = (odd if k % 2 else even)[k // 2].reshape(groups, shard, pack_width)
         whole = lax.dynamic_update_index_in_dim(whole, part, member ^ k, 1)
     whole = whole.reshape(width, pack_width)
     at_output = head_columns + 2 * kv_columns
@@ -303,12 +353,7 @@
 
     mine = jnp.stack([gate_weight, up_weight, down_weight.transpose(0, 2, 1)], axis=1)
     mine = mine.reshape(MEMBERS, LOCAL_EXPERTS, 3, shard, hidden)
-    shelf = jnp.zeros((LOCAL_EXPERTS, 3, MEMBERS, shard, hidden), bf16)
-    for k in range(MEMBERS):
-        part = lax.dynamic_index_in_dim(mine, member ^ k, 0, keepdims=False)
-        if k:
-            part = links.swap(part, k)
-        shelf = lax.dynamic_update_index_in_dim(shelf, part, member ^ k, 2)
+    shelf = links.send_parts(mine).transpose(1, 2, 0, 3, 4)
     shelf = shelf.reshape(LOCAL_EXPERTS, 3, MEMBERS * shard, hidden)
     expert_full = jnp.zeros((LOCAL_EXPERTS, 3, groups, MEMBERS * shard, hidden), bf16)
     for back, piece in enumerate(links.line_gather(shelf)):
@@ -316,7 +361,8 @@
             expert_full, piece, (group + groups - back) % groups, 2
         )
     expert_full = expert_full.reshape(LOCAL_EXPERTS, 3, width, hidden)
-    cotangents = links.group_gather(cotangent)
+    late_cotangent, whole = lax.optimization_barrier((cotangent, whole))
+    cotangents = links.chips_gather(late_cotangent)
 
     inputs = tokens.astype(f32)
     cosine_table, sine_table = rope_tables(row_count)
@@ -366,48 +412,56 @@
         ],
         axis=1,
     )
-    packets = links.group_gather(packet)
-
-    order = (0, 1, 2, 3, 6, 7, 4, 5)
+    packets = links.chips_gather(packet)
+
     first = (member * LOCAL_EXPERTS).astype(jnp.int32).reshape(1)
-    out_terms, back_terms, expert_grads = {}, {}, []
-    for turn in (order[:4], order[4:]):
-        packet_stack = jnp.concatenate([part for k in turn for part in packets[k]], axis=0)
-        cotangent_stack = jnp.concatenate([part for k in turn for part in cotangents[k]], axis=0)
+    out_terms, back_terms = {}, {}
+    grads = None
+    turns = ((0,), (2, 6), (4,))
+    for turn in turns:
+        stacks = []
+        for blocks in (packets, cotangents):
+            even = jnp.concatenate([part for k in turn for part in blocks[k]], axis=0)
+            even = even.reshape(len(turn), row_count, even.shape[-1])
+            stacks.append(jnp.concatenate([even, links.swap(even, 1)], axis=0))
         outs, backs, grads = run_experts(
-            first,
-            packet_stack.reshape(len(turn), row_count, width + EXTRA),
-            cotangent_stack.reshape(len(turn), row_count, width),
-            expert_full,
+            first, stacks[0], stacks[1], expert_full, grads, turn == turns[-1]
         )
-        expert_grads.append(grads)
         for at, k in enumerate(turn):
-            out_terms[k], back_terms[k] = outs[at], backs[at]
-
-    back_total = links.group_reduce(back_terms)
-
-    def pick(owner):
-        parts = [
-            lax.dynamic_index_in_dim(
-                grads.reshape(LOCAL_EXPERTS, 3, groups, MEMBERS, shard, hidden), owner, 2, keepdims=False
+            out_terms[k], out_terms[k + 1] = outs[at], outs[len(turn) + at]
+            back_terms[k] = links.join_cores(backs[at], backs[len(turn) + at])
+
+    back_total = links.chips_reduce(back_terms)
+
+    grads = grads.reshape(LOCAL_EXPERTS, 3, groups, MEMBERS, shard, hidden)
+    shelf_grad = links.line_reduce(
+        lambda owner: lax.dynamic_index_in_dim(grads, owner, 2, keepdims=False).astype(f32)
+    ).astype(bf16)
+    expert_shards = links.send_parts(shelf_grad.transpose(2, 0, 1, 3, 4)).astype(f32)
+    expert_shards = expert_shards.reshape(EXPERTS, 3, shard, hidden)
+
+    out_terms, back_total = lax.optimization_barrier((out_terms, back_total))
+    mixture = links.chips_reduce(
+        {k: links.join_cores(out_terms[k], out_terms[k + 1]) for k in (6, 2, 4, 0)}
+    )
+    layer_out = (middle + mixture).astype(bf16)
+
+    def reduce_pack(parts):
+        spare = -sum(part.shape[1] for part in parts) % EXTRA
+        pack = jnp.concatenate(parts + [jnp.zeros((width, spare), f32)], axis=1).astype(bf16)
+        columns = pack.shape[1]
+        pack = pack.reshape(groups, MEMBERS // 2, 2, shard, columns)
+        core, chip = member % 2, member // 2
+        own = lax.dynamic_index_in_dim(pack, core, 2, keepdims=False)
+        other = lax.dynamic_index_in_dim(pack, 1 - core, 2, keepdims=False)
+        joined = links.join_cores(own, other)
+        terms = {
+            2 * bits: lax.dynamic_index_in_dim(joined, chip ^ bits, 1, keepdims=False).reshape(
+                groups * shard, columns
             )
-            for grads in expert_grads
-        ]
-        return parts[0] + parts[1]
-
-    shelf_grad = links.line_reduce(pick).astype(bf16)
-    expert_shards = jnp.zeros((MEMBERS, LOCAL_EXPERTS, 3, shard, hidden), f32)
-    for k in range(MEMBERS):
-        part = lax.dynamic_index_in_dim(shelf_grad, member ^ k, 2, keepdims=False)
-        if k:
-            part = links.swap(part, k)
-        expert_shards = lax.dynamic_update_index_in_dim(
-            expert_shards, part.astype(f32), member ^ k, 0
-        )
-    expert_shards = expert_shards.reshape(EXPERTS, 3, shard, hidden)
-
-    mixture = links.group_reduce(out_terms)
-    layer_out = (middle + mixture).astype(bf16)
+            for bits in range(MEMBERS // 2)
+        }
+        return links.direct_reduce(links.chips_reduce(terms).reshape(groups, shard, columns))
 
     upstream = cotangent.astype(f32)
     share_grad = (
@@ -456,38 +510,18 @@
     input_norm_grad, grad_gain_one = norm_back(inputs, scale_one, gain_one, normed_one_grad)
     grad_tokens = middle_grad + input_norm_grad
 
-    grad_pack = jnp.concatenate(
-        [
-            grad_qkv,
-            grad_output_turned,
-            grad_router,
-            grad_gain_one[:, None],
-            grad_gain_two[:, None],
-            jnp.zeros((width, EXTRA - EXPERTS - 2), f32),
-        ],
-        axis=1,
-    ).astype(bf16)
-    grad_pack = grad_pack.reshape(groups, MEMBERS, shard, pack_width)
-    terms = {
-        k: lax.dynamic_index_in_dim(grad_pack, member ^ k, 1, keepdims=False).reshape(
-            groups * shard, pack_width
-        )
-        for k in range(MEMBERS)
-    }
-    group_total = links.group_reduce(terms).reshape(groups, shard, pack_width)
-    total = links.line_reduce(
-        lambda owner: lax.dynamic_index_in_dim(group_total, owner, 0, keepdims=False)
-    )
+    first_total = reduce_pack([grad_output_turned, grad_router, grad_gain_two[:, None]])
+    second_total = reduce_pack([grad_qkv, grad_gain_one[:, None]])
     return (
         layer_out,
         grad_tokens,
-        total[:, at_extra + EXPERTS],
-        total[:, :head_columns],
-        total[:, head_columns : head_columns + kv_columns],
-        total[:, head_columns + kv_columns : at_output],
-        total[:, at_output:at_extra].T,
-        total[:, at_extra + EXPERTS + 1],
-        total[:, at_extra : at_extra + EXPERTS],
+        second_total[:, at_output],
+        second_total[:, :head_columns],
+        second_total[:, head_columns : head_columns + kv_columns],
+        second_total[:, head_columns + kv_columns : at_output],
+        first_total[:, :head_columns].T,
+        first_total[:, head_columns + EXPERTS],
+        first_total[:, head_columns : head_columns + EXPERTS],
         expert_shards[:, 0],
         expert_shards[:, 1],
         expert_shards[:, 2].transpose(0, 2, 1),

time: 777 us -> 735 us (0.946)
  waiting for transfers between devices: 286 us -> 221 us
  other arithmetic: 69 us -> 121 us
  local copies, waits for them, and re-layouts: 112 us -> 80.5 us
  starting transfers between devices: 112 us -> 104 us
    ppermute x86 -> x76, waiting for transfers between devices: 200 us -> 165 us  [swap(): lax.ppermute(value, 'fsdp', [(i, i ^ bits) for i in range(self.count)])]
    ppermute x24 -> x12, waiting for transfers between devices: 86.3 us -> 56 us  [shift(): return lax.ppermute(value, 'fsdp', pairs)]
    ppermute x24 -> x12, starting transfers between devices: 57.2 us -> 28.6 us  [shift(): return lax.ppermute(value, 'fsdp', pairs)]
    concatenate x9 -> x11, other arithmetic: 0.57 us -> 27.2 us  [the longest x6 21.1 us: local(): stacks.append(jnp.concatenate([even, links.swap(even, 1)], axis=0))]
    ppermute x86 -> x76, starting transfers between devices: 54.5 us -> 75.5 us  [swap(): lax.ppermute(value, 'fsdp', [(i, i ^ bits) for i in range(self.count)])]
    dynamic_slice x2 -> x0, local copies, waits for them, and re-layouts: 20.4 us -> none  [the longest x1 16.9 us: pick(): lax.dynamic_index_in_dim(grads.reshape(LOCAL_EXPERTS, 3, groups, MEMBERS,...]
    unnamed x170 -> x133, local copies, waits for them, and re-layouts: 24.2 us -> 8.29 us
    add x9 -> x15, other arithmetic: 4.83 us -> 13.7 us  [the longest x7 12.4 us: join_cores(): return own.astype(f32) + self.swap(other, 1).astype(f32)]
  transfers between devices with their start and end apart: 110 -> 88, of which waited for: 40 -> 32; matrix products, arithmetic and copies ran while one was open for 30% -> 35% of each run, Pallas kernels for 7% -> 9%
where the time goes in v2:
time: 735 us; the launch traced here: 726 us
  waiting for transfers between devices  221 us (30%)
  other arithmetic  121 us (16%)
  Pallas kernels  120 us (16%)
  starting transfers between devices  104 us (14%)
  local copies, waits for them, and re-layouts  80.5 us (11%)
  matrix products  75.9 us (10%)
    ppermute x76, waiting for transfers between devices, swap(): lax.ppermute(value, 'fsdp', [(i, i ^ bits) for i in range(self.count)])  165 us
    pallas_call x3, Pallas kernels, run_experts(): pl.pallas_call(functools.partial(expert_kernel, fresh=fresh, last=last),...  120 us
    ppermute x76, starting transfers between devices, swap(): lax.ppermute(value, 'fsdp', [(i, i ^ bits) for i in range(self.count)])  75.5 us
    ppermute x12, waiting for transfers between devices, shift(): return lax.ppermute(value, 'fsdp', pairs)  56 us
    ppermute x12, starting transfers between devices, shift(): return lax.ppermute(value, 'fsdp', pairs)  28.6 us
    concatenate x6, other arithmetic, local(): stacks.append(jnp.concatenate([even, links.swap(even, 1)], axis=0))  21.1 us
    dot_general x6, matrix products, dot(): return jnp.dot(left, right, preferred_element_type=f32)  16.1 us
  transfers between devices with their start and end apart: 88, of which 32 were waited for; matrix products, arithmetic and copies ran while one was open for 35% of the time, Pallas kernels for 9%

profile of v2, /device:TPU:0, one launch (start us, length us, event | category | flops | bytes accessed | tf_op | source)
XLA Modules:
  0.0 726.1 jit_solution(4732893770694247944)
XLA Ops:
  31.4 8.7 %collective-permute-done.3 = bf16[64,3200]{1,0:T(8,128)(2,1)S(1)} collective-permute-done((bf16[64,3200]{1,0:T(8,128)(2,1)S(1)}, bf16[64,3200]{1,0:T(8,128)(2,1)S(1)}, u32[]{:S(2)}, u32[]{:S(2)}) %collective-permute-start.3) | collective-permute-done | bytes 409632 | tf_op jit(solution)/shard_map/ppermute | solution.py:74
  81.4 31.5 %collective-permute-done.17 = bf16[2,3,256,512]{3,2,1,0:T(8,128)(2,1)} collective-permute-done((bf16[2,3,256,512]{3,2,1,0:T(8,128)(2,1)S(1)}, bf16[2,3,256,512]{3,2,1,0:T(8,128)(2,1)}, u32[]{:S(2)}, u32[]{:S(2)}) %collective-permute-start.17) | collective-permute-done | bytes 1572896 | tf_op jit(solution)/shard_map/ppermute | solution.py:80
  136.4 7.3 %fusion.111 = (f32[8,2,512]{2,1,0:T(2,128)S(1)}, f32[8,2,512,512]{2,3,1,0:T(8,128)}) fusion(bf16[512,8,64,1]{0,2,3,1:T(8,128)(2,1)S(1)} %fusion.68, bf16[512,8,2,64]{0,3,2,1:T(8,128)(2,1)S(1)} %fusion.28, pred[512,512]{0,1:T(8,128)(4,1)S(1)} %copy-done.35), kind=kOutput, calls=%fused_computation.297 | convolution fusion | flops 549445632 | bytes 18644992 | tf_op jit(solution)/shard_map/qkgd,pkd->kgqp/dot_general | solution.py:61
  143.7 8.2 %fusion.3 = f32[8,2,512]{2,1,0:T(2,128)S(1)} fusion(f32[8,2,512,512]{2,3,1,0:T(8,128)} %get-tuple-element.197, f32[8,2,512]{2,1,0:T(2,128)S(1)} %get-tuple-element.196), kind=kLoop, calls=%fused_computation.9 | loop fusion | flops 8380416 | bytes 16842752 | tf_op jit(solution)/shard_map/reduce_sum | solution.py:388
  152.0 7.6 %fusion.38 = bf16[8,64,2,512]{3,1,2,0:T(8,128)(2,1)S(1)} fusion(bf16[512,8,64,1]{0,2,3,1:T(8,128)(2,1)S(1)} %bitcast.378, f32[8,2,512,512]{2,3,1,0:T(8,128)} %get-tuple-element.197, f32[8,2,512]{2,1,0:T(2,128)S(1)} %fusion.3, f32[8,2,512]{2,1,0:T(2,128)S(1)} %get-tuple-element.196), kind=kOutput, calls=%fused_computation.97 | convolution fusion | flops 549978112 | bytes 18415616 | tf_op jit(solution)/shard_map/kgqp,pkd->qkgd/dot_general | solution.py:392
  181.5 8.3 %collective-permute-done.36 = bf16[256,1024]{1,0:T(8,128)(2,1)} collective-permute-done((bf16[256,1024]{1,0:T(8,128)(2,1)}, bf16[256,1024]{1,0:T(8,128)(2,1)}, u32[]{:S(2)}, u32[]{:S(2)}) %collective-permute-start.36) | collective-permute-done | bytes 524320 | tf_op jit(solution)/shard_map/ppermute | solution.py:74
  189.7 12.6 %collective-permute-done.25 = bf16[256,1152]{1,0:T(8,128)(2,1)} collective-permute-done((bf16[256,1152]{1,0:T(8,128)(2,1)}, bf16[256,1152]{1,0:T(8,128)(2,1)}, u32[]{:S(2)}, u32[]{:S(2)}) %collective-permute-start.25) | collective-permute-done | bytes 589856 | tf_op jit(solution)/shard_map/ppermute | solution.py:74
  241.5 10.1 %collective-permute-done.19 = bf16[2,3,256,512]{3,2,1,0:T(8,128)(2,1)S(1)} collective-permute-done((bf16[2,3,256,512]{3,2,1,0:T(8,128)(2,1)}, bf16[2,3,256,512]{3,2,1,0:T(8,128)(2,1)S(1)}, u32[]{:S(2)}, u32[]{:S(2)}) %collective-permute-start.19) | collective-permute-done | bytes 1572896 | tf_op jit(solution)/shard_map/ppermute | solution.py:80
  259.3 30.1 %experts.3 = (bf16[2,512,1024]{2,1,0:T(8,128)(2,1)}, bf16[2,512,1152]{2,1,0:T(8,128)(2,1)}, f32[2,3,1024,512]{3,2,1,0:T(8,128)}) custom-call(s32[1]{0:T(128)} %bitcast.33.first_ref, bf16[2,512,1152]{2,1,0:T(8,128)(2,1)} %pad_maximum_fusion.3.packet_ref, bf16[2,512,1024]{2,1,0:T(8,128)(2,1)} %pad_maximum_fusion.7.cotangent_ref, ...), custom_call_target="tpu_custom_call" | custom-call | flops 19327352832 | bytes 27262976 | tf_op jit(solution)/shard_map/experts/pallas_call | solution.py:269
  313.9 56.0 %experts.4 = (bf16[4,512,1024]{2,1,0:T(8,128)(2,1)}, bf16[4,512,1152]{2,1,0:T(8,128)(2,1)}, f32[2,3,1024,512]{3,2,1,0:T(8,128)}) custom-call(s32[1]{0:T(128)} %bitcast.33.first_ref, bf16[4,512,1152]{2,1,0:T(8,128)(2,1)} %pad_maximum_fusion.packet_ref, bf16[4,512,1024]{2,1,0:T(8,128)(2,1)} %pad_maximum_fusion.1.cotangent_ref, ...), custom_call_target="tpu_custom_call" | custom-call | flops 38654705664 | bytes 35651584 | tf_op jit(solution)/shard_map/experts/pallas_call | solution.py:269
  373.7 33.5 %experts.5 = (bf16[2,512,1024]{2,1,0:T(8,128)(2,1)}, bf16[2,512,1152]{2,1,0:T(8,128)(2,1)}, bf16[2,3,1024,512]{3,2,1,0:T(8,128)(2,1)}) custom-call(s32[1]{0:T(128)} %bitcast.33.first_ref, bf16[2,512,1152]{2,1,0:T(8,128)(2,1)} %pad_maximum_fusion.5.packet_ref, bf16[2,512,1024]{2,1,0:T(8,128)(2,1)} %pad_maximum_fusion.9.cotangent_ref, ...), custom_call_target="tpu_custom_call" | custom-call | flops 19327352832 | bytes 27262976 | tf_op jit(solution)/shard_map/experts/pallas_call | solution.py:269
  422.9 11.6 %collective-permute-done.43 = bf16[256,1152]{1,0:T(8,128)(2,1)S(1)} collective-permute-done((bf16[256,1152]{1,0:T(8,128)(2,1)S(1)}, bf16[256,1152]{1,0:T(8,128)(2,1)S(1)}, u32[]{:S(2)}, u32[]{:S(2)}) %collective-permute-start.43) | collective-permute-done | bytes 589856 | tf_op jit(solution)/shard_map/ppermute | solution.py:74
  439.5 8.4 %collective-permute-done.78 = bf16[2,3,8,32,512]{4,3,2,1,0:T(8,128)(2,1)S(1)} collective-permute-done((bf16[2,3,8,32,512]{4,3,2,1,0:T(8,128)(2,1)S(1)}, bf16[2,3,8,32,512]{4,3,2,1,0:T(8,128)(2,1)S(1)}, u32[]{:S(2)}, u32[]{:S(2)}) %collective-permute-start.78) | collective-permute-done | bytes 1572896 | tf_op jit(solution)/shard_map/ppermute | solution.py:80
  478.0 8.4 %collective-permute-done.53 = bf16[256,1024]{1,0:T(8,128)(2,1)S(1)} collective-permute-done((bf16[256,1024]{1,0:T(8,128)(2,1)S(1)}, bf16[256,1024]{1,0:T(8,128)(2,1)S(1)}, u32[]{:S(2)}, u32[]{:S(2)}) %collective-permute-start.53) | collective-permute-done | bytes 524320 | tf_op jit(solution)/shard_map/ppermute | solution.py:74
  501.2 9.8 %collective-permute-done.54 = bf16[256,1024]{1,0:T(8,128)(2,1)S(1)} collective-permute-done((bf16[256,1024]{1,0:T(8,128)(2,1)S(1)}, bf16[256,1024]{1,0:T(8,128)(2,1)S(1)}, u32[]{:S(2)}, u32[]{:S(2)}) %collective-permute-start.54) | collective-permute-done | bytes 524320 | tf_op jit(solution)/shard_map/ppermute | solution.py:74
  520.2 9.4 %fusion.45 = bf16[8,64,512]{2,1,0:T(8,128)(2,1)} fusion(bf16[512,8,2,64]{0,3,2,1:T(8,128)(2,1)S(1)} %bitcast.346, f32[8,2,512,512]{2,3,1,0:T(8,128)} %get-tuple-element.197, f32[8,2,512]{2,1,0:T(2,128)S(1)} %bitcast.399), kind=kOutput, calls=%fused_computation.101 | convolution fusion | flops 545521664 | bytes 18382848 | tf_op jit(solution)/shard_map/kgqp,qkgd->pkd/dot_general | solution.py:491
  529.6 13.0 %fusion = (f32[8,2,512]{2,1,0:T(2,128)S(1)}, f32[8,512,512,2]{2,1,3,0:T(8,128)}) fusion(f32[8,2,512,512]{2,3,1,0:T(8,128)} %get-tuple-element.197, f32[8,2,512]{2,1,0:T(2,128)S(1)} %bitcast.400, bf16[512,8,64,1]{0,2,3,1:T(8,128)(2,1)S(1)} %bitcast.379, bf16[512,8,2,64]{0,3,2,1:T(8,128)(2,1)S(1)} %bitcast.347), kind=kOutput, calls=%fused_computation.2 | convolution fusion | flops 549445632 | bytes 35192832 | tf_op jit(solution)/shard_map/qkgd,pkd->kgqp/dot_general | solution.py:487
  542.9 10.9 %fusion.2 = bf16[8,2,512,512]{2,3,1,0:T(8,128)(2,1)} fusion(f32[8,512,512,2]{2,1,3,0:T(8,128)} %get-tuple-element.204, f32[8,2,512,512]{2,3,1,0:T(8,128)S(1)} %bitcast.334, f32[8,2,512]{2,1,0:T(2,128)S(1)} %get-tuple-element.203, f32[8,2,512]{2,1,0:T(2,128)S(1)} %bitcast.401), kind=kLoop, calls=%fused_computation.4 | loop fusion | flops 20971520 | bytes 42008576 | tf_op jit(solution)/shard_map/convert_element_type | solution.py:489
  592.1 7.8 %concatenate.141 = bf16[4,4,2,32,2176]{4,3,2,1,0:T(8,128)(2,1)} concatenate(bf16[4,4,2,32,2048]{4,3,2,1,0:T(8,128)(2,1)} %bitcast.370, bf16[4,4,2,32,1]{4,3,2,1,0:T(8,128)(2,1)} %concatenate.147, bf16[4,4,2,32,127]{4,3,2,1,0:T(8,128)(2,1)} %broadcast_in_dim.187), dimensions={4} | concatenate | bytes 8912896 | tf_op jit(solution)/shard_map/concatenate | solution.py:451
  628.6 7.8 %collective-permute-start.77 = (bf16[32,1152]{1,0:T(8,128)(2,1)S(1)}, bf16[32,1152]{1,0:T(8,128)(2,1)S(1)}, u32[]{:S(2)}, u32[]{:S(2)}) collective-permute-start(bf16[32,1152]{1,0:T(8,128)(2,1)S(1)} %get-tuple-element.182), channel_id=1, source_target_pairs={{0,24},{1,25},{2,26},{3,27},{4,28},{5,29},{6,30},{7,31},{8,16},{9,... | collective-permute-start | bytes 221192 | tf_op jit(solution)/shard_map/ppermute | solution.py:74
  638.9 13.8 %collective-permute-done.77 = bf16[32,1152]{1,0:T(8,128)(2,1)S(1)} collective-permute-done((bf16[32,1152]{1,0:T(8,128)(2,1)S(1)}, bf16[32,1152]{1,0:T(8,128)(2,1)S(1)}, u32[]{:S(2)}, u32[]{:S(2)}) %collective-permute-start.77) | collective-permute-done | bytes 73760 | tf_op jit(solution)/shard_map/ppermute | solution.py:74
  669.8 10.3 %collective-permute-done.62 = bf16[64,2176]{1,0:T(8,128)(2,1)S(1)} collective-permute-done((bf16[64,2176]{1,0:T(8,128)(2,1)S(1)}, bf16[64,2176]{1,0:T(8,128)(2,1)S(1)}, u32[]{:S(2)}, u32[]{:S(2)}) %collective-permute-start.62) | collective-permute-done | bytes 278560 | tf_op jit(solution)/shard_map/ppermute | solution.py:74
  683.5 9.5 %collective-permute-done.63 = bf16[64,2176]{1,0:T(8,128)(2,1)S(1)} collective-permute-done((bf16[64,2176]{1,0:T(8,128)(2,1)S(1)}, bf16[64,2176]{1,0:T(8,128)(2,1)S(1)}, u32[]{:S(2)}, u32[]{:S(2)}) %collective-permute-start.63) | collective-permute-done | bytes 278560 | tf_op jit(solution)/shard_map/ppermute | solution.py:74
  712.8 7.9 %collective-permute-done.85 = bf16[2,2,3,32,512]{4,3,2,1,0:T(8,128)(2,1)S(1)} collective-permute-done((bf16[2,2,3,32,512]{4,3,2,1,0:T(8,128)(2,1)S(1)}, bf16[2,2,3,32,512]{4,3,2,1,0:T(8,128)(2,1)S(1)}, u32[]{:S(2)}, u32[]{:S(2)}) %collective-permute-start.85) | collective-permute-done | bytes 393248 | tf_op jit(solution)/shard_map/ppermute | solution.py:74
  (482 shorter events, 380.1 us)
Async XLA Ops:
  14.1 48.5 %collective-permute-start.13 = (bf16[2,2,3,32,512]{4,3,2,1,0:T(8,128)(2,1)}, bf16[2,2,3,32,512]{4,3,2,1,0:T(8,128)(2,1)S(1)}, u32[]{:S(2)}, u32[]{:S(2)}) collective-permute-start(bf16[2,2,3,32,512]{4,3,2,1,0:T(8,128)(2,1)} %get-tuple-element.159), channel_id=1, source_target_pairs={{0,4},{1,5},{2,6},{3,7},{4,0},{5,1},{6,2},{7,3},{8,12},{9,13},{10,... | collective-permute-start | bytes 1179656 | tf_op jit(solution)/shard_map/ppermute | solution.py:74
  15.8 46.8 %collective-permute-start.14 = (bf16[2,2,3,32,512]{4,3,2,1,0:T(8,128)(2,1)}, bf16[2,2,3,32,512]{4,3,2,1,0:T(8,128)(2,1)S(1)}, u32[]{:S(2)}, u32[]{:S(2)}) collective-permute-start(bf16[2,2,3,32,512]{4,3,2,1,0:T(8,128)(2,1)} %get-tuple-element.158), channel_id=1, source_target_pairs={{0,6},{1,7},{2,4},{3,5},{4,2},{5,3},{6,0},{7,1},{8,14},{9,15},{10,... | collective-permute-start | bytes 1179656 | tf_op jit(solution)/shard_map/ppermute | solution.py:74
  62.5 53.5 %collective-permute-start.9 = (bf16[4,128,3200]{2,1,0:T(8,128)(2,1)}, bf16[4,128,3200]{2,1,0:T(8,128)(2,1)}, u32[]{:S(2)}, u32[]{:S(2)}) collective-permute-start(bf16[4,128,3200]{2,1,0:T(8,128)(2,1)} %pad_maximum_fusion.2), channel_id=1, source_target_pairs={{0,1},{1,0},{2,3},{3,2},{4,5},{5,4},{6,7},{7,6},{8,9},{9,8},{10,11... | collective-permute-start | bytes 9830408 | tf_op jit(solution)/shard_map/ppermute | solution.py:74
  70.8 43.4 %collective-permute-start.16 = (bf16[2,3,256,512]{3,2,1,0:T(8,128)(2,1)S(1)}, bf16[2,3,256,512]{3,2,1,0:T(8,128)(2,1)}, u32[]{:S(2)}, u32[]{:S(2)}) collective-permute-start(bf16[2,3,256,512]{3,2,1,0:T(8,128)(2,1)S(1)} %bitcast.358), channel_id=1, source_target_pairs={{0,8},{1,9},{2,10},{3,11},{4,12},{5,13},{6,14},{7,15},{8,16},{9,17... | collective-permute-start | bytes 4718600 | tf_op jit(solution)/shard_map/ppermute | solution.py:80
  74.5 38.4 %collective-permute-start.17 = (bf16[2,3,256,512]{3,2,1,0:T(8,128)(2,1)S(1)}, bf16[2,3,256,512]{3,2,1,0:T(8,128)(2,1)}, u32[]{:S(2)}, u32[]{:S(2)}) collective-permute-start(bf16[2,3,256,512]{3,2,1,0:T(8,128)(2,1)S(1)} %bitcast.359), channel_id=1, source_target_pairs={{8,0},{9,1},{10,2},{11,3},{12,4},{13,5},{14,6},{15,7},{16,8},{17,9... | collective-permute-start | bytes 4718600 | tf_op jit(solution)/shard_map/ppermute | solution.py:80
  112.9 61.7 %collective-permute-start.18 = (bf16[2,3,256,512]{3,2,1,0:T(8,128)(2,1)}, bf16[2,3,256,512]{3,2,1,0:T(8,128)(2,1)}, u32[]{:S(2)}, u32[]{:S(2)}) collective-permute-start(bf16[2,3,256,512]{3,2,1,0:T(8,128)(2,1)} %collective-permute-done.17), channel_id=1, source_target_pairs={{8,0},{9,1},{10,2},{11,3},{12,4},{13,5},{14,6},{15,7},{16,8},{17,9... | collective-permute-start | bytes 4718600 | tf_op jit(solution)/shard_map/ppermute | solution.py:80
  114.2 63.2 %collective-permute-start.20 = (bf16[2,3,256,512]{3,2,1,0:T(8,128)(2,1)}, bf16[2,3,256,512]{3,2,1,0:T(8,128)(2,1)}, u32[]{:S(2)}, u32[]{:S(2)}) collective-permute-start(bf16[2,3,256,512]{3,2,1,0:T(8,128)(2,1)} %collective-permute-done.16), channel_id=1, source_target_pairs={{8,16},{9,17},{10,18},{11,19},{12,20},{13,21},{14,22},{15,23},{16,... | collective-permute-start | bytes 4718600 | tf_op jit(solution)/shard_map/ppermute | solution.py:80
  127.1 51.8 %collective-permute-start.31 = (bf16[256,1024]{1,0:T(8,128)(2,1)}, bf16[256,1024]{1,0:T(8,128)(2,1)}, u32[]{:S(2)}, u32[]{:S(2)}) collective-permute-start(bf16[256,1024]{1,0:T(8,128)(2,1)} %get-tuple-element.174), channel_id=1, source_target_pairs={{0,4},{1,5},{2,6},{3,7},{4,0},{5,1},{6,2},{7,3},{8,12},{9,13},{10,... | collective-permute-start | bytes 1572872 | tf_op jit(solution)/shard_map/ppermute | solution.py:74
  128.7 52.3 %collective-permute-start.29 = (bf16[256,1024]{1,0:T(8,128)(2,1)}, bf16[256,1024]{1,0:T(8,128)(2,1)}, u32[]{:S(2)}, u32[]{:S(2)}) collective-permute-start(bf16[256,1024]{1,0:T(8,128)(2,1)} %get-tuple-element.174), channel_id=1, source_target_pairs={{0,2},{1,3},{2,0},{3,1},{4,6},{5,7},{6,4},{7,5},{8,10},{9,11},{10,... | collective-permute-start | bytes 1572872 | tf_op jit(solution)/shard_map/ppermute | solution.py:74
  189.7 37.2 %collective-permute-start.11 = (bf16[1,512,1024]{2,1,0:T(8,128)(2,1)}, bf16[1,512,1024]{2,1,0:T(8,128)(2,1)}, u32[]{:S(2)}, u32[]{:S(2)}) collective-permute-start(bf16[1,512,1024]{2,1,0:T(8,128)(2,1)} %bitcast.35), channel_id=1, source_target_pairs={{0,1},{1,0},{2,3},{3,2},{4,5},{5,4},{6,7},{7,6},{8,9},{9,8},{10,11... | collective-permute-start | bytes 3145736 | tf_op jit(solution)/shard_map/ppermute | solution.py:74
  234.0 59.1 %collective-permute-start.37 = (bf16[1,512,1024]{2,1,0:T(8,128)(2,1)}, bf16[1,512,1024]{2,1,0:T(8,128)(2,1)}, u32[]{:S(2)}, u32[]{:S(2)}) collective-permute-start(bf16[1,512,1024]{2,1,0:T(8,128)(2,1)} %maximum_bitcast_fusion.1), channel_id=1, source_target_pairs={{0,1},{1,0},{2,3},{3,2},{4,5},{5,4},{6,7},{7,6},{8,9},{9,8},{10,11... | collective-permute-start | bytes 3145736 | tf_op jit(solution)/shard_map/ppermute | solution.py:74
  236.5 61.3 %collective-permute-start.35 = (bf16[1,512,1152]{2,1,0:T(8,128)(2,1)}, bf16[1,512,1152]{2,1,0:T(8,128)(2,1)}, u32[]{:S(2)}, u32[]{:S(2)}) collective-permute-start(bf16[1,512,1152]{2,1,0:T(8,128)(2,1)} %maximum_bitcast_fusion), channel_id=1, source_target_pairs={{0,1},{1,0},{2,3},{3,2},{4,5},{5,4},{6,7},{7,6},{8,9},{9,8},{10,11... | collective-permute-start | bytes 3538952 | tf_op jit(solution)/shard_map/ppermute | solution.py:74
  239.4 64.9 %collective-permute-start.33 = (bf16[2,512,1024]{2,1,0:T(8,128)(2,1)}, bf16[2,512,1024]{2,1,0:T(8,128)(2,1)}, u32[]{:S(2)}, u32[]{:S(2)}) collective-permute-start(bf16[2,512,1024]{2,1,0:T(8,128)(2,1)} %bitcast.67), channel_id=1, source_target_pairs={{0,1},{1,0},{2,3},{3,2},{4,5},{5,4},{6,7},{7,6},{8,9},{9,8},{10,11... | collective-permute-start | bytes 6291464 | tf_op jit(solution)/shard_map/ppermute | solution.py:74
  251.6 57.2 %collective-permute-start.27 = (bf16[2,512,1152]{2,1,0:T(8,128)(2,1)}, bf16[2,512,1152]{2,1,0:T(8,128)(2,1)}, u32[]{:S(2)}, u32[]{:S(2)}) collective-permute-start(bf16[2,512,1152]{2,1,0:T(8,128)(2,1)} %bitcast.66), channel_id=1, source_target_pairs={{0,1},{1,0},{2,3},{3,2},{4,5},{5,4},{6,7},{7,6},{8,9},{9,8},{10,11... | collective-permute-start | bytes 7077896 | tf_op jit(solution)/shard_map/ppermute | solution.py:74
  373.2 42.8 %collective-permute-start.42 = (bf16[512,1152]{1,0:T(8,128)(2,1)}, bf16[512,1152]{1,0:T(8,128)(2,1)}, u32[]{:S(2)}, u32[]{:S(2)}) collective-permute-start(bf16[512,1152]{1,0:T(8,128)(2,1)} %get-tuple-element.112), channel_id=1, source_target_pairs={{0,1},{1,0},{2,3},{3,2},{4,5},{5,4},{6,7},{7,6},{8,9},{9,8},{10,11... | collective-permute-start | bytes 3538952 | tf_op jit(solution)/shard_map/ppermute | solution.py:74
  373.2 42.8 %collective-permute-start.39 = (bf16[512,1152]{1,0:T(8,128)(2,1)}, bf16[512,1152]{1,0:T(8,128)(2,1)}, u32[]{:S(2)}, u32[]{:S(2)}) collective-permute-start(bf16[512,1152]{1,0:T(8,128)(2,1)} %get-tuple-element.113), channel_id=1, source_target_pairs={{0,1},{1,0},{2,3},{3,2},{4,5},{5,4},{6,7},{7,6},{8,9},{9,8},{10,11... | collective-permute-start | bytes 3538952 | tf_op jit(solution)/shard_map/ppermute | solution.py:74
  410.5 37.3 %collective-permute-start.78 = (bf16[2,3,8,32,512]{4,3,2,1,0:T(8,128)(2,1)S(1)}, bf16[2,3,8,32,512]{4,3,2,1,0:T(8,128)(2,1)S(1)}, u32[]{:S(2)}, u32[]{:S(2)}) collective-permute-start(bf16[2,3,8,32,512]{4,3,2,1,0:T(8,128)(2,1)S(1)} %dynamic-slice_bitcast_fusion.1), channel_id=1, source_target_pairs={{0,8},{1,9},{2,10},{3,11},{4,12},{5,13},{6,14},{7,15}} | collective-permute-start | bytes 4718600 | tf_op jit(solution)/shard_map/ppermute | solution.py:80
  419.4 37.1 %collective-permute-start.40 = (bf16[256,1152]{1,0:T(8,128)(2,1)S(1)}, bf16[256,1152]{1,0:T(8,128)(2,1)S(1)}, u32[]{:S(2)}, u32[]{:S(2)}) collective-permute-start(bf16[256,1152]{1,0:T(8,128)(2,1)S(1)} %slice.554), channel_id=1, source_target_pairs={{0,2},{1,3},{2,0},{3,1},{4,6},{5,7},{6,4},{7,5},{8,10},{9,11},{10,... | collective-permute-start | bytes 1769480 | tf_op jit(solution)/shard_map/ppermute | solution.py:74
  451.0 40.1 %collective-permute-start.79 = (bf16[2,3,8,32,512]{4,3,2,1,0:T(8,128)(2,1)}, bf16[2,3,8,32,512]{4,3,2,1,0:T(8,128)(2,1)}, u32[]{:S(2)}, u32[]{:S(2)}) collective-permute-start(bf16[2,3,8,32,512]{4,3,2,1,0:T(8,128)(2,1)} %fusion.13), channel_id=1, source_target_pairs={{0,8},{1,9},{2,10},{3,11},{4,12},{5,13},{6,14},{7,15},{8,16},{9,17... | collective-permute-start | bytes 4718600 | tf_op jit(solution)/shard_map/ppermute | solution.py:80
  496.9 106.1 %collective-permute-start.81 = (bf16[2,3,8,32,512]{4,3,2,1,0:T(8,128)(2,1)}, bf16[2,3,8,32,512]{4,3,2,1,0:T(8,128)(2,1)}, u32[]{:S(2)}, u32[]{:S(2)}) collective-permute-start(bf16[2,3,8,32,512]{4,3,2,1,0:T(8,128)(2,1)} %get-tuple-element.105), channel_id=1, source_target_pairs={{24,16},{25,17},{26,18},{27,19},{28,20},{29,21},{30,22},{31,23}} | collective-permute-start | bytes 4718600 | tf_op jit(solution)/shard_map/ppermute | solution.py:80
  603.0 60.2 %collective-permute-start.58 = (bf16[4,4,32,2176]{3,2,1,0:T(8,128)(2,1)}, bf16[4,4,32,2176]{3,2,1,0:T(8,128)(2,1)}, u32[]{:S(2)}, u32[]{:S(2)}) collective-permute-start(bf16[4,4,32,2176]{3,2,1,0:T(8,128)(2,1)} %dynamic-slice_bitcast_fusion), channel_id=1, source_target_pairs={{0,1},{1,0},{2,3},{3,2},{4,5},{5,4},{6,7},{7,6},{8,9},{9,8},{10,11... | collective-permute-start | bytes 6684680 | tf_op jit(solution)/shard_map/ppermute | solution.py:74
  606.7 52.4 %collective-permute-start.82 = (bf16[2,3,8,32,512]{4,3,2,1,0:T(8,128)(2,1)}, bf16[2,3,8,32,512]{4,3,2,1,0:T(8,128)(2,1)}, u32[]{:S(2)}, u32[]{:S(2)}) collective-permute-start(bf16[2,3,8,32,512]{4,3,2,1,0:T(8,128)(2,1)} %fusion.14), channel_id=1, source_target_pairs={{16,8},{17,9},{18,10},{19,11},{20,12},{21,13},{22,14},{23,15},{24,... | collective-permute-start | bytes 4718600 | tf_op jit(solution)/shard_map/ppermute | solution.py:80
  652.8 40.4 %collective-permute-start.80 = (bf16[2,3,8,32,512]{4,3,2,1,0:T(8,128)(2,1)S(1)}, bf16[2,3,8,32,512]{4,3,2,1,0:T(8,128)(2,1)S(1)}, u32[]{:S(2)}, u32[]{:S(2)}) collective-permute-start(bf16[2,3,8,32,512]{4,3,2,1,0:T(8,128)(2,1)S(1)} %copy-done.46), channel_id=1, source_target_pairs={{0,8},{1,9},{2,10},{3,11},{4,12},{5,13},{6,14},{7,15},{8,16},{9,17... | collective-permute-start | bytes 4718600 | tf_op jit(solution)/shard_map/ppermute | solution.py:80
  661.7 37.4 %collective-permute-start.83 = (bf16[2,3,8,32,512]{4,3,2,1,0:T(8,128)(2,1)S(1)}, bf16[2,3,8,32,512]{4,3,2,1,0:T(8,128)(2,1)S(1)}, u32[]{:S(2)}, u32[]{:S(2)}) collective-permute-start(bf16[2,3,8,32,512]{4,3,2,1,0:T(8,128)(2,1)S(1)} %add_convert_fusion), channel_id=1, source_target_pairs={{8,0},{9,1},{10,2},{11,3},{12,4},{13,5},{14,6},{15,7},{16,8},{17,9... | collective-permute-start | bytes 4718600 | tf_op jit(solution)/shard_map/ppermute | solution.py:80
  (128 other events, 1641.5 us)

commit v3 on v2

--- a/solution.py
+++ b/solution.py
@@ -173,32 +173,75 @@
     return lax.dot_general(left, right, (((1,), (1,)), ((), ())), preferred_element_type=f32)
 
 
-def expert_kernel(first_ref, packet_ref, cotangent_ref, weight_ref, *refs, fresh, last):
-    if fresh:
-        (out_ref, back_ref, grad_ref, packet_turned, cotangent_turned, sums) = refs
-    elif last:
-        (prior_ref, out_ref, back_ref, rounded_ref, packet_turned, cotangent_turned, grad_ref, sums,
-         arrival) = refs
+def expert_kernel(first_ref, *refs, layout, fresh, last):
+    refs = list(refs)
+    packet_parts = [[refs.pop(0) for _ in range(number)] for number in layout]
+    cotangent_parts = [[refs.pop(0) for _ in range(number)] for number in layout]
+    weight_parts = refs.pop(0)
+    prior_ref = None if fresh else refs.pop(0)
+    out_refs, back_refs = (refs.pop(0), refs.pop(0)), (refs.pop(0), refs.pop(0))
+    if last:
+        rounded_ref = refs.pop(0)
+        grad_ref = refs.pop(0)
     else:
-        (prior_ref, out_ref, back_ref, grad_ref, packet_turned, cotangent_turned, sums, arrival) = refs
-    width = cotangent_ref.shape[-1]
-    rows = cotangent_ref.shape[1]
+        grad_ref = refs.pop(0)
+    packet_buffer, cotangent_buffer, weight_ref, packet_turned, cotangent_turned, sums = refs[:6]
+    block_sem, weight_sem, prior_sem = refs[6:]
+    rows, width = cotangent_buffer.shape[1:]
+    groups, _, _, depth, _ = weight_parts.shape
+    blocks = len(layout)
+    at = pl.program_id(0)
     first = first_ref[0]
-    start = pl.program_id(0) == 0
-
-    @pl.when(start)
+
+    def block_copies(block):
+        copies = []
+        for kind, (parts, buffer) in enumerate(
+            ((packet_parts, packet_buffer), (cotangent_parts, cotangent_buffer))
+        ):
+            size = rows // layout[block]
+            for number, part in enumerate(parts[block]):
+                place = buffer.at[block, pl.ds(number * size, size)]
+                copies.append(
+                    pltpu.make_async_copy(part, place, block_sem.at[block, 2 * kind + number])
+                )
+        return copies
+
+    def weight_copies():
+        return [
+            pltpu.make_async_copy(
+                weight_parts.at[g], weight_ref.at[:, :, pl.ds(g * depth, depth)], weight_sem.at[g]
+            )
+            for g in range(groups)
+        ]
+
+    def prior_copy():
+        return pltpu.make_async_copy(prior_ref, grad_ref, prior_sem)
+
+    @pl.when(at == 0)
     def _():
+        for copy in block_copies(0) + weight_copies():
+            copy.start()
         if fresh:
             grad_ref[...] = jnp.zeros_like(grad_ref)
         else:
-            copy = pltpu.make_async_copy(prior_ref, grad_ref, arrival)
-            copy.start()
+            prior_copy().start()
+        for block in range(1, blocks):
+            for copy in block_copies(block):
+                copy.start()
+        for copy in weight_copies():
             copy.wait()
 
+    for block in range(blocks):
+
+        @pl.when(at == block)
+        def _():
+            for copy in block_copies(block):
+                copy.wait()
+
     lane = lax.broadcasted_iota(jnp.int32, (rows, EXTRA), 1)
-    normed = packet_ref[0, :, :width]
-    upstream = cotangent_ref[0]
-    shares = packet_ref[0, :, width:].astype(f32)
+    normed = packet_buffer[at, :, :width]
+    upstream = cotangent_buffer[at]
+    shares = packet_buffer[at, :, width:].astype(f32)
     extra = jnp.zeros((rows, EXTRA), f32)
     packet_turned[...] = normed.T
     cotangent_turned[...] = upstream.T
@@ -211,6 +254,12 @@
                 dot(upstream, weight_ref[local, 2]),
             )
         )
+    if not fresh:
+
+        @pl.when(at == 0)
+        def _():
+            prior_copy().wait()
+
     for local in range(LOCAL_EXPERTS):
         gate_pre, up_pre, inner_raw = begun[local]
         expert = first + local
@@ -234,64 +283,94 @@
         if local == 0:
             sums[0], sums[1] = out_term, back_term
         else:
-            out_ref[0] = (sums[0] + out_term).astype(bf16)
-            back_ref[0, :, :width] = (sums[1] + back_term).astype(bf16)
+            sums[0] += out_term
+            sums[1] += back_term
         grad_ref[local, 0] += dot(packet_turned[...], gate_grad)
         grad_ref[local, 1] += dot(packet_turned[...], up_grad)
         grad_ref[local, 2] += dot(cotangent_turned[...], inner_shared)
         high = share_grad.astype(bf16).astype(f32)
         extra = extra + jnp.where(is_high, high, 0.0) + jnp.where(is_low, share_grad - high, 0.0)
-    back_ref[0, :, width:] = extra.astype(bf16)
+    for side in range(2):
+
+        @pl.when((at < blocks // 2) == (side == 0))
+        def _():
+            out_refs[side][0] = sums[0].astype(bf16)
+            back_refs[side][0, :, :width] = sums[1].astype(bf16)
+            back_refs[side][0, :, width:] = extra.astype(bf16)
+
     if last:
-        @pl.when(pl.program_id(0) == pl.num_programs(0) - 1)
+
+        @pl.when(at == blocks - 1)
         def _():
-            rounded_ref[...] = grad_ref[...].astype(bf16)
+            for g in range(groups):
+                rounded_ref[g] = grad_ref[:, :, pl.ds(g * depth, depth)].astype(bf16)
 
 
 def run_experts(first, packets, cotangents, weights, prior, last):
-    block_count, rows, wide = packets.shape
-    width = cotangents.shape[-1]
-    hidden = weights.shape[-1]
+    layout = tuple(len(parts) for parts in packets)
+    blocks = len(layout)
+    rows = sum(part.shape[0] for part in packets[0])
+    wide, width = packets[0][0].shape[1], cotangents[0][0].shape[1]
+    groups, _, _, depth, hidden = weights.shape
     grad_shape = (LOCAL_EXPERTS, 3, width, hidden)
     fresh = prior is None
-    in_specs = [
-        pl.BlockSpec((1, rows, wide), lambda i, s: (i, 0, 0)),
-        pl.BlockSpec((1, rows, width), lambda i, s: (i, 0, 0)),
-        pl.BlockSpec(grad_shape, lambda i, s: (0, 0, 0, 0), pipeline_mode=pl.Buffered(1)),
+    operands = [part for parts in packets for part in parts]
+    operands += [part for parts in cotangents for part in parts]
+    operands += [weights] + ([] if fresh else [prior])
+    half = blocks // 2
+
+    def own_side(i, s):
+        return (jnp.minimum(i, half - 1), 0, 0)
+
+    def other_side(i, s):
+        return (jnp.maximum(i - half, 0), 0, 0)
+
+    def whole(i, s):
+        return (0, 0, 0, 0, 0) if last else (0, 0, 0, 0)
+
+    last_shape = weights.shape if last else grad_shape
+    scratch = [pltpu.VMEM(grad_shape, f32)] if last else []
+    scratch += [
+        pltpu.VMEM((blocks, rows, wide), bf16),
+        pltpu.VMEM((blocks, rows, width), bf16),
+        pltpu.VMEM(grad_shape, bf16),
+        pltpu.VMEM((width, rows), bf16),
+        pltpu.VMEM((width, rows), bf16),
+        pltpu.VMEM((2, rows, width), f32),
+        pltpu.SemaphoreType.DMA((blocks, 4)),
+        pltpu.SemaphoreType.DMA((groups,)),
+        pltpu.SemaphoreType.DMA,
     ]
-    scratch = [pltpu.VMEM((width, rows), bf16), pltpu.VMEM((width, rows), bf16)]
-    if last:
-        scratch.append(pltpu.VMEM(grad_shape, f32))
-    scratch.append(pltpu.VMEM((2, rows, width), f32))
-    if not fresh:
-        in_specs.append(pl.BlockSpec(memory_space=pl.ANY))
-        scratch.append(pltpu.SemaphoreType.DMA)
     return pl.pallas_call(
-        functools.partial(expert_kernel, fresh=fresh, last=last),
+        functools.partial(expert_kernel, layout=layout, fresh=fresh, last=last),
         grid_spec=pltpu.PrefetchScalarGridSpec(
             num_scalar_prefetch=1,
-            grid=(block_count,),
-            in_specs=in_specs,
+            grid=(blocks,),
+            in_specs=[pl.BlockSpec(memory_space=pl.ANY)] * len(operands),
             out_specs=[
-                pl.BlockSpec((1, rows, width), lambda i, s: (i, 0, 0)),
-                pl.BlockSpec((1, rows, wide), lambda i, s: (i, 0, 0)),
-                pl.BlockSpec(grad_shape, lambda i, s: (0, 0, 0, 0), pipeline_mode=pl.Buffered(1)),
+                pl.BlockSpec((1, rows, width), own_side),
+                pl.BlockSpec((1, rows, width), other_side),
+                pl.BlockSpec((1, rows, wide), own_side),
+                pl.BlockSpec((1, rows, wide), other_side),
+                pl.BlockSpec(last_shape, whole, pipeline_mode=pl.Buffered(1)),
             ],
             scratch_shapes=scratch,
         ),
         out_shape=[
-            jax.ShapeDtypeStruct((block_count, rows, width), bf16),
-            jax.ShapeDtypeStruct((block_count, rows, wide), bf16),
-            jax.ShapeDtypeStruct(grad_shape, bf16 if last else f32),
+            jax.ShapeDtypeStruct((half, rows, width), bf16),
+            jax.ShapeDtypeStruct((half, rows, width), bf16),
+            jax.ShapeDtypeStruct((half, rows, wide), bf16),
+            jax.ShapeDtypeStruct((half, rows, wide), bf16),
+            jax.ShapeDtypeStruct(last_shape, bf16 if last else f32),
         ],
-        compiler_params=pltpu.CompilerParams(vmem_limit_bytes=60 * 1024 * 1024),
+        compiler_params=pltpu.CompilerParams(vmem_limit_bytes=62 * 1024 * 1024),
         cost_estimate=pl.CostEstimate(
-            flops=block_count * LOCAL_EXPERTS * 9 * 2 * rows * width * hidden,
-            bytes_accessed=block_count * rows * width * 8 + 36 * width * hidden,
-            transcendentals=block_count * LOCAL_EXPERTS * rows * hidden,
+            flops=blocks * LOCAL_EXPERTS * 9 * 2 * rows * width * hidden,
+            bytes_accessed=blocks * rows * width * 8 + 36 * width * hidden,
+            transcendentals=blocks * LOCAL_EXPERTS * rows * hidden,
         ),
         name="experts",
-    )(first, packets, cotangents, weights, *(() if fresh else (prior,)))
+    )(first, *operands)
 
 
 def local(
@@ -355,12 +434,8 @@
     mine = mine.reshape(MEMBERS, LOCAL_EXPERTS, 3, shard, hidden)
     shelf = links.send_parts(mine).transpose(1, 2, 0, 3, 4)
     shelf = shelf.reshape(LOCAL_EXPERTS, 3, MEMBERS * shard, hidden)
-    expert_full = jnp.zeros((LOCAL_EXPERTS, 3, groups, MEMBERS * shard, hidden), bf16)
-    for back, piece in enumerate(links.line_gather(shelf)):
-        expert_full = lax.dynamic_update_index_in_dim(
-            expert_full, piece, (group + groups - back) % groups, 2
-        )
-    expert_full = expert_full.reshape(LOCAL_EXPERTS, 3, width, hidden)
+    lines = [[m + MEMBERS * g for g in range(groups)] for m in range(MEMBERS)]
+    expert_full = lax.all_gather(shelf, "fsdp", axis_index_groups=lines)
     late_cotangent, whole = lax.optimization_barrier((cotangent, whole))
     cotangents = links.chips_gather(late_cotangent)
 
@@ -413,6 +488,8 @@
         axis=1,
     )
     packets = links.chips_gather(packet)
+    packets[0] = (packet,)
+    cotangents[0] = (late_cotangent,)
 
     first = (member * LOCAL_EXPERTS).astype(jnp.int32).reshape(1)
     out_terms, back_terms = {}, {}
@@ -421,28 +498,26 @@
     for turn in turns:
         stacks = []
         for blocks in (packets, cotangents):
-            even = jnp.concatenate([part for k in turn for part in blocks[k]], axis=0)
-            even = even.reshape(len(turn), row_count, even.shape[-1])
-            stacks.append(jnp.concatenate([even, links.swap(even, 1)], axis=0))
-        outs, backs, grads = run_experts(
+            even = [blocks[k] for k in turn]
+            stacks.append(even + [tuple(links.swap(part, 1) for part in parts) for parts in even])
+        out_own, out_other, back_own, back_other, grads = run_experts(
             first, stacks[0], stacks[1], expert_full, grads, turn == turns[-1]
         )
+        back_join = links.join_cores(back_own, back_other)
         for at, k in enumerate(turn):
-            out_terms[k], out_terms[k + 1] = outs[at], outs[len(turn) + at]
-            back_terms[k] = links.join_cores(backs[at], backs[len(turn) + at])
+            out_terms[k] = (out_own[at], out_other[at])
+            back_terms[k] = back_join[at]
 
     back_total = links.chips_reduce(back_terms)
 
-    grads = grads.reshape(LOCAL_EXPERTS, 3, groups, MEMBERS, shard, hidden)
-    shelf_grad = links.line_reduce(
-        lambda owner: lax.dynamic_index_in_dim(grads, owner, 2, keepdims=False).astype(f32)
-    ).astype(bf16)
+    shelf_grad = lax.psum_scatter(grads, "fsdp", scatter_dimension=0, axis_index_groups=lines)
+    shelf_grad = shelf_grad.reshape(LOCAL_EXPERTS, 3, MEMBERS, shard, hidden)
     expert_shards = links.send_parts(shelf_grad.transpose(2, 0, 1, 3, 4)).astype(f32)
     expert_shards = expert_shards.reshape(EXPERTS, 3, shard, hidden)
 
     out_terms, back_total = lax.optimization_barrier((out_terms, back_total))
     mixture = links.chips_reduce(
-        {k: links.join_cores(out_terms[k], out_terms[k + 1]) for k in (6, 2, 4, 0)}
+        {k: links.join_cores(*out_terms[k]) for k in (6, 2, 4, 0)}
     )
     layer_out = (middle + mixture).astype(bf16)
 

time: 735 us -> 613 us (0.83)
  other arithmetic: 121 us -> 52.6 us
  waiting for transfers between devices: 221 us -> 188 us
  starting transfers between devices: 104 us -> 77.5 us
  between operations: 3.31 us -> 16.8 us
    ppermute x12 -> x0, waiting for transfers between devices: 56 us -> none  [shift(): return lax.ppermute(value, 'fsdp', pairs)]
    ppermute x12 -> x0, starting transfers between devices: 28.6 us -> none  [shift(): return lax.ppermute(value, 'fsdp', pairs)]
    concatenate x8 -> x0, other arithmetic: 27 us -> none  [the longest x6 21.1 us: local(): stacks.append(jnp.concatenate([even, links.swap(even, 1)], axis=0))]
    ppermute x76 -> x83, waiting for transfers between devices: 165 us -> 185 us  [swap(): lax.ppermute(value, 'fsdp', [(i, i ^ bits) for i in range(self.count)])]
    convert_element_type x4 -> x0, other arithmetic: 14 us -> none  [the longest x2 7.71 us: line_reduce(): rising = self.shift(up.astype(bf16), range(0, step), 1)]
    squeeze x7 -> x1, local copies, waits for them, and re-layouts: 13.9 us -> 4.35 us  [local(): out_terms[k] = (out_own[at], out_other[at])]
    unnamed x133 -> x139, local copies, waits for them, and re-layouts: 8.29 us -> 17.5 us
    dynamic_update_slice x3 -> x0, other arithmetic: 7.64 us -> none  [local(): lax.dynamic_update_index_in_dim(expert_full, piece, (group + groups - bac...]
  transfers between devices with their start and end apart: 88 -> 85, of which waited for: 32 -> 34; matrix products, arithmetic and copies ran while one was open for 35% -> 29% of each run, Pallas kernels for 9% -> 19%
where the time goes in v3:
time: 613 us; the launch traced here: 604 us
  waiting for transfers between devices  188 us (31%)
  Pallas kernels  117 us (19%)
  local copies, waits for them, and re-layouts  81.6 us (13%)
  starting transfers between devices  77.5 us (13%)
  matrix products  71.4 us (12%)
  other arithmetic  52.6 us (9%)
  between operations  16.8 us (3%)
    ppermute x83, waiting for transfers between devices, swap(): lax.ppermute(value, 'fsdp', [(i, i ^ bits) for i in range(self.count)])  185 us
    pallas_call x3, Pallas kernels, run_experts(): pl.pallas_call(functools.partial(expert_kernel, layout=layout, fresh=fres...  117 us
    ppermute x83, starting transfers between devices, swap(): lax.ppermute(value, 'fsdp', [(i, i ^ bits) for i in range(self.count)])  77.4 us
    unnamed x139, local copies, waits for them, and re-layouts  17.5 us
    dot_general x6, matrix products, dot(): return jnp.dot(left, right, preferred_element_type=f32)  16 us
    dot_general x1, matrix products, local(): jnp.einsum('qkgd,pkd->kgqp', mixed_grad, value_rows, preferred_element_ty...  15 us
    concatenate x4, local copies, waits for them, and re-layouts, reduce_pack(): jnp.concatenate(parts + [jnp.zeros((width, spare), f32)], axis=1)  14.4 us
  transfers between devices with their start and end apart: 85, of which 34 were waited for; matrix products, arithmetic and copies ran while one was open for 29% of the time, Pallas kernels for 19%

profile of v3, /device:TPU:0, one launch (start us, length us, event | category | flops | bytes accessed | tf_op | source)
XLA Modules:
  0.0 604.5 jit_solution(2201090364149622843)
XLA Ops:
  23.4 7.9 %collective-permute-done.1 = bf16[32,3200]{1,0:T(8,128)(2,1)S(1)} collective-permute-done((bf16[32,3200]{1,0:T(8,128)(2,1)S(1)}, bf16[32,3200]{1,0:T(8,128)(2,1)S(1)}, u32[]{:S(2)}, u32[]{:S(2)}) %collective-permute-start.1) | collective-permute-done | bytes 204832 | tf_op jit(solution)/shard_map/ppermute | solution.py:74
  36.6 14.6 %collective-permute-done.3 = bf16[64,3200]{1,0:T(8,128)(2,1)S(1)} collective-permute-done((bf16[64,3200]{1,0:T(8,128)(2,1)S(1)}, bf16[64,3200]{1,0:T(8,128)(2,1)S(1)}, u32[]{:S(2)}, u32[]{:S(2)}) %collective-permute-start.3) | collective-permute-done | bytes 409632 | tf_op jit(solution)/shard_map/ppermute | solution.py:74
  75.7 7.7 %collective-permute-done.13 = bf16[2,2,3,32,512]{4,3,2,1,0:T(8,128)(2,1)} collective-permute-done((bf16[2,2,3,32,512]{4,3,2,1,0:T(8,128)(2,1)}, bf16[2,2,3,32,512]{4,3,2,1,0:T(8,128)(2,1)}, u32[]{:S(2)}, u32[]{:S(2)}) %collective-permute-start.13) | collective-permute-done | bytes 393248 | tf_op jit(solution)/shard_map/ppermute | solution.py:74
  117.8 7.4 %fusion.110 = (f32[8,2,512]{2,1,0:T(2,128)S(1)}, f32[8,2,512,512]{2,3,1,0:T(8,128)}) fusion(bf16[512,8,64,1]{0,2,3,1:T(8,128)(2,1)S(1)} %fusion.67, bf16[512,8,2,64]{0,3,2,1:T(8,128)(2,1)S(1)} %fusion.23, pred[512,512]{0,1:T(8,128)(4,1)S(1)} %copy-done.33), kind=kOutput, calls=%fused_computation.269 | convolution fusion | flops 549445632 | bytes 18644992 | tf_op jit(solution)/shard_map/qkgd,pkd->kgqp/dot_general | solution.py:61
  125.2 8.4 %fusion.3 = f32[8,2,512]{2,1,0:T(2,128)S(1)} fusion(f32[8,2,512,512]{2,3,1,0:T(8,128)} %get-tuple-element.236, f32[8,2,512]{2,1,0:T(2,128)S(1)} %get-tuple-element.235), kind=kLoop, calls=%fused_computation.9 | loop fusion | flops 8380416 | bytes 16842752 | tf_op jit(solution)/shard_map/reduce_sum | solution.py:463
  133.6 7.7 %fusion.32 = bf16[8,64,2,512]{3,1,2,0:T(8,128)(2,1)S(1)} fusion(bf16[512,8,64,1]{0,2,3,1:T(8,128)(2,1)S(1)} %bitcast.344, f32[8,2,512,512]{2,3,1,0:T(8,128)} %get-tuple-element.236, f32[8,2,512]{2,1,0:T(2,128)S(1)} %fusion.3, f32[8,2,512]{2,1,0:T(2,128)S(1)} %get-tuple-element.235), kind=kOutput, calls=%fused_computation.71 | convolution fusion | flops 549978112 | bytes 18415616 | tf_op jit(solution)/shard_map/kgqp,pkd->qkgd/dot_general | solution.py:467
  155.0 10.3 %collective-permute-done.16.refs_0_ = bf16[256,1152]{1,0:T(8,128)(2,1)} collective-permute-done((bf16[256,1152]{1,0:T(8,128)(2,1)S(1)}, bf16[256,1152]{1,0:T(8,128)(2,1)}, u32[]{:S(2)}, u32[]{:S(2)}) %collective-permute-start.16) | collective-permute-done | bytes 589856 | tf_op jit(solution)/shard_map/ppermute | solution.py:74
  167.3 10.5 %collective-permute-done.17.refs_1_ = bf16[256,1152]{1,0:T(8,128)(2,1)S(1)} collective-permute-done((bf16[256,1152]{1,0:T(8,128)(2,1)S(1)}, bf16[256,1152]{1,0:T(8,128)(2,1)S(1)}, u32[]{:S(2)}, u32[]{:S(2)}) %collective-permute-start.17) | collective-permute-done | bytes 589856 | tf_op jit(solution)/shard_map/ppermute | solution.py:74
  179.3 8.6 %collective-permute-done.27.refs_10_ = bf16[256,1024]{1,0:T(8,128)(2,1)S(1)} collective-permute-done((bf16[256,1024]{1,0:T(8,128)(2,1)}, bf16[256,1024]{1,0:T(8,128)(2,1)S(1)}, u32[]{:S(2)}, u32[]{:S(2)}) %collective-permute-start.27) | collective-permute-done | bytes 524320 | tf_op jit(solution)/shard_map/ppermute | solution.py:74
  191.8 12.1 %collective-permute-done.18.refs_2_ = bf16[256,1152]{1,0:T(8,128)(2,1)} collective-permute-done((bf16[256,1152]{1,0:T(8,128)(2,1)}, bf16[256,1152]{1,0:T(8,128)(2,1)}, u32[]{:S(2)}, u32[]{:S(2)}) %collective-permute-start.18) | collective-permute-done | bytes 589856 | tf_op jit(solution)/shard_map/ppermute | solution.py:74
  209.8 31.8 %experts.3 = (bf16[1,512,1024]{2,1,0:T(8,128)(2,1)}, bf16[1,512,1024]{2,1,0:T(8,128)(2,1)}, bf16[1,512,1152]{2,1,0:T(8,128)(2,1)}, bf16[1,512,1152]{2,1,0:T(8,128)(2,1)}, f32[2,3,1024,512]{3,2,1,0:T(8,128)}) custom-call(s32[1]{0:T(128)} %bitcast.33.first_ref, bf16[512,1152]{1,0:T(8,128)(2,1)} %copy-done.23, ...), custom_call_target="tpu_custom_call" | custom-call | flops 19327352832 | bytes 27262976 | tf_op jit(solution)/shard_map/experts/pallas_call | solution.py:344
  242.7 54.1 %experts.4 = (bf16[2,512,1024]{2,1,0:T(8,128)(2,1)}, bf16[2,512,1024]{2,1,0:T(8,128)(2,1)}, bf16[2,512,1152]{2,1,0:T(8,128)(2,1)}, bf16[2,512,1152]{2,1,0:T(8,128)(2,1)}, f32[2,3,1024,512]{3,2,1,0:T(8,128)}) custom-call(s32[1]{0:T(128)} %bitcast.33.first_ref, bf16[256,1152]{1,0:T(8,128)(2,1)} %collective-permute-done.16.refs_0_, ...), custom_call_target="tpu_custom_call" | custom-call | flops 38654705664 | bytes 35651584 | tf_op jit(solution)/shard_map/experts/pallas_call | solution.py:344
  297.0 30.6 %experts.5 = (bf16[1,512,1024]{2,1,0:T(8,128)(2,1)}, bf16[1,512,1024]{2,1,0:T(8,128)(2,1)}, bf16[1,512,1152]{2,1,0:T(8,128)(2,1)}, bf16[1,512,1152]{2,1,0:T(8,128)(2,1)}, bf16[4,2,3,256,512]{4,3,2,1,0:T(8,128)(2,1)}) custom-call(s32[1]{0:T(128)} %bitcast.33.first_ref, bf16[256,1152]{1,0:T(8,128)(2,1)} %copy-done.53, ...), custom_call_target="tpu_custom_call" | custom-call | flops 19327352832 | bytes 27262976 | tf_op jit(solution)/shard_map/experts/pallas_call | solution.py:344
  340.1 11.1 %collective-permute-done.46 = bf16[256,1152]{1,0:T(8,128)(2,1)S(1)} collective-permute-done((bf16[256,1152]{1,0:T(8,128)(2,1)S(1)}, bf16[256,1152]{1,0:T(8,128)(2,1)S(1)}, u32[]{:S(2)}, u32[]{:S(2)}) %collective-permute-start.46) | collective-permute-done | bytes 589856 | tf_op jit(solution)/shard_map/ppermute | solution.py:74
  354.8 9.1 %collective-permute-done.48 = bf16[256,1152]{1,0:T(8,128)(2,1)S(1)} collective-permute-done((bf16[256,1152]{1,0:T(8,128)(2,1)S(1)}, bf16[256,1152]{1,0:T(8,128)(2,1)S(1)}, u32[]{:S(2)}, u32[]{:S(2)}) %collective-permute-start.48) | collective-permute-done | bytes 589856 | tf_op jit(solution)/shard_map/ppermute | solution.py:74
  365.7 11.9 %collective-permute-done.47 = bf16[256,1152]{1,0:T(8,128)(2,1)S(1)} collective-permute-done((bf16[256,1152]{1,0:T(8,128)(2,1)S(1)}, bf16[256,1152]{1,0:T(8,128)(2,1)S(1)}, u32[]{:S(2)}, u32[]{:S(2)}) %collective-permute-start.47) | collective-permute-done | bytes 589856 | tf_op jit(solution)/shard_map/ppermute | solution.py:74
  399.6 7.2 %collective-permute-done.56 = bf16[256,1024]{1,0:T(8,128)(2,1)S(1)} collective-permute-done((bf16[256,1024]{1,0:T(8,128)(2,1)S(1)}, bf16[256,1024]{1,0:T(8,128)(2,1)S(1)}, u32[]{:S(2)}, u32[]{:S(2)}) %collective-permute-start.56) | collective-permute-done | bytes 524320 | tf_op jit(solution)/shard_map/ppermute | solution.py:74
  408.5 12.6 %collective-permute-done.54 = bf16[256,1024]{1,0:T(8,128)(2,1)S(1)} collective-permute-done((bf16[256,1024]{1,0:T(8,128)(2,1)S(1)}, bf16[256,1024]{1,0:T(8,128)(2,1)S(1)}, u32[]{:S(2)}, u32[]{:S(2)}) %collective-permute-start.54) | collective-permute-done | bytes 524320 | tf_op jit(solution)/shard_map/ppermute | solution.py:74
  422.5 8.7 %collective-permute-done.57 = bf16[256,1024]{1,0:T(8,128)(2,1)S(1)} collective-permute-done((bf16[256,1024]{1,0:T(8,128)(2,1)S(1)}, bf16[256,1024]{1,0:T(8,128)(2,1)S(1)}, u32[]{:S(2)}, u32[]{:S(2)}) %collective-permute-start.57) | collective-permute-done | bytes 524320 | tf_op jit(solution)/shard_map/ppermute | solution.py:74
  442.1 15.0 %fusion = (f32[8,2,512]{2,1,0:T(2,128)S(1)}, f32[8,512,512,2]{2,1,3,0:T(8,128)}) fusion(f32[8,2,512,512]{2,3,1,0:T(8,128)} %get-tuple-element.236, f32[8,2,512]{2,1,0:T(2,128)} %bitcast.367, bf16[512,8,64,1]{0,2,3,1:T(8,128)(2,1)S(1)} %bitcast.345, bf16[512,8,2,64]{0,3,2,1:T(8,128)(2,1)S(1)} %bitcast.312), kind=kOutput, calls=%fused_computation.2 | convolution fusion | flops 549445632 | bytes 35192832 | tf_op jit(solution)/shard_map/qkgd,pkd->kgqp/dot_general | solution.py:562
  457.2 8.7 %fusion.2 = bf16[8,2,512,512]{2,3,1,0:T(8,128)(2,1)S(1)} fusion(f32[8,512,512,2]{2,1,3,0:T(8,128)} %get-tuple-element.243, f32[8,2,512,512]{2,3,1,0:T(8,128)S(1)} %bitcast.308, f32[8,2,512]{2,1,0:T(2,128)S(1)} %get-tuple-element.242, f32[8,2,512]{2,1,0:T(2,128)S(1)} %bitcast.368), kind=kLoop, calls=%fused_computation.4 | loop fusion | flops 20971520 | bytes 42008576 | tf_op jit(solution)/shard_map/convert_element_type | solution.py:564
  472.9 7.1 %broadcast_multiply_fusion = (f32[512,8,64]{0,2,1:T(8,128)S(1)}, f32[512,8,64]{0,2,1:T(8,128)}) fusion(f32[512,64]{0,1:T(8,128)S(1)} %copy-done.14, bf16[512,8,2,64]{0,3,2,1:T(8,128)(2,1)S(1)} %copy-done.2, bf16[8,2,512,512]{2,3,1,0:T(8,128)(2,1)} %copy-done), kind=kOutput, calls=%fused_computation.152 | convolution fusion | flops 537133056 | bytes 11665408 | tf_op jit(solution)/shard_map/kgqp,qkgd->pkd/dot_general | solution.py:571
  511.7 8.0 %concatenate.99 = bf16[4,4,2,32,2176]{4,3,2,1,0:T(8,128)(2,1)} concatenate(bf16[4,4,2,32,2048]{4,3,2,1,0:T(8,128)(2,1)} %bitcast.334, bf16[4,4,2,32,1]{4,3,2,1,0:T(8,128)(2,1)} %concatenate.105, bf16[4,4,2,32,127]{4,3,2,1,0:T(8,128)(2,1)} %broadcast_in_dim.166), dimensions={4} | concatenate | bytes 8912896 | tf_op jit(solution)/shard_map/concatenate | solution.py:526
  585.8 6.5 %collective-permute-done.80 = bf16[2,2,3,32,512]{4,3,2,1,0:T(8,128)(2,1)S(1)} collective-permute-done((bf16[2,2,3,32,512]{4,3,2,1,0:T(8,128)(2,1)S(1)}, bf16[2,2,3,32,512]{4,3,2,1,0:T(8,128)(2,1)S(1)}, u32[]{:S(2)}, u32[]{:S(2)}) %collective-permute-start.80) | collective-permute-done | bytes 393248 | tf_op jit(solution)/shard_map/ppermute | solution.py:74
  (460 shorter events, 270.1 us)
Async XLA Ops:
  7.2 202.6 %all-gather.2.cloned.1.call-start = ((), (), s32[]{:S(2)}) async-start(), calls=%async_computation.1 | async-start | bytes 7864320 | tf_op jit(solution)/shard_map/all_gather | solution.py:438
  61.3 29.7 %collective-permute-start.9 = (bf16[4,128,3200]{2,1,0:T(8,128)(2,1)}, bf16[4,128,3200]{2,1,0:T(8,128)(2,1)}, u32[]{:S(2)}, u32[]{:S(2)}) collective-permute-start(bf16[4,128,3200]{2,1,0:T(8,128)(2,1)} %pad_maximum_fusion), channel_id=1, source_target_pairs={{0,1},{1,0},{2,3},{3,2},{4,5},{5,4},{6,7},{7,6},{8,9},{9,8},{10,11... | collective-permute-start | bytes 9830408 | tf_op jit(solution)/shard_map/ppermute | solution.py:74
  91.0 481.8 %reduce-scatter.2.cloned.1.call-start = ((), (), s32[]{:S(2)}) async-start(), calls=%async_computation.2 | async-start | bytes 7864320 | tf_op jit(solution)/shard_map/reduce_scatter | solution.py:513
  105.8 45.6 %collective-permute-start.28 = (bf16[256,1024]{1,0:T(8,128)(2,1)}, bf16[256,1024]{1,0:T(8,128)(2,1)}, u32[]{:S(2)}, u32[]{:S(2)}) collective-permute-start(bf16[256,1024]{1,0:T(8,128)(2,1)} %get-tuple-element.212), channel_id=1, source_target_pairs={{0,4},{1,5},{2,6},{3,7},{4,0},{5,1},{6,2},{7,3},{8,12},{9,13},{10,... | collective-permute-start | bytes 1572872 | tf_op jit(solution)/shard_map/ppermute | solution.py:74
  108.4 44.6 %collective-permute-start.26 = (bf16[256,1024]{1,0:T(8,128)(2,1)}, bf16[256,1024]{1,0:T(8,128)(2,1)}, u32[]{:S(2)}, u32[]{:S(2)}) collective-permute-start(bf16[256,1024]{1,0:T(8,128)(2,1)} %get-tuple-element.212), channel_id=1, source_target_pairs={{0,2},{1,3},{2,0},{3,1},{4,6},{5,7},{6,4},{7,5},{8,10},{9,11},{10,... | collective-permute-start | bytes 1572872 | tf_op jit(solution)/shard_map/ppermute | solution.py:74
  108.9 40.7 %collective-permute-start.25 = (bf16[256,1024]{1,0:T(8,128)(2,1)}, bf16[256,1024]{1,0:T(8,128)(2,1)}, u32[]{:S(2)}, u32[]{:S(2)}) collective-permute-start(bf16[256,1024]{1,0:T(8,128)(2,1)} %get-tuple-element.213), channel_id=1, source_target_pairs={{0,2},{1,3},{2,0},{3,1},{4,6},{5,7},{6,4},{7,5},{8,10},{9,11},{10,... | collective-permute-start | bytes 1572872 | tf_op jit(solution)/shard_map/ppermute | solution.py:74
  110.4 42.6 %collective-permute-start.37 = (bf16[256,1024]{1,0:T(8,128)(2,1)}, bf16[256,1024]{1,0:T(8,128)(2,1)}, u32[]{:S(2)}, u32[]{:S(2)}) collective-permute-start(bf16[256,1024]{1,0:T(8,128)(2,1)} %get-tuple-element.213), channel_id=1, source_target_pairs={{0,4},{1,5},{2,6},{3,7},{4,0},{5,1},{6,2},{7,3},{8,12},{9,13},{10,... | collective-permute-start | bytes 1572872 | tf_op jit(solution)/shard_map/ppermute | solution.py:74
  153.0 34.9 %collective-permute-start.27 = (bf16[256,1024]{1,0:T(8,128)(2,1)}, bf16[256,1024]{1,0:T(8,128)(2,1)S(1)}, u32[]{:S(2)}, u32[]{:S(2)}) collective-permute-start(bf16[256,1024]{1,0:T(8,128)(2,1)} %collective-permute-done.25.refs_8_), channel_id=1, source_target_pairs={{0,4},{1,5},{2,6},{3,7},{4,0},{5,1},{6,2},{7,3},{8,12},{9,13},{10,... | collective-permute-start | bytes 1572872 | tf_op jit(solution)/shard_map/ppermute | solution.py:74
  165.2 40.7 %collective-permute-start.10 = (bf16[512,1152]{1,0:T(8,128)(2,1)S(1)}, bf16[512,1152]{1,0:T(8,128)(2,1)}, u32[]{:S(2)}, u32[]{:S(2)}) collective-permute-start(bf16[512,1152]{1,0:T(8,128)(2,1)S(1)} %concatenate.91.refs_0_), channel_id=1, source_target_pairs={{0,1},{1,0},{2,3},{3,2},{4,5},{5,4},{6,7},{7,6},{8,9},{9,8},{10,11... | collective-permute-start | bytes 3538952 | tf_op jit(solution)/shard_map/ppermute | solution.py:74
  191.3 50.3 %collective-permute-start.22 = (bf16[256,1152]{1,0:T(8,128)(2,1)}, bf16[256,1152]{1,0:T(8,128)(2,1)}, u32[]{:S(2)}, u32[]{:S(2)}) collective-permute-start(bf16[256,1152]{1,0:T(8,128)(2,1)} %copy-done.54), channel_id=1, source_target_pairs={{0,1},{1,0},{2,3},{3,2},{4,5},{5,4},{6,7},{7,6},{8,9},{9,8},{10,11... | collective-permute-start | bytes 1769480 | tf_op jit(solution)/shard_map/ppermute | solution.py:74
  204.0 37.8 %collective-permute-start.32 = (bf16[256,1024]{1,0:T(8,128)(2,1)}, bf16[256,1024]{1,0:T(8,128)(2,1)}, u32[]{:S(2)}, u32[]{:S(2)}) collective-permute-start(bf16[256,1024]{1,0:T(8,128)(2,1)} %copy-done.56), channel_id=1, source_target_pairs={{0,1},{1,0},{2,3},{3,2},{4,5},{5,4},{6,7},{7,6},{8,9},{9,8},{10,11... | collective-permute-start | bytes 1572872 | tf_op jit(solution)/shard_map/ppermute | solution.py:74
  205.4 36.8 %collective-permute-start.33 = (bf16[256,1024]{1,0:T(8,128)(2,1)}, bf16[256,1024]{1,0:T(8,128)(2,1)}, u32[]{:S(2)}, u32[]{:S(2)}) collective-permute-start(bf16[256,1024]{1,0:T(8,128)(2,1)} %copy-done.57), channel_id=1, source_target_pairs={{0,1},{1,0},{2,3},{3,2},{4,5},{5,4},{6,7},{7,6},{8,9},{9,8},{10,11... | collective-permute-start | bytes 1572872 | tf_op jit(solution)/shard_map/ppermute | solution.py:74
  205.4 36.9 %collective-permute-start.23 = (bf16[256,1152]{1,0:T(8,128)(2,1)}, bf16[256,1152]{1,0:T(8,128)(2,1)}, u32[]{:S(2)}, u32[]{:S(2)}) collective-permute-start(bf16[256,1152]{1,0:T(8,128)(2,1)} %collective-permute-done.18.refs_2_), channel_id=1, source_target_pairs={{0,1},{1,0},{2,3},{3,2},{4,5},{5,4},{6,7},{7,6},{8,9},{9,8},{10,11... | collective-permute-start | bytes 1769480 | tf_op jit(solution)/shard_map/ppermute | solution.py:74
  206.2 36.5 %collective-permute-start.24 = (bf16[256,1152]{1,0:T(8,128)(2,1)}, bf16[256,1152]{1,0:T(8,128)(2,1)}, u32[]{:S(2)}, u32[]{:S(2)}) collective-permute-start(bf16[256,1152]{1,0:T(8,128)(2,1)} %collective-permute-done.20.refs_3_), channel_id=1, source_target_pairs={{0,1},{1,0},{2,3},{3,2},{4,5},{5,4},{6,7},{7,6},{8,9},{9,8},{10,11... | collective-permute-start | bytes 1769480 | tf_op jit(solution)/shard_map/ppermute | solution.py:74
  241.6 55.4 %collective-permute-start.39 = (bf16[256,1024]{1,0:T(8,128)(2,1)}, bf16[256,1024]{1,0:T(8,128)(2,1)}, u32[]{:S(2)}, u32[]{:S(2)}) collective-permute-start(bf16[256,1024]{1,0:T(8,128)(2,1)} %collective-permute-done.28.refs_5_), channel_id=1, source_target_pairs={{0,1},{1,0},{2,3},{3,2},{4,5},{5,4},{6,7},{7,6},{8,9},{9,8},{10,11... | collective-permute-start | bytes 1572872 | tf_op jit(solution)/shard_map/ppermute | solution.py:74
  241.7 55.2 %collective-permute-start.38 = (bf16[256,1024]{1,0:T(8,128)(2,1)}, bf16[256,1024]{1,0:T(8,128)(2,1)}, u32[]{:S(2)}, u32[]{:S(2)}) collective-permute-start(bf16[256,1024]{1,0:T(8,128)(2,1)} %collective-permute-done.37.refs_4_), channel_id=1, source_target_pairs={{0,1},{1,0},{2,3},{3,2},{4,5},{5,4},{6,7},{7,6},{8,9},{9,8},{10,11... | collective-permute-start | bytes 1572872 | tf_op jit(solution)/shard_map/ppermute | solution.py:74
  242.2 54.8 %collective-permute-start.36 = (bf16[256,1152]{1,0:T(8,128)(2,1)}, bf16[256,1152]{1,0:T(8,128)(2,1)}, u32[]{:S(2)}, u32[]{:S(2)}) collective-permute-start(bf16[256,1152]{1,0:T(8,128)(2,1)} %collective-permute-done.19.refs_1_), channel_id=1, source_target_pairs={{0,1},{1,0},{2,3},{3,2},{4,5},{5,4},{6,7},{7,6},{8,9},{9,8},{10,11... | collective-permute-start | bytes 1769480 | tf_op jit(solution)/shard_map/ppermute | solution.py:74
  242.3 54.7 %collective-permute-start.35 = (bf16[256,1152]{1,0:T(8,128)(2,1)}, bf16[256,1152]{1,0:T(8,128)(2,1)}, u32[]{:S(2)}, u32[]{:S(2)}) collective-permute-start(bf16[256,1152]{1,0:T(8,128)(2,1)} %copy-done.53), channel_id=1, source_target_pairs={{0,1},{1,0},{2,3},{3,2},{4,5},{5,4},{6,7},{7,6},{8,9},{9,8},{10,11... | collective-permute-start | bytes 1769480 | tf_op jit(solution)/shard_map/ppermute | solution.py:74
  296.8 35.7 %collective-permute-start.41 = (bf16[2,512,1152]{2,1,0:T(8,128)(2,1)}, bf16[2,512,1152]{2,1,0:T(8,128)(2,1)}, u32[]{:S(2)}, u32[]{:S(2)}) collective-permute-start(bf16[2,512,1152]{2,1,0:T(8,128)(2,1)} %get-tuple-element.49), channel_id=1, source_target_pairs={{0,1},{1,0},{2,3},{3,2},{4,5},{5,4},{6,7},{7,6},{8,9},{9,8},{10,11... | collective-permute-start | bytes 7077896 | tf_op jit(solution)/shard_map/ppermute | solution.py:74
  328.1 26.4 %collective-permute-start.40 = (bf16[1,512,1152]{2,1,0:T(8,128)(2,1)}, bf16[1,512,1152]{2,1,0:T(8,128)(2,1)S(1)}, u32[]{:S(2)}, u32[]{:S(2)}) collective-permute-start(bf16[1,512,1152]{2,1,0:T(8,128)(2,1)} %get-tuple-element.47), channel_id=1, source_target_pairs={{0,1},{1,0},{2,3},{3,2},{4,5},{5,4},{6,7},{7,6},{8,9},{9,8},{10,11... | collective-permute-start | bytes 3538952 | tf_op jit(solution)/shard_map/ppermute | solution.py:74
  388.2 33.9 %collective-permute-start.49 = (bf16[512,1024]{1,0:T(8,128)(2,1)}, bf16[512,1024]{1,0:T(8,128)(2,1)S(1)}, u32[]{:S(2)}, u32[]{:S(2)}) collective-permute-start(bf16[512,1024]{1,0:T(8,128)(2,1)} %bitcast.383), channel_id=1, source_target_pairs={{0,1},{1,0},{2,3},{3,2},{4,5},{5,4},{6,7},{7,6},{8,9},{9,8},{10,11... | collective-permute-start | bytes 3145736 | tf_op jit(solution)/shard_map/ppermute | solution.py:74
  395.0 27.5 %collective-permute-start.51 = (bf16[256,1024]{1,0:T(8,128)(2,1)S(1)}, bf16[256,1024]{1,0:T(8,128)(2,1)S(1)}, u32[]{:S(2)}, u32[]{:S(2)}) collective-permute-start(bf16[256,1024]{1,0:T(8,128)(2,1)S(1)} %slice.530), channel_id=1, source_target_pairs={{0,2},{1,3},{2,0},{3,1},{4,6},{5,7},{6,4},{7,5},{8,10},{9,11},{10,... | collective-permute-start | bytes 1572872 | tf_op jit(solution)/shard_map/ppermute | solution.py:74
  493.7 29.2 %collective-permute-start.69 = (bf16[4,4,32,1152]{3,2,1,0:T(8,128)(2,1)}, bf16[4,4,32,1152]{3,2,1,0:T(8,128)(2,1)}, u32[]{:S(2)}, u32[]{:S(2)}) collective-permute-start(bf16[4,4,32,1152]{3,2,1,0:T(8,128)(2,1)} %dynamic-slice_bitcast_fusion.1), channel_id=1, source_target_pairs={{0,1},{1,0},{2,3},{3,2},{4,5},{5,4},{6,7},{7,6},{8,9},{9,8},{10,11... | collective-permute-start | bytes 3538952 | tf_op jit(solution)/shard_map/ppermute | solution.py:74
  522.9 26.7 %collective-permute-start.59 = (bf16[4,4,32,2176]{3,2,1,0:T(8,128)(2,1)}, bf16[4,4,32,2176]{3,2,1,0:T(8,128)(2,1)}, u32[]{:S(2)}, u32[]{:S(2)}) collective-permute-start(bf16[4,4,32,2176]{3,2,1,0:T(8,128)(2,1)} %dynamic-slice_bitcast_fusion), channel_id=1, source_target_pairs={{0,1},{1,0},{2,3},{3,2},{4,5},{5,4},{6,7},{7,6},{8,9},{9,8},{10,11... | collective-permute-start | bytes 6684680 | tf_op jit(solution)/shard_map/ppermute | solution.py:74
  (128 other events, 1348.8 us)
Sparse Core Ops, SparseCore 0:
  91.1 118.6 all-gather.1
  380.3 110.0 reduce-scatter.1

commit v4 on v3

--- a/solution.py
+++ b/solution.py
@@ -30,36 +30,6 @@
     angles = jnp.arange(row_count, dtype=jnp.float32)[:, None] * frequency[None, :]
     angles = jnp.concatenate([angles, angles], axis=1)
     return (jnp.cos(angles), jnp.sin(angles))
-
-
-def rotate_apply(values, cosine_table, sine_table):
-    half_dim = values.shape[-1] // 2
-    turned = jnp.concatenate([-values[..., half_dim:], values[..., :half_dim]], axis=-1)
-    return values * cosine_table + turned * sine_table
-
-
-def rotate_back(grads, cosine_table, sine_table):
-    half_dim = grads.shape[-1] // 2
-    scaled = grads * sine_table
-    turned = jnp.concatenate([scaled[..., half_dim:], -scaled[..., :half_dim]], axis=-1)
-    return grads * cosine_table + turned
-
-
-def norm_rows(values, gain_row):
-    row_scale = lax.rsqrt(jnp.mean(values * values, axis=-1, keepdims=True) + norm_eps)
-    return (row_scale, values * row_scale * gain_row)
-
-
-def norm_back(values, row_scale, gain_row, normed_grad):
-    weighted = normed_grad * gain_row
-    grad_gain = jnp.sum(normed_grad * values * row_scale, axis=0)
-    correction = jnp.mean(weighted * values, axis=-1, keepdims=True)
-    return (row_scale * weighted - values * row_scale**3 * correction, grad_gain)
-
-
-def attention_scores(query_rot, key_rot, allowed):
-    raw_scores = jnp.einsum("qkgd,pkd->kgqp", query_rot, key_rot, preferred_element_type=f32)
-    return jnp.where(allowed, attention_scale * raw_scores, masked_value)
 
 
 class Exchange:
@@ -134,17 +104,30 @@
         cross_low = self.swap(far_low, 2)
         return {0: (top, low), 2: (near_top, near_low), 4: (far_top, far_low), 6: (cross_top, cross_low)}
 
+    def chips_reduce_begin(self, joined):
+        half = joined[0].shape[0] // 2
+        cross_top = self.swap(joined[6][:half].astype(bf16), 2)
+        cross_low = self.swap(joined[6][half:].astype(bf16), 4)
+        near_top = self.swap(joined[2][:half].astype(bf16), 2)
+        far_low = self.swap(joined[4][half:].astype(bf16), 4)
+        return cross_top, cross_low, near_top, far_low, joined[2][half:], joined[4][:half]
+
+    def chips_reduce_end(self, begun):
+        cross_top, cross_low, near_top, far_low, near_rest, far_rest = begun
+        near_low = self.swap((near_rest + cross_low.astype(f32)).astype(bf16), 2)
+        far_top = self.swap((far_rest + cross_top.astype(f32)).astype(bf16), 4)
+        return near_top, near_low, far_top, far_low
+
+    @staticmethod
+    def add_pieces(own, pieces):
+        near_top, near_low, far_top, far_low = (piece.astype(f32) for piece in pieces)
+        half = own.shape[0] // 2
+        return jnp.concatenate(
+            [own[:half] + near_top + far_top, own[half:] + near_low + far_low], axis=0
+        )
+
     def chips_reduce(self, joined):
-        half = joined[0].shape[0] // 2
-        cross_top = self.swap(joined[6][:half].astype(bf16), 2).astype(f32)
-        cross_low = self.swap(joined[6][half:].astype(bf16), 4).astype(f32)
-        near_top = self.swap(joined[2][:half].astype(bf16), 2).astype(f32)
-        far_low = self.swap(joined[4][half:].astype(bf16), 4).astype(f32)
-        near_low = self.swap((joined[2][half:] + cross_low).astype(bf16), 2).astype(f32)
-        far_top = self.swap((joined[4][:half] + cross_top).astype(bf16), 4).astype(f32)
-        return jnp.concatenate(
-            [joined[0][:half] + near_top + far_top, joined[0][half:] + near_low + far_low], axis=0
-        )
+        return self.add_pieces(joined[0], self.chips_reduce_end(self.chips_reduce_begin(joined)))
 
     def join_cores(self, own, other):
         return own.astype(f32) + self.swap(other, 1).astype(f32)
@@ -373,6 +356,359 @@
     )(first, *operands)
 
 
+TILE = 256
+PAIR = 2 * HEAD_DIM
+
+
+def columns_at(index, size):
+    return pl.ds(pl.multiple_of(index * size, size), size)
+
+
+def swap_halves(values):
+    width, half_dim = values.shape[1], HEAD_DIM // 2
+    lane = lax.broadcasted_iota(jnp.int32, values.shape, 1)
+    return jnp.where(
+        lane % HEAD_DIM < half_dim,
+        pltpu.roll(values, width - half_dim, 1),
+        pltpu.roll(values, half_dim, 1),
+    )
+
+
+def row_scale_of(values):
+    return lax.rsqrt(jnp.mean(values * values, axis=1, keepdims=True) + norm_eps)
+
+
+def scores_of(keys, queries, length, first_query):
+    scores = attention_scale * dot_turned(keys, queries)
+    key_at = lax.broadcasted_iota(jnp.int32, scores.shape, 0)
+    query_at = lax.broadcasted_iota(jnp.int32, scores.shape, 1) + first_query
+    return jnp.where((key_at <= query_at) & (key_at < length), scores, masked_value)
+
+
+def head_of(block, index):
+    return block[:, index * HEAD_DIM : (index + 1) * HEAD_DIM]
+
+
+def forward_kernel(
+    length_ref, tokens_ref, routes_ref, cosine_ref, sine_ref, gains_ref, weight_ref,
+    packet_ref, middle_ref, rotated_ref, mixed_ref, log_ref, share_ref, normed_ref,
+):
+    rows, width = tokens_ref.shape
+    head_columns, kv_columns = HEADS * HEAD_DIM, KV_HEADS * HEAD_DIM
+    at_value = head_columns + kv_columns
+    at_output = at_value + kv_columns
+    at_extra = at_output + head_columns
+    length = length_ref[0]
+    group = HEADS // KV_HEADS
+
+    inputs = tokens_ref[...].astype(f32)
+    normed_ref[...] = (inputs * row_scale_of(inputs) * gains_ref[0:1, :]).astype(bf16)
+
+    def project_turned(c, carry):
+        where = columns_at(c, TILE)
+        value = dot(normed_ref[...], weight_ref[:, where])
+        value = value * cosine_ref[...] + swap_halves(value) * sine_ref[...]
+        rotated_ref[:, where] = value.astype(bf16)
+        return carry
+
+    def project(c, carry):
+        where = columns_at(c, TILE)
+        rotated_ref[:, where] = dot(normed_ref[...], weight_ref[:, where]).astype(bf16)
+        return carry
+
+    lax.fori_loop(0, at_value // TILE, project_turned, 0)
+    lax.fori_loop(at_value // TILE, at_output // TILE, project, 0)
+
+    block = rows // 2
+
+    def attend(j, carry):
+        queries = rotated_ref[:, columns_at(j, group * PAIR)]
+        keys = rotated_ref[:, columns_at(j + head_columns // PAIR, PAIR)]
+        values_turned = rotated_ref[:, columns_at(j + at_value // PAIR, PAIR)].T
+        outs = []
+        for head in range(2 * group):
+            kv = head // group
+            key, query = head_of(keys, kv), head_of(queries, head)
+            value = values_turned[kv * HEAD_DIM : (kv + 1) * HEAD_DIM]
+            parts, logs = [], []
+            for b in range(2):
+                reach = (b + 1) * block
+                scores = scores_of(key[:reach], query[b * block : reach], length, b * block)
+                best = jnp.max(scores, axis=0, keepdims=True)
+                exponent = jnp.exp(scores - best)
+                total = jnp.sum(exponent, axis=0, keepdims=True)
+                chance = (exponent * (1.0 / total)).astype(bf16)
+                parts.append(dot(value[:, :reach], chance))
+                logs.append(best + jnp.log(total))
+            outs.append(jnp.concatenate(parts, axis=1))
+            log_ref[j, head : head + 1, :] = jnp.concatenate(logs, axis=1)
+        mixed_ref[:, columns_at(j, group * PAIR)] = jnp.concatenate(outs, axis=0).T.astype(bf16)
+        return carry
+
+    lax.fori_loop(0, KV_HEADS // 2, attend, 0)
+
+    def mix(c, carry):
+        where = columns_at(c, TILE)
+        branch = dot_turned(mixed_ref[...], weight_ref[where, at_output:at_extra])
+        middle_ref[:, where] = tokens_ref[:, where].astype(f32) + residual_scale * branch
+        return carry
+
+    lax.fori_loop(0, width // TILE, mix, 0)
+    middle = middle_ref[...]
+    normed_two = (middle * row_scale_of(middle) * gains_ref[1:2, :]).astype(bf16)
+    packet_ref[:, :width] = normed_two
+    logits = dot(normed_two, weight_ref[:, at_extra:])
+    lane = lax.broadcasted_iota(jnp.int32, logits.shape, 1)
+    routed = lane == routes_ref[:, 0:1]
+    for k in range(1, routes_ref.shape[1]):
+        routed = routed | (lane == routes_ref[:, k : k + 1])
+    best = jnp.max(jnp.where(routed, logits, masked_value), axis=1, keepdims=True)
+    weights = jnp.where(routed, jnp.exp(jnp.where(routed, logits, best) - best), 0.0)
+    shares = weights / jnp.sum(weights, axis=1, keepdims=True)
+    share_ref[...] = shares
+    high = shares.astype(bf16).astype(f32)
+    packet_ref[:, width:] = (high + pltpu.roll(shares - high, EXPERTS, 1)).astype(bf16)
+
+
+def column_of(row, lanes):
+    return jnp.broadcast_to(row, (lanes, row.shape[1])).T
+
+
+def middle_kernel(
+    joined_ref, near_top_ref, near_low_ref, far_top_ref, far_low_ref, packet_ref, middle_ref,
+    cotangent_ref, share_ref, gains_ref, mixed_ref, output_ref, extra_ref,
+    middle_grad_ref, mixed_grad_ref, pack_ref, back_ref, branch_ref, turned_ref,
+):
+    rows, width = cotangent_ref.shape
+    half = rows // 2
+    back_ref[:half] = joined_ref[:half] + near_top_ref[...].astype(f32) + far_top_ref[...].astype(f32)
+    back_ref[half:] = joined_ref[half:] + near_low_ref[...].astype(f32) + far_low_ref[...].astype(f32)
+    shares = share_ref[...]
+    share_grad = back_ref[:, width:]
+    share_grad = share_grad + pltpu.roll(share_grad, EXTRA - EXPERTS, 1)
+    weighted_mean = jnp.sum(shares * share_grad, axis=1, keepdims=True)
+    logit_grad = (shares * (share_grad - weighted_mean)).astype(bf16)
+    normed_grad = back_ref[:, :width] + dot_turned(logit_grad, extra_ref[...])
+    middle = middle_ref[...]
+    scale = row_scale_of(middle)
+    scaled = middle * scale
+    gain_grad = jnp.sum(normed_grad * scaled, axis=0, keepdims=True)
+    weighted = normed_grad * gains_ref[1:2, :]
+    correction = jnp.mean(weighted * middle, axis=1, keepdims=True)
+    middle_grad = cotangent_ref[...].astype(f32) + scale * weighted - scaled * (scale * scale * correction)
+    middle_grad_ref[...] = middle_grad
+    branch_ref[...] = (residual_scale * middle_grad).astype(bf16)
+    router_grad = dot(packet_ref[:, :width].T, logit_grad)
+    lane = lax.broadcasted_iota(jnp.int32, router_grad.shape, 1)
+    pack_ref[:, width:] = jnp.where(
+        lane == EXPERTS, column_of(gain_grad, EXTRA), router_grad
+    ).astype(bf16)
+    turned_ref[...] = branch_ref[...].T
+
+    def step(c, carry):
+        where = columns_at(c, TILE)
+        pack_ref[:, where] = dot(turned_ref[...], mixed_ref[:, where]).astype(bf16)
+        mixed_grad_ref[:, where] = dot(branch_ref[...], output_ref[:, where]).astype(bf16)
+        return carry
+
+    lax.fori_loop(0, output_ref.shape[1] // TILE, step, 0)
+
+
+def attention_back_kernel(
+    length_ref, rotated_ref, mixed_grad_ref, log_ref, cosine_ref, sine_ref, grad_ref
+):
+    rows = rotated_ref.shape[0]
+    head_columns, kv_columns = HEADS * HEAD_DIM, KV_HEADS * HEAD_DIM
+    at_value = head_columns + kv_columns
+    length = length_ref[0]
+    group = HEADS // KV_HEADS
+    block = rows // 2
+
+    def attend(j, carry):
+        wide = columns_at(j, group * PAIR)
+        key_place = columns_at(j + head_columns // PAIR, PAIR)
+        value_place = columns_at(j + at_value // PAIR, PAIR)
+        queries, grads = rotated_ref[:, wide], mixed_grad_ref[:, wide]
+        keys, values = rotated_ref[:, key_place], rotated_ref[:, value_place]
+        keys_turned = keys.T
+        query_grads, key_grads, value_grads = [], [], []
+        for kv in range(2):
+            key, value = head_of(keys, kv), head_of(values, kv)
+            key_turned = keys_turned[kv * HEAD_DIM : (kv + 1) * HEAD_DIM]
+            key_sums, value_sums = [], []
+            for member in range(group):
+                head = kv * group + member
+                query, grad = head_of(queries, head), head_of(grads, head)
+                query_parts = []
+                for b in range(2):
+                    reach = (b + 1) * block
+                    query_block, grad_block = query[b * block : reach], grad[b * block : reach]
+                    scores = scores_of(key[:reach], query_block, length, b * block)
+                    chance = jnp.exp(scores - log_ref[j, head : head + 1, b * block : reach])
+                    chance_grad = dot_turned(value[:reach], grad_block)
+                    delta = jnp.sum(chance * chance_grad, axis=0, keepdims=True)
+                    score_grad = (attention_scale * chance * (chance_grad - delta)).astype(bf16)
+                    value_sums.append(dot(chance.astype(bf16), grad_block))
+                    key_sums.append(dot(score_grad, query_block))
+                    query_parts.append(dot(key_turned[:, :reach], score_grad))
+                query_grads.append(jnp.concatenate(query_parts, axis=1))
+            for sums, into in ((key_sums, key_grads), (value_sums, value_grads)):
+                short = sum(sums[2::2], sums[0])
+                long = sum(sums[3::2], sums[1])
+                into.append(jnp.concatenate([short + long[:block], long[block:]], axis=0))
+        query_grad = jnp.concatenate(query_grads, axis=0).T
+        query_grad = query_grad * cosine_ref[...] - swap_halves(query_grad) * sine_ref[...]
+        grad_ref[:, wide] = query_grad.astype(bf16)
+        key_grad = jnp.concatenate(key_grads, axis=1)
+        key_grad = key_grad * cosine_ref[:, :PAIR] - swap_halves(key_grad) * sine_ref[:, :PAIR]
+        grad_ref[:, key_place] = key_grad.astype(bf16)
+        grad_ref[:, value_place] = jnp.concatenate(value_grads, axis=1).astype(bf16)
+        return carry
+
+    lax.fori_loop(0, KV_HEADS // 2, attend, 0)
+
+
+def inputs_kernel(
+    tokens_ref, gains_ref, projected_ref, weight_ref, middle_grad_ref,
+    grad_ref, pack_ref, normed_grad_ref, turned_ref,
+):
+    width = tokens_ref.shape[1]
+    projections = projected_ref.shape[1]
+    inputs = tokens_ref[...].astype(f32)
+    scale = row_scale_of(inputs)
+    scaled = inputs * scale
+    turned_ref[...] = (scaled * gains_ref[0:1, :]).astype(bf16).T
+
+    def to_weight(c, carry):
+        where = columns_at(c, TILE)
+        pack_ref[:, where] = dot(turned_ref[...], projected_ref[:, where]).astype(bf16)
+        return carry
+
+    def to_input(c, carry):
+        where = columns_at(c, TILE)
+        normed_grad_ref[:, where] = dot_turned(projected_ref[...], weight_ref[where, :])
+        return carry
+
+    lax.fori_loop(0, projections // TILE, to_weight, 0)
+    lax.fori_loop(0, width // TILE, to_input, 0)
+    normed_grad = normed_grad_ref[...]
+    gain_grad = column_of(jnp.sum(normed_grad * scaled, axis=0, keepdims=True), EXTRA)
+    lane = lax.broadcasted_iota(jnp.int32, gain_grad.shape, 1)
+    pack_ref[:, projections:] = jnp.where(lane == 0, gain_grad, 0.0).astype(bf16)
+    weighted = normed_grad * gains_ref[0:1, :]
+    correction = jnp.mean(weighted * inputs, axis=1, keepdims=True)
+    grad_ref[...] = middle_grad_ref[...] + scale * weighted - scaled * (scale * scale * correction)
+
+
+def call_kernel(body, name, operands, out_shape, scratch, flops):
+    specs, arrays = [], []
+    for operand in operands:
+        array, shape, index = operand
+        if shape == "scalar":
+            specs.append(pl.BlockSpec(memory_space=pltpu.SMEM))
+        else:
+            shape = array.shape if shape is None else shape
+            index = (0,) * len(shape) if index is None else index
+            specs.append(pl.BlockSpec(shape, lambda i, index=index: index))
+        arrays.append(array)
+    outs = [jax.ShapeDtypeStruct(shape, dtype) for shape, dtype in out_shape]
+    return pl.pallas_call(
+        body,
+        grid=(1,),
+        in_specs=specs,
+        out_specs=[
+            pl.BlockSpec(out.shape, lambda i, rank=len(out.shape): (0,) * rank) for out in outs
+        ],
+        out_shape=outs,
+        scratch_shapes=[pltpu.VMEM(shape, dtype) for shape, dtype in scratch],
+        compiler_params=pltpu.CompilerParams(vmem_limit_bytes=62 * 1024 * 1024),
+        cost_estimate=pl.CostEstimate(
+            flops=flops,
+            bytes_accessed=sum(a.size * a.dtype.itemsize for a in arrays)
+            + sum(o.size * o.dtype.itemsize for o in outs),
+            transcendentals=0,
+        ),
+        name=name,
+    )(*arrays)
+
+
+def rope_lanes(row_count):
+    cosine_table, sine_table = rope_tables(row_count)
+    half_dim = HEAD_DIM // 2
+    signed = jnp.concatenate([-sine_table[:, :half_dim], sine_table[:, half_dim:]], axis=1)
+    repeats = TILE // HEAD_DIM
+    return jnp.tile(cosine_table, (1, repeats)), jnp.tile(signed, (1, repeats))
+
+
+def attention_forward(tokens, lengths, routes, tables, gains, whole):
+    rows, width = tokens.shape
+    head_columns, kv_columns = HEADS * HEAD_DIM, KV_HEADS * HEAD_DIM
+    return call_kernel(
+        forward_kernel,
+        "attention_forward",
+        [
+            (lengths, "scalar", None), (tokens, None, None), (routes, None, None),
+            (tables[0], None, None), (tables[1], None, None), (gains, None, None),
+            (whole, None, None),
+        ],
+        [
+            ((rows, width + EXTRA), bf16), ((rows, width), f32),
+            ((rows, head_columns + 2 * kv_columns), bf16), ((rows, head_columns), bf16),
+            ((KV_HEADS // 2, 2 * HEADS // KV_HEADS, rows), f32), ((rows, EXTRA), f32),
+        ],
+        [((rows, width), bf16)],
+        8 * rows * width * head_columns,
+    )
+
+
+def middle_back(joined, pieces, packet, middle, cotangent, shares, gains, mixed, whole):
+    rows, width = cotangent.shape
+    head_columns, kv_columns = HEADS * HEAD_DIM, KV_HEADS * HEAD_DIM
+    at_output = head_columns + 2 * kv_columns
+    return call_kernel(
+        middle_kernel,
+        "middle_back",
+        [(a, None, None) for a in (joined, *pieces, packet, middle, cotangent, shares, gains, mixed)]
+        + [
+            (whole, (width, head_columns), (0, at_output // head_columns)),
+            (whole, (width, EXTRA), (0, (at_output + head_columns) // EXTRA)),
+        ],
+        [((rows, width), f32), ((rows, head_columns), bf16), ((width, head_columns + EXTRA), bf16)],
+        [((rows, width + EXTRA), f32), ((rows, width), bf16), ((width, rows), bf16)],
+        4 * rows * width * head_columns,
+    )
+
+
+def attention_back(lengths, rotated, mixed_grad, logs, tables):
+    return call_kernel(
+        attention_back_kernel,
+        "attention_back",
+        [
+            (lengths, "scalar", None), (rotated, None, None), (mixed_grad, None, None),
+            (logs, None, None), (tables[0], None, None), (tables[1], None, None),
+        ],
+        [(rotated.shape, bf16)],
+        [],
+        10 * rotated.shape[0] ** 2 * HEADS * HEAD_DIM,
+    )[0]
+
+
+def inputs_back(tokens, gains, projected_grad, whole, middle_grad):
+    rows, width = tokens.shape
+    projections = projected_grad.shape[1]
+    return call_kernel(
+        inputs_kernel,
+        "inputs_back",
+        [
+            (tokens, None, None), (gains, None, None), (projected_grad, None, None),
+            (whole, (width, projections), (0, 0)), (middle_grad, None, None),
+        ],
+        [((rows, width), f32), ((width, projections + EXTRA), bf16)],
+        [((rows, width), f32), ((width, rows), bf16)],
+        4 * rows * width * projections,
+    )
+
+
 def local(
     tokens,
     lengths,
@@ -397,7 +733,13 @@
     shard = query_weight.shape[0]
     hidden = gate_weight.shape[2]
     head_columns, kv_columns = HEADS * HEAD_DIM, KV_HEADS * HEAD_DIM
-    group_size = HEADS // KV_HEADS
+
+    mine = jnp.stack([gate_weight, up_weight, down_weight.transpose(0, 2, 1)], axis=1)
+    mine = mine.reshape(MEMBERS, LOCAL_EXPERTS, 3, shard, hidden)
+    shelf = links.send_parts(mine).transpose(1, 2, 0, 3, 4)
+    shelf = shelf.reshape(LOCAL_EXPERTS, 3, MEMBERS * shard, hidden)
+    lines = [[m + MEMBERS * g for g in range(groups)] for m in range(MEMBERS)]
+    expert_full = lax.all_gather(shelf, "fsdp", axis_index_groups=lines)
 
     packed = jnp.concatenate(
         [
@@ -415,77 +757,25 @@
     pack_width = packed.shape[1]
     column = links.direct_gather(packed).reshape(groups * shard, pack_width)
     spread = links.chips_gather(column)
-    even = jnp.stack([jnp.concatenate(spread[k], axis=0) for k in (0, 2, 4, 6)])
-    odd = links.swap(even, 1)
+    spread[0] = (column,)
     whole = jnp.zeros((groups, MEMBERS, shard, pack_width), bf16)
     for k in range(MEMBERS):
-        part = (odd if k % 2 else even)[k // 2].reshape(groups, shard, pack_width)
+        parts = spread[k & 6]
+        if k & 1:
+            parts = [links.swap(part, 1) for part in parts]
+        part = jnp.concatenate(parts, axis=0).reshape(groups, shard, pack_width)
         whole = lax.dynamic_update_index_in_dim(whole, part, member ^ k, 1)
     whole = whole.reshape(width, pack_width)
     at_output = head_columns + 2 * kv_columns
     at_extra = at_output + head_columns
-    qkv_full = whole[:, :at_output]
-    output_turned = whole[:, at_output:at_extra]
-    router_full = whole[:, at_extra : at_extra + EXPERTS]
-    gain_one = whole[:, at_extra + EXPERTS].astype(f32)
-    gain_two = whole[:, at_extra + EXPERTS + 1].astype(f32)
-
-    mine = jnp.stack([gate_weight, up_weight, down_weight.transpose(0, 2, 1)], axis=1)
-    mine = mine.reshape(MEMBERS, LOCAL_EXPERTS, 3, shard, hidden)
-    shelf = links.send_parts(mine).transpose(1, 2, 0, 3, 4)
-    shelf = shelf.reshape(LOCAL_EXPERTS, 3, MEMBERS * shard, hidden)
-    lines = [[m + MEMBERS * g for g in range(groups)] for m in range(MEMBERS)]
-    expert_full = lax.all_gather(shelf, "fsdp", axis_index_groups=lines)
+    gains = whole[:, at_extra + EXPERTS : at_extra + EXPERTS + 2].astype(f32).T
+
     late_cotangent, whole = lax.optimization_barrier((cotangent, whole))
     cotangents = links.chips_gather(late_cotangent)
 
-    inputs = tokens.astype(f32)
-    cosine_table, sine_table = rope_tables(row_count)
-    scale_one, normed_raw = norm_rows(inputs, gain_one)
-    normed_one = normed_raw.astype(bf16)
-    projected = dot(normed_one, qkv_full)
-    queries = projected[:, :head_columns].reshape(row_count, KV_HEADS, group_size, HEAD_DIM)
-    key_rows = projected[:, head_columns : head_columns + kv_columns].reshape(
-        row_count, KV_HEADS, HEAD_DIM
-    )
-    value_rows = (
-        projected[:, head_columns + kv_columns :].astype(bf16).reshape(row_count, KV_HEADS, HEAD_DIM)
-    )
-    query_rot = rotate_apply(
-        queries, cosine_table[:, None, None, :], sine_table[:, None, None, :]
-    ).astype(bf16)
-    key_rot = rotate_apply(key_rows, cosine_table[:, None, :], sine_table[:, None, :]).astype(bf16)
-    position = jnp.arange(row_count, dtype=jnp.int32)
-    allowed = (position[None, :] <= position[:, None]) & (position[None, :] < lengths[0])
-    scores = attention_scores(query_rot, key_rot, allowed)
-    maxima = jnp.max(scores, axis=-1, keepdims=True)
-    exponent = jnp.exp(scores - maxima)
-    totals = jnp.sum(exponent, axis=-1, keepdims=True)
-    log_total = maxima + jnp.log(totals)
-    softmax_rows = exponent / totals
-    mixed = (
-        jnp.einsum("kgqp,pkd->qkgd", softmax_rows.astype(bf16), value_rows, preferred_element_type=f32)
-        .astype(bf16)
-        .reshape(row_count, head_columns)
-    )
-    middle = inputs + residual_scale * dot_turned(mixed, output_turned)
-    scale_two, normed_raw_two = norm_rows(middle, gain_two)
-    normed_two = normed_raw_two.astype(bf16)
-    logits = dot(normed_two, router_full)
-    expert_ids = jnp.arange(EXPERTS, dtype=jnp.int32)
-    routed = jnp.any(routes[:, :, None] == expert_ids[None, None, :], axis=1)
-    best = jnp.max(jnp.where(routed, logits, masked_value), axis=1, keepdims=True)
-    weights = jnp.where(routed, jnp.exp(jnp.where(routed, logits, best) - best), 0.0)
-    shares = weights / jnp.sum(weights, axis=1, keepdims=True)
-    share_high = lax.reduce_precision(shares, 8, 7)
-    packet = jnp.concatenate(
-        [
-            normed_two,
-            share_high.astype(bf16),
-            (shares - share_high).astype(bf16),
-            jnp.zeros((row_count, EXTRA - 2 * EXPERTS), bf16),
-        ],
-        axis=1,
+    tables = rope_lanes(row_count)
+    packet, middle, rotated, mixed, logs, shares = attention_forward(
+        tokens, lengths, routes, tables, gains, whole
     )
     packets = links.chips_gather(packet)
     packets[0] = (packet,)
@@ -508,85 +798,46 @@
             out_terms[k] = (out_own[at], out_other[at])
             back_terms[k] = back_join[at]
 
-    back_total = links.chips_reduce(back_terms)
+    back_pieces = links.chips_reduce_end(links.chips_reduce_begin(back_terms))
+    out_join = {k: links.join_cores(*out_terms[k]) for k in (6, 2, 4, 0)}
 
     shelf_grad = lax.psum_scatter(grads, "fsdp", scatter_dimension=0, axis_index_groups=lines)
     shelf_grad = shelf_grad.reshape(LOCAL_EXPERTS, 3, MEMBERS, shard, hidden)
     expert_shards = links.send_parts(shelf_grad.transpose(2, 0, 1, 3, 4)).astype(f32)
     expert_shards = expert_shards.reshape(EXPERTS, 3, shard, hidden)
 
-    out_terms, back_total = lax.optimization_barrier((out_terms, back_total))
-    mixture = links.chips_reduce(
-        {k: links.join_cores(*out_terms[k]) for k in (6, 2, 4, 0)}
-    )
-    layer_out = (middle + mixture).astype(bf16)
-
-    def reduce_pack(parts):
-        spare = -sum(part.shape[1] for part in parts) % EXTRA
-        pack = jnp.concatenate(parts + [jnp.zeros((width, spare), f32)], axis=1).astype(bf16)
+    def pack_begin(pack):
         columns = pack.shape[1]
         pack = pack.reshape(groups, MEMBERS // 2, 2, shard, columns)
         core, chip = member % 2, member // 2
         own = lax.dynamic_index_in_dim(pack, core, 2, keepdims=False)
         other = lax.dynamic_index_in_dim(pack, 1 - core, 2, keepdims=False)
         joined = links.join_cores(own, other)
-        terms = {
+        return {
             2 * bits: lax.dynamic_index_in_dim(joined, chip ^ bits, 1, keepdims=False).reshape(
                 groups * shard, columns
             )
             for bits in range(MEMBERS // 2)
         }
-        return links.direct_reduce(links.chips_reduce(terms).reshape(groups, shard, columns))
-
-    upstream = cotangent.astype(f32)
-    share_grad = (
-        back_total[:, width : width + EXPERTS] + back_total[:, width + EXPERTS : width + 2 * EXPERTS]
-    )
-    share_grad = jnp.where(routed, share_grad, 0.0)
-    logit_grad = (
-        shares * (share_grad - jnp.sum(shares * share_grad, axis=1, keepdims=True))
-    ).astype(bf16)
-    normed_two_grad = back_total[:, :width] + dot_turned(logit_grad, router_full)
-    grad_router = dot(normed_two.T, logit_grad)
-    middle_norm_grad, grad_gain_two = norm_back(middle, scale_two, gain_two, normed_two_grad)
-    middle_grad = upstream + middle_norm_grad
-    branch_grad = (residual_scale * middle_grad).astype(bf16)
-    grad_output_turned = dot(branch_grad.T, mixed)
-    mixed_grad = (
-        dot(branch_grad, output_turned)
-        .astype(bf16)
-        .reshape(row_count, KV_HEADS, group_size, HEAD_DIM)
-    )
-    scores_again = attention_scores(query_rot, key_rot, allowed)
-    softmax_again = jnp.exp(scores_again - log_total)
-    prob_grad = jnp.einsum("qkgd,pkd->kgqp", mixed_grad, value_rows, preferred_element_type=f32)
-    row_delta = jnp.sum(prob_grad * softmax_again, axis=-1, keepdims=True)
-    score_grad = (attention_scale * softmax_again * (prob_grad - row_delta)).astype(bf16)
-    value_grad = (
-        jnp.einsum("kgqp,qkgd->pkd", softmax_again.astype(bf16), mixed_grad, preferred_element_type=f32)
-        .astype(bf16)
-        .reshape(row_count, kv_columns)
-    )
-    query_rot_grad = jnp.einsum("kgqp,pkd->qkgd", score_grad, key_rot, preferred_element_type=f32)
-    key_rot_grad = jnp.einsum("kgqp,qkgd->pkd", score_grad, query_rot, preferred_element_type=f32)
-    query_grad = (
-        rotate_back(query_rot_grad, cosine_table[:, None, None, :], sine_table[:, None, None, :])
-        .astype(bf16)
-        .reshape(row_count, head_columns)
-    )
-    key_grad = (
-        rotate_back(key_rot_grad, cosine_table[:, None, :], sine_table[:, None, :])
-        .astype(bf16)
-        .reshape(row_count, kv_columns)
-    )
-    qkv_grad = jnp.concatenate([query_grad, key_grad, value_grad], axis=1)
-    grad_qkv = dot(normed_one.T, qkv_grad)
-    normed_one_grad = dot_turned(qkv_grad, qkv_full)
-    input_norm_grad, grad_gain_one = norm_back(inputs, scale_one, gain_one, normed_one_grad)
-    grad_tokens = middle_grad + input_norm_grad
-
-    first_total = reduce_pack([grad_output_turned, grad_router, grad_gain_two[:, None]])
-    second_total = reduce_pack([grad_qkv, grad_gain_one[:, None]])
+
+    def pack_end(terms):
+        total = links.chips_reduce(terms)
+        return links.direct_reduce(total.reshape(groups, shard, total.shape[1]))
+
+    middle_grad, mixed_grad, first_pack = middle_back(
+        back_terms[0], back_pieces, packet, middle, cotangent, shares, gains, mixed, whole
+    )
+    out_join, middle_grad = lax.optimization_barrier((out_join, middle_grad))
+    out_begun = links.chips_reduce_begin(out_join)
+    projected_grad = attention_back(lengths, rotated, mixed_grad, logs, tables)
+    out_begun, projected_grad = lax.optimization_barrier((out_begun, projected_grad))
+    out_pieces = links.chips_reduce_end(out_begun)
+    first_terms = pack_begin(first_pack)
+    grad_tokens, second_pack = inputs_back(tokens, gains, projected_grad, whole, middle_grad)
+    second_terms = pack_begin(second_pack)
+    first_total = pack_end(first_terms)
+    second_total = pack_end(second_terms)
+    layer_out = (middle + links.add_pieces(out_join[0], out_pieces)).astype(bf16)
     return (
         layer_out,
         grad_tokens,

time: 613 us -> 496 us (0.81)
  matrix products: 71.4 us -> 0 us
  Pallas kernels: 117 us -> 186 us
  waiting for transfers between devices: 188 us -> 142 us
  local copies, waits for them, and re-layouts: 81.6 us -> 46.3 us
  other arithmetic: 52.6 us -> 29 us
    dot_general x15 -> x0, matrix products: 71.4 us -> none  [the longest x6 16 us: dot(): return jnp.dot(left, right, preferred_element_type=f32)]
    pallas_call x0 -> x4, Pallas kernels: none -> 69.8 us  [call_kernel(): pl.pallas_call(body, grid=(1,), in_specs=specs, out_specs=[pl.BlockSpec(o...]
    ppermute x83 -> x89, waiting for transfers between devices: 185 us -> 142 us  [swap(): lax.ppermute(value, 'fsdp', [(i, i ^ bits) for i in range(self.count)])]
    concatenate x8 -> x0, local copies, waits for them, and re-layouts: 15.9 us -> none  [the longest x4 14.4 us: reduce_pack(): jnp.concatenate(parts + [jnp.zeros((width, spare), f32)], axis=1)]
    reduce_sum x4 -> x0, other arithmetic: 10.2 us -> none  [the longest x1 8.38 us: local(): totals = jnp.sum(exponent, axis=-1, keepdims=True)]
    unnamed x139 -> x59, local copies, waits for them, and re-layouts: 17.5 us -> 7.38 us
    add x7 -> x8, other arithmetic: 8.58 us -> 16.4 us  [join_cores(): return own.astype(f32) + self.swap(other, 1).astype(f32)]
    convert_element_type x18 -> x9, other arithmetic: 13.3 us -> 5.66 us  [the longest x4 2.2 us: chips_reduce_end(): far_top = self.swap((far_rest + cross_top.astype(f32)).astype(bf16), 4)]
  transfers between devices with their start and end apart: 85 -> 91, of which waited for: 34 -> 36; matrix products, arithmetic and copies ran while one was open for 29% -> 13% of each run, Pallas kernels for 19% -> 38%
where the time goes in v4:
time: 496 us; the launch traced here: 492 us
  Pallas kernels  186 us (38%)
  waiting for transfers between devices  142 us (29%)
  starting transfers between devices  72.6 us (15%)
  local copies, waits for them, and re-layouts  46.3 us (9%)
  other arithmetic  29 us (6%)
  between operations  16 us (3%)
    ppermute x89, waiting for transfers between devices, swap(): lax.ppermute(value, 'fsdp', [(i, i ^ bits) for i in range(self.count)])  142 us
    pallas_call x3, Pallas kernels, run_experts(): pl.pallas_call(functools.partial(expert_kernel, layout=layout, fresh=fres...  116 us
    ppermute x89, starting transfers between devices, swap(): lax.ppermute(value, 'fsdp', [(i, i ^ bits) for i in range(self.count)])  72.3 us
    pallas_call x4, Pallas kernels, call_kernel(): pl.pallas_call(body, grid=(1,), in_specs=specs, out_specs=[pl.BlockSpec(o...  69.8 us
    add x8, other arithmetic, join_cores(): return own.astype(f32) + self.swap(other, 1).astype(f32)  16.4 us
  transfers between devices with their start and end apart: 91, of which 36 were waited for; matrix products, arithmetic and copies ran while one was open for 13% of the time, Pallas kernels for 38%

profile of v4, /device:TPU:0, one launch (start us, length us, event | category | flops | bytes accessed | tf_op | source)
XLA Modules:
  0.0 492.2 jit_solution(9966771706492146328)
XLA Ops:
  27.6 3.8 collective-permute-done.1
  34.3 4.7 collective-permute-done.19
  47.9 5.8 %collective-permute-done.4 = bf16[64,3200]{1,0:T(8,128)(2,1)S(1)} collective-permute-done((bf16[64,3200]{1,0:T(8,128)(2,1)}, bf16[64,3200]{1,0:T(8,128)(2,1)S(1)}, u32[]{:S(2)}, u32[]{:S(2)}) %collective-permute-start.4) | collective-permute-done | bytes 409632 | tf_op jit(solution)/shard_map/ppermute | solution.py:44
  53.7 8.4 %collective-permute-done.5 = bf16[64,3200]{1,0:T(8,128)(2,1)S(1)} collective-permute-done((bf16[64,3200]{1,0:T(8,128)(2,1)}, bf16[64,3200]{1,0:T(8,128)(2,1)S(1)}, u32[]{:S(2)}, u32[]{:S(2)}) %collective-permute-start.5) | collective-permute-done | bytes 409632 | tf_op jit(solution)/shard_map/ppermute | solution.py:44
  64.9 9.2 %collective-permute-done.12 = bf16[64,3200]{1,0:T(8,128)(2,1)S(1)} collective-permute-done((bf16[64,3200]{1,0:T(8,128)(2,1)S(1)}, bf16[64,3200]{1,0:T(8,128)(2,1)S(1)}, u32[]{:S(2)}, u32[]{:S(2)}) %collective-permute-start.12) | collective-permute-done | bytes 409632 | tf_op jit(solution)/shard_map/ppermute | solution.py:44
  83.6 24.5 %attention_forward.1 = (bf16[512,1152]{1,0:T(8,128)(2,1)}, f32[512,1024]{1,0:T(8,128)}, bf16[512,2048]{1,0:T(8,128)(2,1)}, bf16[512,1024]{1,0:T(8,128)(2,1)}, f32[4,4,512]{2,1,0:T(4,128)}, /*index=5*/f32[512,128]{1,0:T(8,128)}) custom-call(s32[1]{0:T(128)S(6)} %copy.154.length_ref, bf16[512,1024]{1,0:T(8,128)(2,1)} %tokens_ref.3, ...), custom_call_target="tpu_custom_call" | custom-call | flops 4294967296 | bytes 15392772 | tf_op jit(solution)/shard_map/attention_forward/pallas_call | solution.py:615
  113.7 12.3 %collective-permute-done.23.refs_0_ = bf16[256,1152]{1,0:T(8,128)(2,1)} collective-permute-done((bf16[256,1152]{1,0:T(8,128)(2,1)S(1)}, bf16[256,1152]{1,0:T(8,128)(2,1)}, u32[]{:S(2)}, u32[]{:S(2)}) %collective-permute-start.23) | collective-permute-done | bytes 589856 | tf_op jit(solution)/shard_map/ppermute | solution.py:44
  127.7 9.3 %collective-permute-done.24.refs_1_ = bf16[256,1152]{1,0:T(8,128)(2,1)S(1)} collective-permute-done((bf16[256,1152]{1,0:T(8,128)(2,1)S(1)}, bf16[256,1152]{1,0:T(8,128)(2,1)S(1)}, u32[]{:S(2)}, u32[]{:S(2)}) %collective-permute-start.24) | collective-permute-done | bytes 589856 | tf_op jit(solution)/shard_map/ppermute | solution.py:44
  141.2 9.1 %collective-permute-done.34.refs_10_ = bf16[256,1024]{1,0:T(8,128)(2,1)S(1)} collective-permute-done((bf16[256,1024]{1,0:T(8,128)(2,1)}, bf16[256,1024]{1,0:T(8,128)(2,1)S(1)}, u32[]{:S(2)}, u32[]{:S(2)}) %collective-permute-start.34) | collective-permute-done | bytes 524320 | tf_op jit(solution)/shard_map/ppermute | solution.py:44
  157.3 3.9 collective-permute-done.25.refs_2_
  163.2 31.5 %experts.3 = (bf16[1,512,1024]{2,1,0:T(8,128)(2,1)}, bf16[1,512,1024]{2,1,0:T(8,128)(2,1)}, bf16[1,512,1152]{2,1,0:T(8,128)(2,1)}, bf16[1,512,1152]{2,1,0:T(8,128)(2,1)}, f32[2,3,1024,512]{3,2,1,0:T(8,128)}) custom-call(s32[1]{0:T(128)} %bitcast.22.first_ref, bf16[512,1152]{1,0:T(8,128)(2,1)} %get-tuple-element.54.refs_0_.packet_ref, ...), custom_call_target="tpu_custom_call" | custom-call | flops 19327352832 | bytes 27262976 | tf_op jit(solution)/shard_map/experts/pallas_call | solution.py:327
  196.6 54.3 %experts.4 = (bf16[2,512,1024]{2,1,0:T(8,128)(2,1)}, bf16[2,512,1024]{2,1,0:T(8,128)(2,1)}, bf16[2,512,1152]{2,1,0:T(8,128)(2,1)}, bf16[2,512,1152]{2,1,0:T(8,128)(2,1)}, f32[2,3,1024,512]{3,2,1,0:T(8,128)}) custom-call(s32[1]{0:T(128)} %bitcast.22.first_ref, bf16[256,1152]{1,0:T(8,128)(2,1)} %collective-permute-done.23.refs_0_, ...), custom_call_target="tpu_custom_call" | custom-call | flops 38654705664 | bytes 35651584 | tf_op jit(solution)/shard_map/experts/pallas_call | solution.py:327
  254.6 30.5 %experts.5 = (bf16[1,512,1024]{2,1,0:T(8,128)(2,1)}, bf16[1,512,1024]{2,1,0:T(8,128)(2,1)}, bf16[1,512,1152]{2,1,0:T(8,128)(2,1)}, bf16[1,512,1152]{2,1,0:T(8,128)(2,1)}, bf16[4,2,3,256,512]{4,3,2,1,0:T(8,128)(2,1)}) custom-call(s32[1]{0:T(128)} %bitcast.22.first_ref, bf16[256,1152]{1,0:T(8,128)(2,1)} %copy-done.21, ...), custom_call_target="tpu_custom_call" | custom-call | flops 19327352832 | bytes 27262976 | tf_op jit(solution)/shard_map/experts/pallas_call | solution.py:327
  305.5 11.2 %collective-permute-done.56 = bf16[256,1152]{1,0:T(8,128)(2,1)S(1)} collective-permute-done((bf16[256,1152]{1,0:T(8,128)(2,1)S(1)}, bf16[256,1152]{1,0:T(8,128)(2,1)S(1)}, u32[]{:S(2)}, u32[]{:S(2)}) %collective-permute-start.56) | collective-permute-done | bytes 589856 | tf_op jit(solution)/shard_map/ppermute | solution.py:44
  321.3 9.8 %collective-permute-done.58.far_low_ref = bf16[256,1152]{1,0:T(8,128)(2,1)S(1)} collective-permute-done((bf16[256,1152]{1,0:T(8,128)(2,1)S(1)}, bf16[256,1152]{1,0:T(8,128)(2,1)S(1)}, u32[]{:S(2)}, u32[]{:S(2)}) %collective-permute-start.58) | collective-permute-done | bytes 589856 | tf_op jit(solution)/shard_map/ppermute | solution.py:44
  331.1 11.7 %collective-permute-done.57.far_top_ref = bf16[256,1152]{1,0:T(8,128)(2,1)} collective-permute-done((bf16[256,1152]{1,0:T(8,128)(2,1)S(1)}, bf16[256,1152]{1,0:T(8,128)(2,1)}, u32[]{:S(2)}, u32[]{:S(2)}) %collective-permute-start.57) | collective-permute-done | bytes 589856 | tf_op jit(solution)/shard_map/ppermute | solution.py:44
  342.8 11.8 %middle_back.1 = (f32[512,1024]{1,0:T(8,128)}, bf16[512,1024]{1,0:T(8,128)(2,1)}, bf16[1024,1152]{1,0:T(8,128)(2,1)}) custom-call(f32[512,1152]{1,0:T(8,128)} %add_bitcast_fusion.joined_ref, bf16[256,1152]{1,0:T(8,128)(2,1)} %collective-permute-done.52.near_top_ref, bf16[256,1152]{1,0:T(8,128)(2,1)} %collective-permute-done.54.near_low_ref, ...), custom_call_target="tpu_custom_call" | custom-call | flops 2147483648 | bytes 28975104 | tf_op jit(solution)/shard_map/middle_back/pallas_call | solution.py:615
  364.1 19.1 %attention_back.1.projected_ref = bf16[512,2048]{1,0:T(8,128)(2,1)} custom-call(s32[1]{0:T(128)S(6)} %copy.154.length_ref, bf16[512,2048]{1,0:T(8,128)(2,1)} %get-tuple-element.77.rotated_ref, bf16[512,1024]{1,0:T(8,128)(2,1)} %get-tuple-element.78.mixed_grad_ref, f32[4,4,512]{2,1,0:T(4,128)} %get-tuple-element.79.log_ref, f32[512,256]{1,0:T(8,128)} %copy.114.cosine_ref, ...), custom_call_target="tpu_custom_call" | custom-call | flops 2684354560 | bytes 6324228 | tf_op jit(solution)/shard_map/attention_back/pallas_call | solution.py:615
  390.2 14.4 %inputs_back.1 = (f32[512,1024]{1,0:T(8,128)}, bf16[1024,2176]{1,0:T(8,128)(2,1)}) custom-call(bf16[512,1024]{1,0:T(8,128)(2,1)} %tokens_ref.3, f32[2,1024]{1,0:T(2,128)} %copy.116.gains_ref, bf16[512,2048]{1,0:T(8,128)(2,1)} %attention_back.1.projected_ref, bf16[1024,3200]{1,0:T(8,128)(2,1)} %bitcast.235, f32[512,1024]{1,0:T(8,128)} %get-tuple-element.87.middle_grad_ref), custom_call_target="tpu_custom_call" | custom-call | flops 4294967296 | bytes 18358272 | tf_op jit(solution)/shard_map/inputs_back/pallas_call | solution.py:615
  422.5 3.3 collective-permute-done.78
  426.6 3.6 collective-permute-start.83
  445.3 5.2 %collective-permute-done.67 = bf16[64,2176]{1,0:T(8,128)(2,1)S(1)} collective-permute-done((bf16[64,2176]{1,0:T(8,128)(2,1)S(1)}, bf16[64,2176]{1,0:T(8,128)(2,1)S(1)}, u32[]{:S(2)}, u32[]{:S(2)}) %collective-permute-start.67) | collective-permute-done | bytes 278560 | tf_op jit(solution)/shard_map/ppermute | solution.py:44
  455.6 4.6 collective-permute-done.68
  475.7 4.3 collective-permute-done.87
  (343 shorter events, 170.0 us)
Async XLA Ops:
  7.2 155.7 %all-gather.2.cloned.1.call-start = ((), (), s32[]{:S(2)}) async-start(), calls=%async_computation.1 | async-start | bytes 7864320 | tf_op jit(solution)/shard_map/all_gather | solution.py:742
  47.0 413.5 %reduce-scatter.2.cloned.1.call-start = ((), (), s32[]{:S(2)}) async-start(), calls=%async_computation.2 | async-start | bytes 7864320 | tf_op jit(solution)/shard_map/reduce_scatter | solution.py:804
  78.6 32.7 %collective-permute-start.35 = (bf16[256,1024]{1,0:T(8,128)(2,1)}, bf16[256,1024]{1,0:T(8,128)(2,1)}, u32[]{:S(2)}, u32[]{:S(2)}) collective-permute-start(bf16[256,1024]{1,0:T(8,128)(2,1)} %get-tuple-element.205), channel_id=1, source_target_pairs={{0,4},{1,5},{2,6},{3,7},{4,0},{5,1},{6,2},{7,3},{8,12},{9,13},{10,... | collective-permute-start | bytes 1572872 | tf_op jit(solution)/shard_map/ppermute | solution.py:44
  79.1 33.1 %collective-permute-start.33 = (bf16[256,1024]{1,0:T(8,128)(2,1)}, bf16[256,1024]{1,0:T(8,128)(2,1)}, u32[]{:S(2)}, u32[]{:S(2)}) collective-permute-start(bf16[256,1024]{1,0:T(8,128)(2,1)} %get-tuple-element.205), channel_id=1, source_target_pairs={{0,2},{1,3},{2,0},{3,1},{4,6},{5,7},{6,4},{7,5},{8,10},{9,11},{10,... | collective-permute-start | bytes 1572872 | tf_op jit(solution)/shard_map/ppermute | solution.py:44
  80.2 30.0 %collective-permute-start.32 = (bf16[256,1024]{1,0:T(8,128)(2,1)S(1)}, bf16[256,1024]{1,0:T(8,128)(2,1)}, u32[]{:S(2)}, u32[]{:S(2)}) collective-permute-start(bf16[256,1024]{1,0:T(8,128)(2,1)S(1)} %get-tuple-element.206), channel_id=1, source_target_pairs={{0,2},{1,3},{2,0},{3,1},{4,6},{5,7},{6,4},{7,5},{8,10},{9,11},{10,... | collective-permute-start | bytes 1572872 | tf_op jit(solution)/shard_map/ppermute | solution.py:44
  81.2 32.5 %collective-permute-start.45 = (bf16[256,1024]{1,0:T(8,128)(2,1)S(1)}, bf16[256,1024]{1,0:T(8,128)(2,1)}, u32[]{:S(2)}, u32[]{:S(2)}) collective-permute-start(bf16[256,1024]{1,0:T(8,128)(2,1)S(1)} %get-tuple-element.206), channel_id=1, source_target_pairs={{0,4},{1,5},{2,6},{3,7},{4,0},{5,1},{6,2},{7,3},{8,12},{9,13},{10,... | collective-permute-start | bytes 1572872 | tf_op jit(solution)/shard_map/ppermute | solution.py:44
  112.2 26.9 %collective-permute-start.42 = (bf16[256,1152]{1,0:T(8,128)(2,1)S(1)}, bf16[256,1152]{1,0:T(8,128)(2,1)S(1)}, u32[]{:S(2)}, u32[]{:S(2)}) collective-permute-start(bf16[256,1152]{1,0:T(8,128)(2,1)S(1)} %get-tuple-element.199), channel_id=1, source_target_pairs={{0,4},{1,5},{2,6},{3,7},{4,0},{5,1},{6,2},{7,3},{8,12},{9,13},{10,... | collective-permute-start | bytes 1769480 | tf_op jit(solution)/shard_map/ppermute | solution.py:44
  126.0 29.8 %collective-permute-start.16 = (bf16[512,1152]{1,0:T(8,128)(2,1)S(1)}, bf16[512,1152]{1,0:T(8,128)(2,1)S(1)}, u32[]{:S(2)}, u32[]{:S(2)}) collective-permute-start(bf16[512,1152]{1,0:T(8,128)(2,1)S(1)} %copy-done.4), channel_id=1, source_target_pairs={{0,1},{1,0},{2,3},{3,2},{4,5},{5,4},{6,7},{7,6},{8,9},{9,8},{10,11... | collective-permute-start | bytes 3538952 | tf_op jit(solution)/shard_map/ppermute | solution.py:44
  155.7 39.0 %collective-permute-start.29 = (bf16[256,1152]{1,0:T(8,128)(2,1)}, bf16[256,1152]{1,0:T(8,128)(2,1)}, u32[]{:S(2)}, u32[]{:S(2)}) collective-permute-start(bf16[256,1152]{1,0:T(8,128)(2,1)} %copy-done.23), channel_id=1, source_target_pairs={{0,1},{1,0},{2,3},{3,2},{4,5},{5,4},{6,7},{7,6},{8,9},{9,8},{10,11... | collective-permute-start | bytes 1769480 | tf_op jit(solution)/shard_map/ppermute | solution.py:44
  156.9 38.4 %collective-permute-start.39 = (bf16[256,1024]{1,0:T(8,128)(2,1)}, bf16[256,1024]{1,0:T(8,128)(2,1)}, u32[]{:S(2)}, u32[]{:S(2)}) collective-permute-start(bf16[256,1024]{1,0:T(8,128)(2,1)} %copy-done.26), channel_id=1, source_target_pairs={{0,1},{1,0},{2,3},{3,2},{4,5},{5,4},{6,7},{7,6},{8,9},{9,8},{10,11... | collective-permute-start | bytes 1572872 | tf_op jit(solution)/shard_map/ppermute | solution.py:44
  161.2 34.2 %collective-permute-start.40 = (bf16[256,1024]{1,0:T(8,128)(2,1)}, bf16[256,1024]{1,0:T(8,128)(2,1)}, u32[]{:S(2)}, u32[]{:S(2)}) collective-permute-start(bf16[256,1024]{1,0:T(8,128)(2,1)} %copy-done.27), channel_id=1, source_target_pairs={{0,1},{1,0},{2,3},{3,2},{4,5},{5,4},{6,7},{7,6},{8,9},{9,8},{10,11... | collective-permute-start | bytes 1572872 | tf_op jit(solution)/shard_map/ppermute | solution.py:44
  162.3 33.5 %collective-permute-start.30 = (bf16[256,1152]{1,0:T(8,128)(2,1)}, bf16[256,1152]{1,0:T(8,128)(2,1)S(1)}, u32[]{:S(2)}, u32[]{:S(2)}) collective-permute-start(bf16[256,1152]{1,0:T(8,128)(2,1)} %collective-permute-done.25.refs_2_), channel_id=1, source_target_pairs={{0,1},{1,0},{2,3},{3,2},{4,5},{5,4},{6,7},{7,6},{8,9},{9,8},{10,11... | collective-permute-start | bytes 1769480 | tf_op jit(solution)/shard_map/ppermute | solution.py:44
  162.3 33.6 %collective-permute-start.31 = (bf16[256,1152]{1,0:T(8,128)(2,1)}, bf16[256,1152]{1,0:T(8,128)(2,1)}, u32[]{:S(2)}, u32[]{:S(2)}) collective-permute-start(bf16[256,1152]{1,0:T(8,128)(2,1)} %collective-permute-done.27.refs_3_), channel_id=1, source_target_pairs={{0,1},{1,0},{2,3},{3,2},{4,5},{5,4},{6,7},{7,6},{8,9},{9,8},{10,11... | collective-permute-start | bytes 1769480 | tf_op jit(solution)/shard_map/ppermute | solution.py:44
  194.7 59.9 %collective-permute-start.47 = (bf16[256,1024]{1,0:T(8,128)(2,1)}, bf16[256,1024]{1,0:T(8,128)(2,1)}, u32[]{:S(2)}, u32[]{:S(2)}) collective-permute-start(bf16[256,1024]{1,0:T(8,128)(2,1)} %collective-permute-done.35.refs_5_), channel_id=1, source_target_pairs={{0,1},{1,0},{2,3},{3,2},{4,5},{5,4},{6,7},{7,6},{8,9},{9,8},{10,11... | collective-permute-start | bytes 1572872 | tf_op jit(solution)/shard_map/ppermute | solution.py:44
  195.3 58.9 %collective-permute-start.46 = (bf16[256,1024]{1,0:T(8,128)(2,1)}, bf16[256,1024]{1,0:T(8,128)(2,1)}, u32[]{:S(2)}, u32[]{:S(2)}) collective-permute-start(bf16[256,1024]{1,0:T(8,128)(2,1)} %collective-permute-done.45.refs_4_), channel_id=1, source_target_pairs={{0,1},{1,0},{2,3},{3,2},{4,5},{5,4},{6,7},{7,6},{8,9},{9,8},{10,11... | collective-permute-start | bytes 1572872 | tf_op jit(solution)/shard_map/ppermute | solution.py:44
  195.4 59.3 %collective-permute-start.44 = (bf16[256,1152]{1,0:T(8,128)(2,1)}, bf16[256,1152]{1,0:T(8,128)(2,1)}, u32[]{:S(2)}, u32[]{:S(2)}) collective-permute-start(bf16[256,1152]{1,0:T(8,128)(2,1)} %collective-permute-done.26.refs_1_), channel_id=1, source_target_pairs={{0,1},{1,0},{2,3},{3,2},{4,5},{5,4},{6,7},{7,6},{8,9},{9,8},{10,11... | collective-permute-start | bytes 1769480 | tf_op jit(solution)/shard_map/ppermute | solution.py:44
  195.8 58.8 %collective-permute-start.43 = (bf16[256,1152]{1,0:T(8,128)(2,1)S(1)}, bf16[256,1152]{1,0:T(8,128)(2,1)}, u32[]{:S(2)}, u32[]{:S(2)}) collective-permute-start(bf16[256,1152]{1,0:T(8,128)(2,1)S(1)} %copy-done.22), channel_id=1, source_target_pairs={{0,1},{1,0},{2,3},{3,2},{4,5},{5,4},{6,7},{7,6},{8,9},{9,8},{10,11... | collective-permute-start | bytes 1769480 | tf_op jit(solution)/shard_map/ppermute | solution.py:44
  250.9 46.4 %collective-permute-start.51 = (bf16[2,512,1152]{2,1,0:T(8,128)(2,1)}, bf16[2,512,1152]{2,1,0:T(8,128)(2,1)}, u32[]{:S(2)}, u32[]{:S(2)}) collective-permute-start(bf16[2,512,1152]{2,1,0:T(8,128)(2,1)} %get-tuple-element.67), channel_id=1, source_target_pairs={{0,1},{1,0},{2,3},{3,2},{4,5},{5,4},{6,7},{7,6},{8,9},{9,8},{10,11... | collective-permute-start | bytes 7077896 | tf_op jit(solution)/shard_map/ppermute | solution.py:44
  254.1 31.6 %collective-permute-start.49 = (bf16[512,1024]{1,0:T(8,128)(2,1)}, bf16[512,1024]{1,0:T(8,128)(2,1)S(1)}, u32[]{:S(2)}, u32[]{:S(2)}) collective-permute-start(bf16[512,1024]{1,0:T(8,128)(2,1)} %get-tuple-element.190), channel_id=1, source_target_pairs={{0,1},{1,0},{2,3},{3,2},{4,5},{5,4},{6,7},{7,6},{8,9},{9,8},{10,11... | collective-permute-start | bytes 3145736 | tf_op jit(solution)/shard_map/ppermute | solution.py:44
  254.6 34.2 %collective-permute-start.41 = (bf16[512,1024]{1,0:T(8,128)(2,1)}, bf16[512,1024]{1,0:T(8,128)(2,1)}, u32[]{:S(2)}, u32[]{:S(2)}) collective-permute-start(bf16[512,1024]{1,0:T(8,128)(2,1)} %get-tuple-element.191), channel_id=1, source_target_pairs={{0,1},{1,0},{2,3},{3,2},{4,5},{5,4},{6,7},{7,6},{8,9},{9,8},{10,11... | collective-permute-start | bytes 3145736 | tf_op jit(solution)/shard_map/ppermute | solution.py:44
  288.8 30.9 %collective-permute-start.50 = (bf16[1,512,1152]{2,1,0:T(8,128)(2,1)}, bf16[1,512,1152]{2,1,0:T(8,128)(2,1)S(1)}, u32[]{:S(2)}, u32[]{:S(2)}) collective-permute-start(bf16[1,512,1152]{2,1,0:T(8,128)(2,1)} %get-tuple-element.65), channel_id=1, source_target_pairs={{0,1},{1,0},{2,3},{3,2},{4,5},{5,4},{6,7},{7,6},{8,9},{9,8},{10,11... | collective-permute-start | bytes 3538952 | tf_op jit(solution)/shard_map/ppermute | solution.py:44
  303.3 27.8 %collective-permute-start.58 = (bf16[256,1152]{1,0:T(8,128)(2,1)S(1)}, bf16[256,1152]{1,0:T(8,128)(2,1)S(1)}, u32[]{:S(2)}, u32[]{:S(2)}) collective-permute-start(bf16[256,1152]{1,0:T(8,128)(2,1)S(1)} %fusion.9), channel_id=1, source_target_pairs={{0,4},{1,5},{2,6},{3,7},{4,0},{5,1},{6,2},{7,3},{8,12},{9,13},{10,... | collective-permute-start | bytes 1769480 | tf_op jit(solution)/shard_map/ppermute | solution.py:44
  364.1 46.0 %collective-permute-start.75 = (bf16[4,4,32,1152]{3,2,1,0:T(8,128)(2,1)}, bf16[4,4,32,1152]{3,2,1,0:T(8,128)(2,1)}, u32[]{:S(2)}, u32[]{:S(2)}) collective-permute-start(bf16[4,4,32,1152]{3,2,1,0:T(8,128)(2,1)} %dynamic-slice_bitcast_fusion.1), channel_id=1, source_target_pairs={{0,1},{1,0},{2,3},{3,2},{4,5},{5,4},{6,7},{7,6},{8,9},{9,8},{10,11... | collective-permute-start | bytes 3538952 | tf_op jit(solution)/shard_map/ppermute | solution.py:44
  408.0 30.5 %collective-permute-start.65 = (bf16[4,4,32,2176]{3,2,1,0:T(8,128)(2,1)}, bf16[4,4,32,2176]{3,2,1,0:T(8,128)(2,1)S(1)}, u32[]{:S(2)}, u32[]{:S(2)}) collective-permute-start(bf16[4,4,32,2176]{3,2,1,0:T(8,128)(2,1)} %dynamic-slice_bitcast_fusion), channel_id=1, source_target_pairs={{0,1},{1,0},{2,3},{3,2},{4,5},{5,4},{6,7},{7,6},{8,9},{9,8},{10,11... | collective-permute-start | bytes 6684680 | tf_op jit(solution)/shard_map/ppermute | solution.py:44
  (97 other events, 1114.7 us)
Sparse Core Ops, SparseCore 0:
  47.1 115.7 all-gather.1
  285.8 110.9 reduce-scatter.1

commit v5 on v4

--- a/solution.py
+++ b/solution.py
@@ -43,42 +43,6 @@
     def swap(self, value, bits):
         return lax.ppermute(value, "fsdp", [(i, i ^ bits) for i in range(self.count)])
 
-    def shift(self, value, senders, step):
-        pairs = [
-            (g * MEMBERS + m, (g + step) * MEMBERS + m) for g in senders for m in range(MEMBERS)
-        ]
-        return lax.ppermute(value, "fsdp", pairs)
-
-    def line_gather(self, piece):
-        groups = self.groups
-        rising, falling = [piece], [piece]
-        for step in range(1, groups):
-            rising.append(self.shift(rising[-1], range(step - 1, groups - 1), 1))
-            falling.append(self.shift(falling[-1], range(1, groups - step + 1), -1))
-        found = [piece]
-        for step in range(1, groups):
-            found.append(jnp.where(self.group >= step, rising[step], falling[groups - step]))
-        return found
-
-    def line_reduce(self, pick):
-        groups = self.groups
-        rising = falling = None
-        for step in range(1, groups):
-            up = pick((self.group + groups - step) % groups)
-            down = pick((self.group + step) % groups)
-            up_owner = self.group + groups - step
-            down_owner = self.group - groups + step
-            if rising is not None:
-                up = up + rising.astype(f32)
-                down = down + falling.astype(f32)
-            del up_owner, down_owner
-            rising = self.shift(up.astype(bf16), range(0, step), 1)
-            falling = self.shift(down.astype(bf16), range(groups - step, groups), -1)
-        own = pick(self.group)
-        if rising is None:
-            return own
-        return own + rising.astype(f32) + falling.astype(f32)
-
     def direct_gather(self, piece):
         stack = jnp.zeros((self.groups,) + piece.shape, piece.dtype)
         for bits in range(self.groups):
@@ -94,43 +58,27 @@
         return total
 
     def chips_gather(self, block):
-        half = block.shape[0] // 2
-        top, low = block[:half], block[half:]
-        near_top = self.swap(top, 2)
-        far_low = self.swap(low, 4)
-        near_low = self.swap(low, 2)
-        far_top = self.swap(top, 4)
-        cross_top = self.swap(near_top, 4)
-        cross_low = self.swap(far_low, 2)
-        return {0: (top, low), 2: (near_top, near_low), 4: (far_top, far_low), 6: (cross_top, cross_low)}
-
-    def chips_reduce_begin(self, joined):
-        half = joined[0].shape[0] // 2
-        cross_top = self.swap(joined[6][:half].astype(bf16), 2)
-        cross_low = self.swap(joined[6][half:].astype(bf16), 4)
-        near_top = self.swap(joined[2][:half].astype(bf16), 2)
-        far_low = self.swap(joined[4][half:].astype(bf16), 4)
-        return cross_top, cross_low, near_top, far_low, joined[2][half:], joined[4][:half]
-
-    def chips_reduce_end(self, begun):
-        cross_top, cross_low, near_top, far_low, near_rest, far_rest = begun
-        near_low = self.swap((near_rest + cross_low.astype(f32)).astype(bf16), 2)
-        far_top = self.swap((far_rest + cross_top.astype(f32)).astype(bf16), 4)
-        return near_top, near_low, far_top, far_low
-
-    @staticmethod
-    def add_pieces(own, pieces):
-        near_top, near_low, far_top, far_low = (piece.astype(f32) for piece in pieces)
+        near, far = self.swap(block, 2), self.swap(block, 4)
+        return {0: (block,), 2: (near,), 4: (far,), 6: self.cross_of(near, far)}
+
+    def cross_of(self, near, far):
+        half = near.shape[0] // 2
+        return self.swap(near[:half], 4), self.swap(far[half:], 2)
+
+    def send_cross(self, own, other):
         half = own.shape[0] // 2
-        return jnp.concatenate(
-            [own[:half] + near_top + far_top, own[half:] + near_low + far_low], axis=0
-        )
-
-    def chips_reduce(self, joined):
-        return self.add_pieces(joined[0], self.chips_reduce_end(self.chips_reduce_begin(joined)))
-
-    def join_cores(self, own, other):
-        return own.astype(f32) + self.swap(other, 1).astype(f32)
+        top = (own[:half].astype(f32) + other[:half].astype(f32)).astype(bf16)
+        low = (own[half:].astype(f32) + other[half:].astype(f32)).astype(bf16)
+        return top, low
+
+    def send_sides(self, near, far, cross):
+        half = near[0].shape[0] // 2
+        cross_top, cross_low = cross
+        near_sum = near[0].astype(f32) + near[1].astype(f32)
+        far_sum = far[0].astype(f32) + far[1].astype(f32)
+        near_all = jnp.concatenate([near_sum[:half], near_sum[half:] + cross_low.astype(f32)], axis=0)
+        far_all = jnp.concatenate([far_sum[:half] + cross_top.astype(f32), far_sum[half:]], axis=0)
+        return near_all.astype(bf16), far_all.astype(bf16)
 
     def send_parts(self, parts):
         chips = parts.reshape((MEMBERS // 2, 2) + parts.shape[1:])
@@ -156,22 +104,21 @@
     return lax.dot_general(left, right, (((1,), (1,)), ((), ())), preferred_element_type=f32)
 
 
-def expert_kernel(first_ref, *refs, layout, fresh, last):
+def expert_kernel(first_ref, *refs, layout, experts, fresh, last, carried):
     refs = list(refs)
     packet_parts = [[refs.pop(0) for _ in range(number)] for number in layout]
     cotangent_parts = [[refs.pop(0) for _ in range(number)] for number in layout]
-    weight_parts = refs.pop(0)
-    prior_ref = None if fresh else refs.pop(0)
+    weight_parts = [refs.pop(0) for _ in experts]
+    prior_refs = [None if new else refs.pop(0) for new in fresh]
+    carried_out = (refs.pop(0), refs.pop(0)) if carried else None
+    carried_back = (refs.pop(0), refs.pop(0)) if carried else None
     out_refs, back_refs = (refs.pop(0), refs.pop(0)), (refs.pop(0), refs.pop(0))
-    if last:
-        rounded_ref = refs.pop(0)
-        grad_ref = refs.pop(0)
-    else:
-        grad_ref = refs.pop(0)
+    result_refs = [refs.pop(0) for _ in experts]
+    grad_refs = [refs.pop(0) if end else result for end, result in zip(last, result_refs)]
     packet_buffer, cotangent_buffer, weight_ref, packet_turned, cotangent_turned, sums = refs[:6]
     block_sem, weight_sem, prior_sem = refs[6:]
     rows, width = cotangent_buffer.shape[1:]
-    groups, _, _, depth, _ = weight_parts.shape
+    groups, _, depth, _ = weight_parts[0].shape
     blocks = len(layout)
     at = pl.program_id(0)
     first = first_ref[0]
@@ -189,30 +136,35 @@
                 )
         return copies
 
-    def weight_copies():
+    def weight_copies(n):
         return [
             pltpu.make_async_copy(
-                weight_parts.at[g], weight_ref.at[:, :, pl.ds(g * depth, depth)], weight_sem.at[g]
+                weight_parts[n].at[g], weight_ref.at[n, :, pl.ds(g * depth, depth)], weight_sem.at[n, g]
             )
             for g in range(groups)
         ]
 
-    def prior_copy():
-        return pltpu.make_async_copy(prior_ref, grad_ref, prior_sem)
+    def prior_copy(n):
+        return pltpu.make_async_copy(prior_refs[n], grad_refs[n], prior_sem.at[n])
 
     @pl.when(at == 0)
     def _():
-        for copy in block_copies(0) + weight_copies():
+        for copy in block_copies(0):
             copy.start()
-        if fresh:
-            grad_ref[...] = jnp.zeros_like(grad_ref)
-        else:
-            prior_copy().start()
+        for n in range(len(experts)):
+            for copy in weight_copies(n):
+                copy.start()
+        for n, new in enumerate(fresh):
+            if new:
+                grad_refs[n][...] = jnp.zeros_like(grad_refs[n])
+            else:
+                prior_copy(n).start()
         for block in range(1, blocks):
             for copy in block_copies(block):
                 copy.start()
-        for copy in weight_copies():
-            copy.wait()
+        for n in range(len(experts)):
+            for copy in weight_copies(n):
+                copy.wait()
 
     for block in range(blocks):
 
@@ -229,22 +181,24 @@
     packet_turned[...] = normed.T
     cotangent_turned[...] = upstream.T
     begun = []
-    for local in range(LOCAL_EXPERTS):
+    for n in range(len(experts)):
         begun.append(
             (
-                dot(normed, weight_ref[local, 0]),
-                dot(normed, weight_ref[local, 1]),
-                dot(upstream, weight_ref[local, 2]),
+                dot(normed, weight_ref[n, 0]),
+                dot(normed, weight_ref[n, 1]),
+                dot(upstream, weight_ref[n, 2]),
             )
         )
-    if not fresh:
+    if not all(fresh):
 
         @pl.when(at == 0)
         def _():
-            prior_copy().wait()
-
-    for local in range(LOCAL_EXPERTS):
-        gate_pre, up_pre, inner_raw = begun[local]
+            for n, new in enumerate(fresh):
+                if not new:
+                    prior_copy(n).wait()
+
+    for n, local in enumerate(experts):
+        gate_pre, up_pre, inner_raw = begun[n]
         expert = first + local
         is_high, is_low = lane == expert, lane == expert + EXPERTS
         share = jnp.sum(jnp.where(is_high | is_low, shares, 0.0), axis=1, keepdims=True)
@@ -259,47 +213,52 @@
         ).astype(bf16)
         up_grad = (inner_grad * activated).astype(bf16)
         inner_shared = (inner * scaled).astype(bf16)
-        out_term = dot_turned(inner_shared, weight_ref[local, 2])
-        back_term = dot_turned(gate_grad, weight_ref[local, 0]) + dot_turned(
-            up_grad, weight_ref[local, 1]
-        )
-        if local == 0:
+        out_term = dot_turned(inner_shared, weight_ref[n, 2])
+        back_term = dot_turned(gate_grad, weight_ref[n, 0]) + dot_turned(up_grad, weight_ref[n, 1])
+        if n == 0:
             sums[0], sums[1] = out_term, back_term
         else:
             sums[0] += out_term
             sums[1] += back_term
-        grad_ref[local, 0] += dot(packet_turned[...], gate_grad)
-        grad_ref[local, 1] += dot(packet_turned[...], up_grad)
-        grad_ref[local, 2] += dot(cotangent_turned[...], inner_shared)
+        grad_refs[n][0] += dot(packet_turned[...], gate_grad)
+        grad_refs[n][1] += dot(packet_turned[...], up_grad)
+        grad_refs[n][2] += dot(cotangent_turned[...], inner_shared)
         high = share_grad.astype(bf16).astype(f32)
         extra = extra + jnp.where(is_high, high, 0.0) + jnp.where(is_low, share_grad - high, 0.0)
     for side in range(2):
 
         @pl.when((at < blocks // 2) == (side == 0))
         def _():
-            out_refs[side][0] = sums[0].astype(bf16)
-            back_refs[side][0, :, :width] = sums[1].astype(bf16)
-            back_refs[side][0, :, width:] = extra.astype(bf16)
-
-    if last:
+            out_total, back_total, extra_total = sums[0], sums[1], extra
+            if carried:
+                out_total = out_total + carried_out[side][0].astype(f32)
+                back_total = back_total + carried_back[side][0, :, :width].astype(f32)
+                extra_total = extra_total + carried_back[side][0, :, width:].astype(f32)
+            out_refs[side][0] = out_total.astype(bf16)
+            back_refs[side][0, :, :width] = back_total.astype(bf16)
+            back_refs[side][0, :, width:] = extra_total.astype(bf16)
+
+    if any(last):
 
         @pl.when(at == blocks - 1)
         def _():
-            for g in range(groups):
-                rounded_ref[g] = grad_ref[:, :, pl.ds(g * depth, depth)].astype(bf16)
-
-
-def run_experts(first, packets, cotangents, weights, prior, last):
+            for n, end in enumerate(last):
+                if end:
+                    for g in range(groups):
+                        result_refs[n][g] = grad_refs[n][:, pl.ds(g * depth, depth)].astype(bf16)
+
+
+def run_experts(first, packets, cotangents, experts, weights, priors, last, carried=None):
     layout = tuple(len(parts) for parts in packets)
     blocks = len(layout)
     rows = sum(part.shape[0] for part in packets[0])
     wide, width = packets[0][0].shape[1], cotangents[0][0].shape[1]
-    groups, _, _, depth, hidden = weights.shape
-    grad_shape = (LOCAL_EXPERTS, 3, width, hidden)
-    fresh = prior is None
+    groups, _, depth, hidden = weights[0].shape
+    grad_shape = (3, width, hidden)
+    fresh = tuple(prior is None for prior in priors)
     operands = [part for parts in packets for part in parts]
     operands += [part for parts in cotangents for part in parts]
-    operands += [weights] + ([] if fresh else [prior])
+    operands += list(weights) + [prior for prior in priors if prior is not None]
     half = blocks // 2
 
     def own_side(i, s):
@@ -308,49 +267,55 @@
     def other_side(i, s):
         return (jnp.maximum(i - half, 0), 0, 0)
 
-    def whole(i, s):
-        return (0, 0, 0, 0, 0) if last else (0, 0, 0, 0)
-
-    last_shape = weights.shape if last else grad_shape
-    scratch = [pltpu.VMEM(grad_shape, f32)] if last else []
+    def whole(shape):
+        return pl.BlockSpec(
+            shape, lambda i, s, rank=len(shape): (0,) * rank, pipeline_mode=pl.Buffered(1)
+        )
+
+    term_specs = [
+        pl.BlockSpec((1, rows, columns), side)
+        for columns in (width, wide)
+        for side in (own_side, other_side)
+    ]
+    in_specs = [pl.BlockSpec(memory_space=pl.ANY)] * len(operands)
+    if carried is not None:
+        in_specs += term_specs
+        operands += list(carried)
+    grads = [((groups, 3, depth, hidden), bf16) if end else (grad_shape, f32) for end in last]
+    scratch = [pltpu.VMEM(grad_shape, f32) for end in last if end]
     scratch += [
         pltpu.VMEM((blocks, rows, wide), bf16),
         pltpu.VMEM((blocks, rows, width), bf16),
-        pltpu.VMEM(grad_shape, bf16),
+        pltpu.VMEM((len(experts),) + grad_shape, bf16),
         pltpu.VMEM((width, rows), bf16),
         pltpu.VMEM((width, rows), bf16),
         pltpu.VMEM((2, rows, width), f32),
         pltpu.SemaphoreType.DMA((blocks, 4)),
-        pltpu.SemaphoreType.DMA((groups,)),
-        pltpu.SemaphoreType.DMA,
+        pltpu.SemaphoreType.DMA((len(experts), groups)),
+        pltpu.SemaphoreType.DMA((len(experts),)),
     ]
     return pl.pallas_call(
-        functools.partial(expert_kernel, layout=layout, fresh=fresh, last=last),
+        functools.partial(
+            expert_kernel, layout=layout, experts=experts, fresh=fresh, last=last,
+            carried=carried is not None,
+        ),
         grid_spec=pltpu.PrefetchScalarGridSpec(
             num_scalar_prefetch=1,
             grid=(blocks,),
-            in_specs=[pl.BlockSpec(memory_space=pl.ANY)] * len(operands),
-            out_specs=[
-                pl.BlockSpec((1, rows, width), own_side),
-                pl.BlockSpec((1, rows, width), other_side),
-                pl.BlockSpec((1, rows, wide), own_side),
-                pl.BlockSpec((1, rows, wide), other_side),
-                pl.BlockSpec(last_shape, whole, pipeline_mode=pl.Buffered(1)),
-            ],
+            in_specs=in_specs,
+            out_specs=term_specs + [whole(shape) for shape, _ in grads],
             scratch_shapes=scratch,
         ),
         out_shape=[
-            jax.ShapeDtypeStruct((half, rows, width), bf16),
-            jax.ShapeDtypeStruct((half, rows, width), bf16),
-            jax.ShapeDtypeStruct((half, rows, wide), bf16),
-            jax.ShapeDtypeStruct((half, rows, wide), bf16),
-            jax.ShapeDtypeStruct(last_shape, bf16 if last else f32),
-        ],
+            jax.ShapeDtypeStruct((half, rows, columns), bf16)
+            for columns in (width, width, wide, wide)
+        ]
+        + [jax.ShapeDtypeStruct(shape, dtype) for shape, dtype in grads],
         compiler_params=pltpu.CompilerParams(vmem_limit_bytes=62 * 1024 * 1024),
         cost_estimate=pl.CostEstimate(
-            flops=blocks * LOCAL_EXPERTS * 9 * 2 * rows * width * hidden,
-            bytes_accessed=blocks * rows * width * 8 + 36 * width * hidden,
-            transcendentals=blocks * LOCAL_EXPERTS * rows * hidden,
+            flops=blocks * len(experts) * 9 * 2 * rows * width * hidden,
+            bytes_accessed=blocks * rows * width * 8 + 18 * len(experts) * width * hidden,
+            transcendentals=blocks * len(experts) * rows * hidden,
         ),
         name="experts",
     )(first, *operands)
@@ -475,14 +440,13 @@
 
 
 def middle_kernel(
-    joined_ref, near_top_ref, near_low_ref, far_top_ref, far_low_ref, packet_ref, middle_ref,
-    cotangent_ref, share_ref, gains_ref, mixed_ref, output_ref, extra_ref,
+    own_ref, other_ref, near_ref, far_ref, packet_ref, middle_ref, cotangent_ref, share_ref, gains_ref, mixed_ref, output_ref, extra_ref,
     middle_grad_ref, mixed_grad_ref, pack_ref, back_ref, branch_ref, turned_ref,
 ):
-    rows, width = cotangent_ref.shape
-    half = rows // 2
-    back_ref[:half] = joined_ref[:half] + near_top_ref[...].astype(f32) + far_top_ref[...].astype(f32)
-    back_ref[half:] = joined_ref[half:] + near_low_ref[...].astype(f32) + far_low_ref[...].astype(f32)
+    width = cotangent_ref.shape[1]
+    back_ref[...] = (own_ref[...].astype(f32) + other_ref[...].astype(f32)) + (
+        near_ref[...].astype(f32) + far_ref[...].astype(f32)
+    )
     shares = share_ref[...]
     share_grad = back_ref[:, width:]
     share_grad = share_grad + pltpu.roll(share_grad, EXTRA - EXPERTS, 1)
@@ -661,14 +625,14 @@
     )
 
 
-def middle_back(joined, pieces, packet, middle, cotangent, shares, gains, mixed, whole):
+def middle_back(pieces, packet, middle, cotangent, shares, gains, mixed, whole):
     rows, width = cotangent.shape
     head_columns, kv_columns = HEADS * HEAD_DIM, KV_HEADS * HEAD_DIM
     at_output = head_columns + 2 * kv_columns
     return call_kernel(
         middle_kernel,
         "middle_back",
-        [(a, None, None) for a in (joined, *pieces, packet, middle, cotangent, shares, gains, mixed)]
+        [(a, None, None) for a in (*pieces, packet, middle, cotangent, shares, gains, mixed)]
         + [
             (whole, (width, head_columns), (0, at_output // head_columns)),
             (whole, (width, EXTRA), (0, (at_output + head_columns) // EXTRA)),
@@ -739,7 +703,9 @@
     shelf = links.send_parts(mine).transpose(1, 2, 0, 3, 4)
     shelf = shelf.reshape(LOCAL_EXPERTS, 3, MEMBERS * shard, hidden)
     lines = [[m + MEMBERS * g for g in range(groups)] for m in range(MEMBERS)]
-    expert_full = lax.all_gather(shelf, "fsdp", axis_index_groups=lines)
+    expert_full = [
+        lax.all_gather(shelf[n], "fsdp", axis_index_groups=lines) for n in range(LOCAL_EXPERTS)
+    ]
 
     packed = jnp.concatenate(
         [
@@ -778,66 +744,97 @@
         tokens, lengths, routes, tables, gains, whole
     )
     packets = links.chips_gather(packet)
-    packets[0] = (packet,)
-    cotangents[0] = (late_cotangent,)
+    def both(blocks, turn):
+        own = [blocks[k] for k in turn]
+        return own + [tuple(links.swap(part, 1) for part in parts) for parts in own]
 
     first = (member * LOCAL_EXPERTS).astype(jnp.int32).reshape(1)
-    out_terms, back_terms = {}, {}
-    grads = None
-    turns = ((0,), (2, 6), (4,))
-    for turn in turns:
-        stacks = []
-        for blocks in (packets, cotangents):
-            even = [blocks[k] for k in turn]
-            stacks.append(even + [tuple(links.swap(part, 1) for part in parts) for parts in even])
-        out_own, out_other, back_own, back_other, grads = run_experts(
-            first, stacks[0], stacks[1], expert_full, grads, turn == turns[-1]
+    chip_rows = both(packets, (0,)), both(cotangents, (0,))
+    side_rows = both(packets, (2, 4)), both(cotangents, (2, 4))
+    cross_rows = both(packets, (6,)), both(cotangents, (6,))
+    *chip_terms, zero = run_experts(first, *chip_rows, (0,), expert_full[:1], [None], (False,))
+    *side_terms, zero = run_experts(first, *side_rows, (0,), expert_full[:1], [zero], (False,))
+    *cross_terms, zero, one = run_experts(
+        first, *cross_rows, (0, 1), expert_full, [zero, None], (True, False)
+    )
+
+    def reduce_groups(grads):
+        return lax.psum_scatter(grads, "fsdp", scatter_dimension=0, axis_index_groups=lines)
+
+    shelf_zero = reduce_groups(zero)
+    out_cross = links.send_cross(cross_terms[0][0], links.swap(cross_terms[1], 1)[0])
+    back_cross = links.send_cross(cross_terms[2][0], links.swap(cross_terms[3], 1)[0])
+    out_cross, back_cross, side_terms = lax.optimization_barrier((out_cross, back_cross, side_terms))
+    back_cross = links.swap(back_cross[0], 2), links.swap(back_cross[1], 4)
+    out_cross = links.swap(out_cross[0], 2), links.swap(out_cross[1], 4)
+    *side_terms, one = run_experts(
+        first, *side_rows, (1,), expert_full[1:], [one], (False,), side_terms
+    )
+    back_other = links.swap(side_terms[3], 1)
+    out_other = links.swap(side_terms[1], 1)
+    back_near, back_far = links.send_sides(
+        (side_terms[2][0], back_other[0]), (side_terms[2][1], back_other[1]), back_cross
+    )
+    back_near, back_far, chip_terms = lax.optimization_barrier((back_near, back_far, chip_terms))
+    back_near, back_far = links.swap(back_near, 2), links.swap(back_far, 4)
+    *chip_terms, one = run_experts(
+        first, *chip_rows, (1,), expert_full[1:], [one], (True,), chip_terms
+    )
+    shelf_one = reduce_groups(one)
+    back_pieces = (chip_terms[2][0], links.swap(chip_terms[3], 1)[0], back_near, back_far)
+    out_near, out_far = links.send_sides(
+        (side_terms[0][0], out_other[0]), (side_terms[0][1], out_other[1]), out_cross
+    )
+    out_near, out_far, back_pieces = lax.optimization_barrier((out_near, out_far, back_pieces))
+    out_near, out_far = links.swap(out_near, 2), links.swap(out_far, 4)
+    out_pieces = chip_terms[0][0], links.swap(chip_terms[1], 1)[0], out_near, out_far
+
+    core, chip = member % 2, member // 2
+
+    def pack_cores(pack):
+        columns = pack.shape[1]
+        pack = pack.reshape(groups, MEMBERS // 2, 2, shard, columns)
+        own = lax.dynamic_index_in_dim(pack, core, 2, keepdims=False)
+        other = links.swap(lax.dynamic_index_in_dim(pack, 1 - core, 2, keepdims=False), 1)
+
+        def part(bits):
+            return tuple(
+                lax.dynamic_index_in_dim(side, chip ^ bits, 1, keepdims=False).reshape(
+                    groups * shard, columns
+                )
+                for side in (own, other)
+            )
+
+        return [part(bits) for bits in range(MEMBERS // 2)]
+
+    def pack_cross(parts):
+        top, low = links.send_cross(*parts[3])
+        return links.swap(top, 2), links.swap(low, 4)
+
+    def pack_sides(parts, cross):
+        near, far = links.send_sides(parts[1], parts[2], cross)
+        near, far = links.swap(near, 2), links.swap(far, 4)
+        total = (parts[0][0].astype(f32) + parts[0][1].astype(f32)) + (
+            near.astype(f32) + far.astype(f32)
         )
-        back_join = links.join_cores(back_own, back_other)
-        for at, k in enumerate(turn):
-            out_terms[k] = (out_own[at], out_other[at])
-            back_terms[k] = back_join[at]
-
-    back_pieces = links.chips_reduce_end(links.chips_reduce_begin(back_terms))
-    out_join = {k: links.join_cores(*out_terms[k]) for k in (6, 2, 4, 0)}
-
-    shelf_grad = lax.psum_scatter(grads, "fsdp", scatter_dimension=0, axis_index_groups=lines)
+        return links.direct_reduce(total.reshape(groups, shard, total.shape[1]))
+
+    middle_grad, mixed_grad, first_pack = middle_back(
+        back_pieces, packet, middle, cotangent, shares, gains, mixed, whole
+    )
+    first_parts = pack_cores(first_pack)
+    projected_grad = attention_back(lengths, rotated, mixed_grad, logs, tables)
+    first_parts, projected_grad = lax.optimization_barrier((first_parts, projected_grad))
+    first_cross = pack_cross(first_parts)
+    grad_tokens, second_pack = inputs_back(tokens, gains, projected_grad, whole, middle_grad)
+    second_parts = pack_cores(second_pack)
+    first_total = pack_sides(first_parts, first_cross)
+    second_total = pack_sides(second_parts, pack_cross(second_parts))
+    layer_out = (middle + sum(piece.astype(f32) for piece in out_pieces)).astype(bf16)
+    shelf_grad = jnp.stack([shelf_zero, shelf_one])
     shelf_grad = shelf_grad.reshape(LOCAL_EXPERTS, 3, MEMBERS, shard, hidden)
     expert_shards = links.send_parts(shelf_grad.transpose(2, 0, 1, 3, 4)).astype(f32)
     expert_shards = expert_shards.reshape(EXPERTS, 3, shard, hidden)
-
-    def pack_begin(pack):
-        columns = pack.shape[1]
-        pack = pack.reshape(groups, MEMBERS // 2, 2, shard, columns)
-        core, chip = member % 2, member // 2
-        own = lax.dynamic_index_in_dim(pack, core, 2, keepdims=False)
-        other = lax.dynamic_index_in_dim(pack, 1 - core, 2, keepdims=False)
-        joined = links.join_cores(own, other)
-        return {
-            2 * bits: lax.dynamic_index_in_dim(joined, chip ^ bits, 1, keepdims=False).reshape(
-                groups * shard, columns
-            )
-            for bits in range(MEMBERS // 2)
-        }
-
-    def pack_end(terms):
-        total = links.chips_reduce(terms)
-        return links.direct_reduce(total.reshape(groups, shard, total.shape[1]))
-
-    middle_grad, mixed_grad, first_pack = middle_back(
-        back_terms[0], back_pieces, packet, middle, cotangent, shares, gains, mixed, whole
-    )
-    out_join, middle_grad = lax.optimization_barrier((out_join, middle_grad))
-    out_begun = links.chips_reduce_begin(out_join)
-    projected_grad = attention_back(lengths, rotated, mixed_grad, logs, tables)
-    out_begun, projected_grad = lax.optimization_barrier((out_begun, projected_grad))
-    out_pieces = links.chips_reduce_end(out_begun)
-    first_terms = pack_begin(first_pack)
-    grad_tokens, second_pack = inputs_back(tokens, gains, projected_grad, whole, middle_grad)
-    second_terms = pack_begin(second_pack)
-    first_total = pack_end(first_terms)
-    second_total = pack_end(second_terms)
-    layer_out = (middle + links.add_pieces(out_join[0], out_pieces)).astype(bf16)
     return (
         layer_out,
         grad_tokens,

time: 496 us -> 538 us (1.085)
  starting transfers between devices: 72.6 us -> 51 us
  local copies, waits for them, and re-layouts: 46.3 us -> 67 us
  waiting for transfers between devices: 142 us -> 162 us
  Pallas kernels: 186 us -> 205 us
    ppermute x89 -> x68, starting transfers between devices: 72.3 us -> 50.6 us  [swap(): lax.ppermute(value, 'fsdp', [(i, i ^ bits) for i in range(self.count)])]
    ppermute x89 -> x68, waiting for transfers between devices: 142 us -> 162 us  [swap(): lax.ppermute(value, 'fsdp', [(i, i ^ bits) for i in range(self.count)])]
    pallas_call x3 -> x5, Pallas kernels: 116 us -> 135 us  [run_experts(): pl.pallas_call(functools.partial(expert_kernel, layout=layout, experts=ex...]
    dynamic_update_slice x8, local copies, waits for them, and re-layouts: 0.82 us -> 11.2 us  [local(): whole = lax.dynamic_update_index_in_dim(whole, part, member ^ k, 1)]
    add x13 -> x8, other arithmetic: 18.6 us -> 8.93 us  [the longest x4 5.76 us: send_sides(): far_sum = far[0].astype(f32) + far[1].astype(f32)]
    dynamic_slice x0 -> x4, local copies, waits for them, and re-layouts: none -> 7.02 us  [part(): lax.dynamic_index_in_dim(side, chip ^ bits, 1, keepdims=False)]
    concatenate x2 -> x8, other arithmetic: 0.11 us -> 6.45 us  [the longest x4 3.73 us: send_sides(): jnp.concatenate([near_sum[:half], near_sum[half:] + cross_low.astype(f32)...]
    slice x14 -> x17, local copies, waits for them, and re-layouts: 7.91 us -> 10.8 us  [the longest x6 6.49 us: cross_of(): return (self.swap(near[:half], 4), self.swap(far[half:], 2))]
  transfers between devices with their start and end apart: 91 -> 72, of which waited for: 36 -> 26; matrix products, arithmetic and copies ran while one was open for 13% -> 16% of each run, Pallas kernels for 38% -> 26%
where the time goes in v5:
time: 538 us; the launch traced here: 533 us
  Pallas kernels  205 us (38%)
  waiting for transfers between devices  162 us (30%)
  local copies, waits for them, and re-layouts  67 us (12%)
  starting transfers between devices  51 us (9%)
  other arithmetic  32.3 us (6%)
  between operations  15.9 us (3%)
    ppermute x68, waiting for transfers between devices, swap(): lax.ppermute(value, 'fsdp', [(i, i ^ bits) for i in range(self.count)])  162 us
    pallas_call x5, Pallas kernels, run_experts(): pl.pallas_call(functools.partial(expert_kernel, layout=layout, experts=ex...  135 us
    pallas_call x4, Pallas kernels, call_kernel(): pl.pallas_call(body, grid=(1,), in_specs=specs, out_specs=[pl.BlockSpec(o...  70.2 us
    ppermute x68, starting transfers between devices, swap(): lax.ppermute(value, 'fsdp', [(i, i ^ bits) for i in range(self.count)])  50.6 us
    dynamic_update_slice x8, local copies, waits for them, and re-layouts, local(): whole = lax.dynamic_update_index_in_dim(whole, part, member ^ k, 1)  11.2 us
  transfers between devices with their start and end apart: 72, of which 26 were waited for; matrix products, arithmetic and copies ran while one was open for 16% of the time, Pallas kernels for 26%

profile of v5, /device:TPU:0, one launch (start us, length us, event | category | flops | bytes accessed | tf_op | source)
XLA Modules:
  0.0 532.8 jit_solution(12186310883876573336)
XLA Ops:
  26.1 5.3 collective-permute-done.1
  33.4 5.6 %collective-permute-done.15 = bf16[2,2,3,32,512]{4,3,2,1,0:T(8,128)(2,1)} collective-permute-done((bf16[2,2,3,32,512]{4,3,2,1,0:T(8,128)(2,1)}, bf16[2,2,3,32,512]{4,3,2,1,0:T(8,128)(2,1)}, u32[]{:S(2)}, u32[]{:S(2)}) %collective-permute-start.15) | collective-permute-done | bytes 393248 | tf_op jit(solution)/shard_map/ppermute | solution.py:44
  49.5 12.6 %collective-permute-done.4 = bf16[128,3200]{1,0:T(8,128)(2,1)} collective-permute-done((bf16[128,3200]{1,0:T(8,128)(2,1)S(1)}, bf16[128,3200]{1,0:T(8,128)(2,1)}, u32[]{:S(2)}, u32[]{:S(2)}) %collective-permute-start.4) | collective-permute-done | bytes 819232 | tf_op jit(solution)/shard_map/ppermute | solution.py:44
  90.1 24.5 %attention_forward.1 = (bf16[512,1152]{1,0:T(8,128)(2,1)}, f32[512,1024]{1,0:T(8,128)}, bf16[512,2048]{1,0:T(8,128)(2,1)}, bf16[512,1024]{1,0:T(8,128)(2,1)}, f32[4,4,512]{2,1,0:T(4,128)}, /*index=5*/f32[512,128]{1,0:T(8,128)}) custom-call(s32[1]{0:T(128)S(6)} %copy.168.length_ref, bf16[512,1024]{1,0:T(8,128)(2,1)} %tokens_ref.3, ...), custom_call_target="tpu_custom_call" | custom-call | flops 4294967296 | bytes 15392772 | tf_op jit(solution)/shard_map/attention_forward/pallas_call | solution.py:579
  119.7 22.5 %collective-permute-done.23.refs_5_ = bf16[512,1024]{1,0:T(8,128)(2,1)} collective-permute-done((bf16[512,1024]{1,0:T(8,128)(2,1)S(1)}, bf16[512,1024]{1,0:T(8,128)(2,1)}, u32[]{:S(2)}, u32[]{:S(2)}) %collective-permute-start.23) | collective-permute-done | bytes 1048608 | tf_op jit(solution)/shard_map/ppermute | solution.py:44
  147.1 20.4 %collective-permute-done.19.refs_1_ = bf16[512,1152]{1,0:T(8,128)(2,1)} collective-permute-done((bf16[512,1152]{1,0:T(8,128)(2,1)}, bf16[512,1152]{1,0:T(8,128)(2,1)}, u32[]{:S(2)}, u32[]{:S(2)}) %collective-permute-start.19) | collective-permute-done | bytes 1179680 | tf_op jit(solution)/shard_map/ppermute | solution.py:44
  167.4 11.1 %collective-permute-done.30.refs_4_ = bf16[256,1024]{1,0:T(8,128)(2,1)S(1)} collective-permute-done((bf16[256,1024]{1,0:T(8,128)(2,1)S(1)}, bf16[256,1024]{1,0:T(8,128)(2,1)S(1)}, u32[]{:S(2)}, u32[]{:S(2)}) %collective-permute-start.30) | collective-permute-done | bytes 524320 | tf_op jit(solution)/shard_map/ppermute | solution.py:44
  181.3 9.0 %collective-permute-done.26.refs_0_ = bf16[256,1152]{1,0:T(8,128)(2,1)} collective-permute-done((bf16[256,1152]{1,0:T(8,128)(2,1)S(1)}, bf16[256,1152]{1,0:T(8,128)(2,1)}, u32[]{:S(2)}, u32[]{:S(2)}) %collective-permute-start.26) | collective-permute-done | bytes 589856 | tf_op jit(solution)/shard_map/ppermute | solution.py:44
  190.8 18.3 %experts.5 = (bf16[1,512,1024]{2,1,0:T(8,128)(2,1)}, bf16[1,512,1024]{2,1,0:T(8,128)(2,1)}, bf16[1,512,1152]{2,1,0:T(8,128)(2,1)}, bf16[1,512,1152]{2,1,0:T(8,128)(2,1)}, f32[3,1024,512]{2,1,0:T(8,128)}) custom-call(s32[1]{0:T(128)} %bitcast.20.first_ref, bf16[512,1152]{1,0:T(8,128)(2,1)} %get-tuple-element.82.refs_0_.packet_ref, ...), custom_call_target="tpu_custom_call" | custom-call | flops 9663676416 | bytes 17825792 | tf_op jit(solution)/shard_map/experts/pallas_call | solution.py:297
  210.8 31.2 %experts.6 = (bf16[2,512,1024]{2,1,0:T(8,128)(2,1)}, bf16[2,512,1024]{2,1,0:T(8,128)(2,1)}, bf16[2,512,1152]{2,1,0:T(8,128)(2,1)}, bf16[2,512,1152]{2,1,0:T(8,128)(2,1)}, f32[3,1024,512]{2,1,0:T(8,128)}) custom-call(s32[1]{0:T(128)} %bitcast.20.first_ref, bf16[512,1152]{1,0:T(8,128)(2,1)} %collective-permute-done.18.refs_0_, ...), custom_call_target="tpu_custom_call" | custom-call | flops 19327352832 | bytes 26214400 | tf_op jit(solution)/shard_map/experts/pallas_call | solution.py:297
  242.8 30.5 %experts.7 = (bf16[1,512,1024]{2,1,0:T(8,128)(2,1)}, bf16[1,512,1024]{2,1,0:T(8,128)(2,1)}, bf16[1,512,1152]{2,1,0:T(8,128)(2,1)}, bf16[1,512,1152]{2,1,0:T(8,12...) custom-call(s32[1]{0:T(128)} %bitcast.20.first_ref, ...), custom_call_target="tpu_custom_call" | custom-call | flops 19327352832 | bytes 27262976 | tf_op jit(solution)/shard_map/experts/pallas_call | solution.py:297
  280.1 34.1 %experts.8 = (bf16[2,512,1024]{2,1,0:T(8,128)(2,1)}, bf16[2,512,1024]{2,1,0:T(8,128)(2,1)}, bf16[2,512,1152]{2,1,0:T(8,128)(2,1)}, bf16[2,512,1152]{2,1,0:T(8,128)(2,1)}, f32[3,1024,512]{2,1,0:T(8,128)}) custom-call(s32[1]{0:T(128)} %bitcast.20.first_ref, bf16[512,1152]{1,0:T(8,128)(2,1)} %collective-permute-done.18.refs_0_, ...), custom_call_target="tpu_custom_call" | custom-call | flops 19327352832 | bytes 26214400 | tf_op jit(solution)/shard_map/experts/pallas_call | solution.py:297
  322.2 8.9 %collective-permute-done.38 = bf16[256,1152]{1,0:T(8,128)(2,1)S(1)} collective-permute-done((bf16[256,1152]{1,0:T(8,128)(2,1)}, bf16[256,1152]{1,0:T(8,128)(2,1)S(1)}, u32[]{:S(2)}, u32[]{:S(2)}) %collective-permute-start.38) | collective-permute-done | bytes 589856 | tf_op jit(solution)/shard_map/ppermute | solution.py:44
  333.7 20.6 %experts.9 = (bf16[1,512,1024]{2,1,0:T(8,128)(2,1)}, bf16[1,512,1024]{2,1,0:T(8,128)(2,1)}, bf16[1,512,1152]{2,1,0:T(8,128)(2,1)}, bf16[1,512,1152]{2,1,0:T(8,128)(2,1)}, bf16[4,3,256,512]{3,2,1,0:T(8,128)(2,1)}) custom-call(s32[1]{0:T(128)} %bitcast.20.first_ref, bf16[512,1152]{1,0:T(8,128)(2,1)} %get-tuple-element.82.refs_0_.packet_ref, ...), custom_call_target="tpu_custom_call" | custom-call | flops 9663676416 | bytes 17825792 | tf_op jit(solution)/shard_map/experts/pallas_call | solution.py:297
  363.3 19.6 %collective-permute-done.44.near_ref = bf16[512,1152]{1,0:T(8,128)(2,1)S(1)} collective-permute-done((bf16[512,1152]{1,0:T(8,128)(2,1)}, bf16[512,1152]{1,0:T(8,128)(2,1)S(1)}, u32[]{:S(2)}, u32[]{:S(2)}) %collective-permute-start.44) | collective-permute-done | bytes 1179680 | tf_op jit(solution)/shard_map/ppermute | solution.py:44
  386.1 12.0 %middle_back.1 = (f32[512,1024]{1,0:T(8,128)}, bf16[512,1024]{1,0:T(8,128)(2,1)}, bf16[1024,1152]{1,0:T(8,128)(2,1)}) custom-call(bf16[512,1152]{1,0:T(8,128)(2,1)} %bitcast.267, bf16[512,1152]{1,0:T(8,128)(2,1)} %bitcast.268, bf16[512,1152]{1,0:T(8,128)(2,1)} %copy-done.11, bf16[512,1152]{1,0:T(8,128)(2,1)} %copy-done.12, ...), custom_call_target="tpu_custom_call" | custom-call | flops 2147483648 | bytes 28975104 | tf_op jit(solution)/shard_map/middle_back/pallas_call | solution.py:579
  399.6 19.0 %attention_back.1.projected_ref = bf16[512,2048]{1,0:T(8,128)(2,1)} custom-call(s32[1]{0:T(128)S(6)} %copy.168.length_ref, bf16[512,2048]{1,0:T(8,128)(2,1)} %get-tuple-element.131.rotated_ref, bf16[512,1024]{1,0:T(8,128)(2,1)} %get-tuple-element.132.mixed_grad_ref, f32[4,4,512]{2,1,0:T(4,128)} %get-tuple-element.133.log_ref, f32[512,256]{1,0:T(8,128)} %copy.122.cosine_ref, ...), custom_call_target="tpu_custom_call" | custom-call | flops 2684354560 | bytes 6324228 | tf_op jit(solution)/shard_map/attention_back/pallas_call | solution.py:579
  420.9 4.2 fusion.2
  427.3 14.8 %inputs_back.1 = (f32[512,1024]{1,0:T(8,128)}, bf16[1024,2176]{1,0:T(8,128)(2,1)}) custom-call(bf16[512,1024]{1,0:T(8,128)(2,1)} %tokens_ref.3, f32[2,1024]{1,0:T(2,128)} %copy.124.gains_ref, bf16[512,2048]{1,0:T(8,128)(2,1)} %attention_back.1.projected_ref, bf16[1024,3200]{1,0:T(8,128)(2,1)} %bitcast.18.weight_ref.output_ref.extra_ref, ...), custom_call_target="tpu_custom_call" | custom-call | flops 4294967296 | bytes 18358272 | tf_op jit(solution)/shard_map/inputs_back/pallas_call | solution.py:579
  479.7 6.0 %collective-permute-done.52 = bf16[64,2176]{1,0:T(8,128)(2,1)S(1)} collective-permute-done((bf16[64,2176]{1,0:T(8,128)(2,1)S(1)}, bf16[64,2176]{1,0:T(8,128)(2,1)S(1)}, u32[]{:S(2)}, u32[]{:S(2)}) %collective-permute-start.52) | collective-permute-done | bytes 278560 | tf_op jit(solution)/shard_map/ppermute | solution.py:44
  489.3 4.9 collective-permute-done.51
  502.2 3.8 collective-permute-start.55
  506.6 5.5 %collective-permute-done.64 = bf16[2,2,3,32,512]{4,3,2,1,0:T(8,128)(2,1)S(1)} collective-permute-done((bf16[2,2,3,32,512]{4,3,2,1,0:T(8,128)(2,1)S(1)}, bf16[2,2,3,32,512]{4,3,2,1,0:T(8,128)(2,1)S(1)}, u32[]{:S(2)}, u32[]{:S(2)}) %collective-permute-start.64) | collective-permute-done | bytes 393248 | tf_op jit(solution)/shard_map/ppermute | solution.py:44
  513.4 7.4 %collective-permute-done.66 = bf16[2,2,3,32,512]{4,3,2,1,0:T(8,128)(2,1)S(1)} collective-permute-done((bf16[2,2,3,32,512]{4,3,2,1,0:T(8,128)(2,1)S(1)}, bf16[2,2,3,32,512]{4,3,2,1,0:T(8,128)(2,1)S(1)}, u32[]{:S(2)}, u32[]{:S(2)}) %collective-permute-start.66) | collective-permute-done | bytes 393248 | tf_op jit(solution)/shard_map/ppermute | solution.py:44
  (307 shorter events, 165.5 us)
Async XLA Ops:
  7.2 183.6 %all-gather.5.cloned.1.call-start = ((), (), s32[]{:S(2)}) async-start(), calls=%async_computation.3 | async-start | bytes 3932160 | tf_op jit(solution)/shard_map/all_gather | solution.py:707
  45.3 196.7 %all-gather.3.cloned.1.call-start = ((), (), s32[]{:S(2)}) async-start(), calls=%async_computation.2 | async-start | bytes 3932160 | tf_op jit(solution)/shard_map/all_gather | solution.py:707
  82.8 34.3 %collective-permute-start.22 = (bf16[512,1024]{1,0:T(8,128)(2,1)S(1)}, bf16[512,1024]{1,0:T(8,128)(2,1)}, u32[]{:S(2)}, u32[]{:S(2)}) collective-permute-start(bf16[512,1024]{1,0:T(8,128)(2,1)S(1)} %copy-done.15), channel_id=1, source_target_pairs={{0,2},{1,3},{2,0},{3,1},{4,6},{5,7},{6,4},{7,5},{8,10},{9,11},{10,... | collective-permute-start | bytes 3145736 | tf_op jit(solution)/shard_map/ppermute | solution.py:44
  87.9 369.8 %reduce-scatter.3.cloned.1.call-start = ((), (), s32[]{:S(2)}) async-start(), calls=%async_computation.4 | async-start | bytes 3932160 | tf_op jit(solution)/shard_map/reduce_scatter | solution.py:762
  116.6 30.5 %collective-permute-start.12 = (bf16[512,1152]{1,0:T(8,128)(2,1)}, bf16[512,1152]{1,0:T(8,128)(2,1)S(1)}, u32[]{:S(2)}, u32[]{:S(2)}) collective-permute-start(bf16[512,1152]{1,0:T(8,128)(2,1)} %get-tuple-element.82.refs_0_.packet_ref), channel_id=1, source_target_pairs={{0,1},{1,0},{2,3},{3,2},{4,5},{5,4},{6,7},{7,6},{8,9},{9,8},{10,11... | collective-permute-start | bytes 3538952 | tf_op jit(solution)/shard_map/ppermute | solution.py:44
  117.1 50.4 %collective-permute-start.19 = (bf16[512,1152]{1,0:T(8,128)(2,1)}, bf16[512,1152]{1,0:T(8,128)(2,1)}, u32[]{:S(2)}, u32[]{:S(2)}) collective-permute-start(bf16[512,1152]{1,0:T(8,128)(2,1)} %get-tuple-element.82.refs_0_.packet_ref), channel_id=1, source_target_pairs={{0,4},{1,5},{2,6},{3,7},{4,0},{5,1},{6,2},{7,3},{8,12},{9,13},{10,... | collective-permute-start | bytes 3538952 | tf_op jit(solution)/shard_map/ppermute | solution.py:44
  142.2 36.4 %collective-permute-start.30 = (bf16[256,1024]{1,0:T(8,128)(2,1)S(1)}, bf16[256,1024]{1,0:T(8,128)(2,1)S(1)}, u32[]{:S(2)}, u32[]{:S(2)}) collective-permute-start(bf16[256,1024]{1,0:T(8,128)(2,1)S(1)} %slice.312), channel_id=1, source_target_pairs={{0,4},{1,5},{2,6},{3,7},{4,0},{5,1},{6,2},{7,3},{8,12},{9,13},{10,... | collective-permute-start | bytes 1572872 | tf_op jit(solution)/shard_map/ppermute | solution.py:44
  143.8 34.8 %collective-permute-start.31 = (bf16[256,1024]{1,0:T(8,128)(2,1)S(1)}, bf16[256,1024]{1,0:T(8,128)(2,1)S(1)}, u32[]{:S(2)}, u32[]{:S(2)}) collective-permute-start(bf16[256,1024]{1,0:T(8,128)(2,1)S(1)} %slice.313), channel_id=1, source_target_pairs={{0,2},{1,3},{2,0},{3,1},{4,6},{5,7},{6,4},{7,5},{8,10},{9,11},{10,... | collective-permute-start | bytes 1572872 | tf_op jit(solution)/shard_map/ppermute | solution.py:44
  145.6 44.7 %collective-permute-start.26 = (bf16[256,1152]{1,0:T(8,128)(2,1)S(1)}, bf16[256,1152]{1,0:T(8,128)(2,1)}, u32[]{:S(2)}, u32[]{:S(2)}) collective-permute-start(bf16[256,1152]{1,0:T(8,128)(2,1)S(1)} %slice.310), channel_id=1, source_target_pairs={{0,4},{1,5},{2,6},{3,7},{4,0},{5,1},{6,2},{7,3},{8,12},{9,13},{10,... | collective-permute-start | bytes 1769480 | tf_op jit(solution)/shard_map/ppermute | solution.py:44
  147.1 62.7 %collective-permute-start.20 = (bf16[512,1152]{1,0:T(8,128)(2,1)}, bf16[512,1152]{1,0:T(8,128)(2,1)S(1)}, u32[]{:S(2)}, u32[]{:S(2)}) collective-permute-start(bf16[512,1152]{1,0:T(8,128)(2,1)} %collective-permute-done.18.refs_0_), channel_id=1, source_target_pairs={{0,1},{1,0},{2,3},{3,2},{4,5},{5,4},{6,7},{7,6},{8,9},{9,8},{10,11... | collective-permute-start | bytes 3538952 | tf_op jit(solution)/shard_map/ppermute | solution.py:44
  167.4 42.8 %collective-permute-start.21 = (bf16[512,1152]{1,0:T(8,128)(2,1)}, bf16[512,1152]{1,0:T(8,128)(2,1)}, u32[]{:S(2)}, u32[]{:S(2)}) collective-permute-start(bf16[512,1152]{1,0:T(8,128)(2,1)} %collective-permute-done.19.refs_1_), channel_id=1, source_target_pairs={{0,1},{1,0},{2,3},{3,2},{4,5},{5,4},{6,7},{7,6},{8,9},{9,8},{10,11... | collective-permute-start | bytes 3538952 | tf_op jit(solution)/shard_map/ppermute | solution.py:44
  178.6 30.6 %collective-permute-start.24 = (bf16[512,1024]{1,0:T(8,128)(2,1)}, bf16[512,1024]{1,0:T(8,128)(2,1)}, u32[]{:S(2)}, u32[]{:S(2)}) collective-permute-start(bf16[512,1024]{1,0:T(8,128)(2,1)} %collective-permute-done.22.refs_4_), channel_id=1, source_target_pairs={{0,1},{1,0},{2,3},{3,2},{4,5},{5,4},{6,7},{7,6},{8,9},{9,8},{10,11... | collective-permute-start | bytes 3145736 | tf_op jit(solution)/shard_map/ppermute | solution.py:44
  180.2 29.5 %collective-permute-start.25 = (bf16[512,1024]{1,0:T(8,128)(2,1)}, bf16[512,1024]{1,0:T(8,128)(2,1)}, u32[]{:S(2)}, u32[]{:S(2)}) collective-permute-start(bf16[512,1024]{1,0:T(8,128)(2,1)} %collective-permute-done.23.refs_5_), channel_id=1, source_target_pairs={{0,1},{1,0},{2,3},{3,2},{4,5},{5,4},{6,7},{7,6},{8,9},{9,8},{10,11... | collective-permute-start | bytes 3145736 | tf_op jit(solution)/shard_map/ppermute | solution.py:44
  209.1 32.9 %collective-permute-start.32 = (bf16[256,1024]{1,0:T(8,128)(2,1)}, bf16[256,1024]{1,0:T(8,128)(2,1)}, u32[]{:S(2)}, u32[]{:S(2)}) collective-permute-start(bf16[256,1024]{1,0:T(8,128)(2,1)} %copy-done.24), channel_id=1, source_target_pairs={{0,1},{1,0},{2,3},{3,2},{4,5},{5,4},{6,7},{7,6},{8,9},{9,8},{10,11... | collective-permute-start | bytes 1572872 | tf_op jit(solution)/shard_map/ppermute | solution.py:44
  209.2 32.8 %collective-permute-start.33 = (bf16[256,1024]{1,0:T(8,128)(2,1)}, bf16[256,1024]{1,0:T(8,128)(2,1)}, u32[]{:S(2)}, u32[]{:S(2)}) collective-permute-start(bf16[256,1024]{1,0:T(8,128)(2,1)} %copy-done.25), channel_id=1, source_target_pairs={{0,1},{1,0},{2,3},{3,2},{4,5},{5,4},{6,7},{7,6},{8,9},{9,8},{10,11... | collective-permute-start | bytes 1572872 | tf_op jit(solution)/shard_map/ppermute | solution.py:44
  209.7 32.3 %collective-permute-start.28 = (bf16[256,1152]{1,0:T(8,128)(2,1)}, bf16[256,1152]{1,0:T(8,128)(2,1)S(1)}, u32[]{:S(2)}, u32[]{:S(2)}) collective-permute-start(bf16[256,1152]{1,0:T(8,128)(2,1)} %collective-permute-done.26.refs_0_), channel_id=1, source_target_pairs={{0,1},{1,0},{2,3},{3,2},{4,5},{5,4},{6,7},{7,6},{8,9},{9,8},{10,11... | collective-permute-start | bytes 1769480 | tf_op jit(solution)/shard_map/ppermute | solution.py:44
  209.8 32.3 %collective-permute-start.29 = (bf16[256,1152]{1,0:T(8,128)(2,1)}, bf16[256,1152]{1,0:T(8,128)(2,1)}, u32[]{:S(2)}, u32[]{:S(2)}) collective-permute-start(bf16[256,1152]{1,0:T(8,128)(2,1)} %collective-permute-done.27.refs_1_), channel_id=1, source_target_pairs={{0,1},{1,0},{2,3},{3,2},{4,5},{5,4},{6,7},{7,6},{8,9},{9,8},{10,11... | collective-permute-start | bytes 1769480 | tf_op jit(solution)/shard_map/ppermute | solution.py:44
  314.6 184.2 %reduce-scatter.5.cloned.1.call-start = ((), (), s32[]{:S(2)}) async-start(), calls=%async_computation.5 | async-start | bytes 3932160 | tf_op jit(solution)/shard_map/reduce_scatter | solution.py:762
  316.8 38.2 %collective-permute-start.40 = (bf16[2,512,1024]{2,1,0:T(8,128)(2,1)}, bf16[2,512,1024]{2,1,0:T(8,128)(2,1)}, u32[]{:S(2)}, u32[]{:S(2)}) collective-permute-start(bf16[2,512,1024]{2,1,0:T(8,128)(2,1)} %get-tuple-element.115), channel_id=1, source_target_pairs={{0,1},{1,0},{2,3},{3,2},{4,5},{5,4},{6,7},{7,6},{8,9},{9,8},{10,11... | collective-permute-start | bytes 6291464 | tf_op jit(solution)/shard_map/ppermute | solution.py:44
  316.8 41.9 %collective-permute-start.42 = (bf16[256,1024]{1,0:T(8,128)(2,1)}, bf16[256,1024]{1,0:T(8,128)(2,1)}, u32[]{:S(2)}, u32[]{:S(2)}) collective-permute-start(bf16[256,1024]{1,0:T(8,128)(2,1)} %get-tuple-element.117), channel_id=1, source_target_pairs={{0,2},{1,3},{2,0},{3,1},{4,6},{5,7},{6,4},{7,5},{8,10},{9,11},{10,... | collective-permute-start | bytes 1572872 | tf_op jit(solution)/shard_map/ppermute | solution.py:44
  319.1 42.0 %collective-permute-start.41 = (bf16[256,1024]{1,0:T(8,128)(2,1)}, bf16[256,1024]{1,0:T(8,128)(2,1)}, u32[]{:S(2)}, u32[]{:S(2)}) collective-permute-start(bf16[256,1024]{1,0:T(8,128)(2,1)} %get-tuple-element.116), channel_id=1, source_target_pairs={{0,4},{1,5},{2,6},{3,7},{4,0},{5,1},{6,2},{7,3},{8,12},{9,13},{10,... | collective-permute-start | bytes 1572872 | tf_op jit(solution)/shard_map/ppermute | solution.py:44
  363.3 57.5 %collective-permute-start.39 = (bf16[1,512,1024]{2,1,0:T(8,128)(2,1)}, bf16[1,512,1024]{2,1,0:T(8,128)(2,1)}, u32[]{:S(2)}, u32[]{:S(2)}) collective-permute-start(bf16[1,512,1024]{2,1,0:T(8,128)(2,1)} %get-tuple-element.113), channel_id=1, source_target_pairs={{0,1},{1,0},{2,3},{3,2},{4,5},{5,4},{6,7},{7,6},{8,9},{9,8},{10,11... | collective-permute-start | bytes 3145736 | tf_op jit(solution)/shard_map/ppermute | solution.py:44
  384.4 36.5 %collective-permute-start.46 = (bf16[512,1024]{1,0:T(8,128)(2,1)}, bf16[512,1024]{1,0:T(8,128)(2,1)}, u32[]{:S(2)}, u32[]{:S(2)}) collective-permute-start(bf16[512,1024]{1,0:T(8,128)(2,1)} %pad_maximum_fusion.4), channel_id=1, source_target_pairs={{0,2},{1,3},{2,0},{3,1},{4,6},{5,7},{6,4},{7,5},{8,10},{9,11},{10,... | collective-permute-start | bytes 3145736 | tf_op jit(solution)/shard_map/ppermute | solution.py:44
  385.5 35.3 %collective-permute-start.47 = (bf16[512,1024]{1,0:T(8,128)(2,1)}, bf16[512,1024]{1,0:T(8,128)(2,1)}, u32[]{:S(2)}, u32[]{:S(2)}) collective-permute-start(bf16[512,1024]{1,0:T(8,128)(2,1)} %pad_maximum_fusion.5), channel_id=1, source_target_pairs={{0,4},{1,5},{2,6},{3,7},{4,0},{5,1},{6,2},{7,3},{8,12},{9,13},{10,... | collective-permute-start | bytes 3145736 | tf_op jit(solution)/shard_map/ppermute | solution.py:44
  (74 other events, 851.8 us)
Sparse Core Ops, SparseCore 0:
  45.5 63.7 all-gather.4
  110.8 62.1 all-gather.2
  314.8 60.4 reduce-scatter.2
  399.7 60.8 reduce-scatter.4

commit v6 on v5

--- a/solution.py
+++ b/solution.py
@@ -58,42 +58,50 @@
         return total
 
     def chips_gather(self, block):
-        near, far = self.swap(block, 2), self.swap(block, 4)
-        return {0: (block,), 2: (near,), 4: (far,), 6: self.cross_of(near, far)}
+        half = block.shape[0] // 2
+        top, low = block[:half], block[half:]
+        near_top, far_low = self.swap(top, 2), self.swap(low, 4)
+        near_low, far_top = self.swap(low, 2), self.swap(top, 4)
+        cross_top, cross_low = self.swap(near_top, 4), self.swap(far_low, 2)
+        return {0: (top, low), 2: (near_top, near_low), 4: (far_top, far_low), 6: (cross_top, cross_low)}
 
     def cross_of(self, near, far):
         half = near.shape[0] // 2
         return self.swap(near[:half], 4), self.swap(far[half:], 2)
 
-    def send_cross(self, own, other):
-        half = own.shape[0] // 2
-        top = (own[:half].astype(f32) + other[:half].astype(f32)).astype(bf16)
-        low = (own[half:].astype(f32) + other[half:].astype(f32)).astype(bf16)
-        return top, low
-
-    def send_sides(self, near, far, cross):
-        half = near[0].shape[0] // 2
+    def send_cross(self, block):
+        half = block.shape[0] // 2
+        return self.swap(block[:half], 2), self.swap(block[half:], 4)
+
+    def add_cross(self, near, far, cross):
+        half = near.shape[0] // 2
         cross_top, cross_low = cross
-        near_sum = near[0].astype(f32) + near[1].astype(f32)
-        far_sum = far[0].astype(f32) + far[1].astype(f32)
-        near_all = jnp.concatenate([near_sum[:half], near_sum[half:] + cross_low.astype(f32)], axis=0)
-        far_all = jnp.concatenate([far_sum[:half] + cross_top.astype(f32), far_sum[half:]], axis=0)
-        return near_all.astype(bf16), far_all.astype(bf16)
-
-    def send_parts(self, parts):
+        near_low = (near[half:].astype(f32) + cross_low.astype(f32)).astype(bf16)
+        far_top = (far[:half].astype(f32) + cross_top.astype(f32)).astype(bf16)
+        return (
+            jnp.concatenate([near[:half], near_low], axis=0),
+            jnp.concatenate([far_top, far[half:]], axis=0),
+        )
+
+    def chip_parts(self, parts):
         chips = parts.reshape((MEMBERS // 2, 2) + parts.shape[1:])
-        chip, core = self.member // 2, self.member % 2
-        arrived = jnp.zeros_like(chips)
+        chip = self.member // 2
+        found = []
         for bits in range(MEMBERS // 2):
             part = lax.dynamic_index_in_dim(chips, chip ^ bits, 0, keepdims=False)
-            if bits:
-                part = self.swap(part, 2 * bits)
+            found.append(self.swap(part, 2 * bits) if bits else part)
+        return found
+
+    def keep_parts(self, found):
+        chip, core = self.member // 2, self.member % 2
+        arrived = jnp.zeros((MEMBERS // 2,) + found[0].shape, found[0].dtype)
+        for bits, part in enumerate(found):
             arrived = lax.dynamic_update_index_in_dim(arrived, part, chip ^ bits, 0)
         kept = lax.dynamic_index_in_dim(arrived, core, 1, keepdims=False)
         other = self.swap(lax.dynamic_index_in_dim(arrived, 1 - core, 1, keepdims=False), 1)
         even = jnp.where(core == 0, kept, other)
         odd = jnp.where(core == 0, other, kept)
-        return jnp.stack([even, odd], axis=1).reshape(parts.shape)
+        return jnp.stack([even, odd], axis=1).reshape((MEMBERS,) + found[0].shape[1:])
 
 
 def dot(left, right):
@@ -104,24 +112,23 @@
     return lax.dot_general(left, right, (((1,), (1,)), ((), ())), preferred_element_type=f32)
 
 
-def expert_kernel(first_ref, *refs, layout, experts, fresh, last, carried):
+def expert_kernel(names_ref, *refs, layout, fresh, last, carried):
     refs = list(refs)
+    experts = range(names_ref.shape[0])
     packet_parts = [[refs.pop(0) for _ in range(number)] for number in layout]
     cotangent_parts = [[refs.pop(0) for _ in range(number)] for number in layout]
     weight_parts = [refs.pop(0) for _ in experts]
-    prior_refs = [None if new else refs.pop(0) for new in fresh]
-    carried_out = (refs.pop(0), refs.pop(0)) if carried else None
-    carried_back = (refs.pop(0), refs.pop(0)) if carried else None
-    out_refs, back_refs = (refs.pop(0), refs.pop(0)), (refs.pop(0), refs.pop(0))
+    prior_refs = [None if fresh else refs.pop(0) for _ in experts]
+    carried_out, carried_back = (refs.pop(0), refs.pop(0)) if carried else (None, None)
+    out_ref, back_ref = refs.pop(0), refs.pop(0)
     result_refs = [refs.pop(0) for _ in experts]
-    grad_refs = [refs.pop(0) if end else result for end, result in zip(last, result_refs)]
+    grad_refs = [refs.pop(0) for _ in experts] if last else result_refs
     packet_buffer, cotangent_buffer, weight_ref, packet_turned, cotangent_turned, sums = refs[:6]
     block_sem, weight_sem, prior_sem = refs[6:]
     rows, width = cotangent_buffer.shape[1:]
     groups, _, depth, _ = weight_parts[0].shape
     blocks = len(layout)
     at = pl.program_id(0)
-    first = first_ref[0]
 
     def block_copies(block):
         copies = []
@@ -151,18 +158,18 @@
     def _():
         for copy in block_copies(0):
             copy.start()
-        for n in range(len(experts)):
+        for n in experts:
             for copy in weight_copies(n):
                 copy.start()
-        for n, new in enumerate(fresh):
-            if new:
+        for n in experts:
+            if fresh:
                 grad_refs[n][...] = jnp.zeros_like(grad_refs[n])
             else:
                 prior_copy(n).start()
         for block in range(1, blocks):
             for copy in block_copies(block):
                 copy.start()
-        for n in range(len(experts)):
+        for n in experts:
             for copy in weight_copies(n):
                 copy.wait()
 
@@ -181,7 +188,7 @@
     packet_turned[...] = normed.T
     cotangent_turned[...] = upstream.T
     begun = []
-    for n in range(len(experts)):
+    for n in experts:
         begun.append(
             (
                 dot(normed, weight_ref[n, 0]),
@@ -189,17 +196,16 @@
                 dot(upstream, weight_ref[n, 2]),
             )
         )
-    if not all(fresh):
+    if not fresh:
 
         @pl.when(at == 0)
         def _():
-            for n, new in enumerate(fresh):
-                if not new:
-                    prior_copy(n).wait()
-
-    for n, local in enumerate(experts):
+            for n in experts:
+                prior_copy(n).wait()
+
+    for n in experts:
         gate_pre, up_pre, inner_raw = begun[n]
-        expert = first + local
+        expert = names_ref[n]
         is_high, is_low = lane == expert, lane == expert + EXPERTS
         share = jnp.sum(jnp.where(is_high | is_low, shares, 0.0), axis=1, keepdims=True)
         sigmoid_gate = jax.nn.sigmoid(gate_pre)
@@ -225,47 +231,36 @@
         grad_refs[n][2] += dot(cotangent_turned[...], inner_shared)
         high = share_grad.astype(bf16).astype(f32)
         extra = extra + jnp.where(is_high, high, 0.0) + jnp.where(is_low, share_grad - high, 0.0)
-    for side in range(2):
-
-        @pl.when((at < blocks // 2) == (side == 0))
-        def _():
-            out_total, back_total, extra_total = sums[0], sums[1], extra
-            if carried:
-                out_total = out_total + carried_out[side][0].astype(f32)
-                back_total = back_total + carried_back[side][0, :, :width].astype(f32)
-                extra_total = extra_total + carried_back[side][0, :, width:].astype(f32)
-            out_refs[side][0] = out_total.astype(bf16)
-            back_refs[side][0, :, :width] = back_total.astype(bf16)
-            back_refs[side][0, :, width:] = extra_total.astype(bf16)
-
-    if any(last):
+    out_total, back_total = sums[0], sums[1]
+    if carried:
+        out_total = out_total + carried_out[0].astype(f32)
+        back_total = back_total + carried_back[0, :, :width].astype(f32)
+        extra = extra + carried_back[0, :, width:].astype(f32)
+    out_ref[0] = out_total.astype(bf16)
+    back_ref[0, :, :width] = back_total.astype(bf16)
+    back_ref[0, :, width:] = extra.astype(bf16)
+
+    if last:
 
         @pl.when(at == blocks - 1)
         def _():
-            for n, end in enumerate(last):
-                if end:
-                    for g in range(groups):
-                        result_refs[n][g] = grad_refs[n][:, pl.ds(g * depth, depth)].astype(bf16)
-
-
-def run_experts(first, packets, cotangents, experts, weights, priors, last, carried=None):
+            for n in experts:
+                for g in range(groups):
+                    result_refs[n][g] = grad_refs[n][:, pl.ds(g * depth, depth)].astype(bf16)
+
+
+def run_experts(names, packets, cotangents, weights, priors=None, last=False, carried=None):
     layout = tuple(len(parts) for parts in packets)
     blocks = len(layout)
     rows = sum(part.shape[0] for part in packets[0])
     wide, width = packets[0][0].shape[1], cotangents[0][0].shape[1]
     groups, _, depth, hidden = weights[0].shape
     grad_shape = (3, width, hidden)
-    fresh = tuple(prior is None for prior in priors)
+    fresh = priors is None
+    count = len(weights)
     operands = [part for parts in packets for part in parts]
     operands += [part for parts in cotangents for part in parts]
-    operands += list(weights) + [prior for prior in priors if prior is not None]
-    half = blocks // 2
-
-    def own_side(i, s):
-        return (jnp.minimum(i, half - 1), 0, 0)
-
-    def other_side(i, s):
-        return (jnp.maximum(i - half, 0), 0, 0)
+    operands += list(weights) + list(priors or ())
 
     def whole(shape):
         return pl.BlockSpec(
@@ -273,31 +268,28 @@
         )
 
     term_specs = [
-        pl.BlockSpec((1, rows, columns), side)
-        for columns in (width, wide)
-        for side in (own_side, other_side)
+        pl.BlockSpec((1, rows, columns), lambda i, s: (i, 0, 0)) for columns in (width, wide)
     ]
     in_specs = [pl.BlockSpec(memory_space=pl.ANY)] * len(operands)
     if carried is not None:
         in_specs += term_specs
         operands += list(carried)
-    grads = [((groups, 3, depth, hidden), bf16) if end else (grad_shape, f32) for end in last]
-    scratch = [pltpu.VMEM(grad_shape, f32) for end in last if end]
+    grads = [((groups, 3, depth, hidden), bf16) if last else (grad_shape, f32)] * count
+    scratch = [pltpu.VMEM(grad_shape, f32)] * (count if last else 0)
     scratch += [
         pltpu.VMEM((blocks, rows, wide), bf16),
         pltpu.VMEM((blocks, rows, width), bf16),
-        pltpu.VMEM((len(experts),) + grad_shape, bf16),
+        pltpu.VMEM((count,) + grad_shape, bf16),
         pltpu.VMEM((width, rows), bf16),
         pltpu.VMEM((width, rows), bf16),
         pltpu.VMEM((2, rows, width), f32),
         pltpu.SemaphoreType.DMA((blocks, 4)),
-        pltpu.SemaphoreType.DMA((len(experts), groups)),
-        pltpu.SemaphoreType.DMA((len(experts),)),
+        pltpu.SemaphoreType.DMA((count, groups)),
+        pltpu.SemaphoreType.DMA((count,)),
     ]
     return pl.pallas_call(
         functools.partial(
-            expert_kernel, layout=layout, experts=experts, fresh=fresh, last=last,
-            carried=carried is not None,
+            expert_kernel, layout=layout, fresh=fresh, last=last, carried=carried is not None
         ),
         grid_spec=pltpu.PrefetchScalarGridSpec(
             num_scalar_prefetch=1,
@@ -307,18 +299,17 @@
             scratch_shapes=scratch,
         ),
         out_shape=[
-            jax.ShapeDtypeStruct((half, rows, columns), bf16)
-            for columns in (width, width, wide, wide)
+            jax.ShapeDtypeStruct((blocks, rows, columns), bf16) for columns in (width, wide)
         ]
         + [jax.ShapeDtypeStruct(shape, dtype) for shape, dtype in grads],
         compiler_params=pltpu.CompilerParams(vmem_limit_bytes=62 * 1024 * 1024),
         cost_estimate=pl.CostEstimate(
-            flops=blocks * len(experts) * 9 * 2 * rows * width * hidden,
-            bytes_accessed=blocks * rows * width * 8 + 18 * len(experts) * width * hidden,
-            transcendentals=blocks * len(experts) * rows * hidden,
+            flops=blocks * count * 9 * 2 * rows * width * hidden,
+            bytes_accessed=blocks * rows * width * 8 + 18 * count * width * hidden,
+            transcendentals=blocks * count * rows * hidden,
         ),
         name="experts",
-    )(first, *operands)
+    )(names, *operands)
 
 
 TILE = 256
@@ -354,15 +345,14 @@
     return block[:, index * HEAD_DIM : (index + 1) * HEAD_DIM]
 
 
-def forward_kernel(
-    length_ref, tokens_ref, routes_ref, cosine_ref, sine_ref, gains_ref, weight_ref,
-    packet_ref, middle_ref, rotated_ref, mixed_ref, log_ref, share_ref, normed_ref,
+def attention_kernel(
+    length_ref, tokens_ref, cosine_ref, sine_ref, gains_ref, weight_ref,
+    rotated_ref, mixed_ref, log_ref, normed_ref,
 ):
-    rows, width = tokens_ref.shape
+    rows = tokens_ref.shape[0]
     head_columns, kv_columns = HEADS * HEAD_DIM, KV_HEADS * HEAD_DIM
     at_value = head_columns + kv_columns
     at_output = at_value + kv_columns
-    at_extra = at_output + head_columns
     length = length_ref[0]
     group = HEADS // KV_HEADS
 
@@ -412,9 +402,16 @@
 
     lax.fori_loop(0, KV_HEADS // 2, attend, 0)
 
+
+def router_kernel(
+    tokens_ref, routes_ref, gains_ref, mixed_ref, output_ref, extra_ref,
+    packet_ref, middle_ref, share_ref,
+):
+    width = tokens_ref.shape[1]
+
     def mix(c, carry):
         where = columns_at(c, TILE)
-        branch = dot_turned(mixed_ref[...], weight_ref[where, at_output:at_extra])
+        branch = dot_turned(mixed_ref[...], output_ref[where, :])
         middle_ref[:, where] = tokens_ref[:, where].astype(f32) + residual_scale * branch
         return carry
 
@@ -422,7 +419,7 @@
     middle = middle_ref[...]
     normed_two = (middle * row_scale_of(middle) * gains_ref[1:2, :]).astype(bf16)
     packet_ref[:, :width] = normed_two
-    logits = dot(normed_two, weight_ref[:, at_extra:])
+    logits = dot(normed_two, extra_ref[...])
     lane = lax.broadcasted_iota(jnp.int32, logits.shape, 1)
     routed = lane == routes_ref[:, 0:1]
     for k in range(1, routes_ref.shape[1]):
@@ -440,13 +437,11 @@
 
 
 def middle_kernel(
-    own_ref, other_ref, near_ref, far_ref, packet_ref, middle_ref, cotangent_ref, share_ref, gains_ref, mixed_ref, output_ref, extra_ref,
+    own_ref, near_ref, far_ref, packet_ref, middle_ref, cotangent_ref, share_ref, gains_ref, mixed_ref, output_ref, extra_ref,
     middle_grad_ref, mixed_grad_ref, pack_ref, back_ref, branch_ref, turned_ref,
 ):
     width = cotangent_ref.shape[1]
-    back_ref[...] = (own_ref[...].astype(f32) + other_ref[...].astype(f32)) + (
-        near_ref[...].astype(f32) + far_ref[...].astype(f32)
-    )
+    back_ref[...] = own_ref[...].astype(f32) + near_ref[...].astype(f32) + far_ref[...].astype(f32)
     shares = share_ref[...]
     share_grad = back_ref[:, width:]
     share_grad = share_grad + pltpu.roll(share_grad, EXTRA - EXPERTS, 1)
@@ -604,39 +599,56 @@
     return jnp.tile(cosine_table, (1, repeats)), jnp.tile(signed, (1, repeats))
 
 
-def attention_forward(tokens, lengths, routes, tables, gains, whole):
+def attention_forward(tokens, lengths, tables, gains, whole):
     rows, width = tokens.shape
     head_columns, kv_columns = HEADS * HEAD_DIM, KV_HEADS * HEAD_DIM
+    projections = head_columns + 2 * kv_columns
     return call_kernel(
-        forward_kernel,
+        attention_kernel,
         "attention_forward",
         [
-            (lengths, "scalar", None), (tokens, None, None), (routes, None, None),
-            (tables[0], None, None), (tables[1], None, None), (gains, None, None),
-            (whole, None, None),
+            (lengths, "scalar", None), (tokens, None, None), (tables[0], None, None),
+            (tables[1], None, None), (gains, None, None), (whole, (width, projections), (0, 0)),
         ],
         [
-            ((rows, width + EXTRA), bf16), ((rows, width), f32),
-            ((rows, head_columns + 2 * kv_columns), bf16), ((rows, head_columns), bf16),
-            ((KV_HEADS // 2, 2 * HEADS // KV_HEADS, rows), f32), ((rows, EXTRA), f32),
+            ((rows, projections), bf16), ((rows, head_columns), bf16),
+            ((KV_HEADS // 2, 2 * HEADS // KV_HEADS, rows), f32),
         ],
         [((rows, width), bf16)],
         8 * rows * width * head_columns,
     )
 
 
+def output_blocks(whole):
+    width = whole.shape[0]
+    head_columns, kv_columns = HEADS * HEAD_DIM, KV_HEADS * HEAD_DIM
+    at_output = head_columns + 2 * kv_columns
+    return [
+        (whole, (width, head_columns), (0, at_output // head_columns)),
+        (whole, (width, EXTRA), (0, (at_output + head_columns) // EXTRA)),
+    ]
+
+
+def router_forward(tokens, routes, gains, mixed, whole):
+    rows, width = tokens.shape
+    return call_kernel(
+        router_kernel,
+        "router_forward",
+        [(a, None, None) for a in (tokens, routes, gains, mixed)] + output_blocks(whole),
+        [((rows, width + EXTRA), bf16), ((rows, width), f32), ((rows, EXTRA), f32)],
+        [],
+        2 * rows * width * mixed.shape[1],
+    )
+
+
 def middle_back(pieces, packet, middle, cotangent, shares, gains, mixed, whole):
     rows, width = cotangent.shape
-    head_columns, kv_columns = HEADS * HEAD_DIM, KV_HEADS * HEAD_DIM
-    at_output = head_columns + 2 * kv_columns
+    head_columns = HEADS * HEAD_DIM
     return call_kernel(
         middle_kernel,
         "middle_back",
         [(a, None, None) for a in (*pieces, packet, middle, cotangent, shares, gains, mixed)]
-        + [
-            (whole, (width, head_columns), (0, at_output // head_columns)),
-            (whole, (width, EXTRA), (0, (at_output + head_columns) // EXTRA)),
-        ],
+        + output_blocks(whole),
         [((rows, width), f32), ((rows, head_columns), bf16), ((width, head_columns + EXTRA), bf16)],
         [((rows, width + EXTRA), f32), ((rows, width), bf16), ((width, rows), bf16)],
         4 * rows * width * head_columns,
@@ -700,12 +712,7 @@
 
     mine = jnp.stack([gate_weight, up_weight, down_weight.transpose(0, 2, 1)], axis=1)
     mine = mine.reshape(MEMBERS, LOCAL_EXPERTS, 3, shard, hidden)
-    shelf = links.send_parts(mine).transpose(1, 2, 0, 3, 4)
-    shelf = shelf.reshape(LOCAL_EXPERTS, 3, MEMBERS * shard, hidden)
-    lines = [[m + MEMBERS * g for g in range(groups)] for m in range(MEMBERS)]
-    expert_full = [
-        lax.all_gather(shelf[n], "fsdp", axis_index_groups=lines) for n in range(LOCAL_EXPERTS)
-    ]
+    arrived = links.chip_parts(mine)
 
     packed = jnp.concatenate(
         [
@@ -722,8 +729,14 @@
     )
     pack_width = packed.shape[1]
     column = links.direct_gather(packed).reshape(groups * shard, pack_width)
+    arrived, column = lax.optimization_barrier((arrived, column))
     spread = links.chips_gather(column)
-    spread[0] = (column,)
+    shelf = links.keep_parts(arrived).transpose(1, 2, 0, 3, 4)
+    shelf = shelf.reshape(LOCAL_EXPERTS, 3, MEMBERS * shard, hidden)
+    lines = [[m + MEMBERS * g for g in range(groups)] for m in range(MEMBERS)]
+    own_full = [
+        lax.all_gather(shelf[n], "fsdp", axis_index_groups=lines) for n in range(LOCAL_EXPERTS)
+    ]
     whole = jnp.zeros((groups, MEMBERS, shard, pack_width), bf16)
     for k in range(MEMBERS):
         parts = spread[k & 6]
@@ -737,57 +750,55 @@
     gains = whole[:, at_extra + EXPERTS : at_extra + EXPERTS + 2].astype(f32).T
 
     late_cotangent, whole = lax.optimization_barrier((cotangent, whole))
-    cotangents = links.chips_gather(late_cotangent)
+    cot_near, cot_far = links.swap(late_cotangent, 2), links.swap(late_cotangent, 4)
 
     tables = rope_lanes(row_count)
-    packet, middle, rotated, mixed, logs, shares = attention_forward(
-        tokens, lengths, routes, tables, gains, whole
-    )
-    packets = links.chips_gather(packet)
-    def both(blocks, turn):
-        own = [blocks[k] for k in turn]
-        return own + [tuple(links.swap(part, 1) for part in parts) for parts in own]
-
-    first = (member * LOCAL_EXPERTS).astype(jnp.int32).reshape(1)
-    chip_rows = both(packets, (0,)), both(cotangents, (0,))
-    side_rows = both(packets, (2, 4)), both(cotangents, (2, 4))
-    cross_rows = both(packets, (6,)), both(cotangents, (6,))
-    *chip_terms, zero = run_experts(first, *chip_rows, (0,), expert_full[:1], [None], (False,))
-    *side_terms, zero = run_experts(first, *side_rows, (0,), expert_full[:1], [zero], (False,))
-    *cross_terms, zero, one = run_experts(
-        first, *cross_rows, (0, 1), expert_full, [zero, None], (True, False)
-    )
-
-    def reduce_groups(grads):
-        return lax.psum_scatter(grads, "fsdp", scatter_dimension=0, axis_index_groups=lines)
-
+    rotated, mixed, logs = attention_forward(tokens, lengths, tables, gains, whole)
+    cot_near, cot_far, mixed = lax.optimization_barrier((cot_near, cot_far, mixed))
+    packet, middle, shares = router_forward(tokens, routes, gains, mixed, whole)
+    near, far = links.swap(packet, 2), links.swap(packet, 4)
+    own_full[0], packet, cot_near, cot_far = lax.optimization_barrier(
+        (own_full[0], packet, cot_near, cot_far)
+    )
+    cot_cross = links.cross_of(cot_near, cot_far)
+
+    names = [
+        jnp.stack([member, member ^ 1]).astype(jnp.int32) * LOCAL_EXPERTS + n
+        for n in range(LOCAL_EXPERTS)
+    ]
+    rows_own = [(packet,)], [(cotangent,)]
+    first_full = own_full[0], links.swap(own_full[0], 1)
+    own_out, own_back, *zero = run_experts(names[0], *rows_own, first_full)
+    near, far, own_back = lax.optimization_barrier((near, far, own_back))
+    cross = links.cross_of(near, far)
+    rows_chips = [cross, (near,), (far,)], [cot_cross, (cot_near,), (cot_far,)]
+    chip_out, chip_back, *zero = run_experts(names[0], *rows_chips, first_full, zero, True)
+    own_full[1], chip_back = lax.optimization_barrier((own_full[1], chip_back))
+    second_full = own_full[1], links.swap(own_full[1], 1)
+    chip_out, chip_back, *one = run_experts(
+        names[1], *rows_chips, second_full, None, False, (chip_out, chip_back)
+    )
+
+    def join_cores(own, other):
+        return (own.astype(f32) + links.swap(other, 1).astype(f32)).astype(bf16)
+
+    def reduce_groups(total):
+        return lax.psum_scatter(total, "fsdp", scatter_dimension=0, axis_index_groups=lines)
+
+    zero = join_cores(*zero)
+    back_cross = links.send_cross(chip_back[0])
+    back_near, back_far = links.add_cross(chip_back[1], chip_back[2], back_cross)
+    zero, back_near, back_far, own_back = lax.optimization_barrier(
+        (zero, back_near, back_far, own_back)
+    )
     shelf_zero = reduce_groups(zero)
-    out_cross = links.send_cross(cross_terms[0][0], links.swap(cross_terms[1], 1)[0])
-    back_cross = links.send_cross(cross_terms[2][0], links.swap(cross_terms[3], 1)[0])
-    out_cross, back_cross, side_terms = lax.optimization_barrier((out_cross, back_cross, side_terms))
-    back_cross = links.swap(back_cross[0], 2), links.swap(back_cross[1], 4)
-    out_cross = links.swap(out_cross[0], 2), links.swap(out_cross[1], 4)
-    *side_terms, one = run_experts(
-        first, *side_rows, (1,), expert_full[1:], [one], (False,), side_terms
-    )
-    back_other = links.swap(side_terms[3], 1)
-    out_other = links.swap(side_terms[1], 1)
-    back_near, back_far = links.send_sides(
-        (side_terms[2][0], back_other[0]), (side_terms[2][1], back_other[1]), back_cross
-    )
-    back_near, back_far, chip_terms = lax.optimization_barrier((back_near, back_far, chip_terms))
     back_near, back_far = links.swap(back_near, 2), links.swap(back_far, 4)
-    *chip_terms, one = run_experts(
-        first, *chip_rows, (1,), expert_full[1:], [one], (True,), chip_terms
-    )
-    shelf_one = reduce_groups(one)
-    back_pieces = (chip_terms[2][0], links.swap(chip_terms[3], 1)[0], back_near, back_far)
-    out_near, out_far = links.send_sides(
-        (side_terms[0][0], out_other[0]), (side_terms[0][1], out_other[1]), out_cross
-    )
-    out_near, out_far, back_pieces = lax.optimization_barrier((out_near, out_far, back_pieces))
-    out_near, out_far = links.swap(out_near, 2), links.swap(out_far, 4)
-    out_pieces = chip_terms[0][0], links.swap(chip_terms[1], 1)[0], out_near, out_far
+    own_out, own_back, *one = run_experts(
+        names[1], *rows_own, second_full, one, True, (own_out, own_back)
+    )
+    one = join_cores(*one)
+    out_cross, back_near, back_far = lax.optimization_barrier((chip_out[0], back_near, back_far))
+    out_cross = links.send_cross(out_cross)
 
     core, chip = member % 2, member // 2
 
@@ -797,43 +808,54 @@
         own = lax.dynamic_index_in_dim(pack, core, 2, keepdims=False)
         other = links.swap(lax.dynamic_index_in_dim(pack, 1 - core, 2, keepdims=False), 1)
 
-        def part(bits):
-            return tuple(
-                lax.dynamic_index_in_dim(side, chip ^ bits, 1, keepdims=False).reshape(
-                    groups * shard, columns
-                )
-                for side in (own, other)
+        joined = own.astype(f32) + other.astype(f32)
+        return [
+            lax.dynamic_index_in_dim(joined, chip ^ bits, 1, keepdims=False).reshape(
+                groups * shard, columns
             )
-
-        return [part(bits) for bits in range(MEMBERS // 2)]
+            for bits in range(MEMBERS // 2)
+        ]
 
     def pack_cross(parts):
-        top, low = links.send_cross(*parts[3])
-        return links.swap(top, 2), links.swap(low, 4)
-
-    def pack_sides(parts, cross):
-        near, far = links.send_sides(parts[1], parts[2], cross)
+        return links.send_cross(parts[3].astype(bf16))
+
+    def pack_add(parts, cross):
+        return links.add_cross(parts[1].astype(bf16), parts[2].astype(bf16), cross)
+
+    def pack_end(parts, near, far):
         near, far = links.swap(near, 2), links.swap(far, 4)
-        total = (parts[0][0].astype(f32) + parts[0][1].astype(f32)) + (
-            near.astype(f32) + far.astype(f32)
-        )
+        total = parts[0] + near.astype(f32) + far.astype(f32)
         return links.direct_reduce(total.reshape(groups, shard, total.shape[1]))
 
     middle_grad, mixed_grad, first_pack = middle_back(
-        back_pieces, packet, middle, cotangent, shares, gains, mixed, whole
-    )
+        (own_back[0], back_near, back_far), packet, middle, cotangent, shares, gains, mixed, whole
+    )
+    out_near, out_far = links.add_cross(chip_out[1], chip_out[2], out_cross)
+    out_near, out_far, one, mixed_grad = lax.optimization_barrier(
+        (out_near, out_far, one, mixed_grad)
+    )
+    shelf_one = reduce_groups(one)
+    out_near, out_far = links.swap(out_near, 2), links.swap(out_far, 4)
     first_parts = pack_cores(first_pack)
     projected_grad = attention_back(lengths, rotated, mixed_grad, logs, tables)
-    first_parts, projected_grad = lax.optimization_barrier((first_parts, projected_grad))
+    out_near, first_parts, projected_grad = lax.optimization_barrier(
+        (out_near, first_parts, projected_grad)
+    )
     first_cross = pack_cross(first_parts)
     grad_tokens, second_pack = inputs_back(tokens, gains, projected_grad, whole, middle_grad)
+    first_near, first_far = pack_add(first_parts, first_cross)
+    first_near, first_far, second_pack = lax.optimization_barrier(
+        (first_near, first_far, second_pack)
+    )
     second_parts = pack_cores(second_pack)
-    first_total = pack_sides(first_parts, first_cross)
-    second_total = pack_sides(second_parts, pack_cross(second_parts))
+    first_total = pack_end(first_parts, first_near, first_far)
+    second_near, second_far = pack_add(second_parts, pack_cross(second_parts))
+    second_total = pack_end(second_parts, second_near, second_far)
+    out_pieces = (own_out[0], out_near, out_far)
     layer_out = (middle + sum(piece.astype(f32) for piece in out_pieces)).astype(bf16)
     shelf_grad = jnp.stack([shelf_zero, shelf_one])
     shelf_grad = shelf_grad.reshape(LOCAL_EXPERTS, 3, MEMBERS, shard, hidden)
-    expert_shards = links.send_parts(shelf_grad.transpose(2, 0, 1, 3, 4)).astype(f32)
+    expert_shards = links.keep_parts(links.chip_parts(shelf_grad.transpose(2, 0, 1, 3, 4))).astype(f32)
     expert_shards = expert_shards.reshape(EXPERTS, 3, shard, hidden)
     return (
         layer_out,

time: 538 us -> 542 us (level)
  local copies, waits for them, and re-layouts: 67 us -> 46.8 us
  waiting for transfers between devices: 162 us -> 181 us
  Pallas kernels: 205 us -> 197 us
  starting transfers between devices: 51 us -> 57.7 us
    all_gather x2, waiting for transfers between devices: 0.02 us -> 17.1 us  [local(): lax.all_gather(shelf[n], 'fsdp', axis_index_groups=lines)]
    pallas_call x5 -> x4, Pallas kernels: 135 us -> 125 us  [run_experts(): pl.pallas_call(functools.partial(expert_kernel, layout=layout, fresh=fres...]
    convert_element_type x6 -> x9, other arithmetic: 4.28 us -> 13.2 us  [the longest x2 9.28 us: join_cores(): return (own.astype(f32) + links.swap(other, 1).astype(f32)).astype(bf16)]
    ppermute x68 -> x61, starting transfers between devices: 50.6 us -> 57.2 us  [swap(): lax.ppermute(value, 'fsdp', [(i, i ^ bits) for i in range(self.count)])]
    dynamic_update_slice x8, local copies, waits for them, and re-layouts: 11.2 us -> 5.18 us  [local(): whole = lax.dynamic_update_index_in_dim(whole, part, member ^ k, 1)]
    dynamic_slice x4 -> x3, local copies, waits for them, and re-layouts: 7.02 us -> 1.51 us  [pack_cores(): lax.dynamic_index_in_dim(joined, chip ^ bits, 1, keepdims=False)]
    pallas_call x4 -> x5, Pallas kernels: 70.2 us -> 71.8 us  [call_kernel(): pl.pallas_call(body, grid=(1,), in_specs=specs, out_specs=[pl.BlockSpec(o...]
    ppermute x68 -> x61, waiting for transfers between devices: 162 us -> 162 us  [swap(): lax.ppermute(value, 'fsdp', [(i, i ^ bits) for i in range(self.count)])]
  transfers between devices with their start and end apart: 72 -> 65, of which waited for: 26 -> 30; matrix products, arithmetic and copies ran while one was open for 16% -> 12% of each run, Pallas kernels for 26% -> 33%
where the time goes in v6:
time: 542 us; the launch traced here: 532 us
  Pallas kernels  197 us (36%)
  waiting for transfers between devices  181 us (33%)
  starting transfers between devices  57.7 us (11%)
  local copies, waits for them, and re-layouts  46.8 us (9%)
  other arithmetic  34.2 us (6%)
  between operations  15.7 us (3%)
    ppermute x61, waiting for transfers between devices, swap(): lax.ppermute(value, 'fsdp', [(i, i ^ bits) for i in range(self.count)])  162 us
    pallas_call x4, Pallas kernels, run_experts(): pl.pallas_call(functools.partial(expert_kernel, layout=layout, fresh=fres...  125 us
    pallas_call x5, Pallas kernels, call_kernel(): pl.pallas_call(body, grid=(1,), in_specs=specs, out_specs=[pl.BlockSpec(o...  71.8 us
    ppermute x61, starting transfers between devices, swap(): lax.ppermute(value, 'fsdp', [(i, i ^ bits) for i in range(self.count)])  57.2 us
    all_gather x2, waiting for transfers between devices, local(): lax.all_gather(shelf[n], 'fsdp', axis_index_groups=lines)  17.1 us
  transfers between devices with their start and end apart: 65, of which 30 were waited for; matrix products, arithmetic and copies ran while one was open for 12% of the time, Pallas kernels for 33%

profile of v6, /device:TPU:0, one launch (start us, length us, event | category | flops | bytes accessed | tf_op | source)
XLA Modules:
  0.0 532.3 jit_solution(7347917917557575411)
XLA Ops:
  10.5 5.1 collective-permute-start.5
  21.9 6.9 %collective-permute-done.3 = bf16[32,3200]{1,0:T(8,128)(2,1)S(1)} collective-permute-done((bf16[32,3200]{1,0:T(8,128)(2,1)S(1)}, bf16[32,3200]{1,0:T(8,128)(2,1)S(1)}, u32[]{:S(2)}, u32[]{:S(2)}) %collective-permute-start.3) | collective-permute-done | bytes 204832 | tf_op jit(solution)/shard_map/ppermute | solution.py:44
  43.8 7.3 %collective-permute-done.8 = bf16[64,3200]{1,0:T(8,128)(2,1)S(1)} collective-permute-done((bf16[64,3200]{1,0:T(8,128)(2,1)S(1)}, bf16[64,3200]{1,0:T(8,128)(2,1)S(1)}, u32[]{:S(2)}, u32[]{:S(2)}) %collective-permute-start.8) | collective-permute-done | bytes 409632 | tf_op jit(solution)/shard_map/ppermute | solution.py:44
  53.6 6.6 %collective-permute-done.13 = bf16[64,3200]{1,0:T(8,128)(2,1)S(1)} collective-permute-done((bf16[64,3200]{1,0:T(8,128)(2,1)S(1)}, bf16[64,3200]{1,0:T(8,128)(2,1)S(1)}, u32[]{:S(2)}, u32[]{:S(2)}) %collective-permute-start.13) | collective-permute-done | bytes 409632 | tf_op jit(solution)/shard_map/ppermute | solution.py:44
  86.8 20.3 %attention_forward.1 = (bf16[512,2048]{1,0:T(8,128)(2,1)}, bf16[512,1024]{1,0:T(8,128)(2,1)}, f32[4,4,512]{2,1,0:T(4,128)}) custom-call(s32[1]{0:T(128)S(6)} %copy.162.length_ref, bf16[512,1024]{1,0:T(8,128)(2,1)} %tokens_ref.5, f32[512,256]{1,0:T(8,128)} %copy.118.cosine_ref, f32[512,256]{1,0:T(8,128)} %copy.119.sine_ref, f32[2,1024]{1,0:T(2,128)} %copy.122.gains_ref, ...), custom_call_target="tpu_custom_call" | custom-call | flops 4294967296 | bytes 11837444 | tf_op jit(solution)/shard_map/attention_forward/pallas_call | solution.py:574
  107.1 6.5 %router_forward.1 = (bf16[512,1152]{1,0:T(8,128)(2,1)}, f32[512,1024]{1,0:T(8,128)}, f32[512,128]{1,0:T(8,128)}) custom-call(bf16[512,1024]{1,0:T(8,128)(2,1)} %tokens_ref.5, s32[512,8]{1,0:T(8,128)} %copy.121.routes_ref, f32[2,1024]{1,0:T(2,128)} %copy.122.gains_ref, bf16[512,1024]{1,0:T(8,128)(2,1)} %get-tuple-element.82.mixed_ref, ...), custom_call_target="tpu_custom_call" | custom-call | flops 1073741824 | bytes 18767872 | tf_op jit(solution)/shard_map/router_forward/pallas_call | solution.py:574
  113.6 17.1 %all-gather.3.cloned.1.call-done.refs_2_.refs_8_ = bf16[4,3,256,512]{3,2,1,0:T(8,128)(2,1)} async-done(((bf16[1,3,256,512]{3,2,1,0:T(8,128)(2,1)}), bf16[4,3,256,512]{3,2,1,0:T(8,128)(2,1)}) %all-gather.3.cloned.1.call-update) | async-done | bytes 3145744 | tf_op jit(solution)/shard_map/all_gather | solution.py:738
  136.7 18.7 %experts.4 = (bf16[1,512,1024]{2,1,0:T(8,128)(2,1)}, bf16[1,512,1152]{2,1,0:T(8,128)(2,1)}, f32[3,1024,512]{2,1,0:T(8,128)}, f32[3,1024,512]{2,1,0:T(8,128)}) custom-call(s32[2]{0:T(128)} %get-tuple-element.217.names_ref, bf16[512,1152]{1,0:T(8,128)(2,1)} %get-tuple-element.91.refs_0_.packet_ref, bf16[512,1024]{1,0:T(8,128)(2,1)} %cotangent_ref.1, ...), custom_call_target="tpu_custom_call" | custom-call | flops 9663676416 | bytes 23068672 | tf_op jit(solution)/shard_map/experts/pallas_call | solution.py:290
  170.3 19.6 %collective-permute-done.29.refs_5_ = bf16[256,1024]{1,0:T(8,128)(2,1)S(1)} collective-permute-done((bf16[256,1024]{1,0:T(8,128)(2,1)S(1)}, bf16[256,1024]{1,0:T(8,128)(2,1)S(1)}, u32[]{:S(2)}, u32[]{:S(2)}) %collective-permute-start.29) | collective-permute-done | bytes 524320 | tf_op jit(solution)/shard_map/ppermute | solution.py:44
  192.7 42.4 %experts.5 = (bf16[3,512,1024]{2,1,0:T(8,128)(2,1)}, bf16[3,512,1152]{2,1,0:T(8,128)(2,1)}, bf16[4,3,256,512]{3,2,1,0:T(8,128)(2,1)}, bf16[4,3,256,512]{3,2,1,0:T(8,128)(2,1)}) custom-call(s32[2]{0:T(128)} %get-tuple-element.217.names_ref, bf16[256,1152]{1,0:T(8,128)(2,1)} %copy-done.17, bf16[256,1152]{1,0:T(8,128)(2,1)} %copy-done.16, ...), custom_call_target="tpu_custom_call" | custom-call | flops 28991029248 | bytes 31457280 | tf_op jit(solution)/shard_map/experts/pallas_call | solution.py:290
  235.7 5.5 %collective-permute-done.30.refs_9_.refs_3_ = bf16[4,3,256,512]{3,2,1,0:T(8,128)(2,1)} collective-permute-done((bf16[4,3,256,512]{3,2,1,0:T(8,128)(2,1)}, bf16[4,3,256,512]{3,2,1,0:T(8,128)(2,1)}, u32[]{:S(2)}, u32[]{:S(2)}) %collective-permute-start.30) | collective-permute-done | bytes 3145760 | tf_op jit(solution)/shard_map/ppermute | solution.py:44
  241.2 42.8 %experts.6 = (bf16[3,512,1024]{2,1,0:T(8,128)(2,1)}, bf16[3,512,1152]{2,1,0:T(8,128)(2,1)}, f32[3,1024,512]{2,1,0:T(8,128)}, f32[3,1024,512]{2,1,0:T(8,128)}) custom-call(s32[2]{0:T(128)} %get-tuple-element.216.names_ref, bf16[256,1152]{1,0:T(8,128)(2,1)} %copy-done.17, bf16[256,1152]{1,0:T(8,128)(2,1)} %copy-done.16, ...), custom_call_target="tpu_custom_call" | custom-call | flops 28991029248 | bytes 31457280 | tf_op jit(solution)/shard_map/experts/pallas_call | solution.py:290
  291.7 9.6 %collective-permute-done.33 = bf16[256,1152]{1,0:T(8,128)(2,1)S(1)} collective-permute-done((bf16[256,1152]{1,0:T(8,128)(2,1)S(1)}, bf16[256,1152]{1,0:T(8,128)(2,1)S(1)}, u32[]{:S(2)}, u32[]{:S(2)}) %collective-permute-start.33) | collective-permute-done | bytes 589856 | tf_op jit(solution)/shard_map/ppermute | solution.py:44
  304.8 21.2 %experts.7 = (bf16[1,512,1024]{2,1,0:T(8,128)(2,1)}, bf16[1,512,1152]{2,1,0:T(8,128)(2,1)}, bf16[4,3,256,512]{3,2,1,0:T(8,128)(2,1)}, bf16[4,3,256,512]{3,2,1,0:T(8,128)(2,1)}) custom-call(s32[2]{0:T(128)} %get-tuple-element.216.names_ref, bf16[512,1152]{1,0:T(8,128)(2,1)} %get-tuple-element.91.refs_0_.packet_ref, bf16[512,1024]{1,0:T(8,128)(2,1)} %cotangent_ref.1, ...), custom_call_target="tpu_custom_call" | custom-call | flops 9663676416 | bytes 23068672 | tf_op jit(solution)/shard_map/experts/pallas_call | solution.py:290
  329.8 24.9 %collective-permute-done.34.near_ref = bf16[512,1152]{1,0:T(8,128)(2,1)S(1)} collective-permute-done((bf16[512,1152]{1,0:T(8,128)(2,1)}, bf16[512,1152]{1,0:T(8,128)(2,1)S(1)}, u32[]{:S(2)}, u32[]{:S(2)}) %collective-permute-start.34) | collective-permute-done | bytes 1179680 | tf_op jit(solution)/shard_map/ppermute | solution.py:44
  358.1 11.5 %middle_back.1 = (f32[512,1024]{1,0:T(8,128)}, bf16[512,1024]{1,0:T(8,128)(2,1)}, bf16[1024,1152]{1,0:T(8,128)(2,1)}) custom-call(bf16[512,1152]{1,0:T(8,128)(2,1)} %bitcast.236, bf16[512,1152]{1,0:T(8,128)(2,1)} %copy-done.8, bf16[512,1152]{1,0:T(8,128)(2,1)} %collective-permute-done.35.far_ref, bf16[512,1152]{1,0:T(8,128)(2,1)} %get-tuple-element.91.refs_0_.packet_ref, ...), custom_call_target="tpu_custom_call" | custom-call | flops 2147483648 | bytes 27795456 | tf_op jit(solution)/shard_map/middle_back/pallas_call | solution.py:574
  384.6 18.7 %attention_back.1.projected_ref = bf16[512,2048]{1,0:T(8,128)(2,1)} custom-call(s32[1]{0:T(128)S(6)} %copy.162.length_ref, bf16[512,2048]{1,0:T(8,128)(2,1)} %get-tuple-element.126.rotated_ref, bf16[512,1024]{1,0:T(8,128)(2,1)} %get-tuple-element.127.mixed_grad_ref, f32[4,4,512]{2,1,0:T(4,128)} %get-tuple-element.128.log_ref, f32[512,256]{1,0:T(8,128)} %copy.118.cosine_ref, ...), custom_call_target="tpu_custom_call" | custom-call | flops 2684354560 | bytes 6324228 | tf_op jit(solution)/shard_map/attention_back/pallas_call | solution.py:574
  403.3 5.1 collective-permute-done.39
  411.5 14.7 %inputs_back.1 = (f32[512,1024]{1,0:T(8,128)}, bf16[1024,2176]{1,0:T(8,128)(2,1)}) custom-call(bf16[512,1024]{1,0:T(8,128)(2,1)} %tokens_ref.5, f32[2,1024]{1,0:T(2,128)} %copy.122.gains_ref, bf16[512,2048]{1,0:T(8,128)(2,1)} %attention_back.1.projected_ref, bf16[1024,3200]{1,0:T(8,128)(2,1)} %bitcast.208, f32[512,1024]{1,0:T(8,128)} %get-tuple-element.132.middle_grad_ref), custom_call_target="tpu_custom_call" | custom-call | flops 4294967296 | bytes 18358272 | tf_op jit(solution)/shard_map/inputs_back/pallas_call | solution.py:574
  433.6 7.0 %collective-permute-done.52 = bf16[128,1152]{1,0:T(8,128)(2,1)S(1)} collective-permute-done((bf16[128,1152]{1,0:T(8,128)(2,1)}, bf16[128,1152]{1,0:T(8,128)(2,1)S(1)}, u32[]{:S(2)}, u32[]{:S(2)}) %collective-permute-start.52) | collective-permute-done | bytes 294944 | tf_op jit(solution)/shard_map/ppermute | solution.py:44
  445.3 18.2 %collective-permute-done.41 = bf16[512,1024]{1,0:T(8,128)(2,1)} collective-permute-done((bf16[512,1024]{1,0:T(8,128)(2,1)S(1)}, bf16[512,1024]{1,0:T(8,128)(2,1)}, u32[]{:S(2)}, u32[]{:S(2)}) %collective-permute-start.41) | collective-permute-done | bytes 1048608 | tf_op jit(solution)/shard_map/ppermute | solution.py:44
  472.5 5.8 %collective-permute-done.45 = bf16[64,2176]{1,0:T(8,128)(2,1)S(1)} collective-permute-done((bf16[64,2176]{1,0:T(8,128)(2,1)S(1)}, bf16[64,2176]{1,0:T(8,128)(2,1)S(1)}, u32[]{:S(2)}, u32[]{:S(2)}) %collective-permute-start.45) | collective-permute-done | bytes 278560 | tf_op jit(solution)/shard_map/ppermute | solution.py:44
  484.6 6.9 %collective-permute-done.46 = bf16[128,2176]{1,0:T(8,128)(2,1)S(1)} collective-permute-done((bf16[128,2176]{1,0:T(8,128)(2,1)S(1)}, bf16[128,2176]{1,0:T(8,128)(2,1)S(1)}, u32[]{:S(2)}, u32[]{:S(2)}) %collective-permute-start.46) | collective-permute-done | bytes 557088 | tf_op jit(solution)/shard_map/ppermute | solution.py:44
  511.3 8.9 %collective-permute-done.59 = bf16[2,2,3,32,512]{4,3,2,1,0:T(8,128)(2,1)S(1)} collective-permute-done((bf16[2,2,3,32,512]{4,3,2,1,0:T(8,128)(2,1)S(1)}, bf16[2,2,3,32,512]{4,3,2,1,0:T(8,128)(2,1)S(1)}, u32[]{:S(2)}, u32[]{:S(2)}) %collective-permute-start.59) | collective-permute-done | bytes 393248 | tf_op jit(solution)/shard_map/ppermute | solution.py:44
  (278 shorter events, 165.3 us)
Async XLA Ops:
  7.2 123.5 %all-gather.3.cloned.1.call-start = ((), (), s32[]{:S(2)}) async-start(), calls=%async_computation.2 | async-start | bytes 3932160 | tf_op jit(solution)/shard_map/all_gather | solution.py:738
  10.5 22.5 %collective-permute-start.5 = (bf16[32,3200]{1,0:T(8,128)(2,1)S(1)}, bf16[32,3200]{1,0:T(8,128)(2,1)S(1)}, u32[]{:S(2)}, u32[]{:S(2)}) collective-permute-start(bf16[32,3200]{1,0:T(8,128)(2,1)S(1)} %concatenate.60), channel_id=1, source_target_pairs={{0,24},{1,25},{2,26},{3,27},{4,28},{5,29},{6,30},{7,31},{8,16},{9,... | collective-permute-start | bytes 614408 | tf_op jit(solution)/shard_map/ppermute | solution.py:44
  66.6 168.5 %all-gather.5.cloned.1.call-start = ((), (), s32[]{:S(2)}) async-start(), calls=%async_computation.3 | async-start | bytes 3932160 | tf_op jit(solution)/shard_map/all_gather | solution.py:738
  77.9 29.2 %collective-permute-start.21 = (bf16[512,1024]{1,0:T(8,128)(2,1)S(1)}, bf16[512,1024]{1,0:T(8,128)(2,1)}, u32[]{:S(2)}, u32[]{:S(2)}) collective-permute-start(bf16[512,1024]{1,0:T(8,128)(2,1)S(1)} %copy-done.9), channel_id=1, source_target_pairs={{0,4},{1,5},{2,6},{3,7},{4,0},{5,1},{6,2},{7,3},{8,12},{9,13},{10,... | collective-permute-start | bytes 3145736 | tf_op jit(solution)/shard_map/ppermute | solution.py:44
  79.5 27.6 %collective-permute-start.20 = (bf16[512,1024]{1,0:T(8,128)(2,1)S(1)}, bf16[512,1024]{1,0:T(8,128)(2,1)}, u32[]{:S(2)}, u32[]{:S(2)}) collective-permute-start(bf16[512,1024]{1,0:T(8,128)(2,1)S(1)} %copy-done.9), channel_id=1, source_target_pairs={{0,2},{1,3},{2,0},{3,1},{4,6},{5,7},{6,4},{7,5},{8,10},{9,11},{10,... | collective-permute-start | bytes 3145736 | tf_op jit(solution)/shard_map/ppermute | solution.py:44
  131.7 350.4 %reduce-scatter.3.cloned.1.call-start = ((), (), s32[]{:S(2)}) async-start(), calls=%async_computation.4 | async-start | bytes 3932160 | tf_op jit(solution)/shard_map/reduce_scatter | solution.py:786
  131.9 28.6 %collective-permute-start.24 = (bf16[512,1152]{1,0:T(8,128)(2,1)S(1)}, bf16[512,1152]{1,0:T(8,128)(2,1)}, u32[]{:S(2)}, u32[]{:S(2)}) collective-permute-start(bf16[512,1152]{1,0:T(8,128)(2,1)S(1)} %copy-done.7), channel_id=1, source_target_pairs={{0,4},{1,5},{2,6},{3,7},{4,0},{5,1},{6,2},{7,3},{8,12},{9,13},{10,... | collective-permute-start | bytes 3538952 | tf_op jit(solution)/shard_map/ppermute | solution.py:44
  133.5 28.2 %collective-permute-start.23 = (bf16[512,1152]{1,0:T(8,128)(2,1)S(1)}, bf16[512,1152]{1,0:T(8,128)(2,1)}, u32[]{:S(2)}, u32[]{:S(2)}) collective-permute-start(bf16[512,1152]{1,0:T(8,128)(2,1)S(1)} %copy-done.7), channel_id=1, source_target_pairs={{0,2},{1,3},{2,0},{3,1},{4,6},{5,7},{6,4},{7,5},{8,10},{9,11},{10,... | collective-permute-start | bytes 3538952 | tf_op jit(solution)/shard_map/ppermute | solution.py:44
  163.9 27.1 %collective-permute-start.27 = (bf16[256,1152]{1,0:T(8,128)(2,1)S(1)}, bf16[256,1152]{1,0:T(8,128)(2,1)S(1)}, u32[]{:S(2)}, u32[]{:S(2)}) collective-permute-start(bf16[256,1152]{1,0:T(8,128)(2,1)S(1)} %slice.206), channel_id=1, source_target_pairs={{0,2},{1,3},{2,0},{3,1},{4,6},{5,7},{6,4},{7,5},{8,10},{9,11},{10,... | collective-permute-start | bytes 1769480 | tf_op jit(solution)/shard_map/ppermute | solution.py:44
  165.5 25.6 %collective-permute-start.26 = (bf16[256,1152]{1,0:T(8,128)(2,1)S(1)}, bf16[256,1152]{1,0:T(8,128)(2,1)S(1)}, u32[]{:S(2)}, u32[]{:S(2)}) collective-permute-start(bf16[256,1152]{1,0:T(8,128)(2,1)S(1)} %slice.205), channel_id=1, source_target_pairs={{0,4},{1,5},{2,6},{3,7},{4,0},{5,1},{6,2},{7,3},{8,12},{9,13},{10,... | collective-permute-start | bytes 1769480 | tf_op jit(solution)/shard_map/ppermute | solution.py:44
  168.2 21.7 %collective-permute-start.29 = (bf16[256,1024]{1,0:T(8,128)(2,1)S(1)}, bf16[256,1024]{1,0:T(8,128)(2,1)S(1)}, u32[]{:S(2)}, u32[]{:S(2)}) collective-permute-start(bf16[256,1024]{1,0:T(8,128)(2,1)S(1)} %slice.208), channel_id=1, source_target_pairs={{0,2},{1,3},{2,0},{3,1},{4,6},{5,7},{6,4},{7,5},{8,10},{9,11},{10,... | collective-permute-start | bytes 1572872 | tf_op jit(solution)/shard_map/ppermute | solution.py:44
  168.8 22.2 %collective-permute-start.28 = (bf16[256,1024]{1,0:T(8,128)(2,1)S(1)}, bf16[256,1024]{1,0:T(8,128)(2,1)S(1)}, u32[]{:S(2)}, u32[]{:S(2)}) collective-permute-start(bf16[256,1024]{1,0:T(8,128)(2,1)S(1)} %slice.207), channel_id=1, source_target_pairs={{0,4},{1,5},{2,6},{3,7},{4,0},{5,1},{6,2},{7,3},{8,12},{9,13},{10,... | collective-permute-start | bytes 1572872 | tf_op jit(solution)/shard_map/ppermute | solution.py:44
  235.2 51.9 %collective-permute-start.31 = (bf16[4,3,256,512]{3,2,1,0:T(8,128)(2,1)}, bf16[4,3,256,512]{3,2,1,0:T(8,128)(2,1)}, u32[]{:S(2)}, u32[]{:S(2)}) collective-permute-start(bf16[4,3,256,512]{3,2,1,0:T(8,128)(2,1)} %get-tuple-element.108), channel_id=1, source_target_pairs={{0,1},{1,0},{2,3},{3,2},{4,5},{5,4},{6,7},{7,6},{8,9},{9,8},{10,11... | collective-permute-start | bytes 9437192 | tf_op jit(solution)/shard_map/ppermute | solution.py:44
  325.9 51.4 %collective-permute-start.38 = (bf16[4,3,256,512]{3,2,1,0:T(8,128)(2,1)}, bf16[4,3,256,512]{3,2,1,0:T(8,128)(2,1)}, u32[]{:S(2)}, u32[]{:S(2)}) collective-permute-start(bf16[4,3,256,512]{3,2,1,0:T(8,128)(2,1)} %get-tuple-element.118), channel_id=1, source_target_pairs={{0,1},{1,0},{2,3},{3,2},{4,5},{5,4},{6,7},{7,6},{8,9},{9,8},{10,11... | collective-permute-start | bytes 9437192 | tf_op jit(solution)/shard_map/ppermute | solution.py:44
  326.0 28.6 %collective-permute-start.34 = (bf16[512,1152]{1,0:T(8,128)(2,1)}, bf16[512,1152]{1,0:T(8,128)(2,1)S(1)}, u32[]{:S(2)}, u32[]{:S(2)}) collective-permute-start(bf16[512,1152]{1,0:T(8,128)(2,1)} %get-tuple-element.114), channel_id=1, source_target_pairs={{0,2},{1,3},{2,0},{3,1},{4,6},{5,7},{6,4},{7,5},{8,10},{9,11},{10,... | collective-permute-start | bytes 3538952 | tf_op jit(solution)/shard_map/ppermute | solution.py:44
  327.6 28.4 %collective-permute-start.35 = (bf16[512,1152]{1,0:T(8,128)(2,1)}, bf16[512,1152]{1,0:T(8,128)(2,1)}, u32[]{:S(2)}, u32[]{:S(2)}) collective-permute-start(bf16[512,1152]{1,0:T(8,128)(2,1)} %get-tuple-element.115), channel_id=1, source_target_pairs={{0,4},{1,5},{2,6},{3,7},{4,0},{5,1},{6,2},{7,3},{8,12},{9,13},{10,... | collective-permute-start | bytes 3538952 | tf_op jit(solution)/shard_map/ppermute | solution.py:44
  329.5 167.0 %reduce-scatter.5.cloned.1.call-start = ((), (), s32[]{:S(2)}) async-start(), calls=%async_computation.5 | async-start | bytes 3932160 | tf_op jit(solution)/shard_map/reduce_scatter | solution.py:786
  382.6 25.9 %collective-permute-start.39 = (bf16[512,1024]{1,0:T(8,128)(2,1)}, bf16[512,1024]{1,0:T(8,128)(2,1)}, u32[]{:S(2)}, u32[]{:S(2)}) collective-permute-start(bf16[512,1024]{1,0:T(8,128)(2,1)} %pad_maximum_fusion.4), channel_id=1, source_target_pairs={{0,2},{1,3},{2,0},{3,1},{4,6},{5,7},{6,4},{7,5},{8,10},{9,11},{10,... | collective-permute-start | bytes 3145736 | tf_op jit(solution)/shard_map/ppermute | solution.py:44
  431.0 36.7 %collective-permute-start.44 = (bf16[4,4,32,2176]{3,2,1,0:T(8,128)(2,1)}, bf16[4,4,32,2176]{3,2,1,0:T(8,128)(2,1)}, u32[]{:S(2)}, u32[]{:S(2)}) collective-permute-start(bf16[4,4,32,2176]{3,2,1,0:T(8,128)(2,1)} %dynamic-slice_bitcast_fusion), channel_id=1, source_target_pairs={{0,1},{1,0},{2,3},{3,2},{4,5},{5,4},{6,7},{7,6},{8,9},{9,8},{10,11... | collective-permute-start | bytes 6684680 | tf_op jit(solution)/shard_map/ppermute | solution.py:44
  432.1 31.3 %collective-permute-start.41 = (bf16[512,1024]{1,0:T(8,128)(2,1)S(1)}, bf16[512,1024]{1,0:T(8,128)(2,1)}, u32[]{:S(2)}, u32[]{:S(2)}) collective-permute-start(bf16[512,1024]{1,0:T(8,128)(2,1)S(1)} %copy-done.10), channel_id=1, source_target_pairs={{0,4},{1,5},{2,6},{3,7},{4,0},{5,1},{6,2},{7,3},{8,12},{9,13},{10,... | collective-permute-start | bytes 3145736 | tf_op jit(solution)/shard_map/ppermute | solution.py:44
  441.7 25.3 %collective-permute-start.54 = (bf16[32,1152]{1,0:T(8,128)(2,1)S(1)}, bf16[32,1152]{1,0:T(8,128)(2,1)S(1)}, u32[]{:S(2)}, u32[]{:S(2)}) collective-permute-start(bf16[32,1152]{1,0:T(8,128)(2,1)S(1)} %get-tuple-element.257), channel_id=1, source_target_pairs={{0,8},{1,9},{2,10},{3,11},{4,12},{5,13},{6,14},{7,15},{8,0},{9,1},... | collective-permute-start | bytes 221192 | tf_op jit(solution)/shard_map/ppermute | solution.py:44
  441.8 25.2 %collective-permute-start.56 = (bf16[32,1152]{1,0:T(8,128)(2,1)S(1)}, bf16[32,1152]{1,0:T(8,128)(2,1)S(1)}, u32[]{:S(2)}, u32[]{:S(2)}) collective-permute-start(bf16[32,1152]{1,0:T(8,128)(2,1)S(1)} %get-tuple-element.258), channel_id=1, source_target_pairs={{0,24},{1,25},{2,26},{3,27},{4,28},{5,29},{6,30},{7,31},{8,16},{9,... | collective-permute-start | bytes 221192 | tf_op jit(solution)/shard_map/ppermute | solution.py:44
  444.3 22.7 %collective-permute-start.55 = (bf16[32,1152]{1,0:T(8,128)(2,1)S(1)}, bf16[32,1152]{1,0:T(8,128)(2,1)S(1)}, u32[]{:S(2)}, u32[]{:S(2)}) collective-permute-start(bf16[32,1152]{1,0:T(8,128)(2,1)S(1)} %get-tuple-element.259), channel_id=1, source_target_pairs={{0,16},{1,17},{2,18},{3,19},{4,20},{5,21},{6,22},{7,23},{8,24},{9,... | collective-permute-start | bytes 221192 | tf_op jit(solution)/shard_map/ppermute | solution.py:44
  500.9 19.5 %collective-permute-start.49 = (bf16[32,2176]{1,0:T(8,128)(2,1)S(1)}, bf16[32,2176]{1,0:T(8,128)(2,1)S(1)}, u32[]{:S(2)}, u32[]{:S(2)}) collective-permute-start(bf16[32,2176]{1,0:T(8,128)(2,1)S(1)} %get-tuple-element.250), channel_id=1, source_target_pairs={{0,8},{1,9},{2,10},{3,11},{4,12},{5,13},{6,14},{7,15},{8,0},{9,1},... | collective-permute-start | bytes 417800 | tf_op jit(solution)/shard_map/ppermute | solution.py:44
  (61 other events, 622.3 us)
Sparse Core Ops, SparseCore 0:
  66.7 63.9 all-gather.2
  132.9 62.1 all-gather.4
  329.6 57.9 reduce-scatter.2
  433.7 62.6 reduce-scatter.4

commit v7 on v6

--- a/solution.py
+++ b/solution.py
@@ -56,14 +56,6 @@
             part = lax.dynamic_index_in_dim(terms, self.group ^ bits, 0, keepdims=False)
             total = total + self.swap(part.astype(bf16), bits * MEMBERS).astype(f32)
         return total
-
-    def chips_gather(self, block):
-        half = block.shape[0] // 2
-        top, low = block[:half], block[half:]
-        near_top, far_low = self.swap(top, 2), self.swap(low, 4)
-        near_low, far_top = self.swap(low, 2), self.swap(top, 4)
-        cross_top, cross_low = self.swap(near_top, 4), self.swap(far_low, 2)
-        return {0: (top, low), 2: (near_top, near_low), 4: (far_top, far_low), 6: (cross_top, cross_low)}
 
     def cross_of(self, near, far):
         half = near.shape[0] // 2
@@ -99,9 +91,13 @@
             arrived = lax.dynamic_update_index_in_dim(arrived, part, chip ^ bits, 0)
         kept = lax.dynamic_index_in_dim(arrived, core, 1, keepdims=False)
         other = self.swap(lax.dynamic_index_in_dim(arrived, 1 - core, 1, keepdims=False), 1)
+        return kept, other
+
+    def in_order(self, kept, other):
+        core = self.member % 2
         even = jnp.where(core == 0, kept, other)
         odd = jnp.where(core == 0, other, kept)
-        return jnp.stack([even, odd], axis=1).reshape((MEMBERS,) + found[0].shape[1:])
+        return jnp.stack([even, odd], axis=1).reshape((MEMBERS,) + kept.shape[1:])
 
 
 def dot(left, right):
@@ -437,11 +433,19 @@
 
 
 def middle_kernel(
-    own_ref, near_ref, far_ref, packet_ref, middle_ref, cotangent_ref, share_ref, gains_ref, mixed_ref, output_ref, extra_ref,
+    own_ref, near_top_ref, near_low_ref, far_top_ref, far_low_ref, packet_ref, middle_ref,
+    cotangent_ref, share_ref, gains_ref, mixed_ref, output_ref, extra_ref,
     middle_grad_ref, mixed_grad_ref, pack_ref, back_ref, branch_ref, turned_ref,
 ):
     width = cotangent_ref.shape[1]
-    back_ref[...] = own_ref[...].astype(f32) + near_ref[...].astype(f32) + far_ref[...].astype(f32)
+    half = own_ref.shape[0] // 2
+    for place, near_ref, far_ref in (
+        (pl.ds(0, half), near_top_ref, far_top_ref),
+        (pl.ds(half, half), near_low_ref, far_low_ref),
+    ):
+        back_ref[place] = (
+            own_ref[place].astype(f32) + near_ref[...].astype(f32) + far_ref[...].astype(f32)
+        )
     shares = share_ref[...]
     share_grad = back_ref[:, width:]
     share_grad = share_grad + pltpu.roll(share_grad, EXTRA - EXPERTS, 1)
@@ -730,9 +734,19 @@
     pack_width = packed.shape[1]
     column = links.direct_gather(packed).reshape(groups * shard, pack_width)
     arrived, column = lax.optimization_barrier((arrived, column))
-    spread = links.chips_gather(column)
-    shelf = links.keep_parts(arrived).transpose(1, 2, 0, 3, 4)
+    half = column.shape[0] // 2
+    top, low = column[:half], column[half:]
+    near_top, far_low = links.swap(top, 2), links.swap(low, 4)
+    near_low, far_top = links.swap(low, 2), links.swap(top, 4)
+    kept, other = links.keep_parts(arrived)
+    kept, other, near_top, far_low = lax.optimization_barrier((kept, other, near_top, far_low))
+    shelf = links.in_order(kept, other).transpose(1, 2, 0, 3, 4)
     shelf = shelf.reshape(LOCAL_EXPERTS, 3, MEMBERS * shard, hidden)
+    cross_top, cross_low = links.swap(near_top, 4), links.swap(far_low, 2)
+    top, low, near_top = lax.optimization_barrier((top, low, near_top))
+    spread = {
+        0: (top, low), 2: (near_top, near_low), 4: (far_top, far_low), 6: (cross_top, cross_low)
+    }
     lines = [[m + MEMBERS * g for g in range(groups)] for m in range(MEMBERS)]
     own_full = [
         lax.all_gather(shelf[n], "fsdp", axis_index_groups=lines) for n in range(LOCAL_EXPERTS)
@@ -769,7 +783,7 @@
     rows_own = [(packet,)], [(cotangent,)]
     first_full = own_full[0], links.swap(own_full[0], 1)
     own_out, own_back, *zero = run_experts(names[0], *rows_own, first_full)
-    near, far, own_back = lax.optimization_barrier((near, far, own_back))
+    near, far, cot_cross, own_back = lax.optimization_barrier((near, far, cot_cross, own_back))
     cross = links.cross_of(near, far)
     rows_chips = [cross, (near,), (far,)], [cot_cross, (cot_near,), (cot_far,)]
     chip_out, chip_back, *zero = run_experts(names[0], *rows_chips, first_full, zero, True)
@@ -786,18 +800,24 @@
         return lax.psum_scatter(total, "fsdp", scatter_dimension=0, axis_index_groups=lines)
 
     zero = join_cores(*zero)
-    back_cross = links.send_cross(chip_back[0])
-    back_near, back_far = links.add_cross(chip_back[1], chip_back[2], back_cross)
-    zero, back_near, back_far, own_back = lax.optimization_barrier(
-        (zero, back_near, back_far, own_back)
-    )
+    zero, chip_back = lax.optimization_barrier((zero, chip_back))
     shelf_zero = reduce_groups(zero)
-    back_near, back_far = links.swap(back_near, 2), links.swap(back_far, 4)
+    half = row_count // 2
+    cross_top, cross_low = links.send_cross(chip_back[0])
+    near_top, far_low = links.swap(chip_back[1, :half], 2), links.swap(chip_back[2, half:], 4)
     own_out, own_back, *one = run_experts(
         names[1], *rows_own, second_full, one, True, (own_out, own_back)
     )
+    cross_top, cross_low, near_top, far_low, own_back = lax.optimization_barrier(
+        (cross_top, cross_low, near_top, far_low, own_back)
+    )
+    near_low = (chip_back[1, half:].astype(f32) + cross_low.astype(f32)).astype(bf16)
+    far_top = (chip_back[2, :half].astype(f32) + cross_top.astype(f32)).astype(bf16)
+    near_low, far_top, one = lax.optimization_barrier((near_low, far_top, one))
+    near_low, far_top = links.swap(near_low, 2), links.swap(far_top, 4)
     one = join_cores(*one)
-    out_cross, back_near, back_far = lax.optimization_barrier((chip_out[0], back_near, back_far))
+    back_pieces = near_top, near_low, far_top, far_low
+    out_cross, back_pieces = lax.optimization_barrier((chip_out[0], back_pieces))
     out_cross = links.send_cross(out_cross)
 
     core, chip = member % 2, member // 2
@@ -828,7 +848,7 @@
         return links.direct_reduce(total.reshape(groups, shard, total.shape[1]))
 
     middle_grad, mixed_grad, first_pack = middle_back(
-        (own_back[0], back_near, back_far), packet, middle, cotangent, shares, gains, mixed, whole
+        (own_back[0], *back_pieces), packet, middle, cotangent, shares, gains, mixed, whole
     )
     out_near, out_far = links.add_cross(chip_out[1], chip_out[2], out_cross)
     out_near, out_far, one, mixed_grad = lax.optimization_barrier(
@@ -838,8 +858,8 @@
     out_near, out_far = links.swap(out_near, 2), links.swap(out_far, 4)
     first_parts = pack_cores(first_pack)
     projected_grad = attention_back(lengths, rotated, mixed_grad, logs, tables)
-    out_near, first_parts, projected_grad = lax.optimization_barrier(
-        (out_near, first_parts, projected_grad)
+    out_near, out_far, shelf_zero, first_parts, projected_grad = lax.optimization_barrier(
+        (out_near, out_far, shelf_zero, first_parts, projected_grad)
     )
     first_cross = pack_cross(first_parts)
     grad_tokens, second_pack = inputs_back(tokens, gains, projected_grad, whole, middle_grad)
@@ -850,12 +870,17 @@
     second_parts = pack_cores(second_pack)
     first_total = pack_end(first_parts, first_near, first_far)
     second_near, second_far = pack_add(second_parts, pack_cross(second_parts))
+    second_near, second_far, shelf_one = lax.optimization_barrier(
+        (second_near, second_far, shelf_one)
+    )
     second_total = pack_end(second_parts, second_near, second_far)
     out_pieces = (own_out[0], out_near, out_far)
     layer_out = (middle + sum(piece.astype(f32) for piece in out_pieces)).astype(bf16)
     shelf_grad = jnp.stack([shelf_zero, shelf_one])
     shelf_grad = shelf_grad.reshape(LOCAL_EXPERTS, 3, MEMBERS, shard, hidden)
-    expert_shards = links.keep_parts(links.chip_parts(shelf_grad.transpose(2, 0, 1, 3, 4))).astype(f32)
+    expert_shards = links.in_order(
+        *links.keep_parts(links.chip_parts(shelf_grad.transpose(2, 0, 1, 3, 4)))
+    ).astype(f32)
     expert_shards = expert_shards.reshape(EXPERTS, 3, shard, hidden)
     return (
         layer_out,

time: 542 us -> 541 us (level)
  waiting for transfers between devices: 181 us -> 171 us
  local copies, waits for them, and re-layouts: 46.8 us -> 56 us
    reduce_scatter x2, waiting for transfers between devices: 2.15 us -> 24.6 us  [reduce_groups(): lax.psum_scatter(total, 'fsdp', scatter_dimension=0, axis_index_groups=li...]
    ppermute x61 -> x63, waiting for transfers between devices: 162 us -> 141 us  [swap(): lax.ppermute(value, 'fsdp', [(i, i ^ bits) for i in range(self.count)])]
    all_gather x2, waiting for transfers between devices: 17.1 us -> 4.62 us  [local(): lax.all_gather(shelf[n], 'fsdp', axis_index_groups=lines)]
    ppermute x61 -> x63, starting transfers between devices: 57.2 us -> 56.8 us  [swap(): lax.ppermute(value, 'fsdp', [(i, i ^ bits) for i in range(self.count)])]
  transfers between devices with their start and end apart: 65 -> 67, of which waited for: 30 -> 33; matrix products, arithmetic and copies ran while one was open for 12% -> 15% of each run, Pallas kernels for 33% -> 29%
where the time goes in v7:
time: 541 us; the launch traced here: 532 us
  Pallas kernels  197 us (36%)
  waiting for transfers between devices  171 us (32%)
  starting transfers between devices  57.3 us (11%)
  local copies, waits for them, and re-layouts  56 us (10%)
  other arithmetic  35.6 us (7%)
  between operations  15.7 us (3%)
    ppermute x63, waiting for transfers between devices, swap(): lax.ppermute(value, 'fsdp', [(i, i ^ bits) for i in range(self.count)])  141 us
    pallas_call x4, Pallas kernels, run_experts(): pl.pallas_call(functools.partial(expert_kernel, layout=layout, fresh=fres...  125 us
    pallas_call x5, Pallas kernels, call_kernel(): pl.pallas_call(body, grid=(1,), in_specs=specs, out_specs=[pl.BlockSpec(o...  72.1 us
    ppermute x63, starting transfers between devices, swap(): lax.ppermute(value, 'fsdp', [(i, i ^ bits) for i in range(self.count)])  56.8 us
    reduce_scatter x2, waiting for transfers between devices, reduce_groups(): lax.psum_scatter(total, 'fsdp', scatter_dimension=0, axis_index_groups=li...  24.6 us
  transfers between devices with their start and end apart: 67, of which 33 were waited for; matrix products, arithmetic and copies ran while one was open for 15% of the time, Pallas kernels for 29%

profile of v7, /device:TPU:0, one launch (start us, length us, event | category | flops | bytes accessed | tf_op | source)
XLA Modules:
  0.0 532.0 jit_solution(15058497874939425839)
XLA Ops:
  10.5 5.1 collective-permute-start.5
  21.9 6.9 %collective-permute-done.3 = bf16[32,3200]{1,0:T(8,128)(2,1)} collective-permute-done((bf16[32,3200]{1,0:T(8,128)(2,1)S(1)}, bf16[32,3200]{1,0:T(8,128)(2,1)}, u32[]{:S(2)}, u32[]{:S(2)}) %collective-permute-start.3) | collective-permute-done | bytes 204832 | tf_op jit(solution)/shard_map/ppermute | solution.py:44
  45.0 7.6 %collective-permute-done.11 = bf16[64,3200]{1,0:T(8,128)(2,1)} collective-permute-done((bf16[64,3200]{1,0:T(8,128)(2,1)S(1)}, bf16[64,3200]{1,0:T(8,128)(2,1)}, u32[]{:S(2)}, u32[]{:S(2)}) %collective-permute-start.11) | collective-permute-done | bytes 409632 | tf_op jit(solution)/shard_map/ppermute | solution.py:44
  54.3 8.0 %collective-permute-done.8 = bf16[64,3200]{1,0:T(8,128)(2,1)S(1)} collective-permute-done((bf16[64,3200]{1,0:T(8,128)(2,1)S(1)}, bf16[64,3200]{1,0:T(8,128)(2,1)S(1)}, u32[]{:S(2)}, u32[]{:S(2)}) %collective-permute-start.8) | collective-permute-done | bytes 409632 | tf_op jit(solution)/shard_map/ppermute | solution.py:44
  100.1 20.3 %attention_forward.1 = (bf16[512,2048]{1,0:T(8,128)(2,1)}, bf16[512,1024]{1,0:T(8,128)(2,1)}, f32[4,4,512]{2,1,0:T(4,128)}) custom-call(s32[1]{0:T(128)S(6)} %copy.165.length_ref, bf16[512,1024]{1,0:T(8,128)(2,1)} %tokens_ref.5, f32[512,256]{1,0:T(8,128)} %copy.124.cosine_ref, f32[512,256]{1,0:T(8,128)} %copy.125.sine_ref, f32[2,1024]{1,0:T(2,128)} %copy.128.gains_ref, ...), custom_call_target="tpu_custom_call" | custom-call | flops 4294967296 | bytes 11837444 | tf_op jit(solution)/shard_map/attention_forward/pallas_call | solution.py:578
  120.4 6.6 %router_forward.1 = (bf16[512,1152]{1,0:T(8,128)(2,1)}, f32[512,1024]{1,0:T(8,128)}, f32[512,128]{1,0:T(8,128)}) custom-call(bf16[512,1024]{1,0:T(8,128)(2,1)} %tokens_ref.5, s32[512,8]{1,0:T(8,128)} %copy.127.routes_ref, f32[2,1024]{1,0:T(2,128)} %copy.128.gains_ref, bf16[512,1024]{1,0:T(8,128)(2,1)} %get-tuple-element.114.mixed_ref, ...), custom_call_target="tpu_custom_call" | custom-call | flops 1073741824 | bytes 18767872 | tf_op jit(solution)/shard_map/router_forward/pallas_call | solution.py:578
  127.0 4.6 all-gather.3.cloned.1.call-done.refs_2_.refs_8_
  139.7 18.4 %experts.4 = (bf16[1,512,1024]{2,1,0:T(8,128)(2,1)}, bf16[1,512,1152]{2,1,0:T(8,128)(2,1)}, f32[3,1024,512]{2,1,0:T(8,128)}, f32[3,1024,512]{2,1,0:T(8,128)}) custom-call(s32[2]{0:T(128)} %get-tuple-element.263.names_ref, bf16[512,1152]{1,0:T(8,128)(2,1)} %get-tuple-element.121.refs_0_.packet_ref, bf16[512,1024]{1,0:T(8,128)(2,1)} %cotangent_ref.1, ...), custom_call_target="tpu_custom_call" | custom-call | flops 9663676416 | bytes 23068672 | tf_op jit(solution)/shard_map/experts/pallas_call | solution.py:286
  162.2 10.4 %collective-permute-done.26.refs_5_ = bf16[256,1024]{1,0:T(8,128)(2,1)S(1)} collective-permute-done((bf16[256,1024]{1,0:T(8,128)(2,1)S(1)}, bf16[256,1024]{1,0:T(8,128)(2,1)S(1)}, u32[]{:S(2)}, u32[]{:S(2)}) %collective-permute-start.26) | collective-permute-done | bytes 524320 | tf_op jit(solution)/shard_map/ppermute | solution.py:44
  177.1 12.7 %collective-permute-done.29.refs_1_ = bf16[256,1152]{1,0:T(8,128)(2,1)S(1)} collective-permute-done((bf16[256,1152]{1,0:T(8,128)(2,1)S(1)}, bf16[256,1152]{1,0:T(8,128)(2,1)S(1)}, u32[]{:S(2)}, u32[]{:S(2)}) %collective-permute-start.29) | collective-permute-done | bytes 589856 | tf_op jit(solution)/shard_map/ppermute | solution.py:44
  191.9 42.3 %experts.5 = (bf16[3,512,1024]{2,1,0:T(8,128)(2,1)}, bf16[3,512,1152]{2,1,0:T(8,128)(2,1)}, bf16[4,3,256,512]{3,2,1,0:T(8,128)(2,1)}, bf16[4,3,256,512]{3,2,1,0:T(8,128)(2,1)}) custom-call(s32[2]{0:T(128)} %get-tuple-element.263.names_ref, bf16[256,1152]{1,0:T(8,128)(2,1)} %copy-done.18, bf16[256,1152]{1,0:T(8,128)(2,1)} %copy-done.17, ...), custom_call_target="tpu_custom_call" | custom-call | flops 28991029248 | bytes 31457280 | tf_op jit(solution)/shard_map/experts/pallas_call | solution.py:286
  234.8 8.8 %collective-permute-done.31 = bf16[4,3,256,512]{3,2,1,0:T(8,128)(2,1)S(1)} collective-permute-done((bf16[4,3,256,512]{3,2,1,0:T(8,128)(2,1)}, bf16[4,3,256,512]{3,2,1,0:T(8,128)(2,1)S(1)}, u32[]{:S(2)}, u32[]{:S(2)}) %collective-permute-start.31) | collective-permute-done | bytes 3145760 | tf_op jit(solution)/shard_map/ppermute | solution.py:44
  248.1 42.7 %experts.6 = (bf16[3,512,1024]{2,1,0:T(8,128)(2,1)}, bf16[3,512,1152]{2,1,0:T(8,128)(2,1)}, f32[3,1024,512]{2,1,0:T(8,128)}, f32[3,1024,512]{2,1,0:T(8,128)}) custom-call(s32[2]{0:T(128)} %get-tuple-element.262.names_ref, bf16[256,1152]{1,0:T(8,128)(2,1)} %copy-done.18, bf16[256,1152]{1,0:T(8,128)(2,1)} %copy-done.17, ...), custom_call_target="tpu_custom_call" | custom-call | flops 28991029248 | bytes 31457280 | tf_op jit(solution)/shard_map/experts/pallas_call | solution.py:286
  297.9 21.2 %experts.7 = (bf16[1,512,1024]{2,1,0:T(8,128)(2,1)}, bf16[1,512,1152]{2,1,0:T(8,128)(2,1)}, bf16[4,3,256,512]{3,2,1,0:T(8,128)(2,1)}, bf16[4,3,256,512]{3,2,1,0:T(8,128)(2,1)}) custom-call(s32[2]{0:T(128)} %get-tuple-element.262.names_ref, bf16[512,1152]{1,0:T(8,128)(2,1)} %get-tuple-element.121.refs_0_.packet_ref, bf16[512,1024]{1,0:T(8,128)(2,1)} %cotangent_ref.1, ...), custom_call_target="tpu_custom_call" | custom-call | flops 9663676416 | bytes 23068672 | tf_op jit(solution)/shard_map/experts/pallas_call | solution.py:286
  327.8 12.4 %collective-permute-done.36.near_low_ref = bf16[256,1152]{1,0:T(8,128)(2,1)S(1)} collective-permute-done((bf16[256,1152]{1,0:T(8,128)(2,1)S(1)}, bf16[256,1152]{1,0:T(8,128)(2,1)S(1)}, u32[]{:S(2)}, u32[]{:S(2)}) %collective-permute-start.36) | collective-permute-done | bytes 589856 | tf_op jit(solution)/shard_map/ppermute | solution.py:44
  344.6 11.7 %middle_back.1 = (f32[512,1024]{1,0:T(8,128)}, bf16[512,1024]{1,0:T(8,128)(2,1)}, bf16[1024,1152]{1,0:T(8,128)(2,1)}) custom-call(bf16[512,1152]{1,0:T(8,128)(2,1)} %bitcast.225, bf16[256,1152]{1,0:T(8,128)(2,1)} %copy-done.8, bf16[256,1152]{1,0:T(8,128)(2,1)} %copy-done.9, bf16[256,1152]{1,0:T(8,128)(2,1)} %copy-done.10, bf16[256,1152]{1,0:T(8,128)(2,1)} %copy-done.7, ...), custom_call_target="tpu_custom_call" | custom-call | flops 2147483648 | bytes 27795456 | tf_op jit(solution)/shard_map/middle_back/pallas_call | solution.py:578
  370.7 18.8 %attention_back.1.projected_ref = bf16[512,2048]{1,0:T(8,128)(2,1)} custom-call(s32[1]{0:T(128)S(6)} %copy.165.length_ref, bf16[512,2048]{1,0:T(8,128)(2,1)} %get-tuple-element.169.rotated_ref, bf16[512,1024]{1,0:T(8,128)(2,1)} %get-tuple-element.170.mixed_grad_ref, f32[4,4,512]{2,1,0:T(4,128)} %get-tuple-element.171.log_ref, f32[512,256]{1,0:T(8,128)} %copy.124.cosine_ref, ...), custom_call_target="tpu_custom_call" | custom-call | flops 2684354560 | bytes 6324228 | tf_op jit(solution)/shard_map/attention_back/pallas_call | solution.py:578
  389.5 5.5 %collective-permute-done.41 = bf16[512,1024]{1,0:T(8,128)(2,1)} collective-permute-done((bf16[512,1024]{1,0:T(8,128)(2,1)}, bf16[512,1024]{1,0:T(8,128)(2,1)}, u32[]{:S(2)}, u32[]{:S(2)}) %collective-permute-start.41) | collective-permute-done | bytes 1048608 | tf_op jit(solution)/shard_map/ppermute | solution.py:44
  397.4 14.7 %inputs_back.1 = (f32[512,1024]{1,0:T(8,128)}, bf16[1024,2176]{1,0:T(8,128)(2,1)}) custom-call(bf16[512,1024]{1,0:T(8,128)(2,1)} %tokens_ref.5, f32[2,1024]{1,0:T(2,128)} %copy.128.gains_ref, bf16[512,2048]{1,0:T(8,128)(2,1)} %attention_back.1.projected_ref, bf16[1024,3200]{1,0:T(8,128)(2,1)} %bitcast.34.weight_ref.output_ref.extra_ref, ...), custom_call_target="tpu_custom_call" | custom-call | flops 4294967296 | bytes 18358272 | tf_op jit(solution)/shard_map/inputs_back/pallas_call | solution.py:578
  429.6 8.6 %collective-permute-done.57 = bf16[32,1152]{1,0:T(8,128)(2,1)S(1)} collective-permute-done((bf16[32,1152]{1,0:T(8,128)(2,1)S(1)}, bf16[32,1152]{1,0:T(8,128)(2,1)S(1)}, u32[]{:S(2)}, u32[]{:S(2)}) %collective-permute-start.57) | collective-permute-done | bytes 73760 | tf_op jit(solution)/shard_map/ppermute | solution.py:44
  448.6 5.1 collective-permute-done.48
  454.0 24.6 %reduce-scatter.5.cloned.1.call-done = bf16[1,3,256,512]{3,2,1,0:T(8,128)(2,1)} async-done(((bf16[4,3,256,512]{3,2,1,0:T(8,128)(2,1)}), bf16[1,3,256,512]{3,2,1,0:T(8,128)(2,1)}) %reduce-scatter.5.cloned.1.call-update) | async-done | bytes 786448 | tf_op jit(solution)/shard_map/reduce_scatter | solution.py:800
  488.2 5.5 %collective-permute-done.59 = bf16[2,2,3,32,512]{4,3,2,1,0:T(8,128)(2,1)S(1)} collective-permute-done((bf16[2,2,3,32,512]{4,3,2,1,0:T(8,128)(2,1)S(1)}, bf16[2,2,3,32,512]{4,3,2,1,0:T(8,128)(2,1)S(1)}, u32[]{:S(2)}, u32[]{:S(2)}) %collective-permute-start.59) | collective-permute-done | bytes 393248 | tf_op jit(solution)/shard_map/ppermute | solution.py:44
  493.8 11.8 %collective-permute-done.49 = bf16[128,2176]{1,0:T(8,128)(2,1)S(1)} collective-permute-done((bf16[128,2176]{1,0:T(8,128)(2,1)S(1)}, bf16[128,2176]{1,0:T(8,128)(2,1)S(1)}, u32[]{:S(2)}, u32[]{:S(2)}) %collective-permute-start.49) | collective-permute-done | bytes 557088 | tf_op jit(solution)/shard_map/ppermute | solution.py:44
  (280 shorter events, 181.9 us)
Async XLA Ops:
  7.2 124.4 %all-gather.3.cloned.1.call-start = ((), (), s32[]{:S(2)}) async-start(), calls=%async_computation.2 | async-start | bytes 3932160 | tf_op jit(solution)/shard_map/all_gather | solution.py:752
  10.5 23.6 %collective-permute-start.5 = (bf16[32,3200]{1,0:T(8,128)(2,1)S(1)}, bf16[32,3200]{1,0:T(8,128)(2,1)S(1)}, u32[]{:S(2)}, u32[]{:S(2)}) collective-permute-start(bf16[32,3200]{1,0:T(8,128)(2,1)S(1)} %concatenate.57), channel_id=1, source_target_pairs={{0,24},{1,25},{2,26},{3,27},{4,28},{5,29},{6,30},{7,31},{8,16},{9,... | collective-permute-start | bytes 614408 | tf_op jit(solution)/shard_map/ppermute | solution.py:44
  39.3 23.0 %collective-permute-start.6 = (bf16[4,2,3,32,512]{4,3,2,1,0:T(8,128)(2,1)S(1)}, bf16[4,2,3,32,512]{4,3,2,1,0:T(8,128)(2,1)}, u32[]{:S(2)}, u32[]{:S(2)}) collective-permute-start(bf16[4,2,3,32,512]{4,3,2,1,0:T(8,128)(2,1)S(1)} %get-tuple-element.292), channel_id=1, source_target_pairs={{0,1},{1,0},{2,3},{3,2},{4,5},{5,4},{6,7},{7,6},{8,9},{9,8},{10,11... | collective-permute-start | bytes 2359304 | tf_op jit(solution)/shard_map/ppermute | solution.py:44
  52.6 27.3 %collective-permute-start.13 = (bf16[64,3200]{1,0:T(8,128)(2,1)}, bf16[64,3200]{1,0:T(8,128)(2,1)}, u32[]{:S(2)}, u32[]{:S(2)}) collective-permute-start(bf16[64,3200]{1,0:T(8,128)(2,1)} %collective-permute-done.11), channel_id=1, source_target_pairs={{0,1},{1,0},{2,3},{3,2},{4,5},{5,4},{6,7},{7,6},{8,9},{9,8},{10,11... | collective-permute-start | bytes 1228808 | tf_op jit(solution)/shard_map/ppermute | solution.py:44
  54.3 34.0 %collective-permute-start.15 = (bf16[64,3200]{1,0:T(8,128)(2,1)}, bf16[64,3200]{1,0:T(8,128)(2,1)}, u32[]{:S(2)}, u32[]{:S(2)}) collective-permute-start(bf16[64,3200]{1,0:T(8,128)(2,1)} %collective-permute-done.14), channel_id=1, source_target_pairs={{0,1},{1,0},{2,3},{3,2},{4,5},{5,4},{6,7},{7,6},{8,9},{9,8},{10,11... | collective-permute-start | bytes 1228808 | tf_op jit(solution)/shard_map/ppermute | solution.py:44
  68.1 166.1 %all-gather.5.cloned.1.call-start = ((), (), s32[]{:S(2)}) async-start(), calls=%async_computation.3 | async-start | bytes 3932160 | tf_op jit(solution)/shard_map/all_gather | solution.py:752
  92.9 27.6 %collective-permute-start.22 = (bf16[512,1024]{1,0:T(8,128)(2,1)S(1)}, bf16[512,1024]{1,0:T(8,128)(2,1)}, u32[]{:S(2)}, u32[]{:S(2)}) collective-permute-start(bf16[512,1024]{1,0:T(8,128)(2,1)S(1)} %copy-done.4), channel_id=1, source_target_pairs={{0,4},{1,5},{2,6},{3,7},{4,0},{5,1},{6,2},{7,3},{8,12},{9,13},{10,... | collective-permute-start | bytes 3145736 | tf_op jit(solution)/shard_map/ppermute | solution.py:44
  93.7 26.8 %collective-permute-start.21 = (bf16[512,1024]{1,0:T(8,128)(2,1)S(1)}, bf16[512,1024]{1,0:T(8,128)(2,1)}, u32[]{:S(2)}, u32[]{:S(2)}) collective-permute-start(bf16[512,1024]{1,0:T(8,128)(2,1)S(1)} %copy-done.4), channel_id=1, source_target_pairs={{0,2},{1,3},{2,0},{3,1},{4,6},{5,7},{6,4},{7,5},{8,10},{9,11},{10,... | collective-permute-start | bytes 3145736 | tf_op jit(solution)/shard_map/ppermute | solution.py:44
  131.6 29.1 %collective-permute-start.24 = (bf16[512,1152]{1,0:T(8,128)(2,1)}, bf16[512,1152]{1,0:T(8,128)(2,1)}, u32[]{:S(2)}, u32[]{:S(2)}) collective-permute-start(bf16[512,1152]{1,0:T(8,128)(2,1)} %get-tuple-element.121.refs_0_.packet_ref), channel_id=1, source_target_pairs={{0,4},{1,5},{2,6},{3,7},{4,0},{5,1},{6,2},{7,3},{8,12},{9,13},{10,... | collective-permute-start | bytes 3538952 | tf_op jit(solution)/shard_map/ppermute | solution.py:44
  133.1 29.1 %collective-permute-start.23 = (bf16[512,1152]{1,0:T(8,128)(2,1)}, bf16[512,1152]{1,0:T(8,128)(2,1)}, u32[]{:S(2)}, u32[]{:S(2)}) collective-permute-start(bf16[512,1152]{1,0:T(8,128)(2,1)} %get-tuple-element.121.refs_0_.packet_ref), channel_id=1, source_target_pairs={{0,2},{1,3},{2,0},{3,1},{4,6},{5,7},{6,4},{7,5},{8,10},{9,11},{10,... | collective-permute-start | bytes 3538952 | tf_op jit(solution)/shard_map/ppermute | solution.py:44
  135.5 259.7 %reduce-scatter.3.cloned.1.call-start = ((), (), s32[]{:S(2)}) async-start(), calls=%async_computation.4 | async-start | bytes 3932160 | tf_op jit(solution)/shard_map/reduce_scatter | solution.py:800
  138.5 34.1 %collective-permute-start.26 = (bf16[256,1024]{1,0:T(8,128)(2,1)S(1)}, bf16[256,1024]{1,0:T(8,128)(2,1)S(1)}, u32[]{:S(2)}, u32[]{:S(2)}) collective-permute-start(bf16[256,1024]{1,0:T(8,128)(2,1)S(1)} %slice.191), channel_id=1, source_target_pairs={{0,2},{1,3},{2,0},{3,1},{4,6},{5,7},{6,4},{7,5},{8,10},{9,11},{10,... | collective-permute-start | bytes 1572872 | tf_op jit(solution)/shard_map/ppermute | solution.py:44
  139.1 33.5 %collective-permute-start.25 = (bf16[256,1024]{1,0:T(8,128)(2,1)S(1)}, bf16[256,1024]{1,0:T(8,128)(2,1)}, u32[]{:S(2)}, u32[]{:S(2)}) collective-permute-start(bf16[256,1024]{1,0:T(8,128)(2,1)S(1)} %slice.190), channel_id=1, source_target_pairs={{0,4},{1,5},{2,6},{3,7},{4,0},{5,1},{6,2},{7,3},{8,12},{9,13},{10,... | collective-permute-start | bytes 1572872 | tf_op jit(solution)/shard_map/ppermute | solution.py:44
  290.8 187.8 %reduce-scatter.5.cloned.1.call-start = ((), (), s32[]{:S(2)}) async-start(), calls=%async_computation.5 | async-start | bytes 3932160 | tf_op jit(solution)/shard_map/reduce_scatter | solution.py:800
  293.9 25.3 %collective-permute-start.35 = (bf16[256,1152]{1,0:T(8,128)(2,1)}, bf16[256,1152]{1,0:T(8,128)(2,1)S(1)}, u32[]{:S(2)}, u32[]{:S(2)}) collective-permute-start(bf16[256,1152]{1,0:T(8,128)(2,1)} %get-tuple-element.269), channel_id=1, source_target_pairs={{0,4},{1,5},{2,6},{3,7},{4,0},{5,1},{6,2},{7,3},{8,12},{9,13},{10,... | collective-permute-start | bytes 1769480 | tf_op jit(solution)/shard_map/ppermute | solution.py:44
  294.4 24.8 %collective-permute-start.34 = (bf16[256,1152]{1,0:T(8,128)(2,1)}, bf16[256,1152]{1,0:T(8,128)(2,1)S(1)}, u32[]{:S(2)}, u32[]{:S(2)}) collective-permute-start(bf16[256,1152]{1,0:T(8,128)(2,1)} %get-tuple-element.270), channel_id=1, source_target_pairs={{0,2},{1,3},{2,0},{3,1},{4,6},{5,7},{6,4},{7,5},{8,10},{9,11},{10,... | collective-permute-start | bytes 1769480 | tf_op jit(solution)/shard_map/ppermute | solution.py:44
  295.0 27.2 %collective-permute-start.33 = (bf16[256,1152]{1,0:T(8,128)(2,1)}, bf16[256,1152]{1,0:T(8,128)(2,1)}, u32[]{:S(2)}, u32[]{:S(2)}) collective-permute-start(bf16[256,1152]{1,0:T(8,128)(2,1)} %get-tuple-element.271), channel_id=1, source_target_pairs={{0,4},{1,5},{2,6},{3,7},{4,0},{5,1},{6,2},{7,3},{8,12},{9,13},{10,... | collective-permute-start | bytes 1769480 | tf_op jit(solution)/shard_map/ppermute | solution.py:44
  296.4 26.0 %collective-permute-start.32 = (bf16[256,1152]{1,0:T(8,128)(2,1)S(1)}, bf16[256,1152]{1,0:T(8,128)(2,1)}, u32[]{:S(2)}, u32[]{:S(2)}) collective-permute-start(bf16[256,1152]{1,0:T(8,128)(2,1)S(1)} %get-tuple-element.272), channel_id=1, source_target_pairs={{0,2},{1,3},{2,0},{3,1},{4,6},{5,7},{6,4},{7,5},{8,10},{9,11},{10,... | collective-permute-start | bytes 1769480 | tf_op jit(solution)/shard_map/ppermute | solution.py:44
  324.4 39.0 %collective-permute-start.40 = (bf16[4,3,256,512]{3,2,1,0:T(8,128)(2,1)}, bf16[4,3,256,512]{3,2,1,0:T(8,128)(2,1)}, u32[]{:S(2)}, u32[]{:S(2)}) collective-permute-start(bf16[4,3,256,512]{3,2,1,0:T(8,128)(2,1)} %get-tuple-element.157), channel_id=1, source_target_pairs={{0,1},{1,0},{2,3},{3,2},{4,5},{5,4},{6,7},{7,6},{8,9},{9,8},{10,11... | collective-permute-start | bytes 9437192 | tf_op jit(solution)/shard_map/ppermute | solution.py:44
  369.1 25.9 %collective-permute-start.41 = (bf16[512,1024]{1,0:T(8,128)(2,1)}, bf16[512,1024]{1,0:T(8,128)(2,1)}, u32[]{:S(2)}, u32[]{:S(2)}) collective-permute-start(bf16[512,1024]{1,0:T(8,128)(2,1)} %get-tuple-element.165), channel_id=1, source_target_pairs={{0,2},{1,3},{2,0},{3,1},{4,6},{5,7},{6,4},{7,5},{8,10},{9,11},{10,... | collective-permute-start | bytes 3145736 | tf_op jit(solution)/shard_map/ppermute | solution.py:44
  369.6 25.6 %collective-permute-start.42 = (bf16[512,1024]{1,0:T(8,128)(2,1)}, bf16[512,1024]{1,0:T(8,128)(2,1)}, u32[]{:S(2)}, u32[]{:S(2)}) collective-permute-start(bf16[512,1024]{1,0:T(8,128)(2,1)} %get-tuple-element.166), channel_id=1, source_target_pairs={{0,4},{1,5},{2,6},{3,7},{4,0},{5,1},{6,2},{7,3},{8,12},{9,13},{10,... | collective-permute-start | bytes 3145736 | tf_op jit(solution)/shard_map/ppermute | solution.py:44
  417.5 22.8 %collective-permute-start.46 = (bf16[4,4,32,2176]{3,2,1,0:T(8,128)(2,1)}, bf16[4,4,32,2176]{3,2,1,0:T(8,128)(2,1)}, u32[]{:S(2)}, u32[]{:S(2)}) collective-permute-start(bf16[4,4,32,2176]{3,2,1,0:T(8,128)(2,1)} %dynamic-slice_bitcast_fusion), channel_id=1, source_target_pairs={{0,1},{1,0},{2,3},{3,2},{4,5},{5,4},{6,7},{7,6},{8,9},{9,8},{10,11... | collective-permute-start | bytes 6684680 | tf_op jit(solution)/shard_map/ppermute | solution.py:44
  484.4 21.2 %collective-permute-start.49 = (bf16[128,2176]{1,0:T(8,128)(2,1)S(1)}, bf16[128,2176]{1,0:T(8,128)(2,1)S(1)}, u32[]{:S(2)}, u32[]{:S(2)}) collective-permute-start(bf16[128,2176]{1,0:T(8,128)(2,1)S(1)} %pad_maximum_fusion.13), channel_id=1, source_target_pairs={{0,2},{1,3},{2,0},{3,1},{4,6},{5,7},{6,4},{7,5},{8,10},{9,11},{10,... | collective-permute-start | bytes 1671176 | tf_op jit(solution)/shard_map/ppermute | solution.py:44
  485.7 27.1 %collective-permute-start.61 = (bf16[2,2,3,32,512]{4,3,2,1,0:T(8,128)(2,1)S(1)}, bf16[2,2,3,32,512]{4,3,2,1,0:T(8,128)(2,1)S(1)}, u32[]{:S(2)}, u32[]{:S(2)}) collective-permute-start(bf16[2,2,3,32,512]{4,3,2,1,0:T(8,128)(2,1)S(1)} %get-tuple-element.285), channel_id=1, source_target_pairs={{0,6},{1,7},{2,4},{3,5},{4,2},{5,3},{6,0},{7,1},{8,14},{9,15},{10,... | collective-permute-start | bytes 1179656 | tf_op jit(solution)/shard_map/ppermute | solution.py:44
  (63 other events, 631.5 us)
Sparse Core Ops, SparseCore 0:
  68.3 63.2 all-gather.2
  135.7 60.3 all-gather.4
  290.9 57.0 reduce-scatter.2
  417.7 60.8 reduce-scatter.4

commit v8 on v7

--- a/solution.py
+++ b/solution.py
@@ -56,10 +56,6 @@
             part = lax.dynamic_index_in_dim(terms, self.group ^ bits, 0, keepdims=False)
             total = total + self.swap(part.astype(bf16), bits * MEMBERS).astype(f32)
         return total
-
-    def cross_of(self, near, far):
-        half = near.shape[0] // 2
-        return self.swap(near[:half], 4), self.swap(far[half:], 2)
 
     def send_cross(self, block):
         half = block.shape[0] // 2
@@ -93,11 +89,12 @@
         other = self.swap(lax.dynamic_index_in_dim(arrived, 1 - core, 1, keepdims=False), 1)
         return kept, other
 
-    def in_order(self, kept, other):
+    def send_parts(self, parts):
+        kept, other = self.keep_parts(self.chip_parts(parts))
         core = self.member % 2
         even = jnp.where(core == 0, kept, other)
         odd = jnp.where(core == 0, other, kept)
-        return jnp.stack([even, odd], axis=1).reshape((MEMBERS,) + kept.shape[1:])
+        return jnp.stack([even, odd], axis=1).reshape(parts.shape)
 
 
 def dot(left, right):
@@ -716,7 +713,12 @@
 
     mine = jnp.stack([gate_weight, up_weight, down_weight.transpose(0, 2, 1)], axis=1)
     mine = mine.reshape(MEMBERS, LOCAL_EXPERTS, 3, shard, hidden)
-    arrived = links.chip_parts(mine)
+    shelf = links.send_parts(mine).transpose(1, 2, 0, 3, 4)
+    shelf = shelf.reshape(LOCAL_EXPERTS, 3, MEMBERS * shard, hidden)
+    lines = [[m + MEMBERS * g for g in range(groups)] for m in range(MEMBERS)]
+    own_full = [
+        lax.all_gather(shelf[n], "fsdp", axis_index_groups=lines) for n in range(LOCAL_EXPERTS)
+    ]
 
     packed = jnp.concatenate(
         [
@@ -733,24 +735,13 @@
     )
     pack_width = packed.shape[1]
     column = links.direct_gather(packed).reshape(groups * shard, pack_width)
-    arrived, column = lax.optimization_barrier((arrived, column))
     half = column.shape[0] // 2
-    top, low = column[:half], column[half:]
-    near_top, far_low = links.swap(top, 2), links.swap(low, 4)
-    near_low, far_top = links.swap(low, 2), links.swap(top, 4)
-    kept, other = links.keep_parts(arrived)
-    kept, other, near_top, far_low = lax.optimization_barrier((kept, other, near_top, far_low))
-    shelf = links.in_order(kept, other).transpose(1, 2, 0, 3, 4)
-    shelf = shelf.reshape(LOCAL_EXPERTS, 3, MEMBERS * shard, hidden)
+    near_top, far_low = links.swap(column[:half], 2), links.swap(column[half:], 4)
+    near_low, far_top = links.swap(column[half:], 2), links.swap(column[:half], 4)
     cross_top, cross_low = links.swap(near_top, 4), links.swap(far_low, 2)
-    top, low, near_top = lax.optimization_barrier((top, low, near_top))
     spread = {
-        0: (top, low), 2: (near_top, near_low), 4: (far_top, far_low), 6: (cross_top, cross_low)
+        0: (column,), 2: (near_top, near_low), 4: (far_top, far_low), 6: (cross_top, cross_low)
     }
-    lines = [[m + MEMBERS * g for g in range(groups)] for m in range(MEMBERS)]
-    own_full = [
-        lax.all_gather(shelf[n], "fsdp", axis_index_groups=lines) for n in range(LOCAL_EXPERTS)
-    ]
     whole = jnp.zeros((groups, MEMBERS, shard, pack_width), bf16)
     for k in range(MEMBERS):
         parts = spread[k & 6]
@@ -768,13 +759,13 @@
 
     tables = rope_lanes(row_count)
     rotated, mixed, logs = attention_forward(tokens, lengths, tables, gains, whole)
-    cot_near, cot_far, mixed = lax.optimization_barrier((cot_near, cot_far, mixed))
+    half = row_count // 2
+    cot_cross = cot_near[:half], cot_far[half:]
+    cot_cross, mixed = lax.optimization_barrier((cot_cross, mixed))
+    cot_cross = links.swap(cot_cross[0], 4), links.swap(cot_cross[1], 2)
     packet, middle, shares = router_forward(tokens, routes, gains, mixed, whole)
     near, far = links.swap(packet, 2), links.swap(packet, 4)
-    own_full[0], packet, cot_near, cot_far = lax.optimization_barrier(
-        (own_full[0], packet, cot_near, cot_far)
-    )
-    cot_cross = links.cross_of(cot_near, cot_far)
+    own_full[0], packet = lax.optimization_barrier((own_full[0], packet))
 
     names = [
         jnp.stack([member, member ^ 1]).astype(jnp.int32) * LOCAL_EXPERTS + n
@@ -784,25 +775,23 @@
     first_full = own_full[0], links.swap(own_full[0], 1)
     own_out, own_back, *zero = run_experts(names[0], *rows_own, first_full)
     near, far, cot_cross, own_back = lax.optimization_barrier((near, far, cot_cross, own_back))
-    cross = links.cross_of(near, far)
+    cross = links.swap(near[:half], 4), links.swap(far[half:], 2)
     rows_chips = [cross, (near,), (far,)], [cot_cross, (cot_near,), (cot_far,)]
     chip_out, chip_back, *zero = run_experts(names[0], *rows_chips, first_full, zero, True)
     own_full[1], chip_back = lax.optimization_barrier((own_full[1], chip_back))
     second_full = own_full[1], links.swap(own_full[1], 1)
+
+    def join_cores(own, other):
+        return (own.astype(f32) + links.swap(other, 1).astype(f32)).astype(bf16)
+
+    def reduce_groups(total):
+        return lax.psum_scatter(total, "fsdp", scatter_dimension=0, axis_index_groups=lines)
+
+    zero, chip_out = lax.optimization_barrier((join_cores(*zero), chip_out))
+    shelf_zero = reduce_groups(zero)
     chip_out, chip_back, *one = run_experts(
         names[1], *rows_chips, second_full, None, False, (chip_out, chip_back)
     )
-
-    def join_cores(own, other):
-        return (own.astype(f32) + links.swap(other, 1).astype(f32)).astype(bf16)
-
-    def reduce_groups(total):
-        return lax.psum_scatter(total, "fsdp", scatter_dimension=0, axis_index_groups=lines)
-
-    zero = join_cores(*zero)
-    zero, chip_back = lax.optimization_barrier((zero, chip_back))
-    shelf_zero = reduce_groups(zero)
-    half = row_count // 2
     cross_top, cross_low = links.send_cross(chip_back[0])
     near_top, far_low = links.swap(chip_back[1, :half], 2), links.swap(chip_back[2, half:], 4)
     own_out, own_back, *one = run_experts(
@@ -817,7 +806,8 @@
     near_low, far_top = links.swap(near_low, 2), links.swap(far_top, 4)
     one = join_cores(*one)
     back_pieces = near_top, near_low, far_top, far_low
-    out_cross, back_pieces = lax.optimization_barrier((chip_out[0], back_pieces))
+    out_cross, one, back_pieces = lax.optimization_barrier((chip_out[0], one, back_pieces))
+    shelf_one = reduce_groups(one)
     out_cross = links.send_cross(out_cross)
 
     core, chip = member % 2, member // 2
@@ -842,45 +832,40 @@
     def pack_add(parts, cross):
         return links.add_cross(parts[1].astype(bf16), parts[2].astype(bf16), cross)
 
-    def pack_end(parts, near, far):
+    def pack_sum(parts, near, far):
         near, far = links.swap(near, 2), links.swap(far, 4)
-        total = parts[0] + near.astype(f32) + far.astype(f32)
-        return links.direct_reduce(total.reshape(groups, shard, total.shape[1]))
+        return parts[0] + near.astype(f32) + far.astype(f32)
 
     middle_grad, mixed_grad, first_pack = middle_back(
         (own_back[0], *back_pieces), packet, middle, cotangent, shares, gains, mixed, whole
     )
     out_near, out_far = links.add_cross(chip_out[1], chip_out[2], out_cross)
-    out_near, out_far, one, mixed_grad = lax.optimization_barrier(
-        (out_near, out_far, one, mixed_grad)
-    )
-    shelf_one = reduce_groups(one)
+    out_near, out_far, mixed_grad = lax.optimization_barrier((out_near, out_far, mixed_grad))
     out_near, out_far = links.swap(out_near, 2), links.swap(out_far, 4)
     first_parts = pack_cores(first_pack)
     projected_grad = attention_back(lengths, rotated, mixed_grad, logs, tables)
-    out_near, out_far, shelf_zero, first_parts, projected_grad = lax.optimization_barrier(
-        (out_near, out_far, shelf_zero, first_parts, projected_grad)
+    shelf_zero, first_parts, projected_grad = lax.optimization_barrier(
+        (shelf_zero, first_parts, projected_grad)
     )
     first_cross = pack_cross(first_parts)
     grad_tokens, second_pack = inputs_back(tokens, gains, projected_grad, whole, middle_grad)
     first_near, first_far = pack_add(first_parts, first_cross)
-    first_near, first_far, second_pack = lax.optimization_barrier(
-        (first_near, first_far, second_pack)
+    first_near, first_far, second_pack, out_near, out_far, shelf_one = lax.optimization_barrier(
+        (first_near, first_far, second_pack, out_near, out_far, shelf_one)
     )
     second_parts = pack_cores(second_pack)
-    first_total = pack_end(first_parts, first_near, first_far)
+    first_sum = pack_sum(first_parts, first_near, first_far)
     second_near, second_far = pack_add(second_parts, pack_cross(second_parts))
-    second_near, second_far, shelf_one = lax.optimization_barrier(
-        (second_near, second_far, shelf_one)
-    )
-    second_total = pack_end(second_parts, second_near, second_far)
+    second_sum = pack_sum(second_parts, second_near, second_far)
+    pack_total = jnp.concatenate([second_sum, first_sum], axis=1)
+    pack_total = links.direct_reduce(pack_total.reshape(groups, shard, pack_total.shape[1]))
+    second_total = pack_total[:, : second_sum.shape[1]]
+    first_total = pack_total[:, second_sum.shape[1] :]
     out_pieces = (own_out[0], out_near, out_far)
     layer_out = (middle + sum(piece.astype(f32) for piece in out_pieces)).astype(bf16)
     shelf_grad = jnp.stack([shelf_zero, shelf_one])
     shelf_grad = shelf_grad.reshape(LOCAL_EXPERTS, 3, MEMBERS, shard, hidden)
-    expert_shards = links.in_order(
-        *links.keep_parts(links.chip_parts(shelf_grad.transpose(2, 0, 1, 3, 4)))
-    ).astype(f32)
+    expert_shards = links.send_parts(shelf_grad.transpose(2, 0, 1, 3, 4)).astype(f32)
     expert_shards = expert_shards.reshape(EXPERTS, 3, shard, hidden)
     return (
         layer_out,

time: 541 us -> 497 us (0.919)
  waiting for transfers between devices: 171 us -> 140 us
  local copies, waits for them, and re-layouts: 56 us -> 47.4 us
    reduce_scatter x2, waiting for transfers between devices: 24.6 us -> 0.04 us  [reduce_groups(): lax.psum_scatter(total, 'fsdp', scatter_dimension=0, axis_index_groups=li...]
    ppermute x63 -> x59, waiting for transfers between devices: 141 us -> 128 us  [swap(): lax.ppermute(value, 'fsdp', [(i, i ^ bits) for i in range(self.count)])]
    all_gather x2, waiting for transfers between devices: 4.62 us -> 11.6 us  [local(): lax.all_gather(shelf[n], 'fsdp', axis_index_groups=lines)]
    ppermute x63 -> x59, starting transfers between devices: 56.8 us -> 55.3 us  [swap(): lax.ppermute(value, 'fsdp', [(i, i ^ bits) for i in range(self.count)])]
  transfers between devices with their start and end apart: 67 -> 63, of which waited for: 33 -> 25; matrix products, arithmetic and copies ran while one was open for 15% -> 14% of each run, Pallas kernels for 29% -> 41%
where the time goes in v8:
time: 497 us; the launch traced here: 488 us
  Pallas kernels  198 us (40%)
  waiting for transfers between devices  140 us (28%)
  starting transfers between devices  55.6 us (11%)
  local copies, waits for them, and re-layouts  47.4 us (10%)
  other arithmetic  31.8 us (6%)
  between operations  15.8 us (3%)
    ppermute x59, waiting for transfers between devices, swap(): lax.ppermute(value, 'fsdp', [(i, i ^ bits) for i in range(self.count)])  128 us
    pallas_call x4, Pallas kernels, run_experts(): pl.pallas_call(functools.partial(expert_kernel, layout=layout, fresh=fres...  125 us
    pallas_call x5, Pallas kernels, call_kernel(): pl.pallas_call(body, grid=(1,), in_specs=specs, out_specs=[pl.BlockSpec(o...  72.5 us
    ppermute x59, starting transfers between devices, swap(): lax.ppermute(value, 'fsdp', [(i, i ^ bits) for i in range(self.count)])  55.3 us
    all_gather x2, waiting for transfers between devices, local(): lax.all_gather(shelf[n], 'fsdp', axis_index_groups=lines)  11.6 us
  transfers between devices with their start and end apart: 63, of which 25 were waited for; matrix products, arithmetic and copies ran while one was open for 14% of the time, Pallas kernels for 41%

profile of v8, /device:TPU:0, one launch (start us, length us, event | category | flops | bytes accessed | tf_op | source)
XLA Modules:
  0.0 488.1 jit_solution(12460594774879489835)
XLA Ops:
  25.3 6.0 %collective-permute-done.1 = bf16[32,3200]{1,0:T(8,128)(2,1)S(1)} collective-permute-done((bf16[32,3200]{1,0:T(8,128)(2,1)S(1)}, bf16[32,3200]{1,0:T(8,128)(2,1)S(1)}, u32[]{:S(2)}, u32[]{:S(2)}) %collective-permute-start.1) | collective-permute-done | bytes 204832 | tf_op jit(solution)/shard_map/ppermute | solution.py:44
  48.3 7.1 %collective-permute-done.4 = bf16[64,3200]{1,0:T(8,128)(2,1)} collective-permute-done((bf16[64,3200]{1,0:T(8,128)(2,1)S(1)}, bf16[64,3200]{1,0:T(8,128)(2,1)}, u32[]{:S(2)}, u32[]{:S(2)}) %collective-permute-start.4) | collective-permute-done | bytes 409632 | tf_op jit(solution)/shard_map/ppermute | solution.py:44
  65.8 4.8 collective-permute-done.13
  86.8 20.3 %attention_forward.1 = (bf16[512,2048]{1,0:T(8,128)(2,1)}, bf16[512,1024]{1,0:T(8,128)(2,1)}, f32[4,4,512]{2,1,0:T(4,128)}) custom-call(s32[1]{0:T(128)S(6)} %copy.169.length_ref, bf16[512,1024]{1,0:T(8,128)(2,1)} %tokens_ref.5, f32[512,256]{1,0:T(8,128)} %copy.124.cosine_ref, f32[512,256]{1,0:T(8,128)} %copy.125.sine_ref, f32[2,1024]{1,0:T(2,128)} %copy.128.gains_ref, ...), custom_call_target="tpu_custom_call" | custom-call | flops 4294967296 | bytes 11837444 | tf_op jit(solution)/shard_map/attention_forward/pallas_call | solution.py:575
  110.1 6.6 %router_forward.1 = (bf16[512,1152]{1,0:T(8,128)(2,1)}, f32[512,1024]{1,0:T(8,128)}, f32[512,128]{1,0:T(8,128)}) custom-call(bf16[512,1024]{1,0:T(8,128)(2,1)} %tokens_ref.5, s32[512,8]{1,0:T(8,128)} %copy.127.routes_ref, f32[2,1024]{1,0:T(2,128)} %copy.128.gains_ref, bf16[512,1024]{1,0:T(8,128)(2,1)} %get-tuple-element.88.mixed_ref, ...), custom_call_target="tpu_custom_call" | custom-call | flops 1073741824 | bytes 18767872 | tf_op jit(solution)/shard_map/router_forward/pallas_call | solution.py:575
  116.6 11.5 %all-gather.3.cloned.1.call-done.refs_2_.refs_8_ = bf16[4,3,256,512]{3,2,1,0:T(8,128)(2,1)} async-done(((bf16[1,3,256,512]{3,2,1,0:T(8,128)(2,1)}), bf16[4,3,256,512]{3,2,1,0:T(8,128)(2,1)}) %all-gather.3.cloned.1.call-update) | async-done | bytes 3145744 | tf_op jit(solution)/shard_map/all_gather | solution.py:720
  134.2 18.7 %experts.4 = (bf16[1,512,1024]{2,1,0:T(8,128)(2,1)}, bf16[1,512,1152]{2,1,0:T(8,128)(2,1)}, f32[3,1024,512]{2,1,0:T(8,128)}, f32[3,1024,512]{2,1,0:T(8,128)}) custom-call(s32[2]{0:T(128)} %get-tuple-element.233.names_ref, bf16[512,1152]{1,0:T(8,128)(2,1)} %get-tuple-element.91.refs_0_.packet_ref, bf16[512,1024]{1,0:T(8,128)(2,1)} %cotangent_ref.1, ...), custom_call_target="tpu_custom_call" | custom-call | flops 9663676416 | bytes 23068672 | tf_op jit(solution)/shard_map/experts/pallas_call | solution.py:283
  152.9 16.3 %collective-permute-done.24.refs_4_ = bf16[256,1024]{1,0:T(8,128)(2,1)S(1)} collective-permute-done((bf16[256,1024]{1,0:T(8,128)(2,1)S(1)}, bf16[256,1024]{1,0:T(8,128)(2,1)S(1)}, u32[]{:S(2)}, u32[]{:S(2)}) %collective-permute-start.24) | collective-permute-done | bytes 524320 | tf_op jit(solution)/shard_map/ppermute | solution.py:44
  174.4 11.5 %collective-permute-done.27.refs_0_ = bf16[256,1152]{1,0:T(8,128)(2,1)S(1)} collective-permute-done((bf16[256,1152]{1,0:T(8,128)(2,1)S(1)}, bf16[256,1152]{1,0:T(8,128)(2,1)S(1)}, u32[]{:S(2)}, u32[]{:S(2)}) %collective-permute-start.27) | collective-permute-done | bytes 589856 | tf_op jit(solution)/shard_map/ppermute | solution.py:44
  189.1 42.3 %experts.5 = (bf16[3,512,1024]{2,1,0:T(8,128)(2,1)}, bf16[3,512,1152]{2,1,0:T(8,128)(2,1)}, bf16[4,3,256,512]{3,2,1,0:T(8,128)(2,1)}, bf16[4,3,256,512]{3,2,1,0:T(8,128)(2,1)}) custom-call(s32[2]{0:T(128)} %get-tuple-element.233.names_ref, bf16[256,1152]{1,0:T(8,128)(2,1)} %copy-done.13, bf16[256,1152]{1,0:T(8,128)(2,1)} %copy-done.14, ...), custom_call_target="tpu_custom_call" | custom-call | flops 28991029248 | bytes 31457280 | tf_op jit(solution)/shard_map/experts/pallas_call | solution.py:283
  232.1 8.8 %collective-permute-done.30 = bf16[4,3,256,512]{3,2,1,0:T(8,128)(2,1)S(1)} collective-permute-done((bf16[4,3,256,512]{3,2,1,0:T(8,128)(2,1)}, bf16[4,3,256,512]{3,2,1,0:T(8,128)(2,1)S(1)}, u32[]{:S(2)}, u32[]{:S(2)}) %collective-permute-start.30) | collective-permute-done | bytes 3145760 | tf_op jit(solution)/shard_map/ppermute | solution.py:44
  240.8 4.6 add_convert_fusion.1
  245.5 43.1 %experts.6 = (bf16[3,512,1024]{2,1,0:T(8,128)(2,1)}, bf16[3,512,1152]{2,1,0:T(8,128)(2,1)}, f32[3,1024,512]{2,1,0:T(8,128)}, f32[3,1024,512]{2,1,0:T(8,128)}) custom-call(s32[2]{0:T(128)} %get-tuple-element.232.names_ref, bf16[256,1152]{1,0:T(8,128)(2,1)} %copy-done.13, bf16[256,1152]{1,0:T(8,128)(2,1)} %copy-done.14, ...), custom_call_target="tpu_custom_call" | custom-call | flops 28991029248 | bytes 31457280 | tf_op jit(solution)/shard_map/experts/pallas_call | solution.py:283
  295.6 21.2 %experts.7 = (bf16[1,512,1024]{2,1,0:T(8,128)(2,1)}, bf16[1,512,1152]{2,1,0:T(8,128)(2,1)}, bf16[4,3,256,512]{3,2,1,0:T(8,128)(2,1)}, bf16[4,3,256,512]{3,2,1,0:T(8,128)(2,1)}) custom-call(s32[2]{0:T(128)} %get-tuple-element.232.names_ref, bf16[512,1152]{1,0:T(8,128)(2,1)} %get-tuple-element.91.refs_0_.packet_ref, bf16[512,1024]{1,0:T(8,128)(2,1)} %cotangent_ref.1, ...), custom_call_target="tpu_custom_call" | custom-call | flops 9663676416 | bytes 23068672 | tf_op jit(solution)/shard_map/experts/pallas_call | solution.py:283
  331.8 7.4 %collective-permute-done.36.near_low_ref = bf16[256,1152]{1,0:T(8,128)(2,1)S(1)} collective-permute-done((bf16[256,1152]{1,0:T(8,128)(2,1)}, bf16[256,1152]{1,0:T(8,128)(2,1)S(1)}, u32[]{:S(2)}, u32[]{:S(2)}) %collective-permute-start.36) | collective-permute-done | bytes 589856 | tf_op jit(solution)/shard_map/ppermute | solution.py:44
  342.6 12.0 %middle_back.1 = (f32[512,1024]{1,0:T(8,128)}, bf16[512,1024]{1,0:T(8,128)(2,1)}, bf16[1024,1152]{1,0:T(8,128)(2,1)}) custom-call(bf16[512,1152]{1,0:T(8,128)(2,1)} %bitcast.221, bf16[256,1152]{1,0:T(8,128)(2,1)} %copy-done.6, bf16[256,1152]{1,0:T(8,128)(2,1)} %copy-done.8, bf16[256,1152]{1,0:T(8,128)(2,1)} %copy-done.9, bf16[256,1152]{1,0:T(8,128)(2,1)} %copy-done.7, ...), custom_call_target="tpu_custom_call" | custom-call | flops 2147483648 | bytes 27795456 | tf_op jit(solution)/shard_map/middle_back/pallas_call | solution.py:575
  364.5 18.8 %attention_back.1.projected_ref = bf16[512,2048]{1,0:T(8,128)(2,1)} custom-call(s32[1]{0:T(128)S(6)} %copy.169.length_ref, bf16[512,2048]{1,0:T(8,128)(2,1)} %get-tuple-element.135.rotated_ref, bf16[512,1024]{1,0:T(8,128)(2,1)} %get-tuple-element.138.mixed_grad_ref, f32[4,4,512]{2,1,0:T(4,128)} %get-tuple-element.139.log_ref, f32[512,256]{1,0:T(8,128)} %copy.124.cosine_ref, ...), custom_call_target="tpu_custom_call" | custom-call | flops 2684354560 | bytes 6324228 | tf_op jit(solution)/shard_map/attention_back/pallas_call | solution.py:575
  386.3 14.7 %inputs_back.1 = (f32[512,1024]{1,0:T(8,128)}, bf16[1024,2176]{1,0:T(8,128)(2,1)}) custom-call(bf16[512,1024]{1,0:T(8,128)(2,1)} %tokens_ref.5, f32[2,1024]{1,0:T(2,128)} %copy.128.gains_ref, bf16[512,2048]{1,0:T(8,128)(2,1)} %attention_back.1.projected_ref, bf16[1024,3200]{1,0:T(8,128)(2,1)} %bitcast.196, f32[512,1024]{1,0:T(8,128)} %get-tuple-element.144.middle_grad_ref), custom_call_target="tpu_custom_call" | custom-call | flops 4294967296 | bytes 18358272 | tf_op jit(solution)/shard_map/inputs_back/pallas_call | solution.py:575
  408.8 7.3 %collective-permute-done.55 = bf16[2,2,3,32,512]{4,3,2,1,0:T(8,128)(2,1)S(1)} collective-permute-done((bf16[2,2,3,32,512]{4,3,2,1,0:T(8,128)(2,1)S(1)}, bf16[2,2,3,32,512]{4,3,2,1,0:T(8,128)(2,1)S(1)}, u32[]{:S(2)}, u32[]{:S(2)}) %collective-permute-start.55) | collective-permute-done | bytes 393248 | tf_op jit(solution)/shard_map/ppermute | solution.py:44
  418.5 11.8 %collective-permute-done.57 = bf16[2,2,3,32,512]{4,3,2,1,0:T(8,128)(2,1)S(1)} collective-permute-done((bf16[2,2,3,32,512]{4,3,2,1,0:T(8,128)(2,1)S(1)}, bf16[2,2,3,32,512]{4,3,2,1,0:T(8,128)(2,1)S(1)}, u32[]{:S(2)}, u32[]{:S(2)}) %collective-permute-start.57) | collective-permute-done | bytes 393248 | tf_op jit(solution)/shard_map/ppermute | solution.py:44
  437.1 7.0 %collective-permute-done.48 = bf16[64,2176]{1,0:T(8,128)(2,1)S(1)} collective-permute-done((bf16[64,2176]{1,0:T(8,128)(2,1)S(1)}, bf16[64,2176]{1,0:T(8,128)(2,1)S(1)}, u32[]{:S(2)}, u32[]{:S(2)}) %collective-permute-start.48) | collective-permute-done | bytes 278560 | tf_op jit(solution)/shard_map/ppermute | solution.py:44
  447.3 11.2 %collective-permute-done.49 = bf16[128,2176]{1,0:T(8,128)(2,1)S(1)} collective-permute-done((bf16[128,2176]{1,0:T(8,128)(2,1)S(1)}, bf16[128,2176]{1,0:T(8,128)(2,1)S(1)}, u32[]{:S(2)}, u32[]{:S(2)}) %collective-permute-start.49) | collective-permute-done | bytes 557088 | tf_op jit(solution)/shard_map/ppermute | solution.py:44
  465.8 3.9 collective-permute-done.54
  469.7 8.6 %collective-permute-done.53 = bf16[32,3328]{1,0:T(8,128)(2,1)S(1)} collective-permute-done((bf16[32,3328]{1,0:T(8,128)(2,1)S(1)}, bf16[32,3328]{1,0:T(8,128)(2,1)S(1)}, u32[]{:S(2)}, u32[]{:S(2)}) %collective-permute-start.53) | collective-permute-done | bytes 213024 | tf_op jit(solution)/shard_map/ppermute | solution.py:44
  (264 shorter events, 146.8 us)
Async XLA Ops:
  7.2 121.0 %all-gather.3.cloned.1.call-start = ((), (), s32[]{:S(2)}) async-start(), calls=%async_computation.2 | async-start | bytes 3932160 | tf_op jit(solution)/shard_map/all_gather | solution.py:720
  20.5 18.5 %collective-permute-start.19 = (bf16[2,2,3,32,512]{4,3,2,1,0:T(8,128)(2,1)}, bf16[2,2,3,32,512]{4,3,2,1,0:T(8,128)(2,1)}, u32[]{:S(2)}, u32[]{:S(2)}) collective-permute-start(bf16[2,2,3,32,512]{4,3,2,1,0:T(8,128)(2,1)} %get-tuple-element.266), channel_id=1, source_target_pairs={{0,4},{1,5},{2,6},{3,7},{4,0},{5,1},{6,2},{7,3},{8,12},{9,13},{10,... | collective-permute-start | bytes 1179656 | tf_op jit(solution)/shard_map/ppermute | solution.py:44
  25.0 18.4 %collective-permute-start.20 = (bf16[2,2,3,32,512]{4,3,2,1,0:T(8,128)(2,1)}, bf16[2,2,3,32,512]{4,3,2,1,0:T(8,128)(2,1)S(1)}, u32[]{:S(2)}, u32[]{:S(2)}) collective-permute-start(bf16[2,2,3,32,512]{4,3,2,1,0:T(8,128)(2,1)} %get-tuple-element.265), channel_id=1, source_target_pairs={{0,6},{1,7},{2,4},{3,5},{4,2},{5,3},{6,0},{7,1},{8,14},{9,15},{10,... | collective-permute-start | bytes 1179656 | tf_op jit(solution)/shard_map/ppermute | solution.py:44
  33.0 23.5 %collective-permute-start.9 = (bf16[64,3200]{1,0:T(8,128)(2,1)S(1)}, bf16[64,3200]{1,0:T(8,128)(2,1)S(1)}, u32[]{:S(2)}, u32[]{:S(2)}) collective-permute-start(bf16[64,3200]{1,0:T(8,128)(2,1)S(1)} %bitcast.238), channel_id=1, source_target_pairs={{0,4},{1,5},{2,6},{3,7},{4,0},{5,1},{6,2},{7,3},{8,12},{9,13},{10,... | collective-permute-start | bytes 1228808 | tf_op jit(solution)/shard_map/ppermute | solution.py:44
  35.1 20.3 %collective-permute-start.4 = (bf16[64,3200]{1,0:T(8,128)(2,1)S(1)}, bf16[64,3200]{1,0:T(8,128)(2,1)}, u32[]{:S(2)}, u32[]{:S(2)}) collective-permute-start(bf16[64,3200]{1,0:T(8,128)(2,1)S(1)} %bitcast.235), channel_id=1, source_target_pairs={{0,2},{1,3},{2,0},{3,1},{4,6},{5,7},{6,4},{7,5},{8,10},{9,11},{10,... | collective-permute-start | bytes 1228808 | tf_op jit(solution)/shard_map/ppermute | solution.py:44
  64.7 166.8 %all-gather.5.cloned.1.call-start = ((), (), s32[]{:S(2)}) async-start(), calls=%async_computation.3 | async-start | bytes 3932160 | tf_op jit(solution)/shard_map/all_gather | solution.py:720
  78.9 28.3 %collective-permute-start.16 = (bf16[512,1024]{1,0:T(8,128)(2,1)S(1)}, bf16[512,1024]{1,0:T(8,128)(2,1)}, u32[]{:S(2)}, u32[]{:S(2)}) collective-permute-start(bf16[512,1024]{1,0:T(8,128)(2,1)S(1)} %copy-done.3), channel_id=1, source_target_pairs={{0,2},{1,3},{2,0},{3,1},{4,6},{5,7},{6,4},{7,5},{8,10},{9,11},{10,... | collective-permute-start | bytes 3145736 | tf_op jit(solution)/shard_map/ppermute | solution.py:44
  79.6 29.5 %collective-permute-start.17 = (bf16[512,1024]{1,0:T(8,128)(2,1)S(1)}, bf16[512,1024]{1,0:T(8,128)(2,1)}, u32[]{:S(2)}, u32[]{:S(2)}) collective-permute-start(bf16[512,1024]{1,0:T(8,128)(2,1)S(1)} %copy-done.3), channel_id=1, source_target_pairs={{0,4},{1,5},{2,6},{3,7},{4,0},{5,1},{6,2},{7,3},{8,12},{9,13},{10,... | collective-permute-start | bytes 3145736 | tf_op jit(solution)/shard_map/ppermute | solution.py:44
  128.2 41.0 %collective-permute-start.22 = (bf16[512,1152]{1,0:T(8,128)(2,1)}, bf16[512,1152]{1,0:T(8,128)(2,1)}, u32[]{:S(2)}, u32[]{:S(2)}) collective-permute-start(bf16[512,1152]{1,0:T(8,128)(2,1)} %get-tuple-element.91.refs_0_.packet_ref), channel_id=1, source_target_pairs={{0,2},{1,3},{2,0},{3,1},{4,6},{5,7},{6,4},{7,5},{8,10},{9,11},{10,... | collective-permute-start | bytes 3538952 | tf_op jit(solution)/shard_map/ppermute | solution.py:44
  129.7 39.6 %collective-permute-start.23 = (bf16[512,1152]{1,0:T(8,128)(2,1)}, bf16[512,1152]{1,0:T(8,128)(2,1)}, u32[]{:S(2)}, u32[]{:S(2)}) collective-permute-start(bf16[512,1152]{1,0:T(8,128)(2,1)} %get-tuple-element.91.refs_0_.packet_ref), channel_id=1, source_target_pairs={{0,4},{1,5},{2,6},{3,7},{4,0},{5,1},{6,2},{7,3},{8,12},{9,13},{10,... | collective-permute-start | bytes 3538952 | tf_op jit(solution)/shard_map/ppermute | solution.py:44
  132.1 252.9 %reduce-scatter.3.cloned.1.call-start = ((), (), s32[]{:S(2)}) async-start(), calls=%async_computation.4 | async-start | bytes 3932160 | tf_op jit(solution)/shard_map/reduce_scatter | solution.py:788
  132.9 36.3 %collective-permute-start.24 = (bf16[256,1024]{1,0:T(8,128)(2,1)S(1)}, bf16[256,1024]{1,0:T(8,128)(2,1)S(1)}, u32[]{:S(2)}, u32[]{:S(2)}) collective-permute-start(bf16[256,1024]{1,0:T(8,128)(2,1)S(1)} %copy-done.10), channel_id=1, source_target_pairs={{0,4},{1,5},{2,6},{3,7},{4,0},{5,1},{6,2},{7,3},{8,12},{9,13},{10,... | collective-permute-start | bytes 1572872 | tf_op jit(solution)/shard_map/ppermute | solution.py:44
  133.5 35.7 %collective-permute-start.25 = (bf16[256,1024]{1,0:T(8,128)(2,1)S(1)}, bf16[256,1024]{1,0:T(8,128)(2,1)}, u32[]{:S(2)}, u32[]{:S(2)}) collective-permute-start(bf16[256,1024]{1,0:T(8,128)(2,1)S(1)} %slice.260), channel_id=1, source_target_pairs={{0,2},{1,3},{2,0},{3,1},{4,6},{5,7},{6,4},{7,5},{8,10},{9,11},{10,... | collective-permute-start | bytes 1572872 | tf_op jit(solution)/shard_map/ppermute | solution.py:44
  245.4 155.9 %reduce-scatter.5.cloned.1.call-start = ((), (), s32[]{:S(2)}) async-start(), calls=%async_computation.5 | async-start | bytes 3932160 | tf_op jit(solution)/shard_map/reduce_scatter | solution.py:788
  291.5 25.2 %collective-permute-start.31 = (bf16[256,1152]{1,0:T(8,128)(2,1)}, bf16[256,1152]{1,0:T(8,128)(2,1)}, u32[]{:S(2)}, u32[]{:S(2)}) collective-permute-start(bf16[256,1152]{1,0:T(8,128)(2,1)} %get-tuple-element.242), channel_id=1, source_target_pairs={{0,2},{1,3},{2,0},{3,1},{4,6},{5,7},{6,4},{7,5},{8,10},{9,11},{10,... | collective-permute-start | bytes 1769480 | tf_op jit(solution)/shard_map/ppermute | solution.py:44
  292.4 24.4 %collective-permute-start.32 = (bf16[256,1152]{1,0:T(8,128)(2,1)}, bf16[256,1152]{1,0:T(8,128)(2,1)}, u32[]{:S(2)}, u32[]{:S(2)}) collective-permute-start(bf16[256,1152]{1,0:T(8,128)(2,1)} %get-tuple-element.241), channel_id=1, source_target_pairs={{0,4},{1,5},{2,6},{3,7},{4,0},{5,1},{6,2},{7,3},{8,12},{9,13},{10,... | collective-permute-start | bytes 1769480 | tf_op jit(solution)/shard_map/ppermute | solution.py:44
  292.9 26.9 %collective-permute-start.33 = (bf16[256,1152]{1,0:T(8,128)(2,1)}, bf16[256,1152]{1,0:T(8,128)(2,1)S(1)}, u32[]{:S(2)}, u32[]{:S(2)}) collective-permute-start(bf16[256,1152]{1,0:T(8,128)(2,1)} %get-tuple-element.240), channel_id=1, source_target_pairs={{0,2},{1,3},{2,0},{3,1},{4,6},{5,7},{6,4},{7,5},{8,10},{9,11},{10,... | collective-permute-start | bytes 1769480 | tf_op jit(solution)/shard_map/ppermute | solution.py:44
  294.4 26.0 %collective-permute-start.34 = (bf16[256,1152]{1,0:T(8,128)(2,1)S(1)}, bf16[256,1152]{1,0:T(8,128)(2,1)S(1)}, u32[]{:S(2)}, u32[]{:S(2)}) collective-permute-start(bf16[256,1152]{1,0:T(8,128)(2,1)S(1)} %get-tuple-element.239), channel_id=1, source_target_pairs={{0,4},{1,5},{2,6},{3,7},{4,0},{5,1},{6,2},{7,3},{8,12},{9,13},{10,... | collective-permute-start | bytes 1769480 | tf_op jit(solution)/shard_map/ppermute | solution.py:44
  357.1 26.2 %collective-permute-start.38 = (bf16[4,4,32,1152]{3,2,1,0:T(8,128)(2,1)}, bf16[4,4,32,1152]{3,2,1,0:T(8,128)(2,1)S(1)}, u32[]{:S(2)}, u32[]{:S(2)}) collective-permute-start(bf16[4,4,32,1152]{3,2,1,0:T(8,128)(2,1)} %dynamic-slice_bitcast_fusion.1), channel_id=1, source_target_pairs={{0,1},{1,0},{2,3},{3,2},{4,5},{5,4},{6,7},{7,6},{8,9},{9,8},{10,11... | collective-permute-start | bytes 3538952 | tf_op jit(solution)/shard_map/ppermute | solution.py:44
  361.6 39.7 %collective-permute-start.43 = (bf16[512,1024]{1,0:T(8,128)(2,1)}, bf16[512,1024]{1,0:T(8,128)(2,1)}, u32[]{:S(2)}, u32[]{:S(2)}) collective-permute-start(bf16[512,1024]{1,0:T(8,128)(2,1)} %get-tuple-element.146), channel_id=1, source_target_pairs={{0,2},{1,3},{2,0},{3,1},{4,6},{5,7},{6,4},{7,5},{8,10},{9,11},{10,... | collective-permute-start | bytes 3145736 | tf_op jit(solution)/shard_map/ppermute | solution.py:44
  363.2 38.1 %collective-permute-start.44 = (bf16[512,1024]{1,0:T(8,128)(2,1)}, bf16[512,1024]{1,0:T(8,128)(2,1)}, u32[]{:S(2)}, u32[]{:S(2)}) collective-permute-start(bf16[512,1024]{1,0:T(8,128)(2,1)} %get-tuple-element.147), channel_id=1, source_target_pairs={{0,4},{1,5},{2,6},{3,7},{4,0},{5,1},{6,2},{7,3},{8,12},{9,13},{10,... | collective-permute-start | bytes 3145736 | tf_op jit(solution)/shard_map/ppermute | solution.py:44
  405.8 28.3 %collective-permute-start.45 = (bf16[4,4,32,2176]{3,2,1,0:T(8,128)(2,1)S(1)}, bf16[4,4,32,2176]{3,2,1,0:T(8,128)(2,1)S(1)}, u32[]{:S(2)}, u32[]{:S(2)}) collective-permute-start(bf16[4,4,32,2176]{3,2,1,0:T(8,128)(2,1)S(1)} %dynamic-slice_bitcast_fusion), channel_id=1, source_target_pairs={{0,1},{1,0},{2,3},{3,2},{4,5},{5,4},{6,7},{7,6},{8,9},{9,8},{10,11... | collective-permute-start | bytes 6684680 | tf_op jit(solution)/shard_map/ppermute | solution.py:44
  407.2 26.6 %collective-permute-start.51 = (bf16[128,1152]{1,0:T(8,128)(2,1)S(1)}, bf16[128,1152]{1,0:T(8,128)(2,1)S(1)}, u32[]{:S(2)}, u32[]{:S(2)}) collective-permute-start(bf16[128,1152]{1,0:T(8,128)(2,1)S(1)} %pad_maximum_fusion.15), channel_id=1, source_target_pairs={{0,4},{1,5},{2,6},{3,7},{4,0},{5,1},{6,2},{7,3},{8,12},{9,13},{10,... | collective-permute-start | bytes 884744 | tf_op jit(solution)/shard_map/ppermute | solution.py:44
  407.9 25.9 %collective-permute-start.50 = (bf16[128,1152]{1,0:T(8,128)(2,1)S(1)}, bf16[128,1152]{1,0:T(8,128)(2,1)S(1)}, u32[]{:S(2)}, u32[]{:S(2)}) collective-permute-start(bf16[128,1152]{1,0:T(8,128)(2,1)S(1)} %pad_maximum_fusion.14), channel_id=1, source_target_pairs={{0,2},{1,3},{2,0},{3,1},{4,6},{5,7},{6,4},{7,5},{8,10},{9,11},{10,... | collective-permute-start | bytes 884744 | tf_op jit(solution)/shard_map/ppermute | solution.py:44
  (57 other events, 581.0 us)
Sparse Core Ops, SparseCore 0:
  64.9 63.2 all-gather.2
  132.2 60.3 all-gather.4
  245.6 57.0 reduce-scatter.2
  340.1 57.2 reduce-scatter.4

commit v9 on v8

--- a/solution.py
+++ b/solution.py
@@ -2,6 +2,7 @@
 
 import jax
 import jax.numpy as jnp
+import numpy as np
 from jax import lax
 from jax.experimental import pallas as pl
 from jax.experimental.pallas import tpu as pltpu
@@ -26,10 +27,10 @@
 
 def rope_tables(row_count):
     half_dim = HEAD_DIM // 2
-    frequency = rope_base ** (-2.0 * jnp.arange(half_dim, dtype=jnp.float32) / HEAD_DIM)
-    angles = jnp.arange(row_count, dtype=jnp.float32)[:, None] * frequency[None, :]
-    angles = jnp.concatenate([angles, angles], axis=1)
-    return (jnp.cos(angles), jnp.sin(angles))
+    frequency = rope_base ** (-2.0 * np.arange(half_dim, dtype=np.float32) / np.float32(HEAD_DIM))
+    angles = np.arange(row_count, dtype=np.float32)[:, None] * frequency.astype(np.float32)[None, :]
+    angles = np.concatenate([angles, angles], axis=1)
+    return (np.cos(angles), np.sin(angles))
 
 
 class Exchange:
@@ -89,12 +90,11 @@
         other = self.swap(lax.dynamic_index_in_dim(arrived, 1 - core, 1, keepdims=False), 1)
         return kept, other
 
-    def send_parts(self, parts):
-        kept, other = self.keep_parts(self.chip_parts(parts))
+    def in_order(self, kept, other):
         core = self.member % 2
         even = jnp.where(core == 0, kept, other)
         odd = jnp.where(core == 0, other, kept)
-        return jnp.stack([even, odd], axis=1).reshape(parts.shape)
+        return jnp.stack([even, odd], axis=1).reshape((MEMBERS,) + kept.shape[1:])
 
 
 def dot(left, right):
@@ -595,9 +595,9 @@
 def rope_lanes(row_count):
     cosine_table, sine_table = rope_tables(row_count)
     half_dim = HEAD_DIM // 2
-    signed = jnp.concatenate([-sine_table[:, :half_dim], sine_table[:, half_dim:]], axis=1)
+    signed = np.concatenate([-sine_table[:, :half_dim], sine_table[:, half_dim:]], axis=1)
     repeats = TILE // HEAD_DIM
-    return jnp.tile(cosine_table, (1, repeats)), jnp.tile(signed, (1, repeats))
+    return jnp.asarray(np.tile(cosine_table, (1, repeats))), jnp.asarray(np.tile(signed, (1, repeats)))
 
 
 def attention_forward(tokens, lengths, tables, gains, whole):
@@ -711,15 +711,6 @@
     hidden = gate_weight.shape[2]
     head_columns, kv_columns = HEADS * HEAD_DIM, KV_HEADS * HEAD_DIM
 
-    mine = jnp.stack([gate_weight, up_weight, down_weight.transpose(0, 2, 1)], axis=1)
-    mine = mine.reshape(MEMBERS, LOCAL_EXPERTS, 3, shard, hidden)
-    shelf = links.send_parts(mine).transpose(1, 2, 0, 3, 4)
-    shelf = shelf.reshape(LOCAL_EXPERTS, 3, MEMBERS * shard, hidden)
-    lines = [[m + MEMBERS * g for g in range(groups)] for m in range(MEMBERS)]
-    own_full = [
-        lax.all_gather(shelf[n], "fsdp", axis_index_groups=lines) for n in range(LOCAL_EXPERTS)
-    ]
-
     packed = jnp.concatenate(
         [
             query_weight,
@@ -735,6 +726,18 @@
     )
     pack_width = packed.shape[1]
     column = links.direct_gather(packed).reshape(groups * shard, pack_width)
+
+    mine = jnp.stack([gate_weight, up_weight, down_weight.transpose(0, 2, 1)], axis=1)
+    mine = mine.reshape(MEMBERS, LOCAL_EXPERTS, 3, shard, hidden)
+    kept, other = links.keep_parts(links.chip_parts(mine))
+    other, column = lax.optimization_barrier((other, column))
+    shelf = links.in_order(kept, other).transpose(1, 2, 0, 3, 4)
+    shelf = shelf.reshape(LOCAL_EXPERTS, 3, MEMBERS * shard, hidden)
+    lines = [[m + MEMBERS * g for g in range(groups)] for m in range(MEMBERS)]
+    own_full = [
+        lax.all_gather(shelf[n], "fsdp", axis_index_groups=lines) for n in range(LOCAL_EXPERTS)
+    ]
+
     half = column.shape[0] // 2
     near_top, far_low = links.swap(column[:half], 2), links.swap(column[half:], 4)
     near_low, far_top = links.swap(column[half:], 2), links.swap(column[:half], 4)
@@ -765,7 +768,7 @@
     cot_cross = links.swap(cot_cross[0], 4), links.swap(cot_cross[1], 2)
     packet, middle, shares = router_forward(tokens, routes, gains, mixed, whole)
     near, far = links.swap(packet, 2), links.swap(packet, 4)
-    own_full[0], packet = lax.optimization_barrier((own_full[0], packet))
+    own_full[0], cot_cross, packet = lax.optimization_barrier((own_full[0], cot_cross, packet))
 
     names = [
         jnp.stack([member, member ^ 1]).astype(jnp.int32) * LOCAL_EXPERTS + n
@@ -774,7 +777,7 @@
     rows_own = [(packet,)], [(cotangent,)]
     first_full = own_full[0], links.swap(own_full[0], 1)
     own_out, own_back, *zero = run_experts(names[0], *rows_own, first_full)
-    near, far, cot_cross, own_back = lax.optimization_barrier((near, far, cot_cross, own_back))
+    near, far, own_back = lax.optimization_barrier((near, far, own_back))
     cross = links.swap(near[:half], 4), links.swap(far[half:], 2)
     rows_chips = [cross, (near,), (far,)], [cot_cross, (cot_near,), (cot_far,)]
     chip_out, chip_back, *zero = run_experts(names[0], *rows_chips, first_full, zero, True)
@@ -855,18 +858,20 @@
     )
     second_parts = pack_cores(second_pack)
     first_sum = pack_sum(first_parts, first_near, first_far)
+    shelf_grad = jnp.stack([shelf_zero, shelf_one])
+    shelf_grad = shelf_grad.reshape(LOCAL_EXPERTS, 3, MEMBERS, shard, hidden)
+    shelf_grad = shelf_grad.transpose(2, 0, 1, 3, 4)
+    second_parts, shelf_grad = lax.optimization_barrier((second_parts, shelf_grad))
     second_near, second_far = pack_add(second_parts, pack_cross(second_parts))
     second_sum = pack_sum(second_parts, second_near, second_far)
     pack_total = jnp.concatenate([second_sum, first_sum], axis=1)
     pack_total = links.direct_reduce(pack_total.reshape(groups, shard, pack_total.shape[1]))
     second_total = pack_total[:, : second_sum.shape[1]]
     first_total = pack_total[:, second_sum.shape[1] :]
+    expert_shards = links.in_order(*links.keep_parts(links.chip_parts(shelf_grad))).astype(f32)
+    expert_shards = expert_shards.reshape(EXPERTS, 3, shard, hidden)
     out_pieces = (own_out[0], out_near, out_far)
     layer_out = (middle + sum(piece.astype(f32) for piece in out_pieces)).astype(bf16)
-    shelf_grad = jnp.stack([shelf_zero, shelf_one])
-    shelf_grad = shelf_grad.reshape(LOCAL_EXPERTS, 3, MEMBERS, shard, hidden)
-    expert_shards = links.send_parts(shelf_grad.transpose(2, 0, 1, 3, 4)).astype(f32)
-    expert_shards = expert_shards.reshape(EXPERTS, 3, shard, hidden)
     return (
         layer_out,
         grad_tokens,

time: 497 us -> 474 us (0.954)
  local copies, waits for them, and re-layouts: 47.4 us -> 37.6 us
  waiting for transfers between devices: 140 us -> 132 us
  other arithmetic: 31.8 us -> 25.4 us
    all_gather x2, waiting for transfers between devices: 11.6 us -> 0.02 us  [local(): lax.all_gather(shelf[n], 'fsdp', axis_index_groups=lines)]
  transfers between devices with their start and end apart: 63 -> 63, of which waited for: 25 -> 33; matrix products, arithmetic and copies ran while one was open for 14% -> 11% of each run, Pallas kernels for 41% -> 42%
where the time goes in v9:
time: 474 us; the launch traced here: 465 us
  Pallas kernels  198 us (42%)
  waiting for transfers between devices  132 us (28%)
  starting transfers between devices  56.4 us (12%)
  local copies, waits for them, and re-layouts  37.6 us (8%)
  other arithmetic  25.4 us (5%)
  between operations  15.8 us (3%)
    ppermute x59, waiting for transfers between devices, swap(): lax.ppermute(value, 'fsdp', [(i, i ^ bits) for i in range(self.count)])  132 us
    pallas_call x4, Pallas kernels, run_experts(): pl.pallas_call(functools.partial(expert_kernel, layout=layout, fresh=fres...  125 us
    pallas_call x5, Pallas kernels, call_kernel(): pl.pallas_call(body, grid=(1,), in_specs=specs, out_specs=[pl.BlockSpec(o...  72.5 us
    ppermute x59, starting transfers between devices, swap(): lax.ppermute(value, 'fsdp', [(i, i ^ bits) for i in range(self.count)])  56.1 us
  transfers between devices with their start and end apart: 63, of which 33 were waited for; matrix products, arithmetic and copies ran while one was open for 11% of the time, Pallas kernels for 42%

profile of v9, /device:TPU:0, one launch (start us, length us, event | category | flops | bytes accessed | tf_op | source)
XLA Modules:
  0.0 465.3 jit_solution(15854102231862492486)
XLA Ops:
  26.0 5.4 %collective-permute-done.5 = bf16[32,3200]{1,0:T(8,128)(2,1)} collective-permute-done((bf16[32,3200]{1,0:T(8,128)(2,1)S(1)}, bf16[32,3200]{1,0:T(8,128)(2,1)}, u32[]{:S(2)}, u32[]{:S(2)}) %collective-permute-start.5) | collective-permute-done | bytes 204832 | tf_op jit(solution)/shard_map/ppermute | solution.py:45
  33.4 4.2 collective-permute-done.1
  49.0 5.8 %collective-permute-done.9 = bf16[64,3200]{1,0:T(8,128)(2,1)} collective-permute-done((bf16[64,3200]{1,0:T(8,128)(2,1)}, bf16[64,3200]{1,0:T(8,128)(2,1)}, u32[]{:S(2)}, u32[]{:S(2)}) %collective-permute-start.9) | collective-permute-done | bytes 409632 | tf_op jit(solution)/shard_map/ppermute | solution.py:45
  54.7 8.2 %collective-permute-done.8 = bf16[64,3200]{1,0:T(8,128)(2,1)} collective-permute-done((bf16[64,3200]{1,0:T(8,128)(2,1)}, bf16[64,3200]{1,0:T(8,128)(2,1)}, u32[]{:S(2)}, u32[]{:S(2)}) %collective-permute-start.8) | collective-permute-done | bytes 409632 | tf_op jit(solution)/shard_map/ppermute | solution.py:45
  68.8 8.3 %collective-permute-done.17 = bf16[64,3200]{1,0:T(8,128)(2,1)S(1)} collective-permute-done((bf16[64,3200]{1,0:T(8,128)(2,1)S(1)}, bf16[64,3200]{1,0:T(8,128)(2,1)S(1)}, u32[]{:S(2)}, u32[]{:S(2)}) %collective-permute-start.17) | collective-permute-done | bytes 409632 | tf_op jit(solution)/shard_map/ppermute | solution.py:45
  85.1 20.3 %attention_forward.1 = (bf16[512,2048]{1,0:T(8,128)(2,1)}, bf16[512,1024]{1,0:T(8,128)(2,1)}, f32[4,4,512]{2,1,0:T(4,128)}) custom-call(s32[1]{0:T(128)S(6)} %copy.150.length_ref, bf16[512,1024]{1,0:T(8,128)(2,1)} %tokens_ref.5, f32[512,256]{1,0:T(8,128)} %constant.201.clone.cosine_ref, f32[512,256]{1,0:T(8,128)} %constant.202.clone.sine_ref, ...), custom_call_target="tpu_custom_call" | custom-call | flops 4294967296 | bytes 11837444 | tf_op jit(solution)/shard_map/attention_forward/pallas_call | solution.py:575
  112.8 6.5 %router_forward.1 = (bf16[512,1152]{1,0:T(8,128)(2,1)}, f32[512,1024]{1,0:T(8,128)}, f32[512,128]{1,0:T(8,128)}) custom-call(bf16[512,1024]{1,0:T(8,128)(2,1)} %tokens_ref.5, s32[512,8]{1,0:T(8,128)} %copy.115.routes_ref, f32[2,1024]{1,0:T(2,128)} %copy.116.gains_ref, bf16[512,1024]{1,0:T(8,128)(2,1)} %get-tuple-element.96.mixed_ref, ...), custom_call_target="tpu_custom_call" | custom-call | flops 1073741824 | bytes 18767872 | tf_op jit(solution)/shard_map/router_forward/pallas_call | solution.py:575
  130.1 18.2 %experts.4 = (bf16[1,512,1024]{2,1,0:T(8,128)(2,1)}, bf16[1,512,1152]{2,1,0:T(8,128)(2,1)}, f32[3,1024,512]{2,1,0:T(8,128)}, f32[3,1024,512]{2,1,0:T(8,128)}) custom-call(s32[2]{0:T(128)} %get-tuple-element.247.names_ref, bf16[512,1152]{1,0:T(8,128)(2,1)} %get-tuple-element.102.refs_0_.packet_ref, bf16[512,1024]{1,0:T(8,128)(2,1)} %cotangent_ref.1, ...), custom_call_target="tpu_custom_call" | custom-call | flops 9663676416 | bytes 23068672 | tf_op jit(solution)/shard_map/experts/pallas_call | solution.py:283
  148.3 4.4 collective-permute-done.24.refs_2_
  157.1 11.1 %collective-permute-done.27.refs_0_ = bf16[256,1152]{1,0:T(8,128)(2,1)S(1)} collective-permute-done((bf16[256,1152]{1,0:T(8,128)(2,1)S(1)}, bf16[256,1152]{1,0:T(8,128)(2,1)S(1)}, u32[]{:S(2)}, u32[]{:S(2)}) %collective-permute-start.27) | collective-permute-done | bytes 589856 | tf_op jit(solution)/shard_map/ppermute | solution.py:45
  171.1 42.3 %experts.5 = (bf16[3,512,1024]{2,1,0:T(8,128)(2,1)}, bf16[3,512,1152]{2,1,0:T(8,128)(2,1)}, bf16[4,3,256,512]{3,2,1,0:T(8,128)(2,1)}, bf16[4,3,256,512]{3,2,1,0:T(8,128)(2,1)}) custom-call(s32[2]{0:T(128)} %get-tuple-element.247.names_ref, bf16[256,1152]{1,0:T(8,128)(2,1)} %copy-done.14, bf16[256,1152]{1,0:T(8,128)(2,1)} %copy-done.15, ...), custom_call_target="tpu_custom_call" | custom-call | flops 28991029248 | bytes 31457280 | tf_op jit(solution)/shard_map/experts/pallas_call | solution.py:283
  214.0 8.8 %collective-permute-done.30 = bf16[4,3,256,512]{3,2,1,0:T(8,128)(2,1)S(1)} collective-permute-done((bf16[4,3,256,512]{3,2,1,0:T(8,128)(2,1)}, bf16[4,3,256,512]{3,2,1,0:T(8,128)(2,1)S(1)}, u32[]{:S(2)}, u32[]{:S(2)}) %collective-permute-start.30) | collective-permute-done | bytes 3145760 | tf_op jit(solution)/shard_map/ppermute | solution.py:45
  222.8 4.6 add_convert_fusion.1
  227.5 43.4 %experts.6 = (bf16[3,512,1024]{2,1,0:T(8,128)(2,1)}, bf16[3,512,1152]{2,1,0:T(8,128)(2,1)}, f32[3,1024,512]{2,1,0:T(8,128)}, f32[3,1024,512]{2,1,0:T(8,128)}) custom-call(s32[2]{0:T(128)} %get-tuple-element.246.names_ref, bf16[256,1152]{1,0:T(8,128)(2,1)} %copy-done.14, bf16[256,1152]{1,0:T(8,128)(2,1)} %copy-done.15, bf16[512,1152]{1,0:T(8,128)(2,1)} %copy-done.12, ...), custom_call_target="tpu_custom_call" | custom-call | flops 28991029248 | bytes 31457280 | tf_op jit(solution)/shard_map/experts/pallas_call | solution.py:283
  277.8 21.2 %experts.7 = (bf16[1,512,1024]{2,1,0:T(8,128)(2,1)}, bf16[1,512,1152]{2,1,0:T(8,128)(2,1)}, bf16[4,3,256,512]{3,2,1,0:T(8,128)(2,1)}, bf16[4,3,256,512]{3,2,1,0:T(8,128)(2,1)}) custom-call(s32[2]{0:T(128)} %get-tuple-element.246.names_ref, bf16[512,1152]{1,0:T(8,128)(2,1)} %get-tuple-element.102.refs_0_.packet_ref, bf16[512,1024]{1,0:T(8,128)(2,1)} %cotangent_ref.1, ...), custom_call_target="tpu_custom_call" | custom-call | flops 9663676416 | bytes 23068672 | tf_op jit(solution)/shard_map/experts/pallas_call | solution.py:283
  314.0 7.4 %collective-permute-done.36.near_low_ref = bf16[256,1152]{1,0:T(8,128)(2,1)S(1)} collective-permute-done((bf16[256,1152]{1,0:T(8,128)(2,1)}, bf16[256,1152]{1,0:T(8,128)(2,1)S(1)}, u32[]{:S(2)}, u32[]{:S(2)}) %collective-permute-start.36) | collective-permute-done | bytes 589856 | tf_op jit(solution)/shard_map/ppermute | solution.py:45
  324.7 12.2 %middle_back.1 = (f32[512,1024]{1,0:T(8,128)}, bf16[512,1024]{1,0:T(8,128)(2,1)}, bf16[1024,1152]{1,0:T(8,128)(2,1)}) custom-call(bf16[512,1152]{1,0:T(8,128)(2,1)} %bitcast.211, bf16[256,1152]{1,0:T(8,128)(2,1)} %copy-done.8, bf16[256,1152]{1,0:T(8,128)(2,1)} %copy-done.10, bf16[256,1152]{1,0:T(8,128)(2,1)} %copy-done.11, bf16[256,1152]{1,0:T(8,128)(2,1)} %copy-done.9, ...), custom_call_target="tpu_custom_call" | custom-call | flops 2147483648 | bytes 27795456 | tf_op jit(solution)/shard_map/middle_back/pallas_call | solution.py:575
  346.5 18.7 %attention_back.1.projected_ref = bf16[512,2048]{1,0:T(8,128)(2,1)} custom-call(s32[1]{0:T(128)S(6)} %copy.150.length_ref, bf16[512,2048]{1,0:T(8,128)(2,1)} %get-tuple-element.144.rotated_ref, bf16[512,1024]{1,0:T(8,128)(2,1)} %get-tuple-element.147.mixed_grad_ref, f32[4,4,512]{2,1,0:T(4,128)} %get-tuple-element.148.log_ref, ...), custom_call_target="tpu_custom_call" | custom-call | flops 2684354560 | bytes 6324228 | tf_op jit(solution)/shard_map/attention_back/pallas_call | solution.py:575
  368.6 14.7 %inputs_back.1 = (f32[512,1024]{1,0:T(8,128)}, bf16[1024,2176]{1,0:T(8,128)(2,1)}) custom-call(bf16[512,1024]{1,0:T(8,128)(2,1)} %tokens_ref.5, f32[2,1024]{1,0:T(2,128)} %copy.116.gains_ref, bf16[512,2048]{1,0:T(8,128)(2,1)} %attention_back.1.projected_ref, bf16[1024,3200]{1,0:T(8,128)(2,1)} %bitcast.182, f32[512,1024]{1,0:T(8,128)} %get-tuple-element.153.middle_grad_ref), custom_call_target="tpu_custom_call" | custom-call | flops 4294967296 | bytes 18358272 | tf_op jit(solution)/shard_map/inputs_back/pallas_call | solution.py:575
  411.5 12.2 %collective-permute-done.56 = bf16[2,2,3,32,512]{4,3,2,1,0:T(8,128)(2,1)S(1)} collective-permute-done((bf16[2,2,3,32,512]{4,3,2,1,0:T(8,128)(2,1)S(1)}, bf16[2,2,3,32,512]{4,3,2,1,0:T(8,128)(2,1)S(1)}, u32[]{:S(2)}, u32[]{:S(2)}) %collective-permute-start.56) | collective-permute-done | bytes 393248 | tf_op jit(solution)/shard_map/ppermute | solution.py:45
  423.7 9.4 %collective-permute-done.49 = bf16[128,2176]{1,0:T(8,128)(2,1)S(1)} collective-permute-done((bf16[128,2176]{1,0:T(8,128)(2,1)S(1)}, bf16[128,2176]{1,0:T(8,128)(2,1)S(1)}, u32[]{:S(2)}, u32[]{:S(2)}) %collective-permute-start.49) | collective-permute-done | bytes 557088 | tf_op jit(solution)/shard_map/ppermute | solution.py:45
  433.5 3.7 collective-permute-start.54
  438.1 5.4 %collective-permute-done.54 = bf16[32,3328]{1,0:T(8,128)(2,1)S(1)} collective-permute-done((bf16[32,3328]{1,0:T(8,128)(2,1)S(1)}, bf16[32,3328]{1,0:T(8,128)(2,1)S(1)}, u32[]{:S(2)}, u32[]{:S(2)}) %collective-permute-start.54) | collective-permute-done | bytes 213024 | tf_op jit(solution)/shard_map/ppermute | solution.py:45
  443.5 8.2 %collective-permute-done.53 = bf16[32,3328]{1,0:T(8,128)(2,1)S(1)} collective-permute-done((bf16[32,3328]{1,0:T(8,128)(2,1)S(1)}, bf16[32,3328]{1,0:T(8,128)(2,1)S(1)}, u32[]{:S(2)}, u32[]{:S(2)}) %collective-permute-start.53) | collective-permute-done | bytes 213024 | tf_op jit(solution)/shard_map/ppermute | solution.py:45
  (251 shorter events, 144.7 us)
Async XLA Ops:
  7.2 116.9 %all-gather.3.cloned.1.call-start = ((), (), s32[]{:S(2)}) async-start(), calls=%async_computation.2 | async-start | bytes 3932160 | tf_op jit(solution)/shard_map/all_gather | solution.py:738
  13.6 17.8 %collective-permute-start.5 = (bf16[32,3200]{1,0:T(8,128)(2,1)S(1)}, bf16[32,3200]{1,0:T(8,128)(2,1)}, u32[]{:S(2)}, u32[]{:S(2)}) collective-permute-start(bf16[32,3200]{1,0:T(8,128)(2,1)S(1)} %concatenate.44), channel_id=1, source_target_pairs={{0,16},{1,17},{2,18},{3,19},{4,20},{5,21},{6,22},{7,23},{8,24},{9,... | collective-permute-start | bytes 614408 | tf_op jit(solution)/shard_map/ppermute | solution.py:45
  16.2 22.6 %collective-permute-start.6 = (bf16[32,3200]{1,0:T(8,128)(2,1)S(1)}, bf16[32,3200]{1,0:T(8,128)(2,1)}, u32[]{:S(2)}, u32[]{:S(2)}) collective-permute-start(bf16[32,3200]{1,0:T(8,128)(2,1)S(1)} %concatenate.44), channel_id=1, source_target_pairs={{0,24},{1,25},{2,26},{3,27},{4,28},{5,29},{6,30},{7,31},{8,16},{9,... | collective-permute-start | bytes 614408 | tf_op jit(solution)/shard_map/ppermute | solution.py:45
  41.0 24.2 %collective-permute-start.7 = (bf16[128,3200]{1,0:T(8,128)(2,1)S(1)}, bf16[128,3200]{1,0:T(8,128)(2,1)S(1)}, u32[]{:S(2)}, u32[]{:S(2)}) collective-permute-start(bf16[128,3200]{1,0:T(8,128)(2,1)S(1)} %bitcast.184), channel_id=1, source_target_pairs={{0,1},{1,0},{2,3},{3,2},{4,5},{5,4},{6,7},{7,6},{8,9},{9,8},{10,11... | collective-permute-start | bytes 2457608 | tf_op jit(solution)/shard_map/ppermute | solution.py:45
  43.5 19.5 %collective-permute-start.13 = (bf16[64,3200]{1,0:T(8,128)(2,1)}, bf16[64,3200]{1,0:T(8,128)(2,1)S(1)}, u32[]{:S(2)}, u32[]{:S(2)}) collective-permute-start(bf16[64,3200]{1,0:T(8,128)(2,1)} %get-tuple-element.285), channel_id=1, source_target_pairs={{0,4},{1,5},{2,6},{3,7},{4,0},{5,1},{6,2},{7,3},{8,12},{9,13},{10,... | collective-permute-start | bytes 1228808 | tf_op jit(solution)/shard_map/ppermute | solution.py:45
  44.7 18.2 %collective-permute-start.8 = (bf16[64,3200]{1,0:T(8,128)(2,1)}, bf16[64,3200]{1,0:T(8,128)(2,1)}, u32[]{:S(2)}, u32[]{:S(2)}) collective-permute-start(bf16[64,3200]{1,0:T(8,128)(2,1)} %get-tuple-element.284), channel_id=1, source_target_pairs={{0,2},{1,3},{2,0},{3,1},{4,6},{5,7},{6,4},{7,5},{8,10},{9,11},{10,... | collective-permute-start | bytes 1228808 | tf_op jit(solution)/shard_map/ppermute | solution.py:45
  48.3 165.3 %all-gather.5.cloned.1.call-start = ((), (), s32[]{:S(2)}) async-start(), calls=%async_computation.3 | async-start | bytes 3932160 | tf_op jit(solution)/shard_map/all_gather | solution.py:738
  80.9 25.5 %collective-permute-start.20 = (bf16[512,1024]{1,0:T(8,128)(2,1)S(1)}, bf16[512,1024]{1,0:T(8,128)(2,1)}, u32[]{:S(2)}, u32[]{:S(2)}) collective-permute-start(bf16[512,1024]{1,0:T(8,128)(2,1)S(1)} %copy-done.4), channel_id=1, source_target_pairs={{0,2},{1,3},{2,0},{3,1},{4,6},{5,7},{6,4},{7,5},{8,10},{9,11},{10,... | collective-permute-start | bytes 3145736 | tf_op jit(solution)/shard_map/ppermute | solution.py:45
  81.8 26.4 %collective-permute-start.21 = (bf16[512,1024]{1,0:T(8,128)(2,1)S(1)}, bf16[512,1024]{1,0:T(8,128)(2,1)}, u32[]{:S(2)}, u32[]{:S(2)}) collective-permute-start(bf16[512,1024]{1,0:T(8,128)(2,1)S(1)} %copy-done.4), channel_id=1, source_target_pairs={{0,4},{1,5},{2,6},{3,7},{4,0},{5,1},{6,2},{7,3},{8,12},{9,13},{10,... | collective-permute-start | bytes 3145736 | tf_op jit(solution)/shard_map/ppermute | solution.py:45
  124.1 28.6 %collective-permute-start.24 = (bf16[512,1152]{1,0:T(8,128)(2,1)}, bf16[512,1152]{1,0:T(8,128)(2,1)S(1)}, u32[]{:S(2)}, u32[]{:S(2)}) collective-permute-start(bf16[512,1152]{1,0:T(8,128)(2,1)} %get-tuple-element.102.refs_0_.packet_ref), channel_id=1, source_target_pairs={{0,2},{1,3},{2,0},{3,1},{4,6},{5,7},{6,4},{7,5},{8,10},{9,11},{10,... | collective-permute-start | bytes 3538952 | tf_op jit(solution)/shard_map/ppermute | solution.py:45
  125.1 28.3 %collective-permute-start.25 = (bf16[512,1152]{1,0:T(8,128)(2,1)}, bf16[512,1152]{1,0:T(8,128)(2,1)}, u32[]{:S(2)}, u32[]{:S(2)}) collective-permute-start(bf16[512,1152]{1,0:T(8,128)(2,1)} %get-tuple-element.102.refs_0_.packet_ref), channel_id=1, source_target_pairs={{0,4},{1,5},{2,6},{3,7},{4,0},{5,1},{6,2},{7,3},{8,12},{9,13},{10,... | collective-permute-start | bytes 3538952 | tf_op jit(solution)/shard_map/ppermute | solution.py:45
  127.2 239.9 %reduce-scatter.3.cloned.1.call-start = ((), (), s32[]{:S(2)}) async-start(), calls=%async_computation.4 | async-start | bytes 3932160 | tf_op jit(solution)/shard_map/reduce_scatter | solution.py:791
  227.4 156.2 %reduce-scatter.5.cloned.1.call-start = ((), (), s32[]{:S(2)}) async-start(), calls=%async_computation.5 | async-start | bytes 3932160 | tf_op jit(solution)/shard_map/reduce_scatter | solution.py:791
  273.8 25.2 %collective-permute-start.31 = (bf16[256,1152]{1,0:T(8,128)(2,1)}, bf16[256,1152]{1,0:T(8,128)(2,1)}, u32[]{:S(2)}, u32[]{:S(2)}) collective-permute-start(bf16[256,1152]{1,0:T(8,128)(2,1)} %get-tuple-element.256), channel_id=1, source_target_pairs={{0,2},{1,3},{2,0},{3,1},{4,6},{5,7},{6,4},{7,5},{8,10},{9,11},{10,... | collective-permute-start | bytes 1769480 | tf_op jit(solution)/shard_map/ppermute | solution.py:45
  274.6 24.4 %collective-permute-start.32 = (bf16[256,1152]{1,0:T(8,128)(2,1)}, bf16[256,1152]{1,0:T(8,128)(2,1)}, u32[]{:S(2)}, u32[]{:S(2)}) collective-permute-start(bf16[256,1152]{1,0:T(8,128)(2,1)} %get-tuple-element.255), channel_id=1, source_target_pairs={{0,4},{1,5},{2,6},{3,7},{4,0},{5,1},{6,2},{7,3},{8,12},{9,13},{10,... | collective-permute-start | bytes 1769480 | tf_op jit(solution)/shard_map/ppermute | solution.py:45
  275.1 26.9 %collective-permute-start.33 = (bf16[256,1152]{1,0:T(8,128)(2,1)}, bf16[256,1152]{1,0:T(8,128)(2,1)S(1)}, u32[]{:S(2)}, u32[]{:S(2)}) collective-permute-start(bf16[256,1152]{1,0:T(8,128)(2,1)} %get-tuple-element.254), channel_id=1, source_target_pairs={{0,2},{1,3},{2,0},{3,1},{4,6},{5,7},{6,4},{7,5},{8,10},{9,11},{10,... | collective-permute-start | bytes 1769480 | tf_op jit(solution)/shard_map/ppermute | solution.py:45
  276.0 26.5 %collective-permute-start.34 = (bf16[256,1152]{1,0:T(8,128)(2,1)S(1)}, bf16[256,1152]{1,0:T(8,128)(2,1)S(1)}, u32[]{:S(2)}, u32[]{:S(2)}) collective-permute-start(bf16[256,1152]{1,0:T(8,128)(2,1)S(1)} %get-tuple-element.253), channel_id=1, source_target_pairs={{0,4},{1,5},{2,6},{3,7},{4,0},{5,1},{6,2},{7,3},{8,12},{9,13},{10,... | collective-permute-start | bytes 1769480 | tf_op jit(solution)/shard_map/ppermute | solution.py:45
  339.4 25.9 %collective-permute-start.38 = (bf16[4,4,32,1152]{3,2,1,0:T(8,128)(2,1)}, bf16[4,4,32,1152]{3,2,1,0:T(8,128)(2,1)S(1)}, u32[]{:S(2)}, u32[]{:S(2)}) collective-permute-start(bf16[4,4,32,1152]{3,2,1,0:T(8,128)(2,1)} %dynamic-slice_bitcast_fusion.1), channel_id=1, source_target_pairs={{0,1},{1,0},{2,3},{3,2},{4,5},{5,4},{6,7},{7,6},{8,9},{9,8},{10,11... | collective-permute-start | bytes 3538952 | tf_op jit(solution)/shard_map/ppermute | solution.py:45
  343.9 39.6 %collective-permute-start.43 = (bf16[512,1024]{1,0:T(8,128)(2,1)}, bf16[512,1024]{1,0:T(8,128)(2,1)}, u32[]{:S(2)}, u32[]{:S(2)}) collective-permute-start(bf16[512,1024]{1,0:T(8,128)(2,1)} %get-tuple-element.155), channel_id=1, source_target_pairs={{0,2},{1,3},{2,0},{3,1},{4,6},{5,7},{6,4},{7,5},{8,10},{9,11},{10,... | collective-permute-start | bytes 3145736 | tf_op jit(solution)/shard_map/ppermute | solution.py:45
  344.5 39.0 %collective-permute-start.44 = (bf16[512,1024]{1,0:T(8,128)(2,1)}, bf16[512,1024]{1,0:T(8,128)(2,1)}, u32[]{:S(2)}, u32[]{:S(2)}) collective-permute-start(bf16[512,1024]{1,0:T(8,128)(2,1)} %get-tuple-element.156), channel_id=1, source_target_pairs={{0,4},{1,5},{2,6},{3,7},{4,0},{5,1},{6,2},{7,3},{8,12},{9,13},{10,... | collective-permute-start | bytes 3145736 | tf_op jit(solution)/shard_map/ppermute | solution.py:45
  398.6 25.0 %collective-permute-start.56 = (bf16[2,2,3,32,512]{4,3,2,1,0:T(8,128)(2,1)S(1)}, bf16[2,2,3,32,512]{4,3,2,1,0:T(8,128)(2,1)S(1)}, u32[]{:S(2)}, u32[]{:S(2)}) collective-permute-start(bf16[2,2,3,32,512]{4,3,2,1,0:T(8,128)(2,1)S(1)} %get-tuple-element.275), channel_id=1, source_target_pairs={{0,4},{1,5},{2,6},{3,7},{4,0},{5,1},{6,2},{7,3},{8,12},{9,13},{10,... | collective-permute-start | bytes 1179656 | tf_op jit(solution)/shard_map/ppermute | solution.py:45
  400.6 37.3 %collective-permute-start.57 = (bf16[2,2,3,32,512]{4,3,2,1,0:T(8,128)(2,1)S(1)}, bf16[2,2,3,32,512]{4,3,2,1,0:T(8,128)(2,1)S(1)}, u32[]{:S(2)}, u32[]{:S(2)}) collective-permute-start(bf16[2,2,3,32,512]{4,3,2,1,0:T(8,128)(2,1)S(1)} %get-tuple-element.274), channel_id=1, source_target_pairs={{0,6},{1,7},{2,4},{3,5},{4,2},{5,3},{6,0},{7,1},{8,14},{9,15},{10,... | collective-permute-start | bytes 1179656 | tf_op jit(solution)/shard_map/ppermute | solution.py:45
  403.1 30.0 %collective-permute-start.49 = (bf16[128,2176]{1,0:T(8,128)(2,1)S(1)}, bf16[128,2176]{1,0:T(8,128)(2,1)S(1)}, u32[]{:S(2)}, u32[]{:S(2)}) collective-permute-start(bf16[128,2176]{1,0:T(8,128)(2,1)S(1)} %pad_maximum_fusion.13), channel_id=1, source_target_pairs={{0,4},{1,5},{2,6},{3,7},{4,0},{5,1},{6,2},{7,3},{8,12},{9,13},{10,... | collective-permute-start | bytes 1671176 | tf_op jit(solution)/shard_map/ppermute | solution.py:45
  406.9 26.2 %collective-permute-start.47 = (bf16[128,2176]{1,0:T(8,128)(2,1)S(1)}, bf16[128,2176]{1,0:T(8,128)(2,1)S(1)}, u32[]{:S(2)}, u32[]{:S(2)}) collective-permute-start(bf16[128,2176]{1,0:T(8,128)(2,1)S(1)} %pad_maximum_fusion.12), channel_id=1, source_target_pairs={{0,2},{1,3},{2,0},{3,1},{4,6},{5,7},{6,4},{7,5},{8,10},{9,11},{10,... | collective-permute-start | bytes 1671176 | tf_op jit(solution)/shard_map/ppermute | solution.py:45
  (56 other events, 551.7 us)
Sparse Core Ops, SparseCore 0:
  48.4 64.2 all-gather.2
  127.3 63.6 all-gather.4
  227.5 60.2 reduce-scatter.2
  322.3 59.8 reduce-scatter.4

commit v10 on v9

--- a/solution.py
+++ b/solution.py
@@ -57,6 +57,14 @@
             part = lax.dynamic_index_in_dim(terms, self.group ^ bits, 0, keepdims=False)
             total = total + self.swap(part.astype(bf16), bits * MEMBERS).astype(f32)
         return total
+
+    def to_sides(self, top, low):
+        near_top, far_low = self.swap(top, 2), self.swap(low, 4)
+        near_low, far_top = self.swap(low, 2), self.swap(top, 4)
+        return (near_top, near_low), (far_top, far_low)
+
+    def to_cross(self, near, far):
+        return self.swap(near[0], 4), self.swap(far[1], 2)
 
     def send_cross(self, block):
         half = block.shape[0] // 2
@@ -162,10 +170,6 @@
         for block in range(1, blocks):
             for copy in block_copies(block):
                 copy.start()
-        for n in experts:
-            for copy in weight_copies(n):
-                copy.wait()
-
     for block in range(blocks):
 
         @pl.when(at == block)
@@ -182,6 +186,12 @@
     cotangent_turned[...] = upstream.T
     begun = []
     for n in experts:
+
+        @pl.when(at == 0)
+        def _():
+            for copy in weight_copies(n):
+                copy.wait()
+
         begun.append(
             (
                 dot(normed, weight_ref[n, 0]),
@@ -398,9 +408,10 @@
 
 def router_kernel(
     tokens_ref, routes_ref, gains_ref, mixed_ref, output_ref, extra_ref,
-    packet_ref, middle_ref, share_ref,
+    packet_top_ref, packet_low_ref, middle_ref, share_ref,
 ):
-    width = tokens_ref.shape[1]
+    rows, width = tokens_ref.shape
+    half = rows // 2
 
     def mix(c, carry):
         where = columns_at(c, TILE)
@@ -411,7 +422,8 @@
     lax.fori_loop(0, width // TILE, mix, 0)
     middle = middle_ref[...]
     normed_two = (middle * row_scale_of(middle) * gains_ref[1:2, :]).astype(bf16)
-    packet_ref[:, :width] = normed_two
+    packet_top_ref[:, :width] = normed_two[:half]
+    packet_low_ref[:, :width] = normed_two[half:]
     logits = dot(normed_two, extra_ref[...])
     lane = lax.broadcasted_iota(jnp.int32, logits.shape, 1)
     routed = lane == routes_ref[:, 0:1]
@@ -422,7 +434,9 @@
     shares = weights / jnp.sum(weights, axis=1, keepdims=True)
     share_ref[...] = shares
     high = shares.astype(bf16).astype(f32)
-    packet_ref[:, width:] = (high + pltpu.roll(shares - high, EXPERTS, 1)).astype(bf16)
+    both = (high + pltpu.roll(shares - high, EXPERTS, 1)).astype(bf16)
+    packet_top_ref[:, width:] = both[:half]
+    packet_low_ref[:, width:] = both[half:]
 
 
 def column_of(row, lanes):
@@ -430,8 +444,8 @@
 
 
 def middle_kernel(
-    own_ref, near_top_ref, near_low_ref, far_top_ref, far_low_ref, packet_ref, middle_ref,
-    cotangent_ref, share_ref, gains_ref, mixed_ref, output_ref, extra_ref,
+    own_ref, near_top_ref, near_low_ref, far_top_ref, far_low_ref, packet_top_ref,
+    packet_low_ref, middle_ref, cotangent_ref, share_ref, gains_ref, mixed_ref, output_ref, extra_ref,
     middle_grad_ref, mixed_grad_ref, pack_ref, back_ref, branch_ref, turned_ref,
 ):
     width = cotangent_ref.shape[1]
@@ -458,7 +472,9 @@
     middle_grad = cotangent_ref[...].astype(f32) + scale * weighted - scaled * (scale * scale * correction)
     middle_grad_ref[...] = middle_grad
     branch_ref[...] = (residual_scale * middle_grad).astype(bf16)
-    router_grad = dot(packet_ref[:, :width].T, logit_grad)
+    router_grad = dot(packet_top_ref[:, :width].T, logit_grad[:half]) + dot(
+        packet_low_ref[:, :width].T, logit_grad[half:]
+    )
     lane = lax.broadcasted_iota(jnp.int32, router_grad.shape, 1)
     pack_ref[:, width:] = jnp.where(
         lane == EXPERTS, column_of(gain_grad, EXTRA), router_grad
@@ -636,19 +652,19 @@
         router_kernel,
         "router_forward",
         [(a, None, None) for a in (tokens, routes, gains, mixed)] + output_blocks(whole),
-        [((rows, width + EXTRA), bf16), ((rows, width), f32), ((rows, EXTRA), f32)],
+        [((rows // 2, width + EXTRA), bf16)] * 2 + [((rows, width), f32), ((rows, EXTRA), f32)],
         [],
         2 * rows * width * mixed.shape[1],
     )
 
 
-def middle_back(pieces, packet, middle, cotangent, shares, gains, mixed, whole):
+def middle_back(pieces, packets, middle, cotangent, shares, gains, mixed, whole):
     rows, width = cotangent.shape
     head_columns = HEADS * HEAD_DIM
     return call_kernel(
         middle_kernel,
         "middle_back",
-        [(a, None, None) for a in (*pieces, packet, middle, cotangent, shares, gains, mixed)]
+        [(a, None, None) for a in (*pieces, *packets, middle, cotangent, shares, gains, mixed)]
         + output_blocks(whole),
         [((rows, width), f32), ((rows, head_columns), bf16), ((width, head_columns + EXTRA), bf16)],
         [((rows, width + EXTRA), f32), ((rows, width), bf16), ((width, rows), bf16)],
@@ -739,12 +755,8 @@
     ]
 
     half = column.shape[0] // 2
-    near_top, far_low = links.swap(column[:half], 2), links.swap(column[half:], 4)
-    near_low, far_top = links.swap(column[half:], 2), links.swap(column[:half], 4)
-    cross_top, cross_low = links.swap(near_top, 4), links.swap(far_low, 2)
-    spread = {
-        0: (column,), 2: (near_top, near_low), 4: (far_top, far_low), 6: (cross_top, cross_low)
-    }
+    side_near, side_far = links.to_sides(column[:half], column[half:])
+    spread = {0: (column,), 2: side_near, 4: side_far, 6: links.to_cross(side_near, side_far)}
     whole = jnp.zeros((groups, MEMBERS, shard, pack_width), bf16)
     for k in range(MEMBERS):
         parts = spread[k & 6]
@@ -757,29 +769,29 @@
     at_extra = at_output + head_columns
     gains = whole[:, at_extra + EXPERTS : at_extra + EXPERTS + 2].astype(f32).T
 
-    late_cotangent, whole = lax.optimization_barrier((cotangent, whole))
-    cot_near, cot_far = links.swap(late_cotangent, 2), links.swap(late_cotangent, 4)
+    half = row_count // 2
+    cot_own = cotangent[:half], cotangent[half:]
+    cot_late, whole = lax.optimization_barrier((cot_own, whole))
+    cot_near, cot_far = links.to_sides(*cot_late)
 
     tables = rope_lanes(row_count)
     rotated, mixed, logs = attention_forward(tokens, lengths, tables, gains, whole)
-    half = row_count // 2
-    cot_cross = cot_near[:half], cot_far[half:]
-    cot_cross, mixed = lax.optimization_barrier((cot_cross, mixed))
-    cot_cross = links.swap(cot_cross[0], 4), links.swap(cot_cross[1], 2)
-    packet, middle, shares = router_forward(tokens, routes, gains, mixed, whole)
-    near, far = links.swap(packet, 2), links.swap(packet, 4)
+    cot_near, cot_far, mixed = lax.optimization_barrier((cot_near, cot_far, mixed))
+    cot_cross = links.to_cross(cot_near, cot_far)
+    *packet, middle, shares = router_forward(tokens, routes, gains, mixed, whole)
+    near, far = links.to_sides(*packet)
     own_full[0], cot_cross, packet = lax.optimization_barrier((own_full[0], cot_cross, packet))
 
     names = [
         jnp.stack([member, member ^ 1]).astype(jnp.int32) * LOCAL_EXPERTS + n
         for n in range(LOCAL_EXPERTS)
     ]
-    rows_own = [(packet,)], [(cotangent,)]
+    rows_own = [packet], [cot_own]
     first_full = own_full[0], links.swap(own_full[0], 1)
     own_out, own_back, *zero = run_experts(names[0], *rows_own, first_full)
     near, far, own_back = lax.optimization_barrier((near, far, own_back))
-    cross = links.swap(near[:half], 4), links.swap(far[half:], 2)
-    rows_chips = [cross, (near,), (far,)], [cot_cross, (cot_near,), (cot_far,)]
+    cross = links.to_cross(near, far)
+    rows_chips = [cross, near, far], [cot_cross, cot_near, cot_far]
     chip_out, chip_back, *zero = run_experts(names[0], *rows_chips, first_full, zero, True)
     own_full[1], chip_back = lax.optimization_barrier((own_full[1], chip_back))
     second_full = own_full[1], links.swap(own_full[1], 1)
@@ -835,10 +847,6 @@
     def pack_add(parts, cross):
         return links.add_cross(parts[1].astype(bf16), parts[2].astype(bf16), cross)
 
-    def pack_sum(parts, near, far):
-        near, far = links.swap(near, 2), links.swap(far, 4)
-        return parts[0] + near.astype(f32) + far.astype(f32)
-
     middle_grad, mixed_grad, first_pack = middle_back(
         (own_back[0], *back_pieces), packet, middle, cotangent, shares, gains, mixed, whole
     )
@@ -857,13 +865,17 @@
         (first_near, first_far, second_pack, out_near, out_far, shelf_one)
     )
     second_parts = pack_cores(second_pack)
-    first_sum = pack_sum(first_parts, first_near, first_far)
+    first_near, first_far = links.swap(first_near, 2), links.swap(first_far, 4)
+    first_sum = first_parts[0] + first_near.astype(f32) + first_far.astype(f32)
     shelf_grad = jnp.stack([shelf_zero, shelf_one])
     shelf_grad = shelf_grad.reshape(LOCAL_EXPERTS, 3, MEMBERS, shard, hidden)
     shelf_grad = shelf_grad.transpose(2, 0, 1, 3, 4)
-    second_parts, shelf_grad = lax.optimization_barrier((second_parts, shelf_grad))
     second_near, second_far = pack_add(second_parts, pack_cross(second_parts))
-    second_sum = pack_sum(second_parts, second_near, second_far)
+    second_near, second_far = links.swap(second_near, 2), links.swap(second_far, 4)
+    second_near, second_far, shelf_grad = lax.optimization_barrier(
+        (second_near, second_far, shelf_grad)
+    )
+    second_sum = second_parts[0] + second_near.astype(f32) + second_far.astype(f32)
     pack_total = jnp.concatenate([second_sum, first_sum], axis=1)
     pack_total = links.direct_reduce(pack_total.reshape(groups, shard, pack_total.shape[1]))
     second_total = pack_total[:, : second_sum.shape[1]]

time: 474 us -> 461 us (0.973)
  waiting for transfers between devices: 132 us -> 117 us
    ppermute x59 -> x63, waiting for transfers between devices: 132 us -> 117 us  [swap(): lax.ppermute(value, 'fsdp', [(i, i ^ bits) for i in range(self.count)])]
    ppermute x59 -> x63, starting transfers between devices: 56.1 us -> 56.7 us  [swap(): lax.ppermute(value, 'fsdp', [(i, i ^ bits) for i in range(self.count)])]
  transfers between devices with their start and end apart: 63 -> 67, of which waited for: 33 -> 29; matrix products, arithmetic and copies ran while one was open for 11% -> 11% of each run, Pallas kernels for 42% -> 44%
where the time goes in v10:
time: 461 us; the launch traced here: 452 us
  Pallas kernels  201 us (44%)
  waiting for transfers between devices  117 us (25%)
  starting transfers between devices  57.1 us (12%)
  local copies, waits for them, and re-layouts  36.4 us (8%)
  other arithmetic  25.6 us (6%)
  between operations  15.9 us (3%)
    pallas_call x4, Pallas kernels, run_experts(): pl.pallas_call(functools.partial(expert_kernel, layout=layout, fresh=fres...  127 us
    ppermute x63, waiting for transfers between devices, swap(): lax.ppermute(value, 'fsdp', [(i, i ^ bits) for i in range(self.count)])  117 us
    pallas_call x5, Pallas kernels, call_kernel(): pl.pallas_call(body, grid=(1,), in_specs=specs, out_specs=[pl.BlockSpec(o...  73.5 us
    ppermute x63, starting transfers between devices, swap(): lax.ppermute(value, 'fsdp', [(i, i ^ bits) for i in range(self.count)])  56.7 us
  transfers between devices with their start and end apart: 67, of which 29 were waited for; matrix products, arithmetic and copies ran while one was open for 11% of the time, Pallas kernels for 44%

profile of v10, /device:TPU:0, one launch (start us, length us, event | category | flops | bytes accessed | tf_op | source)
XLA Modules:
  0.0 452.4 jit_solution(16347651389910192832)
XLA Ops:
  26.6 4.8 %collective-permute-done.5 = bf16[32,3200]{1,0:T(8,128)(2,1)} collective-permute-done((bf16[32,3200]{1,0:T(8,128)(2,1)S(1)}, bf16[32,3200]{1,0:T(8,128)(2,1)}, u32[]{:S(2)}, u32[]{:S(2)}) %collective-permute-start.5) | collective-permute-done | bytes 204832 | tf_op jit(solution)/shard_map/ppermute | solution.py:45
  33.4 5.6 %collective-permute-done.1 = bf16[2,2,3,32,512]{4,3,2,1,0:T(8,128)(2,1)} collective-permute-done((bf16[2,2,3,32,512]{4,3,2,1,0:T(8,128)(2,1)}, bf16[2,2,3,32,512]{4,3,2,1,0:T(8,128)(2,1)}, u32[]{:S(2)}, u32[]{:S(2)}) %collective-permute-start.1) | collective-permute-done | bytes 393248 | tf_op jit(solution)/shard_map/ppermute | solution.py:45
  49.9 6.3 %collective-permute-done.9 = bf16[64,3200]{1,0:T(8,128)(2,1)} collective-permute-done((bf16[64,3200]{1,0:T(8,128)(2,1)}, bf16[64,3200]{1,0:T(8,128)(2,1)}, u32[]{:S(2)}, u32[]{:S(2)}) %collective-permute-start.9) | collective-permute-done | bytes 409632 | tf_op jit(solution)/shard_map/ppermute | solution.py:45
  56.2 8.2 %collective-permute-done.8 = bf16[64,3200]{1,0:T(8,128)(2,1)} collective-permute-done((bf16[64,3200]{1,0:T(8,128)(2,1)}, bf16[64,3200]{1,0:T(8,128)(2,1)}, u32[]{:S(2)}, u32[]{:S(2)}) %collective-permute-start.8) | collective-permute-done | bytes 409632 | tf_op jit(solution)/shard_map/ppermute | solution.py:45
  70.5 7.6 %collective-permute-done.17 = bf16[64,3200]{1,0:T(8,128)(2,1)S(1)} collective-permute-done((bf16[64,3200]{1,0:T(8,128)(2,1)S(1)}, bf16[64,3200]{1,0:T(8,128)(2,1)S(1)}, u32[]{:S(2)}, u32[]{:S(2)}) %collective-permute-start.17) | collective-permute-done | bytes 409632 | tf_op jit(solution)/shard_map/ppermute | solution.py:45
  87.6 20.4 %attention_forward.1 = (bf16[512,2048]{1,0:T(8,128)(2,1)}, bf16[512,1024]{1,0:T(8,128)(2,1)}, f32[4,4,512]{2,1,0:T(4,128)}) custom-call(s32[1]{0:T(128)S(6)} %copy.150.length_ref, bf16[512,1024]{1,0:T(8,128)(2,1)} %tokens_ref.5, f32[512,256]{1,0:T(8,128)} %constant.201.clone.cosine_ref, f32[512,256]{1,0:T(8,128)} %constant.202.clone.sine_ref, ...), custom_call_target="tpu_custom_call" | custom-call | flops 4294967296 | bytes 11837444 | tf_op jit(solution)/shard_map/attention_forward/pallas_call | solution.py:591
  112.3 7.3 %router_forward.1 = (bf16[256,1152]{1,0:T(8,128)(2,1)}, bf16[256,1152]{1,0:T(8,128)(2,1)}, f32[512,1024]{1,0:T(8,128)}, f32[512,128]{1,0:T(8,128)}) custom-call(bf16[512,1024]{1,0:T(8,128)(2,1)} %tokens_ref.5, s32[512,8]{1,0:T(8,128)} %copy.115.routes_ref, f32[2,1024]{1,0:T(2,128)} %copy.116.gains_ref, bf16[512,1024]{1,0:T(8,128)(2,1)} %get-tuple-element.102.mixed_ref, ...), custom_call_target="tpu_custom_call" | custom-call | flops 1073741824 | bytes 18767872 | tf_op jit(solution)/shard_map/router_forward/pallas_call | solution.py:591
  129.2 19.3 %experts.4 = (bf16[1,512,1024]{2,1,0:T(8,128)(2,1)}, bf16[1,512,1152]{2,1,0:T(8,128)(2,1)}, f32[3,1024,512]{2,1,0:T(8,128)}, f32[3,1024,512]{2,1,0:T(8,128)}) custom-call(s32[2]{0:T(128)} %get-tuple-element.257.names_ref, bf16[256,1152]{1,0:T(8,128)(2,1)} %get-tuple-element.109.refs_0_.packet_top_ref, ...), custom_call_target="tpu_custom_call" | custom-call | flops 9663676416 | bytes 23068672 | tf_op jit(solution)/shard_map/experts/pallas_call | solution.py:293
  148.5 5.0 %collective-permute-done.27.refs_3_ = bf16[256,1152]{1,0:T(8,128)(2,1)} collective-permute-done((bf16[256,1152]{1,0:T(8,128)(2,1)S(1)}, bf16[256,1152]{1,0:T(8,128)(2,1)}, u32[]{:S(2)}, u32[]{:S(2)}) %collective-permute-start.27) | collective-permute-done | bytes 589856 | tf_op jit(solution)/shard_map/ppermute | solution.py:45
  156.6 12.7 %collective-permute-done.31.refs_0_ = bf16[256,1152]{1,0:T(8,128)(2,1)S(1)} collective-permute-done((bf16[256,1152]{1,0:T(8,128)(2,1)S(1)}, bf16[256,1152]{1,0:T(8,128)(2,1)S(1)}, u32[]{:S(2)}, u32[]{:S(2)}) %collective-permute-start.31) | collective-permute-done | bytes 589856 | tf_op jit(solution)/shard_map/ppermute | solution.py:45
  170.6 42.7 %experts.5 = (bf16[3,512,1024]{2,1,0:T(8,128)(2,1)}, bf16[3,512,1152]{2,1,0:T(8,128)(2,1)}, bf16[4,3,256,512]{3,2,1,0:T(8,128)(2,1)}, bf16[4,3,256,512]{3,2,1,0:T(8,128)(2,1)}) custom-call(s32[2]{0:T(128)} %get-tuple-element.257.names_ref, bf16[256,1152]{1,0:T(8,128)(2,1)} %copy-done.15, bf16[256,1152]{1,0:T(8,128)(2,1)} %copy-done.16, ...), custom_call_target="tpu_custom_call" | custom-call | flops 28991029248 | bytes 31457280 | tf_op jit(solution)/shard_map/experts/pallas_call | solution.py:293
  213.8 8.8 %collective-permute-done.34 = bf16[4,3,256,512]{3,2,1,0:T(8,128)(2,1)S(1)} collective-permute-done((bf16[4,3,256,512]{3,2,1,0:T(8,128)(2,1)}, bf16[4,3,256,512]{3,2,1,0:T(8,128)(2,1)S(1)}, u32[]{:S(2)}, u32[]{:S(2)}) %collective-permute-start.34) | collective-permute-done | bytes 3145760 | tf_op jit(solution)/shard_map/ppermute | solution.py:45
  222.6 4.4 add_convert_fusion.1
  227.1 43.5 %experts.6 = (bf16[3,512,1024]{2,1,0:T(8,128)(2,1)}, bf16[3,512,1152]{2,1,0:T(8,128)(2,1)}, f32[3,1024,512]{2,1,0:T(8,128)}, f32[3,1024,512]{2,1,0:T(8,128)}) custom-call(s32[2]{0:T(128)} %get-tuple-element.256.names_ref, bf16[256,1152]{1,0:T(8,128)(2,1)} %copy-done.15, bf16[256,1152]{1,0:T(8,128)(2,1)} %copy-done.16, bf16[256,1152]{1,0:T(8,128)(2,1)} %copy-done.14, ...), custom_call_target="tpu_custom_call" | custom-call | flops 28991029248 | bytes 31457280 | tf_op jit(solution)/shard_map/experts/pallas_call | solution.py:293
  277.6 21.8 %experts.7 = (bf16[1,512,1024]{2,1,0:T(8,128)(2,1)}, bf16[1,512,1152]{2,1,0:T(8,128)(2,1)}, bf16[4,3,256,512]{3,2,1,0:T(8,128)(2,1)}, bf16[4,3,256,512]{3,2,1,0:T(8,128)(2,1)}) custom-call(s32[2]{0:T(128)} %get-tuple-element.256.names_ref, bf16[256,1152]{1,0:T(8,128)(2,1)} %get-tuple-element.109.refs_0_.packet_top_ref, ...), custom_call_target="tpu_custom_call" | custom-call | flops 9663676416 | bytes 23068672 | tf_op jit(solution)/shard_map/experts/pallas_call | solution.py:293
  314.4 7.4 %collective-permute-done.40.near_low_ref = bf16[256,1152]{1,0:T(8,128)(2,1)S(1)} collective-permute-done((bf16[256,1152]{1,0:T(8,128)(2,1)}, bf16[256,1152]{1,0:T(8,128)(2,1)S(1)}, u32[]{:S(2)}, u32[]{:S(2)}) %collective-permute-start.40) | collective-permute-done | bytes 589856 | tf_op jit(solution)/shard_map/ppermute | solution.py:45
  326.2 12.4 %middle_back.1 = (f32[512,1024]{1,0:T(8,128)}, bf16[512,1024]{1,0:T(8,128)(2,1)}, bf16[1024,1152]{1,0:T(8,128)(2,1)}) custom-call(bf16[512,1152]{1,0:T(8,128)(2,1)} %bitcast.215, bf16[256,1152]{1,0:T(8,128)(2,1)} %copy-done.9, bf16[256,1152]{1,0:T(8,128)(2,1)} %copy-done.11, bf16[256,1152]{1,0:T(8,128)(2,1)} %collective-permute-done.41.far_top_ref, ...), custom_call_target="tpu_custom_call" | custom-call | flops 2147483648 | bytes 27795456 | tf_op jit(solution)/shard_map/middle_back/pallas_call | solution.py:591
  346.4 18.7 %attention_back.1.projected_ref = bf16[512,2048]{1,0:T(8,128)(2,1)} custom-call(s32[1]{0:T(128)S(6)} %copy.150.length_ref, bf16[512,2048]{1,0:T(8,128)(2,1)} %get-tuple-element.156.rotated_ref, bf16[512,1024]{1,0:T(8,128)(2,1)} %get-tuple-element.159.mixed_grad_ref, f32[4,4,512]{2,1,0:T(4,128)} %get-tuple-element.160.log_ref, ...), custom_call_target="tpu_custom_call" | custom-call | flops 2684354560 | bytes 6324228 | tf_op jit(solution)/shard_map/attention_back/pallas_call | solution.py:591
  370.3 14.8 %inputs_back.1 = (f32[512,1024]{1,0:T(8,128)}, bf16[1024,2176]{1,0:T(8,128)(2,1)}) custom-call(bf16[512,1024]{1,0:T(8,128)(2,1)} %tokens_ref.5, f32[2,1024]{1,0:T(2,128)} %copy.116.gains_ref, bf16[512,2048]{1,0:T(8,128)(2,1)} %attention_back.1.projected_ref, bf16[1024,3200]{1,0:T(8,128)(2,1)} %bitcast.192, f32[512,1024]{1,0:T(8,128)} %get-tuple-element.165.middle_grad_ref), custom_call_target="tpu_custom_call" | custom-call | flops 4294967296 | bytes 18358272 | tf_op jit(solution)/shard_map/inputs_back/pallas_call | solution.py:591
  389.1 3.5 fusion.2
  396.2 6.6 %collective-permute-done.50 = bf16[64,2176]{1,0:T(8,128)(2,1)S(1)} collective-permute-done((bf16[64,2176]{1,0:T(8,128)(2,1)S(1)}, bf16[64,2176]{1,0:T(8,128)(2,1)S(1)}, u32[]{:S(2)}, u32[]{:S(2)}) %collective-permute-start.50) | collective-permute-done | bytes 278560 | tf_op jit(solution)/shard_map/ppermute | solution.py:45
  405.0 12.1 %collective-permute-done.51 = bf16[128,2176]{1,0:T(8,128)(2,1)S(1)} collective-permute-done((bf16[128,2176]{1,0:T(8,128)(2,1)S(1)}, bf16[128,2176]{1,0:T(8,128)(2,1)S(1)}, u32[]{:S(2)}, u32[]{:S(2)}) %collective-permute-start.51) | collective-permute-done | bytes 557088 | tf_op jit(solution)/shard_map/ppermute | solution.py:45
  419.9 3.5 collective-permute-start.58
  428.5 8.4 %collective-permute-done.60 = bf16[2,2,3,32,512]{4,3,2,1,0:T(8,128)(2,1)S(1)} collective-permute-done((bf16[2,2,3,32,512]{4,3,2,1,0:T(8,128)(2,1)S(1)}, bf16[2,2,3,32,512]{4,3,2,1,0:T(8,128)(2,1)S(1)}, u32[]{:S(2)}, u32[]{:S(2)}) %collective-permute-start.60) | collective-permute-done | bytes 393248 | tf_op jit(solution)/shard_map/ppermute | solution.py:45
  (260 shorter events, 131.0 us)
Async XLA Ops:
  7.2 116.0 %all-gather.3.cloned.1.call-start = ((), (), s32[]{:S(2)}) async-start(), calls=%async_computation.2 | async-start | bytes 3932160 | tf_op jit(solution)/shard_map/all_gather | solution.py:754
  16.2 24.1 %collective-permute-start.6 = (bf16[32,3200]{1,0:T(8,128)(2,1)S(1)}, bf16[32,3200]{1,0:T(8,128)(2,1)S(1)}, u32[]{:S(2)}, u32[]{:S(2)}) collective-permute-start(bf16[32,3200]{1,0:T(8,128)(2,1)S(1)} %concatenate.44), channel_id=1, source_target_pairs={{0,24},{1,25},{2,26},{3,27},{4,28},{5,29},{6,30},{7,31},{8,16},{9,... | collective-permute-start | bytes 614408 | tf_op jit(solution)/shard_map/ppermute | solution.py:45
  42.5 23.8 %collective-permute-start.7 = (bf16[128,3200]{1,0:T(8,128)(2,1)S(1)}, bf16[128,3200]{1,0:T(8,128)(2,1)}, u32[]{:S(2)}, u32[]{:S(2)}) collective-permute-start(bf16[128,3200]{1,0:T(8,128)(2,1)S(1)} %bitcast.194), channel_id=1, source_target_pairs={{0,1},{1,0},{2,3},{3,2},{4,5},{5,4},{6,7},{7,6},{8,9},{9,8},{10,11... | collective-permute-start | bytes 2457608 | tf_op jit(solution)/shard_map/ppermute | solution.py:45
  43.7 20.7 %collective-permute-start.13 = (bf16[64,3200]{1,0:T(8,128)(2,1)}, bf16[64,3200]{1,0:T(8,128)(2,1)S(1)}, u32[]{:S(2)}, u32[]{:S(2)}) collective-permute-start(bf16[64,3200]{1,0:T(8,128)(2,1)} %get-tuple-element.297), channel_id=1, source_target_pairs={{0,4},{1,5},{2,6},{3,7},{4,0},{5,1},{6,2},{7,3},{8,12},{9,13},{10,... | collective-permute-start | bytes 1228808 | tf_op jit(solution)/shard_map/ppermute | solution.py:45
  45.7 18.8 %collective-permute-start.8 = (bf16[64,3200]{1,0:T(8,128)(2,1)}, bf16[64,3200]{1,0:T(8,128)(2,1)}, u32[]{:S(2)}, u32[]{:S(2)}) collective-permute-start(bf16[64,3200]{1,0:T(8,128)(2,1)} %get-tuple-element.296), channel_id=1, source_target_pairs={{0,2},{1,3},{2,0},{3,1},{4,6},{5,7},{6,4},{7,5},{8,10},{9,11},{10,... | collective-permute-start | bytes 1228808 | tf_op jit(solution)/shard_map/ppermute | solution.py:45
  49.2 164.1 %all-gather.5.cloned.1.call-start = ((), (), s32[]{:S(2)}) async-start(), calls=%async_computation.3 | async-start | bytes 3932160 | tf_op jit(solution)/shard_map/all_gather | solution.py:754
  82.6 25.4 %collective-permute-start.20 = (bf16[256,1024]{1,0:T(8,128)(2,1)}, bf16[256,1024]{1,0:T(8,128)(2,1)}, u32[]{:S(2)}, u32[]{:S(2)}) collective-permute-start(bf16[256,1024]{1,0:T(8,128)(2,1)} %get-tuple-element.98.refs_2_), channel_id=1, source_target_pairs={{0,2},{1,3},{2,0},{3,1},{4,6},{5,7},{6,4},{7,5},{8,10},{9,11},{10,... | collective-permute-start | bytes 1572872 | tf_op jit(solution)/shard_map/ppermute | solution.py:45
  83.6 24.5 %collective-permute-start.22 = (bf16[256,1024]{1,0:T(8,128)(2,1)}, bf16[256,1024]{1,0:T(8,128)(2,1)S(1)}, u32[]{:S(2)}, u32[]{:S(2)}) collective-permute-start(bf16[256,1024]{1,0:T(8,128)(2,1)} %get-tuple-element.98.refs_2_), channel_id=1, source_target_pairs={{0,4},{1,5},{2,6},{3,7},{4,0},{5,1},{6,2},{7,3},{8,12},{9,13},{10,... | collective-permute-start | bytes 1572872 | tf_op jit(solution)/shard_map/ppermute | solution.py:45
  85.1 23.0 %collective-permute-start.21 = (bf16[256,1024]{1,0:T(8,128)(2,1)}, bf16[256,1024]{1,0:T(8,128)(2,1)S(1)}, u32[]{:S(2)}, u32[]{:S(2)}) collective-permute-start(bf16[256,1024]{1,0:T(8,128)(2,1)} %get-tuple-element.99.refs_3_), channel_id=1, source_target_pairs={{0,2},{1,3},{2,0},{3,1},{4,6},{5,7},{6,4},{7,5},{8,10},{9,11},{10,... | collective-permute-start | bytes 1572872 | tf_op jit(solution)/shard_map/ppermute | solution.py:45
  86.2 22.6 %collective-permute-start.23 = (bf16[256,1024]{1,0:T(8,128)(2,1)}, bf16[256,1024]{1,0:T(8,128)(2,1)}, u32[]{:S(2)}, u32[]{:S(2)}) collective-permute-start(bf16[256,1024]{1,0:T(8,128)(2,1)} %get-tuple-element.99.refs_3_), channel_id=1, source_target_pairs={{0,4},{1,5},{2,6},{3,7},{4,0},{5,1},{6,2},{7,3},{8,12},{9,13},{10,... | collective-permute-start | bytes 1572872 | tf_op jit(solution)/shard_map/ppermute | solution.py:45
  124.2 242.8 %reduce-scatter.3.cloned.1.call-start = ((), (), s32[]{:S(2)}) async-start(), calls=%async_computation.4 | async-start | bytes 3932160 | tf_op jit(solution)/shard_map/reduce_scatter | solution.py:803
  125.0 23.5 %collective-permute-start.26 = (bf16[256,1152]{1,0:T(8,128)(2,1)S(1)}, bf16[256,1152]{1,0:T(8,128)(2,1)S(1)}, u32[]{:S(2)}, u32[]{:S(2)}) collective-permute-start(bf16[256,1152]{1,0:T(8,128)(2,1)S(1)} %copy-done.7), channel_id=1, source_target_pairs={{0,2},{1,3},{2,0},{3,1},{4,6},{5,7},{6,4},{7,5},{8,10},{9,11},{10,... | collective-permute-start | bytes 1769480 | tf_op jit(solution)/shard_map/ppermute | solution.py:45
  126.1 27.4 %collective-permute-start.27 = (bf16[256,1152]{1,0:T(8,128)(2,1)S(1)}, bf16[256,1152]{1,0:T(8,128)(2,1)}, u32[]{:S(2)}, u32[]{:S(2)}) collective-permute-start(bf16[256,1152]{1,0:T(8,128)(2,1)S(1)} %copy-done.8), channel_id=1, source_target_pairs={{0,2},{1,3},{2,0},{3,1},{4,6},{5,7},{6,4},{7,5},{8,10},{9,11},{10,... | collective-permute-start | bytes 1769480 | tf_op jit(solution)/shard_map/ppermute | solution.py:45
  127.0 26.5 %collective-permute-start.28 = (bf16[256,1152]{1,0:T(8,128)(2,1)S(1)}, bf16[256,1152]{1,0:T(8,128)(2,1)}, u32[]{:S(2)}, u32[]{:S(2)}) collective-permute-start(bf16[256,1152]{1,0:T(8,128)(2,1)S(1)} %copy-done.7), channel_id=1, source_target_pairs={{0,4},{1,5},{2,6},{3,7},{4,0},{5,1},{6,2},{7,3},{8,12},{9,13},{10,... | collective-permute-start | bytes 1769480 | tf_op jit(solution)/shard_map/ppermute | solution.py:45
  127.5 27.4 %collective-permute-start.29 = (bf16[256,1152]{1,0:T(8,128)(2,1)S(1)}, bf16[256,1152]{1,0:T(8,128)(2,1)}, u32[]{:S(2)}, u32[]{:S(2)}) collective-permute-start(bf16[256,1152]{1,0:T(8,128)(2,1)S(1)} %copy-done.8), channel_id=1, source_target_pairs={{0,4},{1,5},{2,6},{3,7},{4,0},{5,1},{6,2},{7,3},{8,12},{9,13},{10,... | collective-permute-start | bytes 1769480 | tf_op jit(solution)/shard_map/ppermute | solution.py:45
  227.0 158.3 %reduce-scatter.5.cloned.1.call-start = ((), (), s32[]{:S(2)}) async-start(), calls=%async_computation.5 | async-start | bytes 3932160 | tf_op jit(solution)/shard_map/reduce_scatter | solution.py:803
  273.6 25.8 %collective-permute-start.35 = (bf16[256,1152]{1,0:T(8,128)(2,1)}, bf16[256,1152]{1,0:T(8,128)(2,1)}, u32[]{:S(2)}, u32[]{:S(2)}) collective-permute-start(bf16[256,1152]{1,0:T(8,128)(2,1)} %get-tuple-element.266), channel_id=1, source_target_pairs={{0,2},{1,3},{2,0},{3,1},{4,6},{5,7},{6,4},{7,5},{8,10},{9,11},{10,... | collective-permute-start | bytes 1769480 | tf_op jit(solution)/shard_map/ppermute | solution.py:45
  274.7 24.7 %collective-permute-start.36 = (bf16[256,1152]{1,0:T(8,128)(2,1)}, bf16[256,1152]{1,0:T(8,128)(2,1)}, u32[]{:S(2)}, u32[]{:S(2)}) collective-permute-start(bf16[256,1152]{1,0:T(8,128)(2,1)} %get-tuple-element.265), channel_id=1, source_target_pairs={{0,4},{1,5},{2,6},{3,7},{4,0},{5,1},{6,2},{7,3},{8,12},{9,13},{10,... | collective-permute-start | bytes 1769480 | tf_op jit(solution)/shard_map/ppermute | solution.py:45
  276.2 25.6 %collective-permute-start.37 = (bf16[256,1152]{1,0:T(8,128)(2,1)}, bf16[256,1152]{1,0:T(8,128)(2,1)S(1)}, u32[]{:S(2)}, u32[]{:S(2)}) collective-permute-start(bf16[256,1152]{1,0:T(8,128)(2,1)} %get-tuple-element.264), channel_id=1, source_target_pairs={{0,2},{1,3},{2,0},{3,1},{4,6},{5,7},{6,4},{7,5},{8,10},{9,11},{10,... | collective-permute-start | bytes 1769480 | tf_op jit(solution)/shard_map/ppermute | solution.py:45
  277.1 25.5 %collective-permute-start.38 = (bf16[256,1152]{1,0:T(8,128)(2,1)S(1)}, bf16[256,1152]{1,0:T(8,128)(2,1)S(1)}, u32[]{:S(2)}, u32[]{:S(2)}) collective-permute-start(bf16[256,1152]{1,0:T(8,128)(2,1)S(1)} %get-tuple-element.263), channel_id=1, source_target_pairs={{0,4},{1,5},{2,6},{3,7},{4,0},{5,1},{6,2},{7,3},{8,12},{9,13},{10,... | collective-permute-start | bytes 1769480 | tf_op jit(solution)/shard_map/ppermute | solution.py:45
  323.6 18.8 %collective-permute-start.44 = (bf16[256,1024]{1,0:T(8,128)(2,1)}, bf16[256,1024]{1,0:T(8,128)(2,1)S(1)}, u32[]{:S(2)}, u32[]{:S(2)}) collective-permute-start(bf16[256,1024]{1,0:T(8,128)(2,1)} %get-tuple-element.292), channel_id=1, source_target_pairs={{0,2},{1,3},{2,0},{3,1},{4,6},{5,7},{6,4},{7,5},{8,10},{9,11},{10,... | collective-permute-start | bytes 1572872 | tf_op jit(solution)/shard_map/ppermute | solution.py:45
  341.0 24.1 %collective-permute-start.42 = (bf16[4,4,32,1152]{3,2,1,0:T(8,128)(2,1)}, bf16[4,4,32,1152]{3,2,1,0:T(8,128)(2,1)S(1)}, u32[]{:S(2)}, u32[]{:S(2)}) collective-permute-start(bf16[4,4,32,1152]{3,2,1,0:T(8,128)(2,1)} %dynamic-slice_bitcast_fusion.1), channel_id=1, source_target_pairs={{0,1},{1,0},{2,3},{3,2},{4,5},{5,4},{6,7},{7,6},{8,9},{9,8},{10,11... | collective-permute-start | bytes 3538952 | tf_op jit(solution)/shard_map/ppermute | solution.py:45
  345.6 39.7 %collective-permute-start.47 = (bf16[512,1024]{1,0:T(8,128)(2,1)}, bf16[512,1024]{1,0:T(8,128)(2,1)}, u32[]{:S(2)}, u32[]{:S(2)}) collective-permute-start(bf16[512,1024]{1,0:T(8,128)(2,1)} %get-tuple-element.167), channel_id=1, source_target_pairs={{0,2},{1,3},{2,0},{3,1},{4,6},{5,7},{6,4},{7,5},{8,10},{9,11},{10,... | collective-permute-start | bytes 3145736 | tf_op jit(solution)/shard_map/ppermute | solution.py:45
  346.0 39.3 %collective-permute-start.48 = (bf16[512,1024]{1,0:T(8,128)(2,1)}, bf16[512,1024]{1,0:T(8,128)(2,1)}, u32[]{:S(2)}, u32[]{:S(2)}) collective-permute-start(bf16[512,1024]{1,0:T(8,128)(2,1)} %get-tuple-element.168), channel_id=1, source_target_pairs={{0,4},{1,5},{2,6},{3,7},{4,0},{5,1},{6,2},{7,3},{8,12},{9,13},{10,... | collective-permute-start | bytes 3145736 | tf_op jit(solution)/shard_map/ppermute | solution.py:45
  (62 other events, 654.5 us)
Sparse Core Ops, SparseCore 0:
  49.3 63.7 all-gather.2
  124.3 63.5 all-gather.4
  227.2 61.0 reduce-scatter.2
  322.6 61.0 reduce-scatter.4

commit v11 on v10

--- a/solution.py
+++ b/solution.py
@@ -170,6 +170,9 @@
         for block in range(1, blocks):
             for copy in block_copies(block):
                 copy.start()
+        for n in experts:
+            for copy in weight_copies(n):
+                copy.wait()
     for block in range(blocks):
 
         @pl.when(at == block)
@@ -186,12 +189,6 @@
     cotangent_turned[...] = upstream.T
     begun = []
     for n in experts:
-
-        @pl.when(at == 0)
-        def _():
-            for copy in weight_copies(n):
-                copy.wait()
-
         begun.append(
             (
                 dot(normed, weight_ref[n, 0]),
@@ -771,7 +768,7 @@
 
     half = row_count // 2
     cot_own = cotangent[:half], cotangent[half:]
-    cot_late, whole = lax.optimization_barrier((cot_own, whole))
+    cot_late, _ = lax.optimization_barrier((cot_own, spread[6]))
     cot_near, cot_far = links.to_sides(*cot_late)
 
     tables = rope_lanes(row_count)

time: 461 us -> 464 us (level)
  transfers between devices with their start and end apart: 67 -> 67, of which waited for: 29 -> 25; matrix products, arithmetic and copies ran while one was open for 11% -> 11% of each run, Pallas kernels for 44% -> 44%
where the time goes in v11:
time: 464 us; the launch traced here: 455 us
  Pallas kernels  200 us (43%)
  waiting for transfers between devices  120 us (26%)
  starting transfers between devices  54.1 us (12%)
  local copies, waits for them, and re-layouts  38.8 us (8%)
  other arithmetic  25.8 us (6%)
  between operations  15.9 us (3%)
    pallas_call x4, Pallas kernels, run_experts(): pl.pallas_call(functools.partial(expert_kernel, layout=layout, fresh=fres...  126 us
    ppermute x63, waiting for transfers between devices, swap(): lax.ppermute(value, 'fsdp', [(i, i ^ bits) for i in range(self.count)])  120 us
    pallas_call x5, Pallas kernels, call_kernel(): pl.pallas_call(body, grid=(1,), in_specs=specs, out_specs=[pl.BlockSpec(o...  73.5 us
    ppermute x63, starting transfers between devices, swap(): lax.ppermute(value, 'fsdp', [(i, i ^ bits) for i in range(self.count)])  53.7 us
  transfers between devices with their start and end apart: 67, of which 25 were waited for; matrix products, arithmetic and copies ran while one was open for 11% of the time, Pallas kernels for 44%

profile of v11, /device:TPU:0, one launch (start us, length us, event | category | flops | bytes accessed | tf_op | source)
XLA Modules:
  0.0 454.7 jit_solution(17026853202953098180)
XLA Ops:
  26.6 4.8 %collective-permute-done.5 = bf16[32,3200]{1,0:T(8,128)(2,1)} collective-permute-done((bf16[32,3200]{1,0:T(8,128)(2,1)S(1)}, bf16[32,3200]{1,0:T(8,128)(2,1)}, u32[]{:S(2)}, u32[]{:S(2)}) %collective-permute-start.5) | collective-permute-done | bytes 204832 | tf_op jit(solution)/shard_map/ppermute | solution.py:45
  33.4 5.6 %collective-permute-done.1 = bf16[2,2,3,32,512]{4,3,2,1,0:T(8,128)(2,1)} collective-permute-done((bf16[2,2,3,32,512]{4,3,2,1,0:T(8,128)(2,1)}, bf16[2,2,3,32,512]{4,3,2,1,0:T(8,128)(2,1)}, u32[]{:S(2)}, u32[]{:S(2)}) %collective-permute-start.1) | collective-permute-done | bytes 393248 | tf_op jit(solution)/shard_map/ppermute | solution.py:45
  49.9 6.3 %collective-permute-done.9 = bf16[64,3200]{1,0:T(8,128)(2,1)} collective-permute-done((bf16[64,3200]{1,0:T(8,128)(2,1)}, bf16[64,3200]{1,0:T(8,128)(2,1)}, u32[]{:S(2)}, u32[]{:S(2)}) %collective-permute-start.9) | collective-permute-done | bytes 409632 | tf_op jit(solution)/shard_map/ppermute | solution.py:45
  56.2 8.2 %collective-permute-done.8 = bf16[64,3200]{1,0:T(8,128)(2,1)} collective-permute-done((bf16[64,3200]{1,0:T(8,128)(2,1)}, bf16[64,3200]{1,0:T(8,128)(2,1)}, u32[]{:S(2)}, u32[]{:S(2)}) %collective-permute-start.8) | collective-permute-done | bytes 409632 | tf_op jit(solution)/shard_map/ppermute | solution.py:45
  67.8 11.0 %collective-permute-done.17 = bf16[64,3200]{1,0:T(8,128)(2,1)S(1)} collective-permute-done((bf16[64,3200]{1,0:T(8,128)(2,1)S(1)}, bf16[64,3200]{1,0:T(8,128)(2,1)S(1)}, u32[]{:S(2)}, u32[]{:S(2)}) %collective-permute-start.17) | collective-permute-done | bytes 409632 | tf_op jit(solution)/shard_map/ppermute | solution.py:45
  90.7 20.3 %attention_forward.1 = (bf16[512,2048]{1,0:T(8,128)(2,1)}, bf16[512,1024]{1,0:T(8,128)(2,1)}, f32[4,4,512]{2,1,0:T(4,128)}) custom-call(s32[1]{0:T(128)S(6)} %copy.150.length_ref, bf16[512,1024]{1,0:T(8,128)(2,1)} %tokens_ref.5, f32[512,256]{1,0:T(8,128)} %constant.201.clone.cosine_ref, f32[512,256]{1,0:T(8,128)} %constant.202.clone.sine_ref, ...), custom_call_target="tpu_custom_call" | custom-call | flops 4294967296 | bytes 11837444 | tf_op jit(solution)/shard_map/attention_forward/pallas_call | solution.py:588
  113.1 7.4 %router_forward.1 = (bf16[256,1152]{1,0:T(8,128)(2,1)}, bf16[256,1152]{1,0:T(8,128)(2,1)}, f32[512,1024]{1,0:T(8,128)}, f32[512,128]{1,0:T(8,128)}) custom-call(bf16[512,1024]{1,0:T(8,128)(2,1)} %tokens_ref.5, s32[512,8]{1,0:T(8,128)} %copy.115.routes_ref, f32[2,1024]{1,0:T(2,128)} %copy.116.gains_ref, bf16[512,1024]{1,0:T(8,128)(2,1)} %get-tuple-element.100.mixed_ref, ...), custom_call_target="tpu_custom_call" | custom-call | flops 1073741824 | bytes 18767872 | tf_op jit(solution)/shard_map/router_forward/pallas_call | solution.py:588
  120.5 4.6 %collective-permute-done.24.refs_6_ = bf16[256,1024]{1,0:T(8,128)(2,1)} collective-permute-done((bf16[256,1024]{1,0:T(8,128)(2,1)}, bf16[256,1024]{1,0:T(8,128)(2,1)}, u32[]{:S(2)}, u32[]{:S(2)}) %collective-permute-start.24) | collective-permute-done | bytes 524320 | tf_op jit(solution)/shard_map/ppermute | solution.py:45
  131.7 18.7 %experts.4 = (bf16[1,512,1024]{2,1,0:T(8,128)(2,1)}, bf16[1,512,1152]{2,1,0:T(8,128)(2,1)}, f32[3,1024,512]{2,1,0:T(8,128)}, f32[3,1024,512]{2,1,0:T(8,128)}) custom-call(s32[2]{0:T(128)} %get-tuple-element.255.names_ref, bf16[256,1152]{1,0:T(8,128)(2,1)} %get-tuple-element.107.refs_0_.packet_top_ref, ...), custom_call_target="tpu_custom_call" | custom-call | flops 9663676416 | bytes 23068672 | tf_op jit(solution)/shard_map/experts/pallas_call | solution.py:290
  150.5 5.5 %collective-permute-done.27.refs_3_ = bf16[256,1152]{1,0:T(8,128)(2,1)} collective-permute-done((bf16[256,1152]{1,0:T(8,128)(2,1)S(1)}, bf16[256,1152]{1,0:T(8,128)(2,1)}, u32[]{:S(2)}, u32[]{:S(2)}) %collective-permute-start.27) | collective-permute-done | bytes 589856 | tf_op jit(solution)/shard_map/ppermute | solution.py:45
  159.2 12.6 %collective-permute-done.31.refs_0_ = bf16[256,1152]{1,0:T(8,128)(2,1)S(1)} collective-permute-done((bf16[256,1152]{1,0:T(8,128)(2,1)S(1)}, bf16[256,1152]{1,0:T(8,128)(2,1)S(1)}, u32[]{:S(2)}, u32[]{:S(2)}) %collective-permute-start.31) | collective-permute-done | bytes 589856 | tf_op jit(solution)/shard_map/ppermute | solution.py:45
  173.8 42.5 %experts.5 = (bf16[3,512,1024]{2,1,0:T(8,128)(2,1)}, bf16[3,512,1152]{2,1,0:T(8,128)(2,1)}, bf16[4,3,256,512]{3,2,1,0:T(8,128)(2,1)}, bf16[4,3,256,512]{3,2,1,0:T(8,128)(2,1)}) custom-call(s32[2]{0:T(128)} %get-tuple-element.255.names_ref, bf16[256,1152]{1,0:T(8,128)(2,1)} %copy-done.15, bf16[256,1152]{1,0:T(8,128)(2,1)} %copy-done.16, ...), custom_call_target="tpu_custom_call" | custom-call | flops 28991029248 | bytes 31457280 | tf_op jit(solution)/shard_map/experts/pallas_call | solution.py:290
  216.9 8.8 %collective-permute-done.34 = bf16[4,3,256,512]{3,2,1,0:T(8,128)(2,1)S(1)} collective-permute-done((bf16[4,3,256,512]{3,2,1,0:T(8,128)(2,1)}, bf16[4,3,256,512]{3,2,1,0:T(8,128)(2,1)S(1)}, u32[]{:S(2)}, u32[]{:S(2)}) %collective-permute-start.34) | collective-permute-done | bytes 3145760 | tf_op jit(solution)/shard_map/ppermute | solution.py:45
  225.6 4.4 add_convert_fusion.1
  230.2 44.0 %experts.6 = (bf16[3,512,1024]{2,1,0:T(8,128)(2,1)}, bf16[3,512,1152]{2,1,0:T(8,128)(2,1)}, f32[3,1024,512]{2,1,0:T(8,128)}, f32[3,1024,512]{2,1,0:T(8,128)}) custom-call(s32[2]{0:T(128)} %get-tuple-element.254.names_ref, bf16[256,1152]{1,0:T(8,128)(2,1)} %copy-done.15, bf16[256,1152]{1,0:T(8,128)(2,1)} %copy-done.16, bf16[256,1152]{1,0:T(8,128)(2,1)} %copy-done.14, ...), custom_call_target="tpu_custom_call" | custom-call | flops 28991029248 | bytes 31457280 | tf_op jit(solution)/shard_map/experts/pallas_call | solution.py:290
  281.2 21.2 %experts.7 = (bf16[1,512,1024]{2,1,0:T(8,128)(2,1)}, bf16[1,512,1152]{2,1,0:T(8,128)(2,1)}, bf16[4,3,256,512]{3,2,1,0:T(8,128)(2,1)}, bf16[4,3,256,512]{3,2,1,0:T(8,128)(2,1)}) custom-call(s32[2]{0:T(128)} %get-tuple-element.254.names_ref, bf16[256,1152]{1,0:T(8,128)(2,1)} %get-tuple-element.107.refs_0_.packet_top_ref, ...), custom_call_target="tpu_custom_call" | custom-call | flops 9663676416 | bytes 23068672 | tf_op jit(solution)/shard_map/experts/pallas_call | solution.py:290
  317.3 7.4 %collective-permute-done.40.near_low_ref = bf16[256,1152]{1,0:T(8,128)(2,1)S(1)} collective-permute-done((bf16[256,1152]{1,0:T(8,128)(2,1)}, bf16[256,1152]{1,0:T(8,128)(2,1)S(1)}, u32[]{:S(2)}, u32[]{:S(2)}) %collective-permute-start.40) | collective-permute-done | bytes 589856 | tf_op jit(solution)/shard_map/ppermute | solution.py:45
  328.3 12.3 %middle_back.1 = (f32[512,1024]{1,0:T(8,128)}, bf16[512,1024]{1,0:T(8,128)(2,1)}, bf16[1024,1152]{1,0:T(8,128)(2,1)}) custom-call(bf16[512,1152]{1,0:T(8,128)(2,1)} %bitcast.215, bf16[256,1152]{1,0:T(8,128)(2,1)} %copy-done.9, bf16[256,1152]{1,0:T(8,128)(2,1)} %copy-done.11, bf16[256,1152]{1,0:T(8,128)(2,1)} %collective-permute-done.41.far_top_ref, ...), custom_call_target="tpu_custom_call" | custom-call | flops 2147483648 | bytes 27795456 | tf_op jit(solution)/shard_map/middle_back/pallas_call | solution.py:588
  350.1 18.8 %attention_back.1.projected_ref = bf16[512,2048]{1,0:T(8,128)(2,1)} custom-call(s32[1]{0:T(128)S(6)} %copy.150.length_ref, bf16[512,2048]{1,0:T(8,128)(2,1)} %get-tuple-element.154.rotated_ref, bf16[512,1024]{1,0:T(8,128)(2,1)} %get-tuple-element.157.mixed_grad_ref, f32[4,4,512]{2,1,0:T(4,128)} %get-tuple-element.158.log_ref, ...), custom_call_target="tpu_custom_call" | custom-call | flops 2684354560 | bytes 6324228 | tf_op jit(solution)/shard_map/attention_back/pallas_call | solution.py:588
  372.3 14.7 %inputs_back.1 = (f32[512,1024]{1,0:T(8,128)}, bf16[1024,2176]{1,0:T(8,128)(2,1)}) custom-call(bf16[512,1024]{1,0:T(8,128)(2,1)} %tokens_ref.5, f32[2,1024]{1,0:T(2,128)} %copy.116.gains_ref, bf16[512,2048]{1,0:T(8,128)(2,1)} %attention_back.1.projected_ref, bf16[1024,3200]{1,0:T(8,128)(2,1)} %bitcast.192, f32[512,1024]{1,0:T(8,128)} %get-tuple-element.163.middle_grad_ref), custom_call_target="tpu_custom_call" | custom-call | flops 4294967296 | bytes 18358272 | tf_op jit(solution)/shard_map/inputs_back/pallas_call | solution.py:588
  398.2 6.7 %collective-permute-done.50 = bf16[64,2176]{1,0:T(8,128)(2,1)S(1)} collective-permute-done((bf16[64,2176]{1,0:T(8,128)(2,1)S(1)}, bf16[64,2176]{1,0:T(8,128)(2,1)S(1)}, u32[]{:S(2)}, u32[]{:S(2)}) %collective-permute-start.50) | collective-permute-done | bytes 278560 | tf_op jit(solution)/shard_map/ppermute | solution.py:45
  407.8 11.0 %collective-permute-done.51 = bf16[128,2176]{1,0:T(8,128)(2,1)S(1)} collective-permute-done((bf16[128,2176]{1,0:T(8,128)(2,1)S(1)}, bf16[128,2176]{1,0:T(8,128)(2,1)S(1)}, u32[]{:S(2)}, u32[]{:S(2)}) %collective-permute-start.51) | collective-permute-done | bytes 557088 | tf_op jit(solution)/shard_map/ppermute | solution.py:45
  422.5 3.7 collective-permute-start.58
  431.1 8.5 %collective-permute-done.61 = bf16[2,2,3,32,512]{4,3,2,1,0:T(8,128)(2,1)S(1)} collective-permute-done((bf16[2,2,3,32,512]{4,3,2,1,0:T(8,128)(2,1)S(1)}, bf16[2,2,3,32,512]{4,3,2,1,0:T(8,128)(2,1)S(1)}, u32[]{:S(2)}, u32[]{:S(2)}) %collective-permute-start.61) | collective-permute-done | bytes 393248 | tf_op jit(solution)/shard_map/ppermute | solution.py:45
  (256 shorter events, 129.6 us)
Async XLA Ops:
  7.2 118.6 %all-gather.3.cloned.1.call-start = ((), (), s32[]{:S(2)}) async-start(), calls=%async_computation.2 | async-start | bytes 3932160 | tf_op jit(solution)/shard_map/all_gather | solution.py:751
  16.2 24.1 %collective-permute-start.6 = (bf16[32,3200]{1,0:T(8,128)(2,1)S(1)}, bf16[32,3200]{1,0:T(8,128)(2,1)S(1)}, u32[]{:S(2)}, u32[]{:S(2)}) collective-permute-start(bf16[32,3200]{1,0:T(8,128)(2,1)S(1)} %concatenate.44), channel_id=1, source_target_pairs={{0,24},{1,25},{2,26},{3,27},{4,28},{5,29},{6,30},{7,31},{8,16},{9,... | collective-permute-start | bytes 614408 | tf_op jit(solution)/shard_map/ppermute | solution.py:45
  42.5 36.8 %collective-permute-start.7 = (bf16[128,3200]{1,0:T(8,128)(2,1)S(1)}, bf16[128,3200]{1,0:T(8,128)(2,1)}, u32[]{:S(2)}, u32[]{:S(2)}) collective-permute-start(bf16[128,3200]{1,0:T(8,128)(2,1)S(1)} %bitcast.194), channel_id=1, source_target_pairs={{0,1},{1,0},{2,3},{3,2},{4,5},{5,4},{6,7},{7,6},{8,9},{9,8},{10,11... | collective-permute-start | bytes 2457608 | tf_op jit(solution)/shard_map/ppermute | solution.py:45
  43.7 21.9 %collective-permute-start.13 = (bf16[64,3200]{1,0:T(8,128)(2,1)}, bf16[64,3200]{1,0:T(8,128)(2,1)S(1)}, u32[]{:S(2)}, u32[]{:S(2)}) collective-permute-start(bf16[64,3200]{1,0:T(8,128)(2,1)} %get-tuple-element.295), channel_id=1, source_target_pairs={{0,4},{1,5},{2,6},{3,7},{4,0},{5,1},{6,2},{7,3},{8,12},{9,13},{10,... | collective-permute-start | bytes 1228808 | tf_op jit(solution)/shard_map/ppermute | solution.py:45
  47.2 20.1 %collective-permute-start.12 = (bf16[64,3200]{1,0:T(8,128)(2,1)}, bf16[64,3200]{1,0:T(8,128)(2,1)S(1)}, u32[]{:S(2)}, u32[]{:S(2)}) collective-permute-start(bf16[64,3200]{1,0:T(8,128)(2,1)} %get-tuple-element.294), channel_id=1, source_target_pairs={{0,4},{1,5},{2,6},{3,7},{4,0},{5,1},{6,2},{7,3},{8,12},{9,13},{10,... | collective-permute-start | bytes 1228808 | tf_op jit(solution)/shard_map/ppermute | solution.py:45
  49.2 167.2 %all-gather.5.cloned.1.call-start = ((), (), s32[]{:S(2)}) async-start(), calls=%async_computation.3 | async-start | bytes 3932160 | tf_op jit(solution)/shard_map/all_gather | solution.py:751
  56.2 25.0 %collective-permute-start.11 = (bf16[64,3200]{1,0:T(8,128)(2,1)}, bf16[64,3200]{1,0:T(8,128)(2,1)S(1)}, u32[]{:S(2)}, u32[]{:S(2)}) collective-permute-start(bf16[64,3200]{1,0:T(8,128)(2,1)} %collective-permute-done.9), channel_id=1, source_target_pairs={{0,1},{1,0},{2,3},{3,2},{4,5},{5,4},{6,7},{7,6},{8,9},{9,8},{10,11... | collective-permute-start | bytes 1228808 | tf_op jit(solution)/shard_map/ppermute | solution.py:45
  79.4 31.7 %collective-permute-start.20 = (bf16[256,1024]{1,0:T(8,128)(2,1)}, bf16[256,1024]{1,0:T(8,128)(2,1)}, u32[]{:S(2)}, u32[]{:S(2)}) collective-permute-start(bf16[256,1024]{1,0:T(8,128)(2,1)} %get-tuple-element.97.refs_2_), channel_id=1, source_target_pairs={{0,2},{1,3},{2,0},{3,1},{4,6},{5,7},{6,4},{7,5},{8,10},{9,11},{10,... | collective-permute-start | bytes 1572872 | tf_op jit(solution)/shard_map/ppermute | solution.py:45
  81.3 29.8 %collective-permute-start.22 = (bf16[256,1024]{1,0:T(8,128)(2,1)}, bf16[256,1024]{1,0:T(8,128)(2,1)}, u32[]{:S(2)}, u32[]{:S(2)}) collective-permute-start(bf16[256,1024]{1,0:T(8,128)(2,1)} %get-tuple-element.97.refs_2_), channel_id=1, source_target_pairs={{0,4},{1,5},{2,6},{3,7},{4,0},{5,1},{6,2},{7,3},{8,12},{9,13},{10,... | collective-permute-start | bytes 1572872 | tf_op jit(solution)/shard_map/ppermute | solution.py:45
  81.7 29.4 %collective-permute-start.21 = (bf16[256,1024]{1,0:T(8,128)(2,1)}, bf16[256,1024]{1,0:T(8,128)(2,1)}, u32[]{:S(2)}, u32[]{:S(2)}) collective-permute-start(bf16[256,1024]{1,0:T(8,128)(2,1)} %get-tuple-element.98.refs_3_), channel_id=1, source_target_pairs={{0,2},{1,3},{2,0},{3,1},{4,6},{5,7},{6,4},{7,5},{8,10},{9,11},{10,... | collective-permute-start | bytes 1572872 | tf_op jit(solution)/shard_map/ppermute | solution.py:45
  85.4 25.6 %collective-permute-start.23 = (bf16[256,1024]{1,0:T(8,128)(2,1)}, bf16[256,1024]{1,0:T(8,128)(2,1)}, u32[]{:S(2)}, u32[]{:S(2)}) collective-permute-start(bf16[256,1024]{1,0:T(8,128)(2,1)} %get-tuple-element.98.refs_3_), channel_id=1, source_target_pairs={{0,4},{1,5},{2,6},{3,7},{4,0},{5,1},{6,2},{7,3},{8,12},{9,13},{10,... | collective-permute-start | bytes 1572872 | tf_op jit(solution)/shard_map/ppermute | solution.py:45
  126.7 243.9 %reduce-scatter.3.cloned.1.call-start = ((), (), s32[]{:S(2)}) async-start(), calls=%async_computation.4 | async-start | bytes 3932160 | tf_op jit(solution)/shard_map/reduce_scatter | solution.py:800
  127.5 22.9 %collective-permute-start.26 = (bf16[256,1152]{1,0:T(8,128)(2,1)S(1)}, bf16[256,1152]{1,0:T(8,128)(2,1)S(1)}, u32[]{:S(2)}, u32[]{:S(2)}) collective-permute-start(bf16[256,1152]{1,0:T(8,128)(2,1)S(1)} %copy-done.7), channel_id=1, source_target_pairs={{0,2},{1,3},{2,0},{3,1},{4,6},{5,7},{6,4},{7,5},{8,10},{9,11},{10,... | collective-permute-start | bytes 1769480 | tf_op jit(solution)/shard_map/ppermute | solution.py:45
  128.1 27.9 %collective-permute-start.27 = (bf16[256,1152]{1,0:T(8,128)(2,1)S(1)}, bf16[256,1152]{1,0:T(8,128)(2,1)}, u32[]{:S(2)}, u32[]{:S(2)}) collective-permute-start(bf16[256,1152]{1,0:T(8,128)(2,1)S(1)} %copy-done.8), channel_id=1, source_target_pairs={{0,2},{1,3},{2,0},{3,1},{4,6},{5,7},{6,4},{7,5},{8,10},{9,11},{10,... | collective-permute-start | bytes 1769480 | tf_op jit(solution)/shard_map/ppermute | solution.py:45
  129.6 26.5 %collective-permute-start.28 = (bf16[256,1152]{1,0:T(8,128)(2,1)S(1)}, bf16[256,1152]{1,0:T(8,128)(2,1)}, u32[]{:S(2)}, u32[]{:S(2)}) collective-permute-start(bf16[256,1152]{1,0:T(8,128)(2,1)S(1)} %copy-done.7), channel_id=1, source_target_pairs={{0,4},{1,5},{2,6},{3,7},{4,0},{5,1},{6,2},{7,3},{8,12},{9,13},{10,... | collective-permute-start | bytes 1769480 | tf_op jit(solution)/shard_map/ppermute | solution.py:45
  130.8 26.7 %collective-permute-start.29 = (bf16[256,1152]{1,0:T(8,128)(2,1)S(1)}, bf16[256,1152]{1,0:T(8,128)(2,1)}, u32[]{:S(2)}, u32[]{:S(2)}) collective-permute-start(bf16[256,1152]{1,0:T(8,128)(2,1)S(1)} %copy-done.8), channel_id=1, source_target_pairs={{0,4},{1,5},{2,6},{3,7},{4,0},{5,1},{6,2},{7,3},{8,12},{9,13},{10,... | collective-permute-start | bytes 1769480 | tf_op jit(solution)/shard_map/ppermute | solution.py:45
  230.1 157.2 %reduce-scatter.5.cloned.1.call-start = ((), (), s32[]{:S(2)}) async-start(), calls=%async_computation.5 | async-start | bytes 3932160 | tf_op jit(solution)/shard_map/reduce_scatter | solution.py:800
  277.1 25.3 %collective-permute-start.35 = (bf16[256,1152]{1,0:T(8,128)(2,1)}, bf16[256,1152]{1,0:T(8,128)(2,1)}, u32[]{:S(2)}, u32[]{:S(2)}) collective-permute-start(bf16[256,1152]{1,0:T(8,128)(2,1)} %get-tuple-element.264), channel_id=1, source_target_pairs={{0,2},{1,3},{2,0},{3,1},{4,6},{5,7},{6,4},{7,5},{8,10},{9,11},{10,... | collective-permute-start | bytes 1769480 | tf_op jit(solution)/shard_map/ppermute | solution.py:45
  277.3 25.1 %collective-permute-start.36 = (bf16[256,1152]{1,0:T(8,128)(2,1)}, bf16[256,1152]{1,0:T(8,128)(2,1)}, u32[]{:S(2)}, u32[]{:S(2)}) collective-permute-start(bf16[256,1152]{1,0:T(8,128)(2,1)} %get-tuple-element.263), channel_id=1, source_target_pairs={{0,4},{1,5},{2,6},{3,7},{4,0},{5,1},{6,2},{7,3},{8,12},{9,13},{10,... | collective-permute-start | bytes 1769480 | tf_op jit(solution)/shard_map/ppermute | solution.py:45
  278.0 27.4 %collective-permute-start.37 = (bf16[256,1152]{1,0:T(8,128)(2,1)}, bf16[256,1152]{1,0:T(8,128)(2,1)S(1)}, u32[]{:S(2)}, u32[]{:S(2)}) collective-permute-start(bf16[256,1152]{1,0:T(8,128)(2,1)} %get-tuple-element.262), channel_id=1, source_target_pairs={{0,2},{1,3},{2,0},{3,1},{4,6},{5,7},{6,4},{7,5},{8,10},{9,11},{10,... | collective-permute-start | bytes 1769480 | tf_op jit(solution)/shard_map/ppermute | solution.py:45
  279.9 25.4 %collective-permute-start.38 = (bf16[256,1152]{1,0:T(8,128)(2,1)S(1)}, bf16[256,1152]{1,0:T(8,128)(2,1)S(1)}, u32[]{:S(2)}, u32[]{:S(2)}) collective-permute-start(bf16[256,1152]{1,0:T(8,128)(2,1)S(1)} %get-tuple-element.261), channel_id=1, source_target_pairs={{0,4},{1,5},{2,6},{3,7},{4,0},{5,1},{6,2},{7,3},{8,12},{9,13},{10,... | collective-permute-start | bytes 1769480 | tf_op jit(solution)/shard_map/ppermute | solution.py:45
  343.1 25.8 %collective-permute-start.42 = (bf16[4,4,32,1152]{3,2,1,0:T(8,128)(2,1)}, bf16[4,4,32,1152]{3,2,1,0:T(8,128)(2,1)S(1)}, u32[]{:S(2)}, u32[]{:S(2)}) collective-permute-start(bf16[4,4,32,1152]{3,2,1,0:T(8,128)(2,1)} %dynamic-slice_bitcast_fusion.1), channel_id=1, source_target_pairs={{0,1},{1,0},{2,3},{3,2},{4,5},{5,4},{6,7},{7,6},{8,9},{9,8},{10,11... | collective-permute-start | bytes 3538952 | tf_op jit(solution)/shard_map/ppermute | solution.py:45
  347.6 39.7 %collective-permute-start.47 = (bf16[512,1024]{1,0:T(8,128)(2,1)}, bf16[512,1024]{1,0:T(8,128)(2,1)}, u32[]{:S(2)}, u32[]{:S(2)}) collective-permute-start(bf16[512,1024]{1,0:T(8,128)(2,1)} %get-tuple-element.165), channel_id=1, source_target_pairs={{0,2},{1,3},{2,0},{3,1},{4,6},{5,7},{6,4},{7,5},{8,10},{9,11},{10,... | collective-permute-start | bytes 3145736 | tf_op jit(solution)/shard_map/ppermute | solution.py:45
  349.1 38.2 %collective-permute-start.48 = (bf16[512,1024]{1,0:T(8,128)(2,1)}, bf16[512,1024]{1,0:T(8,128)(2,1)}, u32[]{:S(2)}, u32[]{:S(2)}) collective-permute-start(bf16[512,1024]{1,0:T(8,128)(2,1)} %get-tuple-element.166), channel_id=1, source_target_pairs={{0,4},{1,5},{2,6},{3,7},{4,0},{5,1},{6,2},{7,3},{8,12},{9,13},{10,... | collective-permute-start | bytes 3145736 | tf_op jit(solution)/shard_map/ppermute | solution.py:45
  (60 other events, 636.3 us)
Sparse Core Ops, SparseCore 0:
  49.3 63.7 all-gather.2
  126.8 63.5 all-gather.4
  230.2 59.8 reduce-scatter.2
  326.2 59.8 reduce-scatter.4
